TPU v7x, 256 devices: a whole 4x4x8 slice. The times are simulated.
256 devices in a mesh: dp: 32 (over z, y_lo, core), node: 8 (over y_hi, x).
Axes of the slice: x: 4, y: 4 (y_hi: 2, y_lo: 2; y = y_hi * 2 + y_lo), z: 8, core: 2. Of those that a mesh axis runs over, the one named last changes fastest.
Arguments:
- tokens: bfloat16 [32768, 3072], P(('dp', 'node')), may hold values from -6 to 6
- cotangent: bfloat16 [32768, 3072], P(('dp', 'node')), may hold values from -6 to 6
- levels: bfloat16 [3072, 3072], P('node'), may hold values from -127 to 127, as said below
- scales: float32 [3072, 12], P('node'), may hold values from 0.00012 to 0.00048
Outputs:
- forward: bfloat16 [32768, 3072], P(('dp', 'node'))
- grad_input: bfloat16 [32768, 3072], P(('dp', 'node'))
- grad_weight: float32 [3072, 3072], P(('dp', 'node'))
Inputs may be any that keep to these rules, and one draw needn't show every extreme that they name: `levels`: every entry is a whole number.
All inputs are finite; a program needn't handle non-finite values.
Results may differ from a plain program's by a relative error of at most 0.0049.
Values may be sent and summed in bfloat16 or wider, within the bound.
No kernel may reach another device: no remote copies, remote signals or barrier semaphores. Data moves between devices by JAX's collectives and lax.ppermute only.
A program may use at most 192 MiB of HBM per device.

v0:
```python
import jax
import jax.numpy as jnp
from jax import lax
from jax.sharding import PartitionSpec as P


def dequantize(level_rows, scale_rows):
    row_count, width = level_rows.shape
    blocked = level_rows.astype(jnp.float32).reshape(
        row_count, scale_rows.shape[1], width // scale_rows.shape[1]
    )
    return (blocked * scale_rows[:, :, None]).reshape(row_count, width).astype(jnp.bfloat16)


def on_device(tokens, cotangent, levels, scales):
    node_count = lax.axis_size("node")
    replica_count = lax.axis_size("dp")
    token_rows, features = tokens.shape
    shard_rows, outputs = levels.shape
    sub_rows = features // (node_count * replica_count)
    factor = float(token_rows * node_count * replica_count) ** (-0.5)
    every_scale = lax.all_gather(scales, "node", axis=0, tiled=True)
    weight = dequantize(lax.all_gather(levels, "node", axis=0, tiled=True), every_scale)
    summed_out = jnp.dot(tokens, weight, preferred_element_type=jnp.float32)
    columns = lax.dot_general(
        cotangent, weight, (((1,), (1,)), ((), ())), preferred_element_type=jnp.float32
    )
    input_back = columns
    summed_out, input_back = (summed_out, input_back)
    forward = summed_out.astype(jnp.bfloat16)
    grad_input = input_back.astype(jnp.bfloat16)
    every_cotangent = lax.all_gather(cotangent, "node", axis=0, tiled=True)
    shaped = tokens.reshape(token_rows, replica_count, node_count, sub_rows)
    picked = lax.all_to_all(shaped, "node", split_axis=2, concat_axis=0, tiled=True).reshape(
        node_count * token_rows, replica_count * sub_rows
    )
    product = lax.dot_general(
        picked, every_cotangent, (((0,), (0,)), ((), ())), preferred_element_type=jnp.float32
    )
    node_part = product * factor
    stacked = node_part.reshape(replica_count, sub_rows, outputs)
    reduced = lax.psum_scatter(stacked, "dp", scatter_dimension=0, tiled=True)
    return (forward, grad_input, reduced.reshape(sub_rows, outputs))


def solution(mesh):
    in_specs = (P(("dp", "node"), None), P(("dp", "node"), None), P("node", None), P("node", None))
    out_specs = (P(("dp", "node"), None), P(("dp", "node"), None), P(("dp", "node"), None))
    return jax.shard_map(
        on_device, mesh=mesh, in_specs=in_specs, out_specs=out_specs, check_vma=False
    )
```

profile of v0, /device:TPU:24, one launch (start us, length us, event | category | flops | bytes accessed | tf_op | source)
XLA Modules:
  0.0 477.5 jit_solution(4190435769086688889)
XLA Ops:
  7.2 0.0 all-gather.5.cloned.1.call-start
  7.2 0.7 all-gather.5.cloned.1.call-update
  7.9 0.0 all-gather.3.cloned.1.call-start
  7.9 4.3 copy.15
  12.2 0.0 all-gather.3.cloned.1.call-update
  12.2 0.0 reduce-scatter.2.cloned.1.call-start
  12.3 1.5 copy.16
  13.8 0.0 copy-start.3
  13.8 0.2 reshape.23
  14.0 0.5 copy.17
  14.5 20.6 %all_to_all.15 = bf16[128,32,8,12]{0,1,3,2:T(8,128)(2,1)S(1)} all-to-all(bf16[128,32,8,12]{0,1,3,2:T(8,128)(2,1)S(1)} %copy.17), channel_id=1, replica_groups=mesh['dp'=32,'node'=8] {'node'}, dimensions={2} | all-to-all | bytes 1572864 | tf_op jit(solution)/shard_map/all_to_all | solution.py:34
  35.2 0.5 copy.18
  35.7 74.6 %all-gather.5.cloned.1.call-done = bf16[1024,3072]{1,0:T(8,128)(2,1)} async-done(((bf16[128,3072]{1,0:T(8,128)(2,1)}), bf16[1024,3072]{1,0:T(8,128)(2,1)}) %all-gather.5.cloned.1.call-update) | async-done | bytes 6291472 | tf_op jit(solution)/shard_map/all_gather | solution.py:32
  110.3 7.1 %convolution_multiply_fusion = f32[384,3072]{1,0:T(8,128)} fusion(bf16[1024,3072]{1,0:T(8,128)(2,1)} %all-gather.5.cloned.1.call-done, bf16[48,8,8,128]{3,2,1,0:T(8,128)(2,1)S(1)} %bitcast.27), kind=kOutput, calls=%fused_computation.2 | convolution fusion | flops 2417098752 | bytes 11796480 | tf_op jit(solution)/shard_map/dot_general | solution.py:37
  117.4 5.5 %reshape.25 = f32[32,12,3072]{2,1,0:T(8,128)} reshape(f32[384,3072]{1,0:T(8,128)} %convolution_multiply_fusion) | data formatting | bytes 9437184 | tf_op jit(solution)/shard_map/reshape | solution.py:41
  122.9 0.0 reduce-scatter.2.cloned.1.call-update
  122.9 0.0 copy-done.3
  122.9 35.3 %all_gather.10 = f32[3072,12]{0,1:T(8,128)S(1)} all-gather(f32[384,12]{0,1:T(8,128)S(1)} %copy-done.3), channel_id=1, replica_groups=mesh['dp'=32,'node'=8] {'node'}, dimensions={0}, use_global_device_ids=true | all-gather | bytes 165888 | tf_op jit(solution)/shard_map/all_gather | solution.py:22
  158.2 0.0 copy-start.1
  158.2 186.5 %all-gather.3.cloned.1.call-done = bf16[3072,3072]{0,1:T(8,128)(2,1)} async-done(((bf16[384,3072]{0,1:T(8,128)(2,1)}), bf16[3072,3072]{0,1:T(8,128)(2,1)}) %all-gather.3.cloned.1.call-update) | async-done | bytes 18874384 | tf_op jit(solution)/shard_map/all_gather | solution.py:23
  344.8 11.0 %fusion = bf16[3072,3072]{0,1:T(8,128)(2,1)S(1)} fusion(bf16[3072,3072]{0,1:T(8,128)(2,1)} %all-gather.3.cloned.1.call-done, f32[3072,12]{0,1:T(8,128)S(1)} %all_gather.10), kind=kLoop, calls=%fused_computation.1 | loop fusion | flops 28311552 | bytes 37896192 | tf_op jit(solution)/shard_map/convert_element_type | solution.py:12
  355.8 0.0 copy-start
  355.8 6.5 %copy-done = bf16[3072,3072]{0,1:T(8,128)(2,1)} copy-done((bf16[3072,3072]{0,1:T(8,128)(2,1)}, bf16[3072,3072]{0,1:T(8,128)(2,1)S(1)}, u32[]{:S(2)}) %copy-start) | copy-done | bytes 18874392
  362.3 0.0 copy-done.1
  362.3 0.0 copy-start.2
  362.3 5.3 %fusion.1 = bf16[128,3072]{0,1:T(8,128)(2,1)S(1)} fusion(bf16[3072,3072]{0,1:T(8,128)(2,1)S(1)} %fusion, bf16[128,3072]{1,0:T(8,128)(2,1)S(1)} %copy-done.1), kind=kOutput, calls=%fused_computation.5 | convolution fusion | flops 2416312320 | bytes 20447232 | tf_op jit(solution)/shard_map/dot_general | solution.py:24
  367.6 1.2 copy.19
  368.8 0.0 copy-done.2
  368.8 9.2 %fusion.2 = bf16[128,3072]{0,1:T(8,128)(2,1)S(1)} fusion(bf16[3072,3072]{0,1:T(8,128)(2,1)} %copy-done, bf16[128,3072]{1,0:T(8,128)(2,1)S(1)} %copy-done.2), kind=kOutput, calls=%fused_computation.6 | convolution fusion | flops 2416312320 | bytes 20447232 | tf_op jit(solution)/shard_map/dot_general | solution.py:25
  378.0 1.2 copy.20
  379.2 91.8 %reduce-scatter.2.cloned.1.call-done = f32[1,12,3072]{2,1,0:T(8,128)} async-done(((f32[32,12,3072]{2,1,0:T(8,128)}), f32[1,12,3072]{2,1,0:T(8,128)}) %reduce-scatter.2.cloned.1.call-update) | async-done | bytes 147472 | tf_op jit(solution)/shard_map/reduce_scatter | solution.py:42
Async XLA Ops:
  7.2 103.1 %all-gather.5.cloned.1.call-start = ((), (), s32[]{:S(2)}) async-start(), calls=%async_computation.3 | async-start | bytes 7077888 | tf_op jit(solution)/shard_map/all_gather | solution.py:32
  7.9 336.9 %all-gather.3.cloned.1.call-start = ((), (), s32[]{:S(2)}) async-start(), calls=%async_computation.2 | async-start | bytes 21233664 | tf_op jit(solution)/shard_map/all_gather | solution.py:23
  12.2 458.7 %reduce-scatter.2.cloned.1.call-start = ((), (), s32[]{:S(2)}) async-start(), calls=%async_computation.4 | async-start | bytes 6488064 | tf_op jit(solution)/shard_map/reduce_scatter | solution.py:42
  13.8 109.1 %copy-start.3 = (f32[384,12]{0,1:T(8,128)S(1)}, f32[384,12]{0,1:T(8,128)}, u32[]{:S(2)}) copy-start(f32[384,12]{0,1:T(8,128)} %param.7) | copy-start | bytes 55300
  158.2 204.0 %copy-start.1 = (bf16[128,3072]{1,0:T(8,128)(2,1)S(1)}, bf16[128,3072]{1,0:T(8,128)(2,1)}, u32[]{:S(2)}) copy-start(bf16[128,3072]{1,0:T(8,128)(2,1)} %param.4) | copy-start | bytes 2359300
  355.8 6.5 %copy-start = (bf16[3072,3072]{0,1:T(8,128)(2,1)}, bf16[3072,3072]{0,1:T(8,128)(2,1)S(1)}, u32[]{:S(2)}) copy-start(bf16[3072,3072]{0,1:T(8,128)(2,1)S(1)} %fusion) | copy-start | bytes 56623108
  362.3 6.5 %copy-start.2 = (bf16[128,3072]{1,0:T(8,128)(2,1)S(1)}, bf16[128,3072]{1,0:T(8,128)(2,1)}, u32[]{:S(2)}) copy-start(bf16[128,3072]{1,0:T(8,128)(2,1)} %param.5) | copy-start | bytes 2359300
Sparse Core Ops, SparseCore 0:
  10.6 99.6 all-gather.4
  112.7 232.0 all-gather.2
  347.9 123.0 reduce-scatter.1
where the time goes:
time: 483 us; the launch traced here: 478 us
  waiting for transfers between devices  354 us (73%)
  blocking collectives  55.9 us (12%)
  matrix products  21.7 us (4%)
  local copies, waits for them, and re-layouts  21.3 us (4%)
  between operations  13.8 us (3%)
  other arithmetic  11 us (2%)
    all_gather x1, waiting for transfers between devices, on_device(): lax.all_gather(levels, 'node', axis=0, tiled=True)  187 us
    reduce_scatter x1, waiting for transfers between devices, on_device(): reduced = lax.psum_scatter(stacked, 'dp', scatter_dimension=0, tiled=True)  91.8 us
    all_gather x1, waiting for transfers between devices, on_device(): every_cotangent = lax.all_gather(cotangent, 'node', axis=0, tiled=True)  74.6 us
    all_gather x1, blocking collectives, on_device(): every_scale = lax.all_gather(scales, 'node', axis=0, tiled=True)  35.3 us
    all_to_all x1, blocking collectives, on_device(): lax.all_to_all(shaped, 'node', split_axis=2, concat_axis=0, tiled=True)  20.6 us
    unnamed x12, local copies, waits for them, and re-layouts  14.6 us
    convert_element_type x1, other arithmetic, dequantize(): (blocked * scale_rows[:, :, None]).reshape(row_count, width)  11 us
  transfers between devices with their start and end apart: 3, of which 3 were waited for; matrix products, arithmetic and copies ran while one was open for 10% of the time, Pallas kernels for 0%

commit v1 on v0

v1 whole, which is shorter than its diff:
```python
import jax
import jax.numpy as jnp
from jax import lax
from jax.experimental import pallas as pl
from jax.experimental.pallas import tpu as pltpu
from jax.sharding import Mesh, PartitionSpec as P

AXES = ("z", "yl", "c", "yh", "x")
SIZES = (8, 2, 2, 2, 4)
BLOCK_STEPS = (0, 3, 1, 2)


def table(move):
    pairs = []
    for z in range(8):
        for yl in range(2):
            for c in range(2):
                for yh in range(2):
                    for x in range(4):
                        pairs.append((place(z, yl, c, yh, x), place(*move(z, yl, c, yh, x))))
    return pairs


def place(z, yl, c, yh, x):
    return (((z % 8 * 2 + yl % 2) * 2 + c % 2) * 2 + yh % 2) * 4 + x % 4


def turn(yh, c):
    return 1 - (yh + c) % 2


def owner(z, yl, c, yh, x, message):
    z_owner = 4 * yh + 2 * c + (z // 4 + turn(yh, c)) % 2
    return z_owner, z % 4 // 2, z % 2, x // 2, x % 2 * 2 + (yl ^ message)


X_UP = table(lambda z, yl, c, yh, x: (z, yl, c, yh, x + 1))
X_DOWN = table(lambda z, yl, c, yh, x: (z, yl, c, yh, x - 1))
CORE = table(lambda z, yl, c, yh, x: (z, yl, c + 1, yh, x))
PAIR = table(lambda z, yl, c, yh, x: (z, yl + 1, c, yh + 1, x))
PAIR_CROSS = table(lambda z, yl, c, yh, x: (z, yl + 1, c + 1, yh + 1, x))
OWNERS = [
    table(lambda z, yl, c, yh, x: owner(z, yl, c, yh, x, message)) for message in range(2)
]


def send(value, pairs):
    return lax.ppermute(value, AXES, pairs)


def after(values, *earlier):
    return lax.optimization_barrier((values, earlier))[0]


def f32(value):
    return value.astype(jnp.float32)


def bf16(value):
    return value.astype(jnp.bfloat16)


def call(kernel, name, where, grid, in_specs, out_specs, out_shape, scratch, flops, operands):
    moved = sum(v.size * v.dtype.itemsize for v in operands)
    moved += sum(v.size * v.dtype.itemsize for v in jax.tree.leaves(out_shape))
    return pl.pallas_call(
        kernel,
        name=name,
        grid_spec=pltpu.PrefetchScalarGridSpec(
            num_scalar_prefetch=1,
            grid=grid,
            in_specs=in_specs,
            out_specs=out_specs,
            scratch_shapes=scratch,
        ),
        out_shape=out_shape,
        compiler_params=pltpu.CompilerParams(vmem_limit_bytes=48 * 2**20),
        cost_estimate=pl.CostEstimate(flops=flops, bytes_accessed=moved, transcendentals=0),
    )(where, *operands)


def fixed(shape, at=lambda where: (0, 0)):
    return pl.BlockSpec(shape, lambda i, where: at(where))


def dequantize_kernel(where, levels, scales, out):
    c = where[0]
    count = scales.shape[1] // 2
    width = out.shape[1] // count
    for b in range(count):
        scale = jnp.where(c == 0, scales[:, b : b + 1], scales[:, count + b : count + b + 1])
        span = slice(b * width, (b + 1) * width)
        out[:, span] = bf16(f32(levels[:, span]) * scale)


def dequantize(where, levels, scales):
    row_count, nh = levels.shape[0], levels.shape[1] // 2
    size = row_count // 3
    return call(
        dequantize_kernel,
        "dequantize",
        where,
        (3,),
        [
            pl.BlockSpec((size, nh), lambda i, where: (i, where[0])),
            pl.BlockSpec((size, scales.shape[1]), lambda i, where: (i, 0)),
        ],
        pl.BlockSpec((size, nh), lambda i, where: (i, 0)),
        jax.ShapeDtypeStruct((row_count, nh), jnp.bfloat16),
        [],
        row_count * nh,
        (levels, scales),
    )


def columns(ref, start, size):
    return ref[:, pl.ds(pl.multiple_of(start, 128), size)]


def gradient_kernel(where, own, sib, pair, psib, cot0, cot1, cot2, cot3, out, lhs):
    c, yh = where[0], where[1]
    half = lhs.shape[0] // 2
    count = own.shape[0]

    @pl.when(pl.program_id(0) == 0)
    def _():
        for r, (ref, base) in enumerate(((own, yh), (sib, yh), (pair, 0), (psib, 0))):
            for h in range(2):
                start = base * 4 * half + c * 2 * half + (h + 1 - (yh + c) % 2) % 2 * half
                block = f32(columns(ref, start, half))
                lhs[h * half : (h + 1) * half, r * count : (r + 1) * count] = bf16(block.T)

    rhs = jnp.concatenate([cot0[...], cot1[...], cot2[...], cot3[...]])
    out[...] = bf16(jnp.dot(lhs[...], rhs, preferred_element_type=jnp.float32))


def gradient(where, token_parts, cot_parts):
    count, outputs = cot_parts[0].shape
    size = token_parts[0].shape[1] // 4
    width = outputs // 6
    return call(
        gradient_kernel,
        "gradient",
        where,
        (6,),
        [fixed(v.shape) for v in token_parts]
        + [pl.BlockSpec((count, width), lambda i, where: (0, i)) for _ in cot_parts],
        pl.BlockSpec((size, width), lambda i, where: (0, i)),
        jax.ShapeDtypeStruct((size, outputs), jnp.bfloat16),
        [pltpu.VMEM((size, 4 * count), jnp.bfloat16)],
        8 * count * size * outputs,
        (*token_parts, *cot_parts),
    )


def forward_kernel(where, own, sib, pair, psib, w0, w1, w2, w3, w4, mine, other, away, cross, lhs):
    yh, x = where[1], where[2]
    count, shard = own.shape[0], w0.shape[0]

    @pl.when(pl.program_id(0) == 0)
    def _():
        for r, (ref, base) in enumerate(((own, yh), (sib, yh), (pair, 0), (psib, 0))):
            for p, step in enumerate(BLOCK_STEPS):
                start = base * 4 * shard + (x + step) % 4 * shard
                lhs[r * count : (r + 1) * count, p * shard : (p + 1) * shard] = columns(
                    ref, start, shard
                )

    far = jnp.where(pl.program_id(0) == 0, w3[...], w4[...])
    rhs = jnp.concatenate([w0[...], w1[...], w2[...], far])
    out = jnp.dot(lhs[...], rhs, preferred_element_type=jnp.float32)
    mine[...] = out[:count]
    other[...] = out[count : 2 * count]
    away[...] = bf16(out[2 * count : 3 * count])
    cross[...] = bf16(out[3 * count :])


def forward_parts(where, token_parts, blocks):
    count = token_parts[0].shape[0]
    shard, nh = blocks[0].shape
    width = nh // 2
    types = (jnp.float32, jnp.float32, jnp.bfloat16, jnp.bfloat16)
    return call(
        forward_kernel,
        "forward",
        where,
        (2,),
        [fixed(v.shape) for v in token_parts]
        + [pl.BlockSpec((shard, width), lambda i, where: (0, i))] * 3
        + [fixed((shard, width))] * 2,
        [pl.BlockSpec((count, width), lambda i, where: (0, i))] * 4,
        [jax.ShapeDtypeStruct((count, nh), kind) for kind in types],
        [pltpu.VMEM((4 * count, 4 * shard), jnp.bfloat16)],
        32 * count * shard * nh,
        (*token_parts, *blocks),
    )


def backward_kernel(where, cot0, cot1, cot2, cot3, w0, w1, w2, w3, w4, mine, give, lhs):
    x = where[2]
    i = pl.program_id(0)
    count = cot0.shape[0]
    size, half = w3.shape

    @pl.when(i == 0)
    def _():
        for r, ref in enumerate((cot0, cot2, cot1, cot3)):
            lhs[r * count : (r + 1) * count] = ref[...]

    far = jnp.concatenate([w3[...], w4[...]], axis=1)
    rhs = jnp.concatenate([w0[...], w1[...], w2[...], far])
    out = lax.dot_general(
        lhs[...], rhs, (((1,), (1,)), ((), ())), preferred_element_type=jnp.float32
    )
    for p, step in enumerate(BLOCK_STEPS):
        start = pl.multiple_of((x + step) % 4 * 3 * size + i * size, 128)
        part = out[:, p * size : (p + 1) * size]
        mine[:, pl.ds(start, size)] = part[: 2 * count]
        give[:, pl.ds(start, size)] = bf16(part[2 * count :])


def backward_parts(where, cot_parts, blocks):
    count = cot_parts[0].shape[0]
    shard, nh = blocks[0].shape
    size = shard // 3
    types = (jnp.float32, jnp.bfloat16)
    return call(
        backward_kernel,
        "backward",
        where,
        (3,),
        [fixed((count, nh), lambda where: (0, where[0])) for _ in cot_parts]
        + [pl.BlockSpec((size, nh), lambda i, where: (i, 0))] * 3
        + [pl.BlockSpec((size, nh // 2), lambda i, where: (i, 0))] * 2,
        [fixed((2 * count, 4 * shard))] * 2,
        [jax.ShapeDtypeStruct((2 * count, 4 * shard), kind) for kind in types],
        [pltpu.VMEM((4 * count, nh), jnp.bfloat16)],
        32 * count * shard * nh,
        (*cot_parts, *blocks),
    )


def rows(value, start, size):
    return lax.dynamic_slice_in_dim(value, start, size, 0)


def joined(here, there, flag):
    return jnp.where(
        flag == 0, jnp.concatenate([here, there], axis=1), jnp.concatenate([there, here], axis=1)
    )


def reduce_over_x(part, x):
    size = part.shape[0] // 4
    total = f32(rows(part, x * size, size))
    for dx in range(1, 4):
        to = table(lambda z, yl, c, yh, x: (z, yl, c, yh, x + dx))
        total = total + f32(send(rows(part, (x + dx) % 4 * size, size), to))
    return total


def on_device(tokens, cotangent, levels, scales):
    z, yl, c, yh, x = (lax.axis_index(name) for name in AXES)
    where = jnp.stack([c, yh, x]).astype(jnp.int32)
    count, features = tokens.shape
    kh = features // 2
    factor = float(count * 256) ** -0.5

    cot_pair = send(cotangent, PAIR)
    token_out = lax.dynamic_slice_in_dim(tokens, (1 - yh) * kh, kh, 1)
    token_pair = send(token_out, PAIR)

    levels, scales = after((levels, scales), token_out)
    own = dequantize(where, levels, scales)
    left, right = send(own, X_UP), send(own, X_DOWN)

    token_pair, cot_pair = after((token_pair, cot_pair), own)
    cot_sib, token_sib = send(cotangent, CORE), send(tokens, CORE)
    token_parts = (tokens, token_sib, token_pair, send(token_pair, CORE))
    cot_parts = (cotangent, cot_sib, cot_pair, send(cot_pair, CORE))

    part = gradient(where, token_parts, after(cot_parts, left, right))
    part = lax.psum_scatter(part, "z", scatter_dimension=0, tiled=True)

    half = own.shape[1] // 2
    blocks = (own, left, right, send(left[:, :half], X_UP), send(right[:, half:], X_DOWN))
    mine, other, away, cross = forward_parts(where, token_parts, blocks)
    back, back_cross, here = send(away, PAIR), send(cross, PAIR_CROSS), send(other, CORE)
    forward = joined(bf16(mine + f32(back)), bf16(here + f32(back_cross)), c)

    cot_parts = after(cot_parts, away)
    mine, give = backward_parts(where, cot_parts, blocks)
    mine = mine + f32(send(give, CORE))
    grad_input = joined(bf16(mine[:count]), send(bf16(mine[count:]), PAIR), yh)

    total = reduce_over_x(part, x) * factor
    size = total.shape[0] // 2
    got = [send(rows(total, (yl ^ m) * size, size), OWNERS[m]) for m in range(2)]
    return forward, grad_input, got[0] + got[1]


def solution(mesh):
    fine = Mesh(mesh.devices.reshape(SIZES), AXES)
    token_spec, node_spec = P(AXES, None), P(("yh", "x"), None)
    return jax.shard_map(
        on_device,
        mesh=fine,
        in_specs=(token_spec, token_spec, node_spec, node_spec),
        out_specs=(token_spec, token_spec, token_spec),
        check_vma=False,
    )
```

time: 483 us -> 168 us (0.35)
  the two profiles are of different devices: /device:TPU:24 before, /device:TPU:27 now
where the time goes in v1:
time: 168 us; the launch traced here: 167 us
  waiting for transfers between devices  81.1 us (48%)
  starting transfers between devices  30.3 us (18%)
  Pallas kernels  22.4 us (13%)
  between operations  14.2 us (8%)
  local copies, waits for them, and re-layouts  14 us (8%)
  other arithmetic  5.2 us (3%)
    ppermute x20, waiting for transfers between devices, send(): return lax.ppermute(value, AXES, pairs)  62.9 us
    ppermute x20, starting transfers between devices, send(): return lax.ppermute(value, AXES, pairs)  30.3 us
    pallas_call x4, Pallas kernels, call(): pl.pallas_call(kernel, name=name, grid_spec=pltpu.PrefetchScalarGridSpec(...  22.4 us
    reduce_scatter x1, waiting for transfers between devices, on_device(): part = lax.psum_scatter(part, 'z', scatter_dimension=0, tiled=True)  18.2 us
    unnamed x42, local copies, waits for them, and re-layouts  9.01 us
  transfers between devices with their start and end apart: 21, of which 11 were waited for; matrix products, arithmetic and copies ran while one was open for 6% of the time, Pallas kernels for 9%

profile of v1, /device:TPU:27, one launch (start us, length us, event | category | flops | bytes accessed | tf_op | source)
XLA Modules:
  0.0 167.2 jit_solution(9512878549316860452)
XLA Ops:
  7.2 0.0 reduce-scatter.2.cloned.1.call-start
  7.2 0.1 collective-permute-start.2
  7.3 1.8 %constant_dynamic-slice_fusion.5 = bf16[128,1536]{1,0:T(8,128)(2,1)} fusion(bf16[128,3072]{1,0:T(8,128)(2,1)} %own.3, s32[]{:T(128)S(6)} %select_n.51), kind=kLoop, calls=%fused_computation.11 | loop fusion | bytes 786436 | tf_op jit(solution)/shard_map/dynamic_slice | solution.py:270
  9.1 2.6 %collective-permute-start.1 = (bf16[128,1536]{1,0:T(8,128)(2,1)}, bf16[128,1536]{1,0:T(8,128)(2,1)S(1)}, u32[]{:S(2)}, u32[]{:S(2)}) collective-permute-start(bf16[128,1536]{1,0:T(8,128)(2,1)} %constant_dynamic-slice_fusion.5), channel_id=1, source_target_pairs={{0,20},{1,21},{2,22},{3,23},{4,16},{5,17},{6,18},{7,19},{8,28},{9,... | collective-permute-start | bytes 1179656 | tf_op jit(solution)/shard_map/ppermute | solution.py:48
  11.7 0.9 copy.7.scales
  12.6 0.1 pad_add_fusion.where
  12.7 1.7 copy-done
  14.4 2.2 %dequantize.1.w0 = bf16[384,1536]{1,0:T(8,128)(2,1)S(1)} custom-call(s32[3]{0:T(128)S(1)} %pad_add_fusion.where, bf16[384,3072]{1,0:T(8,128)(2,1)S(1)} %copy-done, f32[384,12]{1,0:T(8,128)S(1)} %copy.7.scales), custom_call_target="tpu_custom_call" | custom-call | flops 589824 | bytes 3557376 | tf_op jit(solution)/shard_map/dequantize/pallas_call | solution.py:66
  16.6 1.3 collective-permute-start.4
  17.9 0.3 collective-permute-start.5
  18.2 1.8 %collective-permute-start.11 = (bf16[128,3072]{1,0:T(8,128)(2,1)S(1)}, bf16[128,3072]{1,0:T(8,128)(2,1)S(1)}, u32[]{:S(2)}, u32[]{:S(2)}) collective-permute-start(bf16[128,3072]{1,0:T(8,128)(2,1)S(1)} %copy-done.3), channel_id=1, source_target_pairs={{0,8},{1,9},{2,10},{3,11},{4,12},{5,13},{6,14},{7,15},{8,0},{9,1},... | collective-permute-start | bytes 2359304 | tf_op jit(solution)/shard_map/ppermute | solution.py:48
  20.0 15.6 %collective-permute-done.1.pair = bf16[128,1536]{1,0:T(8,128)(2,1)S(1)} collective-permute-done((bf16[128,1536]{1,0:T(8,128)(2,1)}, bf16[128,1536]{1,0:T(8,128)(2,1)S(1)}, u32[]{:S(2)}, u32[]{:S(2)}) %collective-permute-start.1) | collective-permute-done | bytes 393248 | tf_op jit(solution)/shard_map/ppermute | solution.py:48
  35.6 1.5 collective-permute-start.12
  37.1 0.1 collective-permute-start
  37.2 0.0 collective-permute-done.11.cot1
  37.2 0.4 collective-permute-start.3
  37.6 5.3 %collective-permute-done.4.w1 = bf16[384,1536]{1,0:T(8,128)(2,1)S(1)} collective-permute-done((bf16[384,1536]{1,0:T(8,128)(2,1)S(1)}, bf16[384,1536]{1,0:T(8,128)(2,1)S(1)}, u32[]{:S(2)}, u32[]{:S(2)}) %collective-permute-start.4) | collective-permute-done | bytes 1179680 | tf_op jit(solution)/shard_map/ppermute | solution.py:48
  42.9 0.9 collective-permute-done.5.w2
  43.8 0.0 collective-permute-done.12.cot3
  43.8 0.0 collective-permute-done.sib
  43.9 0.2 copy-done.18
  44.0 0.8 copy-done.20
  44.8 0.0 collective-permute-done.3.psib
  44.8 7.5 %gradient.1 = bf16[768,3072]{1,0:T(8,128)(2,1)} custom-call(s32[3]{0:T(128)S(1)} %pad_add_fusion.where, bf16[128,3072]{1,0:T(8,128)(2,1)S(1)} %copy-done.1, bf16[128,3072]{1,0:T(8,128)(2,1)S(1)} %collective-permute-done.sib, bf16[128,1536]{1,0:T(8,128)(2,1)S(1)} %collective-permute-done.1.pair, bf16[128,1536]{1,0:T(8,128)(2,1)S(1)} %collective-permute-done.3.psib, ...), custom_call_target="tpu_custom_call" | custom-call | flops 2415919104 | bytes 10223616 | tf_op jit(solution)/shard_map/gradient/pallas_call | solution.py:66
  52.4 0.9 copy-done.4
  53.3 0.9 copy-done.6
  54.2 0.9 copy-done.8
  55.1 0.7 copy-done.12
  55.8 0.0 reduce-scatter.2.cloned.1.call-update
  55.8 1.2 copy-done.19
  57.1 1.0 collective-permute-start.6
  58.1 1.1 slice.19
  59.2 0.6 collective-permute-start.7
  59.9 9.7 %collective-permute-done.6.w3 = bf16[384,768]{1,0:T(8,128)(2,1)S(1)} collective-permute-done((bf16[384,768]{1,0:T(8,128)(2,1)S(1)}, bf16[384,768]{1,0:T(8,128)(2,1)S(1)}, u32[]{:S(2)}, u32[]{:S(2)}) %collective-permute-start.6) | collective-permute-done | bytes 589856 | tf_op jit(solution)/shard_map/ppermute | solution.py:48
  69.6 1.9 %collective-permute-done.7.w4 = bf16[384,768]{1,0:T(8,128)(2,1)S(1)} collective-permute-done((bf16[384,768]{1,0:T(8,128)(2,1)S(1)}, bf16[384,768]{1,0:T(8,128)(2,1)S(1)}, u32[]{:S(2)}, u32[]{:S(2)}) %collective-permute-start.7) | collective-permute-done | bytes 589856 | tf_op jit(solution)/shard_map/ppermute | solution.py:48
  71.4 5.8 %forward.1 = (f32[128,1536]{1,0:T(8,128)S(1)}, f32[128,1536]{1,0:T(8,128)S(1)}, bf16[128,1536]{1,0:T(8,128)(2,1)}, bf16[128,1536]{1,0:T(8,128)(2,1)S(1)}) custom-call(s32[3]{0:T(128)S(1)} %pad_add_fusion.where, bf16[128,3072]{1,0:T(8,128)(2,1)S(1)} %copy-done.1, bf16[128,3072]{1,0:T(8,128)(2,1)S(1)} %copy-done.9, ...), custom_call_target="tpu_custom_call" | custom-call | flops 2415919104 | bytes 9437184 | tf_op jit(solution)/shard_map/forward/pallas_call | solution.py:66
  77.2 0.9 copy-done.10
  78.1 6.8 %backward.1 = (f32[256,1536]{1,0:T(8,128)}, bf16[256,1536]{1,0:T(8,128)(2,1)}) custom-call(s32[3]{0:T(128)S(1)} %pad_add_fusion.where, bf16[128,3072]{1,0:T(8,128)(2,1)S(1)} %copy-done.3, bf16[128,3072]{1,0:T(8,128)(2,1)S(1)} %copy-done.5, bf16[128,3072]{1,0:T(8,128)(2,1)} %collective-permute-done.2.cot2, bf16[128,3072]{1,0:T(8,128)(2,1)S(1)} %copy-done.7, ...), custom_call_target="tpu_custom_call" | custom-call | flops 2415919104 | bytes 10223616 | tf_op jit(solution)/shard_map/backward/pallas_call | solution.py:66
  85.0 3.8 %collective-permute-start.13 = (bf16[256,1536]{1,0:T(8,128)(2,1)}, bf16[256,1536]{1,0:T(8,128)(2,1)S(1)}, u32[]{:S(2)}, u32[]{:S(2)}) collective-permute-start(bf16[256,1536]{1,0:T(8,128)(2,1)} %get-tuple-element.34), channel_id=1, source_target_pairs={{0,8},{1,9},{2,10},{3,11},{4,12},{5,13},{6,14},{7,15},{8,0},{9,1},... | collective-permute-start | bytes 2359304 | tf_op jit(solution)/shard_map/ppermute | solution.py:48
  88.8 0.2 collective-permute-start.9
  89.0 3.0 %collective-permute-start.10 = (bf16[128,1536]{1,0:T(8,128)(2,1)}, bf16[128,1536]{1,0:T(8,128)(2,1)S(1)}, u32[]{:S(2)}, u32[]{:S(2)}) collective-permute-start(bf16[128,1536]{1,0:T(8,128)(2,1)} %copy-done.15), channel_id=1, source_target_pairs={{0,28},{1,29},{2,30},{3,31},{4,24},{5,25},{6,26},{7,27},{8,20},{9,... | collective-permute-start | bytes 1179656 | tf_op jit(solution)/shard_map/ppermute | solution.py:48
  92.0 0.8 copy-done.17
  92.7 1.1 add_convert_fusion.2
  93.8 0.2 add_convert_fusion
  94.0 0.1 fusion
  94.1 0.1 collective-permute-start.14
  94.2 8.0 %collective-permute-done.10 = bf16[128,1536]{1,0:T(8,128)(2,1)S(1)} collective-permute-done((bf16[128,1536]{1,0:T(8,128)(2,1)}, bf16[128,1536]{1,0:T(8,128)(2,1)S(1)}, u32[]{:S(2)}, u32[]{:S(2)}) %collective-permute-start.10) | collective-permute-done | bytes 393248 | tf_op jit(solution)/shard_map/ppermute | solution.py:48
  102.2 0.1 add_convert_fusion.1
  102.2 18.2 %reduce-scatter.2.cloned.1.call-done = bf16[96,3072]{1,0:T(8,128)(2,1)} async-done(((bf16[768,3072]{1,0:T(8,128)(2,1)}), bf16[96,3072]{1,0:T(8,128)(2,1)}) %reduce-scatter.2.cloned.1.call-update) | async-done | bytes 589840 | tf_op jit(solution)/shard_map/reduce_scatter | solution.py:283
  120.5 1.1 constant_dynamic-slice_fusion.4
  121.6 0.4 collective-permute-start.17
  121.9 2.1 %collective-permute-start.16 = (bf16[24,3072]{1,0:T(8,128)(2,1)S(1)}, bf16[24,3072]{1,0:T(8,128)(2,1)S(1)}, u32[]{:S(2)}, u32[]{:S(2)}) collective-permute-start(bf16[24,3072]{1,0:T(8,128)(2,1)S(1)} %get-tuple-element.43), channel_id=1, source_target_pairs={{0,2},{1,3},{2,0},{3,1},{4,6},{5,7},{6,4},{7,5},{8,10},{9,11},{10,... | collective-permute-start | bytes 442376 | tf_op jit(solution)/shard_map/ppermute | solution.py:48
  124.0 1.5 collective-permute-start.15
  125.5 1.1 maximum_select_fusion
  126.6 3.9 %collective-permute-done.16 = bf16[24,3072]{1,0:T(8,128)(2,1)S(1)} collective-permute-done((bf16[24,3072]{1,0:T(8,128)(2,1)S(1)}, bf16[24,3072]{1,0:T(8,128)(2,1)S(1)}, u32[]{:S(2)}, u32[]{:S(2)}) %collective-permute-start.16) | collective-permute-done | bytes 147488 | tf_op jit(solution)/shard_map/ppermute | solution.py:48
  130.5 0.5 collective-permute-done.15
  131.0 1.0 add_multiply_fusion
  132.0 0.1 constant_dynamic-slice_fusion
  132.1 4.3 %collective-permute-start.18 = (f32[12,3072]{1,0:T(8,128)S(1)}, f32[12,3072]{1,0:T(8,128)S(1)}, u32[]{:S(2)}, u32[]{:S(2)}) collective-permute-start(f32[12,3072]{1,0:T(8,128)S(1)} %get-tuple-element.45), channel_id=1, source_target_pairs={{0,32},{1,34},{2,36},{3,38},{4,128},{5,130},{6,132},{7,134},{8,64}... | collective-permute-start | bytes 442376 | tf_op jit(solution)/shard_map/ppermute | solution.py:48
  136.4 5.2 %collective-permute-start.19 = (f32[12,3072]{1,0:T(8,128)S(1)}, f32[12,3072]{1,0:T(8,128)S(1)}, u32[]{:S(2)}, u32[]{:S(2)}) collective-permute-start(f32[12,3072]{1,0:T(8,128)S(1)} %get-tuple-element.44), channel_id=1, source_target_pairs={{0,33},{1,35},{2,37},{3,39},{4,129},{5,131},{6,133},{7,135},{8,65}... | collective-permute-start | bytes 442376 | tf_op jit(solution)/shard_map/ppermute | solution.py:48
  141.6 1.1 maximum_select_fusion.1
  142.7 11.8 %collective-permute-done.18 = f32[12,3072]{1,0:T(8,128)S(1)} collective-permute-done((f32[12,3072]{1,0:T(8,128)S(1)}, f32[12,3072]{1,0:T(8,128)S(1)}, u32[]{:S(2)}, u32[]{:S(2)}) %collective-permute-start.18) | collective-permute-done | bytes 147488 | tf_op jit(solution)/shard_map/ppermute | solution.py:48
  154.4 5.3 %collective-permute-done.19 = f32[12,3072]{1,0:T(8,128)S(1)} collective-permute-done((f32[12,3072]{1,0:T(8,128)S(1)}, f32[12,3072]{1,0:T(8,128)S(1)}, u32[]{:S(2)}, u32[]{:S(2)}) %collective-permute-start.19) | collective-permute-done | bytes 147488 | tf_op jit(solution)/shard_map/ppermute | solution.py:48
  159.7 0.7 add.82
  (40 shorter events, 0.1 us)
Async XLA Ops:
  7.2 113.3 %reduce-scatter.2.cloned.1.call-start = ((), (), s32[]{:S(2)}) async-start(), calls=%async_computation.1 | async-start | bytes 5308416 | tf_op jit(solution)/shard_map/reduce_scatter | solution.py:283
  7.2 28.3 %collective-permute-start.2 = (bf16[128,3072]{1,0:T(8,128)(2,1)}, bf16[128,3072]{1,0:T(8,128)(2,1)}, u32[]{:S(2)}, u32[]{:S(2)}) collective-permute-start(bf16[128,3072]{1,0:T(8,128)(2,1)} %cot0.1), channel_id=1, source_target_pairs={{0,20},{1,21},{2,22},{3,23},{4,16},{5,17},{6,18},{7,19},{8,28},{9,... | collective-permute-start | bytes 2359304 | tf_op jit(solution)/shard_map/ppermute | solution.py:48
  9.1 26.5 %collective-permute-start.1 = (bf16[128,1536]{1,0:T(8,128)(2,1)}, bf16[128,1536]{1,0:T(8,128)(2,1)S(1)}, u32[]{:S(2)}, u32[]{:S(2)}) collective-permute-start(bf16[128,1536]{1,0:T(8,128)(2,1)} %constant_dynamic-slice_fusion.5), channel_id=1, source_target_pairs={{0,20},{1,21},{2,22},{3,23},{4,16},{5,17},{6,18},{7,19},{8,28},{9,... | collective-permute-start | bytes 1179656 | tf_op jit(solution)/shard_map/ppermute | solution.py:48
  12.7 1.7 copy-start
  14.4 3.8 %copy-start.3 = (bf16[128,3072]{1,0:T(8,128)(2,1)S(1)}, bf16[128,3072]{1,0:T(8,128)(2,1)}, u32[]{:S(2)}) copy-start(bf16[128,3072]{1,0:T(8,128)(2,1)} %cot0.1) | copy-start | bytes 2359300
  14.4 22.7 %copy-start.1 = (bf16[128,3072]{1,0:T(8,128)(2,1)S(1)}, bf16[128,3072]{1,0:T(8,128)(2,1)}, u32[]{:S(2)}) copy-start(bf16[128,3072]{1,0:T(8,128)(2,1)} %own.3) | copy-start | bytes 2359300
  16.6 35.8 %copy-start.2 = (bf16[384,1536]{1,0:T(8,128)(2,1)}, bf16[384,1536]{1,0:T(8,128)(2,1)S(1)}, u32[]{:S(2)}) copy-start(bf16[384,1536]{1,0:T(8,128)(2,1)S(1)} %dequantize.1.w0) | copy-start | bytes 3538948
  16.6 26.3 %collective-permute-start.4 = (bf16[384,1536]{1,0:T(8,128)(2,1)S(1)}, bf16[384,1536]{1,0:T(8,128)(2,1)S(1)}, u32[]{:S(2)}, u32[]{:S(2)}) collective-permute-start(bf16[384,1536]{1,0:T(8,128)(2,1)S(1)} %dequantize.1.w0), channel_id=1, source_target_pairs={{0,1},{1,2},{2,3},{3,0},{4,5},{5,6},{6,7},{7,4},{8,9},{9,10},{10,1... | collective-permute-start | bytes 3538952 | tf_op jit(solution)/shard_map/ppermute | solution.py:48
  17.9 25.9 %collective-permute-start.5 = (bf16[384,1536]{1,0:T(8,128)(2,1)S(1)}, bf16[384,1536]{1,0:T(8,128)(2,1)S(1)}, u32[]{:S(2)}, u32[]{:S(2)}) collective-permute-start(bf16[384,1536]{1,0:T(8,128)(2,1)S(1)} %dequantize.1.w0), channel_id=1, source_target_pairs={{0,3},{1,0},{2,1},{3,2},{4,7},{5,4},{6,5},{7,6},{8,11},{9,8},{10,9... | collective-permute-start | bytes 3538952 | tf_op jit(solution)/shard_map/ppermute | solution.py:48
  18.2 19.0 %collective-permute-start.11 = (bf16[128,3072]{1,0:T(8,128)(2,1)S(1)}, bf16[128,3072]{1,0:T(8,128)(2,1)S(1)}, u32[]{:S(2)}, u32[]{:S(2)}) collective-permute-start(bf16[128,3072]{1,0:T(8,128)(2,1)S(1)} %copy-done.3), channel_id=1, source_target_pairs={{0,8},{1,9},{2,10},{3,11},{4,12},{5,13},{6,14},{7,15},{8,0},{9,1},... | collective-permute-start | bytes 2359304 | tf_op jit(solution)/shard_map/ppermute | solution.py:48
  35.6 8.3 %collective-permute-start.12 = (bf16[128,3072]{1,0:T(8,128)(2,1)}, bf16[128,3072]{1,0:T(8,128)(2,1)S(1)}, u32[]{:S(2)}, u32[]{:S(2)}) collective-permute-start(bf16[128,3072]{1,0:T(8,128)(2,1)} %collective-permute-done.2.cot2), channel_id=1, source_target_pairs={{0,8},{1,9},{2,10},{3,11},{4,12},{5,13},{6,14},{7,15},{8,0},{9,1},... | collective-permute-start | bytes 2359304 | tf_op jit(solution)/shard_map/ppermute | solution.py:48
  37.1 6.7 %collective-permute-start = (bf16[128,3072]{1,0:T(8,128)(2,1)S(1)}, bf16[128,3072]{1,0:T(8,128)(2,1)S(1)}, u32[]{:S(2)}, u32[]{:S(2)}) collective-permute-start(bf16[128,3072]{1,0:T(8,128)(2,1)S(1)} %copy-done.1), channel_id=1, source_target_pairs={{0,8},{1,9},{2,10},{3,11},{4,12},{5,13},{6,14},{7,15},{8,0},{9,1},... | collective-permute-start | bytes 2359304 | tf_op jit(solution)/shard_map/ppermute | solution.py:48
  37.2 7.6 %collective-permute-start.3 = (bf16[128,1536]{1,0:T(8,128)(2,1)S(1)}, bf16[128,1536]{1,0:T(8,128)(2,1)S(1)}, u32[]{:S(2)}, u32[]{:S(2)}) collective-permute-start(bf16[128,1536]{1,0:T(8,128)(2,1)S(1)} %collective-permute-done.1.pair), channel_id=1, source_target_pairs={{0,8},{1,9},{2,10},{3,11},{4,12},{5,13},{6,14},{7,15},{8,0},{9,1},... | collective-permute-start | bytes 1179656 | tf_op jit(solution)/shard_map/ppermute | solution.py:48
  42.9 1.1 copy-start.18
  43.8 1.0 copy-start.20
  52.4 0.9 copy-start.4
  53.3 0.9 copy-start.6
  54.2 0.9 copy-start.8
  55.1 0.7 copy-start.12
  55.8 1.3 copy-start.19
  57.1 14.4 %copy-start.9 = (bf16[128,3072]{1,0:T(8,128)(2,1)S(1)}, bf16[128,3072]{1,0:T(8,128)(2,1)}, u32[]{:S(2)}) copy-start(bf16[128,3072]{1,0:T(8,128)(2,1)} %copy-done.8) | copy-start | bytes 2359300
  57.1 14.4 %copy-start.13 = (bf16[128,1536]{1,0:T(8,128)(2,1)S(1)}, bf16[128,1536]{1,0:T(8,128)(2,1)}, u32[]{:S(2)}) copy-start(bf16[128,1536]{1,0:T(8,128)(2,1)} %copy-done.12) | copy-start | bytes 1179652
  57.1 12.4 %collective-permute-start.6 = (bf16[384,768]{1,0:T(8,128)(2,1)S(1)}, bf16[384,768]{1,0:T(8,128)(2,1)S(1)}, u32[]{:S(2)}, u32[]{:S(2)}) collective-permute-start(bf16[384,768]{1,0:T(8,128)(2,1)S(1)} %slice.18), channel_id=1, source_target_pairs={{0,1},{1,2},{2,3},{3,0},{4,5},{5,6},{6,7},{7,4},{8,9},{9,10},{10,1... | collective-permute-start | bytes 1769480 | tf_op jit(solution)/shard_map/ppermute | solution.py:48
  59.2 18.9 %copy-start.5 = (bf16[128,3072]{1,0:T(8,128)(2,1)S(1)}, bf16[128,3072]{1,0:T(8,128)(2,1)}, u32[]{:S(2)}) copy-start(bf16[128,3072]{1,0:T(8,128)(2,1)} %copy-done.4) | copy-start | bytes 2359300
  59.2 18.9 %copy-start.7 = (bf16[128,3072]{1,0:T(8,128)(2,1)S(1)}, bf16[128,3072]{1,0:T(8,128)(2,1)}, u32[]{:S(2)}) copy-start(bf16[128,3072]{1,0:T(8,128)(2,1)} %copy-done.6) | copy-start | bytes 2359300
  59.2 12.2 %collective-permute-start.7 = (bf16[384,768]{1,0:T(8,128)(2,1)S(1)}, bf16[384,768]{1,0:T(8,128)(2,1)S(1)}, u32[]{:S(2)}, u32[]{:S(2)}) collective-permute-start(bf16[384,768]{1,0:T(8,128)(2,1)S(1)} %slice.19), channel_id=1, source_target_pairs={{0,3},{1,0},{2,1},{3,2},{4,7},{5,4},{6,5},{7,6},{8,11},{9,8},{10,9... | collective-permute-start | bytes 1769480 | tf_op jit(solution)/shard_map/ppermute | solution.py:48
  77.2 0.9 copy-start.10
  78.1 6.9 %copy-start.14 = (f32[128,1536]{1,0:T(8,128)}, f32[128,1536]{1,0:T(8,128)S(1)}, u32[]{:S(2)}) copy-start(f32[128,1536]{1,0:T(8,128)S(1)} %get-tuple-element.26) | copy-start | bytes 2359300
  78.1 6.9 %copy-start.15 = (bf16[128,1536]{1,0:T(8,128)(2,1)}, bf16[128,1536]{1,0:T(8,128)(2,1)S(1)}, u32[]{:S(2)}) copy-start(bf16[128,1536]{1,0:T(8,128)(2,1)S(1)} %get-tuple-element.27) | copy-start | bytes 1179652
  78.1 14.6 %copy-start.11 = (f32[128,1536]{1,0:T(8,128)S(1)}, f32[128,1536]{1,0:T(8,128)}, u32[]{:S(2)}) copy-start(f32[128,1536]{1,0:T(8,128)} %copy-done.10) | copy-start | bytes 2359300
  78.1 13.9 %collective-permute-start.8 = (bf16[128,1536]{1,0:T(8,128)(2,1)}, bf16[128,1536]{1,0:T(8,128)(2,1)S(1)}, u32[]{:S(2)}, u32[]{:S(2)}) collective-permute-start(bf16[128,1536]{1,0:T(8,128)(2,1)} %get-tuple-element.25), channel_id=1, source_target_pairs={{0,20},{1,21},{2,22},{3,23},{4,16},{5,17},{6,18},{7,19},{8,28},{9,... | collective-permute-start | bytes 1179656 | tf_op jit(solution)/shard_map/ppermute | solution.py:48
  85.0 8.8 %copy-start.16 = (f32[256,1536]{1,0:T(8,128)S(1)}, f32[256,1536]{1,0:T(8,128)}, u32[]{:S(2)}) copy-start(f32[256,1536]{1,0:T(8,128)} %get-tuple-element.33) | copy-start | bytes 4718596
  85.0 8.8 %collective-permute-start.13 = (bf16[256,1536]{1,0:T(8,128)(2,1)}, bf16[256,1536]{1,0:T(8,128)(2,1)S(1)}, u32[]{:S(2)}, u32[]{:S(2)}) collective-permute-start(bf16[256,1536]{1,0:T(8,128)(2,1)} %get-tuple-element.34), channel_id=1, source_target_pairs={{0,8},{1,9},{2,10},{3,11},{4,12},{5,13},{6,14},{7,15},{8,0},{9,1},... | collective-permute-start | bytes 2359304 | tf_op jit(solution)/shard_map/ppermute | solution.py:48
  88.8 13.3 %collective-permute-start.9 = (f32[128,1536]{1,0:T(8,128)}, f32[128,1536]{1,0:T(8,128)S(1)}, u32[]{:S(2)}, u32[]{:S(2)}) collective-permute-start(f32[128,1536]{1,0:T(8,128)} %copy-done.14), channel_id=1, source_target_pairs={{0,8},{1,9},{2,10},{3,11},{4,12},{5,13},{6,14},{7,15},{8,0},{9,1},... | collective-permute-start | bytes 2359304 | tf_op jit(solution)/shard_map/ppermute | solution.py:48
  89.0 13.2 %collective-permute-start.10 = (bf16[128,1536]{1,0:T(8,128)(2,1)}, bf16[128,1536]{1,0:T(8,128)(2,1)S(1)}, u32[]{:S(2)}, u32[]{:S(2)}) collective-permute-start(bf16[128,1536]{1,0:T(8,128)(2,1)} %copy-done.15), channel_id=1, source_target_pairs={{0,28},{1,29},{2,30},{3,31},{4,24},{5,25},{6,26},{7,27},{8,20},{9,... | collective-permute-start | bytes 1179656 | tf_op jit(solution)/shard_map/ppermute | solution.py:48
  92.0 0.8 copy-start.17
  94.1 47.5 %collective-permute-start.14 = (bf16[128,1536]{1,0:T(8,128)(2,1)S(1)}, bf16[128,1536]{1,0:T(8,128)(2,1)S(1)}, u32[]{:S(2)}, u32[]{:S(2)}) collective-permute-start(bf16[128,1536]{1,0:T(8,128)(2,1)S(1)} %get-tuple-element.40), channel_id=1, source_target_pairs={{0,20},{1,21},{2,22},{3,23},{4,16},{5,17},{6,18},{7,19},{8,28},{9,... | collective-permute-start | bytes 1179656 | tf_op jit(solution)/shard_map/ppermute | solution.py:48
  121.6 5.0 %collective-permute-start.17 = (bf16[24,3072]{1,0:T(8,128)(2,1)S(1)}, bf16[24,3072]{1,0:T(8,128)(2,1)S(1)}, u32[]{:S(2)}, u32[]{:S(2)}) collective-permute-start(bf16[24,3072]{1,0:T(8,128)(2,1)S(1)} %get-tuple-element.42), channel_id=1, source_target_pairs={{0,3},{1,0},{2,1},{3,2},{4,7},{5,4},{6,5},{7,6},{8,11},{9,8},{10,9... | collective-permute-start | bytes 442376 | tf_op jit(solution)/shard_map/ppermute | solution.py:48
  121.9 8.6 %collective-permute-start.16 = (bf16[24,3072]{1,0:T(8,128)(2,1)S(1)}, bf16[24,3072]{1,0:T(8,128)(2,1)S(1)}, u32[]{:S(2)}, u32[]{:S(2)}) collective-permute-start(bf16[24,3072]{1,0:T(8,128)(2,1)S(1)} %get-tuple-element.43), channel_id=1, source_target_pairs={{0,2},{1,3},{2,0},{3,1},{4,6},{5,7},{6,4},{7,5},{8,10},{9,11},{10,... | collective-permute-start | bytes 442376 | tf_op jit(solution)/shard_map/ppermute | solution.py:48
  124.0 7.0 %collective-permute-start.15 = (bf16[24,3072]{1,0:T(8,128)(2,1)S(1)}, bf16[24,3072]{1,0:T(8,128)(2,1)S(1)}, u32[]{:S(2)}, u32[]{:S(2)}) collective-permute-start(bf16[24,3072]{1,0:T(8,128)(2,1)S(1)} %get-tuple-element.41), channel_id=1, source_target_pairs={{0,1},{1,2},{2,3},{3,0},{4,5},{5,6},{6,7},{7,4},{8,9},{9,10},{10,1... | collective-permute-start | bytes 442376 | tf_op jit(solution)/shard_map/ppermute | solution.py:48
  132.1 22.3 %collective-permute-start.18 = (f32[12,3072]{1,0:T(8,128)S(1)}, f32[12,3072]{1,0:T(8,128)S(1)}, u32[]{:S(2)}, u32[]{:S(2)}) collective-permute-start(f32[12,3072]{1,0:T(8,128)S(1)} %get-tuple-element.45), channel_id=1, source_target_pairs={{0,32},{1,34},{2,36},{3,38},{4,128},{5,130},{6,132},{7,134},{8,64}... | collective-permute-start | bytes 442376 | tf_op jit(solution)/shard_map/ppermute | solution.py:48
  136.4 23.3 %collective-permute-start.19 = (f32[12,3072]{1,0:T(8,128)S(1)}, f32[12,3072]{1,0:T(8,128)S(1)}, u32[]{:S(2)}, u32[]{:S(2)}) collective-permute-start(f32[12,3072]{1,0:T(8,128)S(1)} %get-tuple-element.44), channel_id=1, source_target_pairs={{0,33},{1,35},{2,37},{3,39},{4,129},{5,131},{6,133},{7,135},{8,65}... | collective-permute-start | bytes 442376 | tf_op jit(solution)/shard_map/ppermute | solution.py:48
Sparse Core Ops, SparseCore 0:
  55.9 64.4 reduce-scatter.1

commit v2 on v1

--- a/solution.py
+++ b/solution.py
@@ -25,20 +25,21 @@
     return (((z % 8 * 2 + yl % 2) * 2 + c % 2) * 2 + yh % 2) * 4 + x % 4
 
 
-def turn(yh, c):
-    return 1 - (yh + c) % 2
+def window(z, c, yh):
+    return (z + 11 - 4 * yh - 2 * c) % 8
 
 
 def owner(z, yl, c, yh, x, message):
-    z_owner = 4 * yh + 2 * c + (z // 4 + turn(yh, c)) % 2
-    return z_owner, z % 4 // 2, z % 2, x // 2, x % 2 * 2 + (yl ^ message)
+    chunk = window(z, c, yh)
+    return 4 * yh + 2 * c + chunk // 4, chunk % 4 // 2, chunk % 2, x // 2, x % 2 * 2 + (yl ^ message)
 
 
 X_UP = table(lambda z, yl, c, yh, x: (z, yl, c, yh, x + 1))
 X_DOWN = table(lambda z, yl, c, yh, x: (z, yl, c, yh, x - 1))
+Z_UP = table(lambda z, yl, c, yh, x: (z + 1, yl, c, yh, x))
+Z_DOWN = table(lambda z, yl, c, yh, x: (z - 1, yl, c, yh, x))
 CORE = table(lambda z, yl, c, yh, x: (z, yl, c + 1, yh, x))
 PAIR = table(lambda z, yl, c, yh, x: (z, yl + 1, c, yh + 1, x))
-PAIR_CROSS = table(lambda z, yl, c, yh, x: (z, yl + 1, c + 1, yh + 1, x))
 OWNERS = [
     table(lambda z, yl, c, yh, x: owner(z, yl, c, yh, x, message)) for message in range(2)
 ]
@@ -60,7 +61,7 @@
     return value.astype(jnp.bfloat16)
 
 
-def call(kernel, name, where, grid, in_specs, out_specs, out_shape, scratch, flops, operands):
+def call(kernel, name, mib, where, grid, in_specs, out_specs, out_shape, scratch, flops, operands):
     moved = sum(v.size * v.dtype.itemsize for v in operands)
     moved += sum(v.size * v.dtype.itemsize for v in jax.tree.leaves(out_shape))
     return pl.pallas_call(
@@ -74,7 +75,7 @@
             scratch_shapes=scratch,
         ),
         out_shape=out_shape,
-        compiler_params=pltpu.CompilerParams(vmem_limit_bytes=48 * 2**20),
+        compiler_params=pltpu.CompilerParams(vmem_limit_bytes=mib * 2**20),
         cost_estimate=pl.CostEstimate(flops=flops, bytes_accessed=moved, transcendentals=0),
     )(where, *operands)
 
@@ -99,6 +100,7 @@
     return call(
         dequantize_kernel,
         "dequantize",
+        12,
         where,
         (3,),
         [
@@ -117,43 +119,86 @@
     return ref[:, pl.ds(pl.multiple_of(start, 128), size)]
 
 
-def gradient_kernel(where, own, sib, pair, psib, cot0, cot1, cot2, cot3, out, lhs):
+def gradient_kernel(where, own, sib, pair, psib, cot0, cot1, cot2, cot3, out, up, down, lhs):
     c, yh = where[0], where[1]
-    half = lhs.shape[0] // 2
-    count = own.shape[0]
+    count, size = own.shape[0], lhs.shape[1]
 
     @pl.when(pl.program_id(0) == 0)
     def _():
         for r, (ref, base) in enumerate(((own, yh), (sib, yh), (pair, 0), (psib, 0))):
-            for h in range(2):
-                start = base * 4 * half + c * 2 * half + (h + 1 - (yh + c) % 2) % 2 * half
-                block = f32(columns(ref, start, half))
-                lhs[h * half : (h + 1) * half, r * count : (r + 1) * count] = bf16(block.T)
+            start = base * 2 * size + c * size
+            lhs[r * count : (r + 1) * count] = columns(ref, start, size)
 
     rhs = jnp.concatenate([cot0[...], cot1[...], cot2[...], cot3[...]])
-    out[...] = bf16(jnp.dot(lhs[...], rhs, preferred_element_type=jnp.float32))
-
-
-def gradient(where, token_parts, cot_parts):
+    out[...] = bf16(
+        lax.dot_general(
+            lhs[...], rhs, (((0,), (0,)), ((), ())), preferred_element_type=jnp.float32
+        )
+    )
+    half = up.shape[0]
+    start = pl.multiple_of((where[3] + 4) % 8 * (2 * half), 2 * half)
+    up[...] = out[pl.ds(start, half)]
+    down[...] = out[pl.ds(start + half, half)]
+
+
+def gradient(where, token_parts, cot_parts, j):
     count, outputs = cot_parts[0].shape
     size = token_parts[0].shape[1] // 4
-    width = outputs // 6
+    width = outputs // 4
+    heights = (size, size // 16, size // 16)
     return call(
         gradient_kernel,
         "gradient",
-        where,
-        (6,),
+        24,
+        where,
+        (2,),
         [fixed(v.shape) for v in token_parts]
-        + [pl.BlockSpec((count, width), lambda i, where: (0, i)) for _ in cot_parts],
-        pl.BlockSpec((size, width), lambda i, where: (0, i)),
-        jax.ShapeDtypeStruct((size, outputs), jnp.bfloat16),
-        [pltpu.VMEM((size, 4 * count), jnp.bfloat16)],
-        8 * count * size * outputs,
+        + [pl.BlockSpec((count, width), lambda i, where: (0, 2 * j + i)) for _ in cot_parts],
+        [pl.BlockSpec((height, width), lambda i, where: (0, i)) for height in heights],
+        [jax.ShapeDtypeStruct((height, 2 * width), jnp.bfloat16) for height in heights],
+        [pltpu.VMEM((4 * count, size), jnp.bfloat16)],
+        4 * count * size * outputs,
         (*token_parts, *cot_parts),
     )
 
 
-def forward_kernel(where, own, sib, pair, psib, w0, w1, w2, w3, w4, mine, other, away, cross, lhs):
+def hop_kernel(where, up, down, near_up, near_down, *outs):
+    half = near_up.shape[0] // 2
+    if up.shape[0] == half:
+        outs[0][:half] = bf16(f32(near_up[:half]) + f32(up[...]))
+        outs[0][half:] = near_up[half:]
+        outs[1][:half] = near_down[:half]
+        outs[1][half:] = bf16(f32(near_down[half:]) + f32(down[...]))
+    elif len(outs) == 2:
+        outs[0][...] = bf16(f32(near_up[...]) + f32(up[...]))
+        outs[1][...] = bf16(f32(near_down[...]) + f32(down[...]))
+    else:
+        outs[0][...] = f32(near_up[...]) + f32(up[...]) + f32(down[...])
+
+
+def hop(where, step, up, down, part):
+    size, width = part.shape[0] // 8, part.shape[1]
+    kinds = [jnp.float32] if step == 3 else [jnp.bfloat16] * 2
+    return call(
+        hop_kernel,
+        "hop",
+        8,
+        where,
+        (1,),
+        [fixed(up.shape), fixed(down.shape)]
+        + [
+            fixed((size, width), lambda where, k=k: ((where[3] + 8 + k) % 8, 0))
+            for k in (3 - step, step - 3)
+        ],
+        [fixed((size, width)) for _ in kinds],
+        [jax.ShapeDtypeStruct((size, width), kind) for kind in kinds],
+        [],
+        2 * size * width,
+        (up, down, part, part),
+    )
+
+
+def forward_kernel(where, own, sib, pair, psib, w0, w1, w2, w3, w4, mine, other, away, lhs):
     yh, x = where[1], where[2]
     count, shard = own.shape[0], w0.shape[0]
 
@@ -171,25 +216,25 @@
     out = jnp.dot(lhs[...], rhs, preferred_element_type=jnp.float32)
     mine[...] = out[:count]
     other[...] = out[count : 2 * count]
-    away[...] = bf16(out[2 * count : 3 * count])
-    cross[...] = bf16(out[3 * count :])
+    away[...] = bf16(out[2 * count :])
 
 
 def forward_parts(where, token_parts, blocks):
     count = token_parts[0].shape[0]
     shard, nh = blocks[0].shape
     width = nh // 2
-    types = (jnp.float32, jnp.float32, jnp.bfloat16, jnp.bfloat16)
+    kinds = ((count, jnp.float32), (count, jnp.float32), (2 * count, jnp.bfloat16))
     return call(
         forward_kernel,
         "forward",
+        28,
         where,
         (2,),
         [fixed(v.shape) for v in token_parts]
         + [pl.BlockSpec((shard, width), lambda i, where: (0, i))] * 3
         + [fixed((shard, width))] * 2,
-        [pl.BlockSpec((count, width), lambda i, where: (0, i))] * 4,
-        [jax.ShapeDtypeStruct((count, nh), kind) for kind in types],
+        [pl.BlockSpec((height, width), lambda i, where: (0, i)) for height, _ in kinds],
+        [jax.ShapeDtypeStruct((height, nh), kind) for height, kind in kinds],
         [pltpu.VMEM((4 * count, 4 * shard), jnp.bfloat16)],
         32 * count * shard * nh,
         (*token_parts, *blocks),
@@ -227,6 +272,7 @@
     return call(
         backward_kernel,
         "backward",
+        28,
         where,
         (3,),
         [fixed((count, nh), lambda where: (0, where[0])) for _ in cot_parts]
@@ -252,50 +298,64 @@
 
 def reduce_over_x(part, x):
     size = part.shape[0] // 4
-    total = f32(rows(part, x * size, size))
+    total = rows(part, x * size, size)
     for dx in range(1, 4):
         to = table(lambda z, yl, c, yh, x: (z, yl, c, yh, x + dx))
-        total = total + f32(send(rows(part, (x + dx) % 4 * size, size), to))
+        total = total + f32(send(bf16(rows(part, (x + dx) % 4 * size, size)), to))
     return total
 
 
 def on_device(tokens, cotangent, levels, scales):
     z, yl, c, yh, x = (lax.axis_index(name) for name in AXES)
-    where = jnp.stack([c, yh, x]).astype(jnp.int32)
+    where = jnp.stack([c, yh, x, window(z, c, yh)]).astype(jnp.int32)
     count, features = tokens.shape
     kh = features // 2
     factor = float(count * 256) ** -0.5
 
     cot_pair = send(cotangent, PAIR)
-    token_out = lax.dynamic_slice_in_dim(tokens, (1 - yh) * kh, kh, 1)
-    token_pair = send(token_out, PAIR)
-
-    levels, scales = after((levels, scales), token_out)
     own = dequantize(where, levels, scales)
     left, right = send(own, X_UP), send(own, X_DOWN)
-
-    token_pair, cot_pair = after((token_pair, cot_pair), own)
-    cot_sib, token_sib = send(cotangent, CORE), send(tokens, CORE)
+    token_out = lax.dynamic_slice_in_dim(after(tokens, own), (1 - yh) * kh, kh, 1)
+    token_pair = send(token_out, PAIR)
+
+    cot_own, token_own = after((cotangent, tokens), token_out)
+    cot_sib, token_sib = send(cot_own, CORE), send(token_own, CORE)
     token_parts = (tokens, token_sib, token_pair, send(token_pair, CORE))
     cot_parts = (cotangent, cot_sib, cot_pair, send(cot_pair, CORE))
 
-    part = gradient(where, token_parts, after(cot_parts, left, right))
-    part = lax.psum_scatter(part, "z", scatter_dimension=0, tiled=True)
-
     half = own.shape[1] // 2
-    blocks = (own, left, right, send(left[:, :half], X_UP), send(right[:, half:], X_DOWN))
-    mine, other, away, cross = forward_parts(where, token_parts, blocks)
-    back, back_cross, here = send(away, PAIR), send(cross, PAIR_CROSS), send(other, CORE)
-    forward = joined(bf16(mine + f32(back)), bf16(here + f32(back_cross)), c)
-
-    cot_parts = after(cot_parts, away)
-    mine, give = backward_parts(where, cot_parts, blocks)
-    mine = mine + f32(send(give, CORE))
-    grad_input = joined(bf16(mine[:count]), send(bf16(mine[count:]), PAIR), yh)
-
-    total = reduce_over_x(part, x) * factor
+    far_left, far_right = left[:, :half], right[:, half:]
+    cot_ready = after(cot_parts, left, right, far_left, far_right)
+    chains = []
+    for j in range(2):
+        chains.append(gradient(where, token_parts, cot_ready, j))
+        cot_ready = after(cot_ready, chains[-1])
+    blocks = (own, left, right, send(far_left, X_UP), send(far_right, X_DOWN))
+    for step in range(4):
+        if step == 2:
+            mine, other, away = forward_parts(where, token_parts, after(blocks, chains))
+            back = f32(send(away, PAIR))
+            held = after([chain[0] for chain in chains], away)
+        if step == 3:
+            part, give = backward_parts(where, cot_parts, after(blocks, chains))
+            give = send(give, CORE)
+            held = after([chain[0] for chain in chains], part)
+            held[1] = after(held[1], back, give)
+        for j in range(2):
+            grad, up, down = chains[j]
+            grad = held[j] if step >= 2 else grad
+            got = hop(where, step, send(up, Z_UP), send(down, Z_DOWN), grad)
+            chains[j] = (grad, *got)
+    sums = [chain[1] for chain in chains]
+
+    part = part + f32(give)
+    grad_input = joined(bf16(part[:count]), send(bf16(part[count:]), PAIR), yh)
+    there = send(bf16(other + back[count:]), CORE)
+    forward = joined(bf16(mine + back[:count]), there, c)
+
+    total = bf16(reduce_over_x(jnp.concatenate(sums, axis=1), x) * factor)
     size = total.shape[0] // 2
-    got = [send(rows(total, (yl ^ m) * size, size), OWNERS[m]) for m in range(2)]
+    got = [f32(send(rows(total, (yl ^ m) * size, size), OWNERS[m])) for m in range(2)]
     return forward, grad_input, got[0] + got[1]
 
 

time: 168 us -> 159 us (0.946)
  the two profiles are of different devices: /device:TPU:27 before, /device:TPU:24 now
where the time goes in v2:
time: 159 us; the launch traced here: 157 us
  waiting for transfers between devices  63.7 us (40%)
  starting transfers between devices  52.8 us (33%)
  Pallas kernels  26.5 us (17%)
  local copies, waits for them, and re-layouts  7.34 us (5%)
  other arithmetic  6 us (4%)
    ppermute x35, waiting for transfers between devices, send(): return lax.ppermute(value, AXES, pairs)  63.7 us
    ppermute x35, starting transfers between devices, send(): return lax.ppermute(value, AXES, pairs)  52.8 us
    pallas_call x13, Pallas kernels, call(): pl.pallas_call(kernel, name=name, grid_spec=pltpu.PrefetchScalarGridSpec(...  26.5 us
    unnamed x31, local copies, waits for them, and re-layouts  4.99 us
  transfers between devices with their start and end apart: 35, of which 18 were waited for; matrix products, arithmetic and copies ran while one was open for 5% of the time, Pallas kernels for 11%

profile of v2, /device:TPU:24, one launch (start us, length us, event | category | flops | bytes accessed | tf_op | source)
XLA Modules:
  0.0 157.4 jit_solution(5581447179318994237)
XLA Ops:
  0.6 2.0 %collective-permute-start.8 = (bf16[128,3072]{1,0:T(8,128)(2,1)}, bf16[128,3072]{1,0:T(8,128)(2,1)S(1)}, u32[]{:S(2)}, u32[]{:S(2)}) collective-permute-start(bf16[128,3072]{1,0:T(8,128)(2,1)} %cot0.3), channel_id=1, source_target_pairs={{0,20},{1,21},{2,22},{3,23},{4,16},{5,17},{6,18},{7,19},{8,28},{9,... | collective-permute-start | bytes 2359304 | tf_op jit(solution)/shard_map/ppermute | solution.py:49
  2.8 0.9 copy.7.scales
  3.6 1.7 %copy-done.8 = bf16[384,3072]{1,0:T(8,128)(2,1)S(1)} copy-done((bf16[384,3072]{1,0:T(8,128)(2,1)S(1)}, bf16[384,3072]{1,0:T(8,128)(2,1)}, u32[]{:S(2)}) %copy-start.8) | copy-done | bytes 2359320
  5.3 3.2 %dequantize.1.w0 = bf16[384,1536]{1,0:T(8,128)(2,1)} custom-call(s32[4]{0:T(128)S(1)} %pad_add_fusion.where, bf16[384,3072]{1,0:T(8,128)(2,1)S(1)} %copy-done.8, f32[384,12]{1,0:T(8,128)S(1)} %copy.7.scales), custom_call_target="tpu_custom_call" | custom-call | flops 589824 | bytes 3557376 | tf_op jit(solution)/shard_map/dequantize/pallas_call | solution.py:67
  8.5 3.2 %collective-permute-start.4 = (bf16[384,1536]{1,0:T(8,128)(2,1)}, bf16[384,1536]{1,0:T(8,128)(2,1)}, u32[]{:S(2)}, u32[]{:S(2)}) collective-permute-start(bf16[384,1536]{1,0:T(8,128)(2,1)} %dequantize.1.w0), channel_id=1, source_target_pairs={{0,3},{1,0},{2,1},{3,2},{4,7},{5,4},{6,5},{7,6},{8,11},{9,8},{10,9... | collective-permute-start | bytes 3538952 | tf_op jit(solution)/shard_map/ppermute | solution.py:49
  11.7 1.4 collective-permute-start.1
  13.1 9.5 %collective-permute-done.8.cot2 = bf16[128,3072]{1,0:T(8,128)(2,1)S(1)} collective-permute-done((bf16[128,3072]{1,0:T(8,128)(2,1)}, bf16[128,3072]{1,0:T(8,128)(2,1)S(1)}, u32[]{:S(2)}, u32[]{:S(2)}) %collective-permute-start.8) | collective-permute-done | bytes 786464 | tf_op jit(solution)/shard_map/ppermute | solution.py:49
  22.6 7.3 %collective-permute-done.1.pair = bf16[128,1536]{1,0:T(8,128)(2,1)S(1)} collective-permute-done((bf16[128,1536]{1,0:T(8,128)(2,1)S(1)}, bf16[128,1536]{1,0:T(8,128)(2,1)S(1)}, u32[]{:S(2)}, u32[]{:S(2)}) %collective-permute-start.1) | collective-permute-done | bytes 393248 | tf_op jit(solution)/shard_map/ppermute | solution.py:49
  29.8 5.9 %collective-permute-done.3.w1 = bf16[384,1536]{1,0:T(8,128)(2,1)} collective-permute-done((bf16[384,1536]{1,0:T(8,128)(2,1)}, bf16[384,1536]{1,0:T(8,128)(2,1)}, u32[]{:S(2)}, u32[]{:S(2)}) %collective-permute-start.3) | collective-permute-done | bytes 1179680 | tf_op jit(solution)/shard_map/ppermute | solution.py:49
  35.8 1.1 slice.26
  36.9 1.1 slice.27
  38.1 1.1 copy-done.6
  39.2 2.6 %gradient.2 = (bf16[768,1536]{1,0:T(8,128)(2,1)S(1)}, bf16[48,1536]{1,0:T(8,128)(2,1)S(1)}, bf16[48,1536]{1,0:T(8,128)(2,1)S(1)}) custom-call(s32[4]{0:T(128)S(1)} %pad_add_fusion.where, bf16[128,3072]{1,0:T(8,128)(2,1)S(1)} %copy-done.2, bf16[128,3072]{1,0:T(8,128)(2,1)S(1)} %collective-permute-done.sib, bf16[128,1536]{1,0:T(8,128)(2,1)S(1)} %collective-permute-done.1.pair, ...), custom_call_target="tpu_custom_call" | custom-call | flops 1207959552 | bytes 8159232 | tf_op jit(solution)/shard_map/gradient/pallas_call | solution.py:67
  41.8 2.0 %collective-permute-start.10 = (bf16[48,1536]{1,0:T(8,128)(2,1)S(1)}, bf16[48,1536]{1,0:T(8,128)(2,1)S(1)}, u32[]{:S(2)}, u32[]{:S(2)}) collective-permute-start(bf16[48,1536]{1,0:T(8,128)(2,1)S(1)} %get-tuple-element.60), channel_id=1, source_target_pairs={{0,32},{1,33},{2,34},{3,35},{4,36},{5,37},{6,38},{7,39},{8,40},{9,... | collective-permute-start | bytes 442376 | tf_op jit(solution)/shard_map/ppermute | solution.py:49
  43.8 4.0 %collective-permute-start.11 = (bf16[48,1536]{1,0:T(8,128)(2,1)S(1)}, bf16[48,1536]{1,0:T(8,128)(2,1)S(1)}, u32[]{:S(2)}, u32[]{:S(2)}) collective-permute-start(bf16[48,1536]{1,0:T(8,128)(2,1)S(1)} %get-tuple-element.61), channel_id=1, source_target_pairs={{0,224},{1,225},{2,226},{3,227},{4,228},{5,229},{6,230},{7,231},{8... | collective-permute-start | bytes 442376 | tf_op jit(solution)/shard_map/ppermute | solution.py:49
  47.9 4.4 %collective-permute-done.10.up = bf16[48,1536]{1,0:T(8,128)(2,1)S(1)} collective-permute-done((bf16[48,1536]{1,0:T(8,128)(2,1)S(1)}, bf16[48,1536]{1,0:T(8,128)(2,1)S(1)}, u32[]{:S(2)}, u32[]{:S(2)}) %collective-permute-start.10) | collective-permute-done | bytes 147488 | tf_op jit(solution)/shard_map/ppermute | solution.py:49
  52.3 0.6 hop.8
  53.4 3.0 %collective-permute-start.6 = (bf16[384,768]{1,0:T(8,128)(2,1)S(1)}, bf16[384,768]{1,0:T(8,128)(2,1)S(1)}, u32[]{:S(2)}, u32[]{:S(2)}) collective-permute-start(bf16[384,768]{1,0:T(8,128)(2,1)S(1)} %slice.27), channel_id=1, source_target_pairs={{0,3},{1,0},{2,1},{3,2},{4,7},{5,4},{6,5},{7,6},{8,11},{9,8},{10,9... | collective-permute-start | bytes 1769480 | tf_op jit(solution)/shard_map/ppermute | solution.py:49
  56.3 2.7 %gradient.3 = (bf16[768,1536]{1,0:T(8,128)(2,1)S(1)}, bf16[48,1536]{1,0:T(8,128)(2,1)S(1)}, bf16[48,1536]{1,0:T(8,128)(2,1)S(1)}) custom-call(s32[4]{0:T(128)S(1)} %pad_add_fusion.where, bf16[128,3072]{1,0:T(8,128)(2,1)S(1)} %copy-done.2, bf16[128,3072]{1,0:T(8,128)(2,1)S(1)} %collective-permute-done.sib, bf16[128,1536]{1,0:T(8,128)(2,1)S(1)} %collective-permute-done.1.pair, ...), custom_call_target="tpu_custom_call" | custom-call | flops 1207959552 | bytes 8159232 | tf_op jit(solution)/shard_map/gradient/pallas_call | solution.py:67
  59.0 2.7 %collective-permute-start.14 = (bf16[48,1536]{1,0:T(8,128)(2,1)S(1)}, bf16[48,1536]{1,0:T(8,128)(2,1)S(1)}, u32[]{:S(2)}, u32[]{:S(2)}) collective-permute-start(bf16[48,1536]{1,0:T(8,128)(2,1)S(1)} %get-tuple-element.71), channel_id=1, source_target_pairs={{0,32},{1,33},{2,34},{3,35},{4,36},{5,37},{6,38},{7,39},{8,40},{9,... | collective-permute-start | bytes 442376 | tf_op jit(solution)/shard_map/ppermute | solution.py:49
  61.7 0.8 collective-permute-start.15
  62.5 3.7 %collective-permute-done.14.up = bf16[48,1536]{1,0:T(8,128)(2,1)S(1)} collective-permute-done((bf16[48,1536]{1,0:T(8,128)(2,1)S(1)}, bf16[48,1536]{1,0:T(8,128)(2,1)S(1)}, u32[]{:S(2)}, u32[]{:S(2)}) %collective-permute-start.14) | collective-permute-done | bytes 147488 | tf_op jit(solution)/shard_map/ppermute | solution.py:49
  66.2 1.6 %collective-permute-start.13 = (bf16[96,1536]{1,0:T(8,128)(2,1)S(1)}, bf16[96,1536]{1,0:T(8,128)(2,1)S(1)}, u32[]{:S(2)}, u32[]{:S(2)}) collective-permute-start(bf16[96,1536]{1,0:T(8,128)(2,1)S(1)} %get-tuple-element.63), channel_id=1, source_target_pairs={{0,224},{1,225},{2,226},{3,227},{4,228},{5,229},{6,230},{7,231},{8... | collective-permute-start | bytes 884744 | tf_op jit(solution)/shard_map/ppermute | solution.py:49
  67.8 0.6 hop.10
  68.5 3.5 %collective-permute-start.16 = (bf16[96,1536]{1,0:T(8,128)(2,1)S(1)}, bf16[96,1536]{1,0:T(8,128)(2,1)S(1)}, u32[]{:S(2)}, u32[]{:S(2)}) collective-permute-start(bf16[96,1536]{1,0:T(8,128)(2,1)S(1)} %get-tuple-element.73), channel_id=1, source_target_pairs={{0,32},{1,33},{2,34},{3,35},{4,36},{5,37},{6,38},{7,39},{8,40},{9,... | collective-permute-start | bytes 884744 | tf_op jit(solution)/shard_map/ppermute | solution.py:49
  72.0 4.1 %collective-permute-done.13.down = bf16[96,1536]{1,0:T(8,128)(2,1)S(1)} collective-permute-done((bf16[96,1536]{1,0:T(8,128)(2,1)S(1)}, bf16[96,1536]{1,0:T(8,128)(2,1)S(1)}, u32[]{:S(2)}, u32[]{:S(2)}) %collective-permute-start.13) | collective-permute-done | bytes 294944 | tf_op jit(solution)/shard_map/ppermute | solution.py:49
  76.2 0.7 hop.9
  76.8 0.5 collective-permute-done.16.up
  77.3 3.4 %collective-permute-done.17.down = bf16[96,1536]{1,0:T(8,128)(2,1)S(1)} collective-permute-done((bf16[96,1536]{1,0:T(8,128)(2,1)S(1)}, bf16[96,1536]{1,0:T(8,128)(2,1)S(1)}, u32[]{:S(2)}, u32[]{:S(2)}) %collective-permute-start.17) | collective-permute-done | bytes 294944 | tf_op jit(solution)/shard_map/ppermute | solution.py:49
  80.7 0.7 hop.11
  81.4 5.8 %forward.1 = (f32[128,1536]{1,0:T(8,128)S(1)}, f32[128,1536]{1,0:T(8,128)S(1)}, bf16[256,1536]{1,0:T(8,128)(2,1)}) custom-call(s32[4]{0:T(128)S(1)} %pad_add_fusion.where, bf16[128,3072]{1,0:T(8,128)(2,1)S(1)} %copy-done.2, bf16[128,3072]{1,0:T(8,128)(2,1)S(1)} %collective-permute-done.sib, bf16[128,1536]{1,0:T(8,128)(2,1)S(1)} %collective-permute-done.1.pair, ...), custom_call_target="tpu_custom_call" | custom-call | flops 2415919104 | bytes 9437184 | tf_op jit(solution)/shard_map/forward/pallas_call | solution.py:67
  87.2 2.9 %collective-permute-start.18 = (bf16[256,1536]{1,0:T(8,128)(2,1)}, bf16[256,1536]{1,0:T(8,128)(2,1)}, u32[]{:S(2)}, u32[]{:S(2)}) collective-permute-start(bf16[256,1536]{1,0:T(8,128)(2,1)} %get-tuple-element.83), channel_id=1, source_target_pairs={{0,20},{1,21},{2,22},{3,23},{4,16},{5,17},{6,18},{7,19},{8,28},{9,... | collective-permute-start | bytes 2359304 | tf_op jit(solution)/shard_map/ppermute | solution.py:49
  90.1 1.8 %collective-permute-start.20 = (bf16[96,1536]{1,0:T(8,128)(2,1)S(1)}, bf16[96,1536]{1,0:T(8,128)(2,1)S(1)}, u32[]{:S(2)}, u32[]{:S(2)}) collective-permute-start(bf16[96,1536]{1,0:T(8,128)(2,1)S(1)} %get-tuple-element.64), channel_id=1, source_target_pairs={{0,32},{1,33},{2,34},{3,35},{4,36},{5,37},{6,38},{7,39},{8,40},{9,... | collective-permute-start | bytes 884744 | tf_op jit(solution)/shard_map/ppermute | solution.py:49
  91.9 1.5 collective-permute-start.21
  93.4 0.6 collective-permute-start.22
  93.9 2.7 %collective-permute-start.23 = (bf16[96,1536]{1,0:T(8,128)(2,1)S(1)}, bf16[96,1536]{1,0:T(8,128)(2,1)S(1)}, u32[]{:S(2)}, u32[]{:S(2)}) collective-permute-start(bf16[96,1536]{1,0:T(8,128)(2,1)S(1)} %get-tuple-element.76), channel_id=1, source_target_pairs={{0,224},{1,225},{2,226},{3,227},{4,228},{5,229},{6,230},{7,231},{8... | collective-permute-start | bytes 884744 | tf_op jit(solution)/shard_map/ppermute | solution.py:49
  96.6 4.7 %collective-permute-done.20.up = bf16[96,1536]{1,0:T(8,128)(2,1)S(1)} collective-permute-done((bf16[96,1536]{1,0:T(8,128)(2,1)S(1)}, bf16[96,1536]{1,0:T(8,128)(2,1)S(1)}, u32[]{:S(2)}, u32[]{:S(2)}) %collective-permute-start.20) | collective-permute-done | bytes 294944 | tf_op jit(solution)/shard_map/ppermute | solution.py:49
  101.3 0.6 collective-permute-done.21.down
  101.8 1.4 hop.12
  103.3 0.7 collective-permute-start.26
  104.0 2.6 %collective-permute-start.27 = (bf16[96,1536]{1,0:T(8,128)(2,1)}, bf16[96,1536]{1,0:T(8,128)(2,1)S(1)}, u32[]{:S(2)}, u32[]{:S(2)}) collective-permute-start(bf16[96,1536]{1,0:T(8,128)(2,1)} %get-tuple-element.87), channel_id=1, source_target_pairs={{0,224},{1,225},{2,226},{3,227},{4,228},{5,229},{6,230},{7,231},{8... | collective-permute-start | bytes 884744 | tf_op jit(solution)/shard_map/ppermute | solution.py:49
  106.5 1.1 collective-permute-done.22.up
  107.6 0.6 collective-permute-done.23.down
  108.2 0.7 hop.13
  108.9 6.2 %backward.1 = (f32[256,1536]{1,0:T(8,128)S(1)}, bf16[256,1536]{1,0:T(8,128)(2,1)}) custom-call(s32[4]{0:T(128)S(1)} %pad_add_fusion.where, bf16[128,3072]{1,0:T(8,128)(2,1)S(1)} %copy-done.4, bf16[128,3072]{1,0:T(8,128)(2,1)S(1)} %collective-permute-done.7.cot1, bf16[128,3072]{1,0:T(8,128)(2,1)S(1)} %copy-done.7, ...), custom_call_target="tpu_custom_call" | custom-call | flops 2415919104 | bytes 10223616 | tf_op jit(solution)/shard_map/backward/pallas_call | solution.py:67
  115.1 1.1 copy-done.9
  116.6 2.9 %collective-permute-start.29 = (bf16[96,1536]{1,0:T(8,128)(2,1)S(1)}, bf16[96,1536]{1,0:T(8,128)(2,1)S(1)}, u32[]{:S(2)}, u32[]{:S(2)}) collective-permute-start(bf16[96,1536]{1,0:T(8,128)(2,1)S(1)} %get-tuple-element.90), channel_id=1, source_target_pairs={{0,224},{1,225},{2,226},{3,227},{4,228},{5,229},{6,230},{7,231},{8... | collective-permute-start | bytes 884744 | tf_op jit(solution)/shard_map/ppermute | solution.py:49
  119.5 0.7 hop.14
  120.2 1.4 convert_element_type.41
  122.1 4.8 %collective-permute-done.28.up = bf16[96,1536]{1,0:T(8,128)(2,1)S(1)} collective-permute-done((bf16[96,1536]{1,0:T(8,128)(2,1)S(1)}, bf16[96,1536]{1,0:T(8,128)(2,1)S(1)}, u32[]{:S(2)}, u32[]{:S(2)}) %collective-permute-start.28) | collective-permute-done | bytes 294944 | tf_op jit(solution)/shard_map/ppermute | solution.py:49
  126.9 0.7 hop.15
  128.0 1.0 collective-permute-start.31
  129.0 1.2 collective-permute-start.30
  130.1 1.3 add_convert_fusion
  132.0 2.5 %collective-permute-done.32 = bf16[24,3072]{1,0:T(8,128)(2,1)S(1)} collective-permute-done((bf16[24,3072]{1,0:T(8,128)(2,1)S(1)}, bf16[24,3072]{1,0:T(8,128)(2,1)S(1)}, u32[]{:S(2)}, u32[]{:S(2)}) %collective-permute-start.32) | collective-permute-done | bytes 147488 | tf_op jit(solution)/shard_map/ppermute | solution.py:49
  134.4 1.6 %collective-permute-done.31 = bf16[24,3072]{1,0:T(8,128)(2,1)S(1)} collective-permute-done((bf16[24,3072]{1,0:T(8,128)(2,1)S(1)}, bf16[24,3072]{1,0:T(8,128)(2,1)S(1)}, u32[]{:S(2)}, u32[]{:S(2)}) %collective-permute-start.31) | collective-permute-done | bytes 147488 | tf_op jit(solution)/shard_map/ppermute | solution.py:49
  136.0 1.9 %collective-permute-done.30 = bf16[24,3072]{1,0:T(8,128)(2,1)S(1)} collective-permute-done((bf16[24,3072]{1,0:T(8,128)(2,1)S(1)}, bf16[24,3072]{1,0:T(8,128)(2,1)S(1)}, u32[]{:S(2)}, u32[]{:S(2)}) %collective-permute-start.30) | collective-permute-done | bytes 147488 | tf_op jit(solution)/shard_map/ppermute | solution.py:49
  138.1 3.2 %collective-permute-start.34 = (bf16[12,3072]{1,0:T(8,128)(2,1)S(1)}, bf16[12,3072]{1,0:T(8,128)(2,1)S(1)}, u32[]{:S(2)}, u32[]{:S(2)}) collective-permute-start(bf16[12,3072]{1,0:T(8,128)(2,1)S(1)} %get-tuple-element.109), channel_id=1, source_target_pairs={{0,25},{1,27},{2,29},{3,31},{4,185},{5,187},{6,189},{7,191},{8,73}... | collective-permute-start | bytes 221192 | tf_op jit(solution)/shard_map/ppermute | solution.py:49
  141.3 6.0 %collective-permute-start.33 = (bf16[12,3072]{1,0:T(8,128)(2,1)S(1)}, bf16[12,3072]{1,0:T(8,128)(2,1)S(1)}, u32[]{:S(2)}, u32[]{:S(2)}) collective-permute-start(bf16[12,3072]{1,0:T(8,128)(2,1)S(1)} %get-tuple-element.108), channel_id=1, source_target_pairs={{0,24},{1,26},{2,28},{3,30},{4,184},{5,186},{6,188},{7,190},{8,72}... | collective-permute-start | bytes 221192 | tf_op jit(solution)/shard_map/ppermute | solution.py:49
  147.3 1.1 maximum_select_fusion
  148.3 6.4 %collective-permute-done.34 = bf16[12,3072]{1,0:T(8,128)(2,1)S(1)} collective-permute-done((bf16[12,3072]{1,0:T(8,128)(2,1)S(1)}, bf16[12,3072]{1,0:T(8,128)(2,1)S(1)}, u32[]{:S(2)}, u32[]{:S(2)}) %collective-permute-start.34) | collective-permute-done | bytes 73760 | tf_op jit(solution)/shard_map/ppermute | solution.py:49
  154.7 0.9 collective-permute-done.33
  155.6 0.7 convert_add_fusion
  156.3 1.1 maximum_select_fusion.1
  (64 shorter events, 2.6 us)
Async XLA Ops:
  0.6 21.9 %collective-permute-start.8 = (bf16[128,3072]{1,0:T(8,128)(2,1)}, bf16[128,3072]{1,0:T(8,128)(2,1)S(1)}, u32[]{:S(2)}, u32[]{:S(2)}) collective-permute-start(bf16[128,3072]{1,0:T(8,128)(2,1)} %cot0.3), channel_id=1, source_target_pairs={{0,20},{1,21},{2,22},{3,23},{4,16},{5,17},{6,18},{7,19},{8,28},{9,... | collective-permute-start | bytes 2359304 | tf_op jit(solution)/shard_map/ppermute | solution.py:49
  3.6 1.7 %copy-start.8 = (bf16[384,3072]{1,0:T(8,128)(2,1)S(1)}, bf16[384,3072]{1,0:T(8,128)(2,1)}, u32[]{:S(2)}) copy-start(bf16[384,3072]{1,0:T(8,128)(2,1)} %levels.1) | copy-start | bytes 7077892
  5.3 6.4 %copy-start.2 = (bf16[128,3072]{1,0:T(8,128)(2,1)S(1)}, bf16[128,3072]{1,0:T(8,128)(2,1)}, u32[]{:S(2)}) copy-start(bf16[128,3072]{1,0:T(8,128)(2,1)} %own.5) | copy-start | bytes 2359300
  5.3 7.8 %copy-start.3 = (bf16[128,3072]{1,0:T(8,128)(2,1)S(1)}, bf16[128,3072]{1,0:T(8,128)(2,1)}, u32[]{:S(2)}) copy-start(bf16[128,3072]{1,0:T(8,128)(2,1)} %cot0.3) | copy-start | bytes 2359300
  8.5 27.3 %collective-permute-start.3 = (bf16[384,1536]{1,0:T(8,128)(2,1)}, bf16[384,1536]{1,0:T(8,128)(2,1)}, u32[]{:S(2)}, u32[]{:S(2)}) collective-permute-start(bf16[384,1536]{1,0:T(8,128)(2,1)} %dequantize.1.w0), channel_id=1, source_target_pairs={{0,1},{1,2},{2,3},{3,0},{4,5},{5,6},{6,7},{7,4},{8,9},{9,10},{10,1... | collective-permute-start | bytes 3538952 | tf_op jit(solution)/shard_map/ppermute | solution.py:49
  8.5 28.4 %collective-permute-start.4 = (bf16[384,1536]{1,0:T(8,128)(2,1)}, bf16[384,1536]{1,0:T(8,128)(2,1)}, u32[]{:S(2)}, u32[]{:S(2)}) collective-permute-start(bf16[384,1536]{1,0:T(8,128)(2,1)} %dequantize.1.w0), channel_id=1, source_target_pairs={{0,3},{1,0},{2,1},{3,2},{4,7},{5,4},{6,5},{7,6},{8,11},{9,8},{10,9... | collective-permute-start | bytes 3538952 | tf_op jit(solution)/shard_map/ppermute | solution.py:49
  11.7 26.4 %copy-start.4 = (bf16[128,3072]{1,0:T(8,128)(2,1)S(1)}, bf16[128,3072]{1,0:T(8,128)(2,1)}, u32[]{:S(2)}) copy-start(bf16[128,3072]{1,0:T(8,128)(2,1)} %cot0.3) | copy-start | bytes 2359300
  11.7 18.1 %collective-permute-start.1 = (bf16[128,1536]{1,0:T(8,128)(2,1)S(1)}, bf16[128,1536]{1,0:T(8,128)(2,1)S(1)}, u32[]{:S(2)}, u32[]{:S(2)}) collective-permute-start(bf16[128,1536]{1,0:T(8,128)(2,1)S(1)} %constant_dynamic-slice_fusion.2), channel_id=1, source_target_pairs={{0,20},{1,21},{2,22},{3,23},{4,16},{5,17},{6,18},{7,19},{8,28},{9,... | collective-permute-start | bytes 1179656 | tf_op jit(solution)/shard_map/ppermute | solution.py:49
  13.1 24.9 %collective-permute-start.7 = (bf16[128,3072]{1,0:T(8,128)(2,1)S(1)}, bf16[128,3072]{1,0:T(8,128)(2,1)S(1)}, u32[]{:S(2)}, u32[]{:S(2)}) collective-permute-start(bf16[128,3072]{1,0:T(8,128)(2,1)S(1)} %copy-done.3), channel_id=1, source_target_pairs={{0,8},{1,9},{2,10},{3,11},{4,12},{5,13},{6,14},{7,15},{8,0},{9,1},... | collective-permute-start | bytes 2359304 | tf_op jit(solution)/shard_map/ppermute | solution.py:49
  22.6 15.5 %copy-start.5 = (bf16[128,3072]{1,0:T(8,128)(2,1)}, bf16[128,3072]{1,0:T(8,128)(2,1)S(1)}, u32[]{:S(2)}) copy-start(bf16[128,3072]{1,0:T(8,128)(2,1)S(1)} %collective-permute-done.8.cot2) | copy-start | bytes 2359300
  22.6 15.4 %collective-permute-start.9 = (bf16[128,3072]{1,0:T(8,128)(2,1)S(1)}, bf16[128,3072]{1,0:T(8,128)(2,1)S(1)}, u32[]{:S(2)}, u32[]{:S(2)}) collective-permute-start(bf16[128,3072]{1,0:T(8,128)(2,1)S(1)} %collective-permute-done.8.cot2), channel_id=1, source_target_pairs={{0,8},{1,9},{2,10},{3,11},{4,12},{5,13},{6,14},{7,15},{8,0},{9,1},... | collective-permute-start | bytes 2359304 | tf_op jit(solution)/shard_map/ppermute | solution.py:49
  29.8 8.2 %collective-permute-start = (bf16[128,3072]{1,0:T(8,128)(2,1)S(1)}, bf16[128,3072]{1,0:T(8,128)(2,1)S(1)}, u32[]{:S(2)}, u32[]{:S(2)}) collective-permute-start(bf16[128,3072]{1,0:T(8,128)(2,1)S(1)} %copy-done.2), channel_id=1, source_target_pairs={{0,8},{1,9},{2,10},{3,11},{4,12},{5,13},{6,14},{7,15},{8,0},{9,1},... | collective-permute-start | bytes 2359304 | tf_op jit(solution)/shard_map/ppermute | solution.py:49
  35.8 2.3 %collective-permute-start.2 = (bf16[128,1536]{1,0:T(8,128)(2,1)S(1)}, bf16[128,1536]{1,0:T(8,128)(2,1)S(1)}, u32[]{:S(2)}, u32[]{:S(2)}) collective-permute-start(bf16[128,1536]{1,0:T(8,128)(2,1)S(1)} %collective-permute-done.1.pair), channel_id=1, source_target_pairs={{0,8},{1,9},{2,10},{3,11},{4,12},{5,13},{6,14},{7,15},{8,0},{9,1},... | collective-permute-start | bytes 1179656 | tf_op jit(solution)/shard_map/ppermute | solution.py:49
  38.1 1.1 copy-start.6
  41.8 10.5 %collective-permute-start.10 = (bf16[48,1536]{1,0:T(8,128)(2,1)S(1)}, bf16[48,1536]{1,0:T(8,128)(2,1)S(1)}, u32[]{:S(2)}, u32[]{:S(2)}) collective-permute-start(bf16[48,1536]{1,0:T(8,128)(2,1)S(1)} %get-tuple-element.60), channel_id=1, source_target_pairs={{0,32},{1,33},{2,34},{3,35},{4,36},{5,37},{6,38},{7,39},{8,40},{9,... | collective-permute-start | bytes 442376 | tf_op jit(solution)/shard_map/ppermute | solution.py:49
  43.8 8.5 %collective-permute-start.11 = (bf16[48,1536]{1,0:T(8,128)(2,1)S(1)}, bf16[48,1536]{1,0:T(8,128)(2,1)S(1)}, u32[]{:S(2)}, u32[]{:S(2)}) collective-permute-start(bf16[48,1536]{1,0:T(8,128)(2,1)S(1)} %get-tuple-element.61), channel_id=1, source_target_pairs={{0,224},{1,225},{2,226},{3,227},{4,228},{5,229},{6,230},{7,231},{8... | collective-permute-start | bytes 442376 | tf_op jit(solution)/shard_map/ppermute | solution.py:49
  52.9 19.1 %collective-permute-start.12 = (bf16[96,1536]{1,0:T(8,128)(2,1)S(1)}, bf16[96,1536]{1,0:T(8,128)(2,1)S(1)}, u32[]{:S(2)}, u32[]{:S(2)}) collective-permute-start(bf16[96,1536]{1,0:T(8,128)(2,1)S(1)} %get-tuple-element.62), channel_id=1, source_target_pairs={{0,32},{1,33},{2,34},{3,35},{4,36},{5,37},{6,38},{7,39},{8,40},{9,... | collective-permute-start | bytes 884744 | tf_op jit(solution)/shard_map/ppermute | solution.py:49
  53.0 28.4 %collective-permute-start.5 = (bf16[384,768]{1,0:T(8,128)(2,1)S(1)}, bf16[384,768]{1,0:T(8,128)(2,1)S(1)}, u32[]{:S(2)}, u32[]{:S(2)}) collective-permute-start(bf16[384,768]{1,0:T(8,128)(2,1)S(1)} %slice.26), channel_id=1, source_target_pairs={{0,1},{1,2},{2,3},{3,0},{4,5},{5,6},{6,7},{7,4},{8,9},{9,10},{10,1... | collective-permute-start | bytes 1769480 | tf_op jit(solution)/shard_map/ppermute | solution.py:49
  53.4 28.0 %collective-permute-start.6 = (bf16[384,768]{1,0:T(8,128)(2,1)S(1)}, bf16[384,768]{1,0:T(8,128)(2,1)S(1)}, u32[]{:S(2)}, u32[]{:S(2)}) collective-permute-start(bf16[384,768]{1,0:T(8,128)(2,1)S(1)} %slice.27), channel_id=1, source_target_pairs={{0,3},{1,0},{2,1},{3,2},{4,7},{5,4},{6,5},{7,6},{8,11},{9,8},{10,9... | collective-permute-start | bytes 1769480 | tf_op jit(solution)/shard_map/ppermute | solution.py:49
  59.0 49.2 %copy-start = (bf16[768,1536]{1,0:T(8,128)(2,1)}, bf16[768,1536]{1,0:T(8,128)(2,1)S(1)}, u32[]{:S(2)}) copy-start(bf16[768,1536]{1,0:T(8,128)(2,1)S(1)} %get-tuple-element.100.near_up.near_down) | copy-start | bytes 7077892
  59.0 7.2 %collective-permute-start.14 = (bf16[48,1536]{1,0:T(8,128)(2,1)S(1)}, bf16[48,1536]{1,0:T(8,128)(2,1)S(1)}, u32[]{:S(2)}, u32[]{:S(2)}) collective-permute-start(bf16[48,1536]{1,0:T(8,128)(2,1)S(1)} %get-tuple-element.71), channel_id=1, source_target_pairs={{0,32},{1,33},{2,34},{3,35},{4,36},{5,37},{6,38},{7,39},{8,40},{9,... | collective-permute-start | bytes 442376 | tf_op jit(solution)/shard_map/ppermute | solution.py:49
  61.7 6.1 %collective-permute-start.15 = (bf16[48,1536]{1,0:T(8,128)(2,1)S(1)}, bf16[48,1536]{1,0:T(8,128)(2,1)S(1)}, u32[]{:S(2)}, u32[]{:S(2)}) collective-permute-start(bf16[48,1536]{1,0:T(8,128)(2,1)S(1)} %get-tuple-element.72), channel_id=1, source_target_pairs={{0,224},{1,225},{2,226},{3,227},{4,228},{5,229},{6,230},{7,231},{8... | collective-permute-start | bytes 442376 | tf_op jit(solution)/shard_map/ppermute | solution.py:49
  66.2 9.9 %collective-permute-start.13 = (bf16[96,1536]{1,0:T(8,128)(2,1)S(1)}, bf16[96,1536]{1,0:T(8,128)(2,1)S(1)}, u32[]{:S(2)}, u32[]{:S(2)}) collective-permute-start(bf16[96,1536]{1,0:T(8,128)(2,1)S(1)} %get-tuple-element.63), channel_id=1, source_target_pairs={{0,224},{1,225},{2,226},{3,227},{4,228},{5,229},{6,230},{7,231},{8... | collective-permute-start | bytes 884744 | tf_op jit(solution)/shard_map/ppermute | solution.py:49
  68.5 8.9 %collective-permute-start.16 = (bf16[96,1536]{1,0:T(8,128)(2,1)S(1)}, bf16[96,1536]{1,0:T(8,128)(2,1)S(1)}, u32[]{:S(2)}, u32[]{:S(2)}) collective-permute-start(bf16[96,1536]{1,0:T(8,128)(2,1)S(1)} %get-tuple-element.73), channel_id=1, source_target_pairs={{0,32},{1,33},{2,34},{3,35},{4,36},{5,37},{6,38},{7,39},{8,40},{9,... | collective-permute-start | bytes 884744 | tf_op jit(solution)/shard_map/ppermute | solution.py:49
  72.0 8.7 %collective-permute-start.17 = (bf16[96,1536]{1,0:T(8,128)(2,1)S(1)}, bf16[96,1536]{1,0:T(8,128)(2,1)S(1)}, u32[]{:S(2)}, u32[]{:S(2)}) collective-permute-start(bf16[96,1536]{1,0:T(8,128)(2,1)S(1)} %get-tuple-element.74), channel_id=1, source_target_pairs={{0,224},{1,225},{2,226},{3,227},{4,228},{5,229},{6,230},{7,231},{8... | collective-permute-start | bytes 884744 | tf_op jit(solution)/shard_map/ppermute | solution.py:49
  87.2 16.1 %copy-start.11 = (f32[128,1536]{1,0:T(8,128)}, f32[128,1536]{1,0:T(8,128)S(1)}, u32[]{:S(2)}) copy-start(f32[128,1536]{1,0:T(8,128)S(1)} %get-tuple-element.82) | copy-start | bytes 2359300
  87.2 16.1 %copy-start.13 = (f32[128,1536]{1,0:T(8,128)}, f32[128,1536]{1,0:T(8,128)S(1)}, u32[]{:S(2)}) copy-start(f32[128,1536]{1,0:T(8,128)S(1)} %get-tuple-element.84) | copy-start | bytes 2359300
  87.2 32.9 %collective-permute-start.18 = (bf16[256,1536]{1,0:T(8,128)(2,1)}, bf16[256,1536]{1,0:T(8,128)(2,1)}, u32[]{:S(2)}, u32[]{:S(2)}) collective-permute-start(bf16[256,1536]{1,0:T(8,128)(2,1)} %get-tuple-element.83), channel_id=1, source_target_pairs={{0,20},{1,21},{2,22},{3,23},{4,16},{5,17},{6,18},{7,19},{8,28},{9,... | collective-permute-start | bytes 2359304 | tf_op jit(solution)/shard_map/ppermute | solution.py:49
  90.1 11.2 %collective-permute-start.20 = (bf16[96,1536]{1,0:T(8,128)(2,1)S(1)}, bf16[96,1536]{1,0:T(8,128)(2,1)S(1)}, u32[]{:S(2)}, u32[]{:S(2)}) collective-permute-start(bf16[96,1536]{1,0:T(8,128)(2,1)S(1)} %get-tuple-element.64), channel_id=1, source_target_pairs={{0,32},{1,33},{2,34},{3,35},{4,36},{5,37},{6,38},{7,39},{8,40},{9,... | collective-permute-start | bytes 884744 | tf_op jit(solution)/shard_map/ppermute | solution.py:49
  91.9 9.9 %collective-permute-start.21 = (bf16[96,1536]{1,0:T(8,128)(2,1)S(1)}, bf16[96,1536]{1,0:T(8,128)(2,1)S(1)}, u32[]{:S(2)}, u32[]{:S(2)}) collective-permute-start(bf16[96,1536]{1,0:T(8,128)(2,1)S(1)} %get-tuple-element.65), channel_id=1, source_target_pairs={{0,224},{1,225},{2,226},{3,227},{4,228},{5,229},{6,230},{7,231},{8... | collective-permute-start | bytes 884744 | tf_op jit(solution)/shard_map/ppermute | solution.py:49
  93.4 14.2 %collective-permute-start.22 = (bf16[96,1536]{1,0:T(8,128)(2,1)S(1)}, bf16[96,1536]{1,0:T(8,128)(2,1)S(1)}, u32[]{:S(2)}, u32[]{:S(2)}) collective-permute-start(bf16[96,1536]{1,0:T(8,128)(2,1)S(1)} %get-tuple-element.75), channel_id=1, source_target_pairs={{0,32},{1,33},{2,34},{3,35},{4,36},{5,37},{6,38},{7,39},{8,40},{9,... | collective-permute-start | bytes 884744 | tf_op jit(solution)/shard_map/ppermute | solution.py:49
  93.9 14.2 %collective-permute-start.23 = (bf16[96,1536]{1,0:T(8,128)(2,1)S(1)}, bf16[96,1536]{1,0:T(8,128)(2,1)S(1)}, u32[]{:S(2)}, u32[]{:S(2)}) collective-permute-start(bf16[96,1536]{1,0:T(8,128)(2,1)S(1)} %get-tuple-element.76), channel_id=1, source_target_pairs={{0,224},{1,225},{2,226},{3,227},{4,228},{5,229},{6,230},{7,231},{8... | collective-permute-start | bytes 884744 | tf_op jit(solution)/shard_map/ppermute | solution.py:49
  103.3 13.3 %collective-permute-start.26 = (bf16[96,1536]{1,0:T(8,128)(2,1)}, bf16[96,1536]{1,0:T(8,128)(2,1)S(1)}, u32[]{:S(2)}, u32[]{:S(2)}) collective-permute-start(bf16[96,1536]{1,0:T(8,128)(2,1)} %get-tuple-element.86), channel_id=1, source_target_pairs={{0,32},{1,33},{2,34},{3,35},{4,36},{5,37},{6,38},{7,39},{8,40},{9,... | collective-permute-start | bytes 884744 | tf_op jit(solution)/shard_map/ppermute | solution.py:49
  104.0 4.9 %copy-start.7 = (bf16[128,3072]{1,0:T(8,128)(2,1)S(1)}, bf16[128,3072]{1,0:T(8,128)(2,1)}, u32[]{:S(2)}) copy-start(bf16[128,3072]{1,0:T(8,128)(2,1)} %copy-done.5) | copy-start | bytes 2359300
  104.0 15.5 %collective-permute-start.27 = (bf16[96,1536]{1,0:T(8,128)(2,1)}, bf16[96,1536]{1,0:T(8,128)(2,1)S(1)}, u32[]{:S(2)}, u32[]{:S(2)}) collective-permute-start(bf16[96,1536]{1,0:T(8,128)(2,1)} %get-tuple-element.87), channel_id=1, source_target_pairs={{0,224},{1,225},{2,226},{3,227},{4,228},{5,229},{6,230},{7,231},{8... | collective-permute-start | bytes 884744 | tf_op jit(solution)/shard_map/ppermute | solution.py:49
  115.1 1.1 copy-start.9
  116.2 5.9 %collective-permute-start.24 = (bf16[256,1536]{1,0:T(8,128)(2,1)}, bf16[256,1536]{1,0:T(8,128)(2,1)}, u32[]{:S(2)}, u32[]{:S(2)}) collective-permute-start(bf16[256,1536]{1,0:T(8,128)(2,1)} %get-tuple-element.97), channel_id=1, source_target_pairs={{0,8},{1,9},{2,10},{3,11},{4,12},{5,13},{6,14},{7,15},{8,0},{9,1},... | collective-permute-start | bytes 2359304 | tf_op jit(solution)/shard_map/ppermute | solution.py:49
  116.2 10.6 %collective-permute-start.28 = (bf16[96,1536]{1,0:T(8,128)(2,1)S(1)}, bf16[96,1536]{1,0:T(8,128)(2,1)S(1)}, u32[]{:S(2)}, u32[]{:S(2)}) collective-permute-start(bf16[96,1536]{1,0:T(8,128)(2,1)S(1)} %get-tuple-element.89), channel_id=1, source_target_pairs={{0,32},{1,33},{2,34},{3,35},{4,36},{5,37},{6,38},{7,39},{8,40},{9,... | collective-permute-start | bytes 884744 | tf_op jit(solution)/shard_map/ppermute | solution.py:49
  116.6 10.3 %collective-permute-start.29 = (bf16[96,1536]{1,0:T(8,128)(2,1)S(1)}, bf16[96,1536]{1,0:T(8,128)(2,1)S(1)}, u32[]{:S(2)}, u32[]{:S(2)}) collective-permute-start(bf16[96,1536]{1,0:T(8,128)(2,1)S(1)} %get-tuple-element.90), channel_id=1, source_target_pairs={{0,224},{1,225},{2,226},{3,227},{4,228},{5,229},{6,230},{7,231},{8... | collective-permute-start | bytes 884744 | tf_op jit(solution)/shard_map/ppermute | solution.py:49
  120.1 1.5 copy-start.12
  120.1 1.6 %copy-start.14 = (f32[128,1536]{1,0:T(8,128)S(1)}, f32[128,1536]{1,0:T(8,128)}, u32[]{:S(2)}) copy-start(f32[128,1536]{1,0:T(8,128)} %copy-done.13) | copy-start | bytes 2359300
  121.7 5.1 %copy-start.1 = (bf16[768,1536]{1,0:T(8,128)(2,1)S(1)}, bf16[768,1536]{1,0:T(8,128)(2,1)}, u32[]{:S(2)}) copy-start(bf16[768,1536]{1,0:T(8,128)(2,1)} %copy-done) | copy-start | bytes 7077892
  122.0 25.3 %collective-permute-start.19 = (bf16[128,1536]{1,0:T(8,128)(2,1)S(1)}, bf16[128,1536]{1,0:T(8,128)(2,1)S(1)}, u32[]{:S(2)}, u32[]{:S(2)}) collective-permute-start(bf16[128,1536]{1,0:T(8,128)(2,1)S(1)} %get-tuple-element.102), channel_id=1, source_target_pairs={{0,8},{1,9},{2,10},{3,11},{4,12},{5,13},{6,14},{7,15},{8,0},{9,1},... | collective-permute-start | bytes 1179656 | tf_op jit(solution)/shard_map/ppermute | solution.py:49
  127.5 2.6 %copy-start.10 = (f32[256,1536]{1,0:T(8,128)S(1)}, f32[256,1536]{1,0:T(8,128)}, u32[]{:S(2)}) copy-start(f32[256,1536]{1,0:T(8,128)} %copy-done.9) | copy-start | bytes 4718596
  127.6 6.8 %collective-permute-start.32 = (bf16[24,3072]{1,0:T(8,128)(2,1)S(1)}, bf16[24,3072]{1,0:T(8,128)(2,1)S(1)}, u32[]{:S(2)}, u32[]{:S(2)}) collective-permute-start(bf16[24,3072]{1,0:T(8,128)(2,1)S(1)} %get-tuple-element.105), channel_id=1, source_target_pairs={{0,3},{1,0},{2,1},{3,2},{4,7},{5,4},{6,5},{7,6},{8,11},{9,8},{10,9... | collective-permute-start | bytes 442376 | tf_op jit(solution)/shard_map/ppermute | solution.py:49
  128.0 8.0 %collective-permute-start.31 = (bf16[24,3072]{1,0:T(8,128)(2,1)S(1)}, bf16[24,3072]{1,0:T(8,128)(2,1)S(1)}, u32[]{:S(2)}, u32[]{:S(2)}) collective-permute-start(bf16[24,3072]{1,0:T(8,128)(2,1)S(1)} %get-tuple-element.104), channel_id=1, source_target_pairs={{0,2},{1,3},{2,0},{3,1},{4,6},{5,7},{6,4},{7,5},{8,10},{9,11},{10,... | collective-permute-start | bytes 442376 | tf_op jit(solution)/shard_map/ppermute | solution.py:49
  129.0 8.9 %collective-permute-start.30 = (bf16[24,3072]{1,0:T(8,128)(2,1)S(1)}, bf16[24,3072]{1,0:T(8,128)(2,1)S(1)}, u32[]{:S(2)}, u32[]{:S(2)}) collective-permute-start(bf16[24,3072]{1,0:T(8,128)(2,1)S(1)} %get-tuple-element.103), channel_id=1, source_target_pairs={{0,1},{1,2},{2,3},{3,0},{4,5},{5,6},{6,7},{7,4},{8,9},{9,10},{10,1... | collective-permute-start | bytes 442376 | tf_op jit(solution)/shard_map/ppermute | solution.py:49
  131.5 24.8 %collective-permute-start.25 = (bf16[128,1536]{1,0:T(8,128)(2,1)S(1)}, bf16[128,1536]{1,0:T(8,128)(2,1)S(1)}, u32[]{:S(2)}, u32[]{:S(2)}) collective-permute-start(bf16[128,1536]{1,0:T(8,128)(2,1)S(1)} %get-tuple-element.107), channel_id=1, source_target_pairs={{0,20},{1,21},{2,22},{3,23},{4,16},{5,17},{6,18},{7,19},{8,28},{9,... | collective-permute-start | bytes 1179656 | tf_op jit(solution)/shard_map/ppermute | solution.py:49
  138.1 16.6 %collective-permute-start.34 = (bf16[12,3072]{1,0:T(8,128)(2,1)S(1)}, bf16[12,3072]{1,0:T(8,128)(2,1)S(1)}, u32[]{:S(2)}, u32[]{:S(2)}) collective-permute-start(bf16[12,3072]{1,0:T(8,128)(2,1)S(1)} %get-tuple-element.109), channel_id=1, source_target_pairs={{0,25},{1,27},{2,29},{3,31},{4,185},{5,187},{6,189},{7,191},{8,73}... | collective-permute-start | bytes 221192 | tf_op jit(solution)/shard_map/ppermute | solution.py:49
  141.3 14.4 %collective-permute-start.33 = (bf16[12,3072]{1,0:T(8,128)(2,1)S(1)}, bf16[12,3072]{1,0:T(8,128)(2,1)S(1)}, u32[]{:S(2)}, u32[]{:S(2)}) collective-permute-start(bf16[12,3072]{1,0:T(8,128)(2,1)S(1)} %get-tuple-element.108), channel_id=1, source_target_pairs={{0,24},{1,26},{2,28},{3,30},{4,184},{5,186},{6,188},{7,190},{8,72}... | collective-permute-start | bytes 221192 | tf_op jit(solution)/shard_map/ppermute | solution.py:49

commit v3 on v2

--- a/solution.py
+++ b/solution.py
@@ -1,3 +1,5 @@
+import functools
+
 import jax
 import jax.numpy as jnp
 from jax import lax
@@ -100,7 +102,7 @@
     return call(
         dequantize_kernel,
         "dequantize",
-        12,
+        60,
         where,
         (3,),
         [
@@ -115,6 +117,30 @@
     )
 
 
+def pack_kernel(where, tokens, cotangent, out):
+    kh = tokens.shape[1]
+    out[:, :kh] = tokens[...]
+    out[:, kh:] = cotangent[...]
+
+
+def pack(where, tokens, cotangent):
+    count, kh = tokens.shape[0], tokens.shape[1] // 2
+    width = kh + cotangent.shape[1]
+    return call(
+        pack_kernel,
+        "pack",
+        60,
+        where,
+        (1,),
+        [fixed((count, kh), lambda where: (0, 1 - where[1])), fixed(cotangent.shape)],
+        fixed((count, width)),
+        jax.ShapeDtypeStruct((count, width), jnp.bfloat16),
+        [],
+        0,
+        (tokens, cotangent),
+    )
+
+
 def columns(ref, start, size):
     return ref[:, pl.ds(pl.multiple_of(start, 128), size)]
 
@@ -141,60 +167,59 @@
     down[...] = out[pl.ds(start + half, half)]
 
 
-def gradient(where, token_parts, cot_parts, j):
+def gradient(where, token_parts, cot_parts):
     count, outputs = cot_parts[0].shape
-    size = token_parts[0].shape[1] // 4
-    width = outputs // 4
+    kh = token_parts[0].shape[1] // 2
+    size, width = kh // 2, outputs // 4
     heights = (size, size // 16, size // 16)
     return call(
         gradient_kernel,
         "gradient",
         24,
         where,
-        (2,),
-        [fixed(v.shape) for v in token_parts]
-        + [pl.BlockSpec((count, width), lambda i, where: (0, 2 * j + i)) for _ in cot_parts],
+        (4,),
+        [fixed(v.shape) for v in token_parts[:2]]
+        + [fixed((count, kh))] * 2
+        + [pl.BlockSpec((count, width), lambda i, where: (0, i))] * 2
+        + [pl.BlockSpec((count, width), lambda i, where: (0, i + 2))] * 2,
         [pl.BlockSpec((height, width), lambda i, where: (0, i)) for height in heights],
-        [jax.ShapeDtypeStruct((height, 2 * width), jnp.bfloat16) for height in heights],
+        [jax.ShapeDtypeStruct((height, outputs), jnp.bfloat16) for height in heights],
         [pltpu.VMEM((4 * count, size), jnp.bfloat16)],
-        4 * count * size * outputs,
+        8 * count * size * outputs,
         (*token_parts, *cot_parts),
     )
 
 
-def hop_kernel(where, up, down, near_up, near_down, *outs):
-    half = near_up.shape[0] // 2
-    if up.shape[0] == half:
-        outs[0][:half] = bf16(f32(near_up[:half]) + f32(up[...]))
-        outs[0][half:] = near_up[half:]
-        outs[1][:half] = near_down[:half]
-        outs[1][half:] = bf16(f32(near_down[half:]) + f32(down[...]))
-    elif len(outs) == 2:
-        outs[0][...] = bf16(f32(near_up[...]) + f32(up[...]))
-        outs[1][...] = bf16(f32(near_down[...]) + f32(down[...]))
-    else:
-        outs[0][...] = f32(near_up[...]) + f32(up[...]) + f32(down[...])
-
-
-def hop(where, step, up, down, part):
+def hop_kernel(where, *refs):
+    *arrived, near, out = refs
+    total = f32(near[...])
+    for ref in arrived:
+        total = total + f32(ref[...])
+    out[...] = total.astype(out.dtype)
+
+
+def first_hop_kernel(where, arrived, near, out, *, upper):
+    half = arrived.shape[0]
+    here, there = (slice(0, half), slice(half, 2 * half))[:: 1 if upper else -1]
+    out[here] = bf16(f32(near[here]) + f32(arrived[...]))
+    out[there] = near[there]
+
+
+def hop(where, part, k, kernel, kind, *arrived):
     size, width = part.shape[0] // 8, part.shape[1]
-    kinds = [jnp.float32] if step == 3 else [jnp.bfloat16] * 2
-    return call(
-        hop_kernel,
+    return call(
+        kernel,
         "hop",
         8,
         where,
         (1,),
-        [fixed(up.shape), fixed(down.shape)]
-        + [
-            fixed((size, width), lambda where, k=k: ((where[3] + 8 + k) % 8, 0))
-            for k in (3 - step, step - 3)
-        ],
-        [fixed((size, width)) for _ in kinds],
-        [jax.ShapeDtypeStruct((size, width), kind) for kind in kinds],
+        [fixed(v.shape) for v in arrived]
+        + [fixed((size, width), lambda where: ((where[3] + 8 + k) % 8, 0))],
+        fixed((size, width)),
+        jax.ShapeDtypeStruct((size, width), kind),
         [],
         2 * size * width,
-        (up, down, part, part),
+        (*arrived, part),
     )
 
 
@@ -230,7 +255,8 @@
         28,
         where,
         (2,),
-        [fixed(v.shape) for v in token_parts]
+        [fixed(v.shape) for v in token_parts[:2]]
+        + [fixed((count, 4 * shard))] * 2
         + [pl.BlockSpec((shard, width), lambda i, where: (0, i))] * 3
         + [fixed((shard, width))] * 2,
         [pl.BlockSpec((height, width), lambda i, where: (0, i)) for height, _ in kinds],
@@ -275,7 +301,8 @@
         28,
         where,
         (3,),
-        [fixed((count, nh), lambda where: (0, where[0])) for _ in cot_parts]
+        [fixed((count, nh), lambda where: (0, where[0]))] * 2
+        + [fixed((count, nh), lambda where: (0, 1 + where[0]))] * 2
         + [pl.BlockSpec((size, nh), lambda i, where: (i, 0))] * 3
         + [pl.BlockSpec((size, nh // 2), lambda i, where: (i, 0))] * 2,
         [fixed((2 * count, 4 * shard))] * 2,
@@ -308,54 +335,53 @@
 def on_device(tokens, cotangent, levels, scales):
     z, yl, c, yh, x = (lax.axis_index(name) for name in AXES)
     where = jnp.stack([c, yh, x, window(z, c, yh)]).astype(jnp.int32)
-    count, features = tokens.shape
-    kh = features // 2
+    count = tokens.shape[0]
     factor = float(count * 256) ** -0.5
 
-    cot_pair = send(cotangent, PAIR)
+    packed = pack(where, tokens, cotangent)
+    pair = send(packed, PAIR)
+
+    levels, scales = after((levels, scales), packed)
     own = dequantize(where, levels, scales)
     left, right = send(own, X_UP), send(own, X_DOWN)
-    token_out = lax.dynamic_slice_in_dim(after(tokens, own), (1 - yh) * kh, kh, 1)
-    token_pair = send(token_out, PAIR)
-
-    cot_own, token_own = after((cotangent, tokens), token_out)
+
+    cot_own, token_own = after((cotangent, tokens), own)
     cot_sib, token_sib = send(cot_own, CORE), send(token_own, CORE)
-    token_parts = (tokens, token_sib, token_pair, send(token_pair, CORE))
-    cot_parts = (cotangent, cot_sib, cot_pair, send(cot_pair, CORE))
-
+    cross = send(pair, CORE)
+    token_parts = (tokens, token_sib, pair, cross)
+    cot_parts = (cotangent, cot_sib, pair, cross)
+
+    grad, up, down = gradient(where, token_parts, cot_parts)
     half = own.shape[1] // 2
     far_left, far_right = left[:, :half], right[:, half:]
-    cot_ready = after(cot_parts, left, right, far_left, far_right)
-    chains = []
-    for j in range(2):
-        chains.append(gradient(where, token_parts, cot_ready, j))
-        cot_ready = after(cot_ready, chains[-1])
     blocks = (own, left, right, send(far_left, X_UP), send(far_right, X_DOWN))
-    for step in range(4):
-        if step == 2:
-            mine, other, away = forward_parts(where, token_parts, after(blocks, chains))
-            back = f32(send(away, PAIR))
-            held = after([chain[0] for chain in chains], away)
-        if step == 3:
-            part, give = backward_parts(where, cot_parts, after(blocks, chains))
-            give = send(give, CORE)
-            held = after([chain[0] for chain in chains], part)
-            held[1] = after(held[1], back, give)
-        for j in range(2):
-            grad, up, down = chains[j]
-            grad = held[j] if step >= 2 else grad
-            got = hop(where, step, send(up, Z_UP), send(down, Z_DOWN), grad)
-            chains[j] = (grad, *got)
-    sums = [chain[1] for chain in chains]
+    up, down = send(up, Z_UP), send(down, Z_DOWN)
+    up = hop(where, grad, 3, functools.partial(first_hop_kernel, upper=True), jnp.bfloat16, up)
+    down = hop(where, grad, -3, functools.partial(first_hop_kernel, upper=False), jnp.bfloat16, down)
+    mine, other, away = forward_parts(where, token_parts, after(blocks, up, down))
+    up, down = send(up, Z_UP), send(down, Z_DOWN)
+    back = f32(send(away, PAIR))
+    grad = after(grad, away)
+    up = hop(where, grad, 2, hop_kernel, jnp.bfloat16, up)
+    down = hop(where, grad, -2, hop_kernel, jnp.bfloat16, down)
+    part, give = backward_parts(where, cot_parts, after(blocks, up, down))
+    up, down = send(up, Z_UP), send(down, Z_DOWN)
+    give = send(give, CORE)
+    grad = after(grad, give, back)
+    up = hop(where, grad, 1, hop_kernel, jnp.bfloat16, up)
+    down = hop(where, grad, -1, hop_kernel, jnp.bfloat16, down)
+    up, down = send(up, Z_UP), send(down, Z_DOWN)
+    total = hop(where, grad, 0, hop_kernel, jnp.float32, up, down)
 
     part = part + f32(give)
     grad_input = joined(bf16(part[:count]), send(bf16(part[count:]), PAIR), yh)
     there = send(bf16(other + back[count:]), CORE)
     forward = joined(bf16(mine + back[:count]), there, c)
 
-    total = bf16(reduce_over_x(jnp.concatenate(sums, axis=1), x) * factor)
+    total = bf16(reduce_over_x(after(total, forward, part), x) * factor)
     size = total.shape[0] // 2
     got = [f32(send(rows(total, (yl ^ m) * size, size), OWNERS[m])) for m in range(2)]
+    got, grad_input = after((got, grad_input))
     return forward, grad_input, got[0] + got[1]
 
 

time: 159 us -> 141 us (0.89)
  the two profiles are of different devices: /device:TPU:24 before, /device:TPU:57 now
where the time goes in v3:
time: 141 us; the launch traced here: 140 us
  waiting for transfers between devices  61.5 us (44%)
  starting transfers between devices  39.9 us (28%)
  Pallas kernels  28.3 us (20%)
  other arithmetic  6.18 us (4%)
  local copies, waits for them, and re-layouts  3.45 us (2%)
    ppermute x25, waiting for transfers between devices, send(): return lax.ppermute(value, AXES, pairs)  61.5 us
    ppermute x25, starting transfers between devices, send(): return lax.ppermute(value, AXES, pairs)  39.9 us
    pallas_call x12, Pallas kernels, call(): pl.pallas_call(kernel, name=name, grid_spec=pltpu.PrefetchScalarGridSpec(...  28.3 us
    select_n x2, other arithmetic, joined(): jnp.where(flag == 0, jnp.concatenate([here, there], axis=1), jnp.concaten...  3.25 us
  transfers between devices with their start and end apart: 25, of which 11 were waited for; matrix products, arithmetic and copies ran while one was open for 4% of the time, Pallas kernels for 18%

profile of v3, /device:TPU:57, one launch (start us, length us, event | category | flops | bytes accessed | tf_op | source)
XLA Modules:
  0.0 140.3 jit_solution(12769878892191758070)
XLA Ops:
  0.7 0.6 pad_add_fusion.where
  1.2 3.0 %pack.1 = bf16[128,4608]{1,0:T(8,128)(2,1)} custom-call(s32[4]{0:T(128)} %pad_add_fusion.where, bf16[128,3072]{1,0:T(8,128)(2,1)} %own.3, bf16[128,3072]{1,0:T(8,128)(2,1)} %cot0.3), custom_call_target="tpu_custom_call" | custom-call | bytes 2752512 | tf_op jit(solution)/shard_map/pack/pallas_call | solution.py:69
  4.3 0.0 collective-permute-start.1
  4.3 0.8 copy.7.scales
  5.1 4.7 %dequantize.1.w0 = bf16[384,1536]{1,0:T(8,128)(2,1)} custom-call(s32[4]{0:T(128)} %pad_add_fusion.where, bf16[384,3072]{1,0:T(8,128)(2,1)} %levels, f32[384,12]{1,0:T(8,128)} %copy.7.scales), custom_call_target="tpu_custom_call" | custom-call | flops 589824 | bytes 3557376 | tf_op jit(solution)/shard_map/dequantize/pallas_call | solution.py:69
  9.8 1.2 collective-permute-start.3
  11.0 1.5 %collective-permute-start.4 = (bf16[384,1536]{1,0:T(8,128)(2,1)}, bf16[384,1536]{1,0:T(8,128)(2,1)S(1)}, u32[]{:S(2)}, u32[]{:S(2)}) collective-permute-start(bf16[384,1536]{1,0:T(8,128)(2,1)} %dequantize.1.w0), channel_id=1, source_target_pairs={{0,3},{1,0},{2,1},{3,2},{4,7},{5,4},{6,5},{7,6},{8,11},{9,8},{10,9... | collective-permute-start | bytes 3538952 | tf_op jit(solution)/shard_map/ppermute | solution.py:51
  12.5 20.0 %collective-permute-done.1.pair.cot2 = bf16[128,4608]{1,0:T(8,128)(2,1)S(1)} collective-permute-done((bf16[128,4608]{1,0:T(8,128)(2,1)}, bf16[128,4608]{1,0:T(8,128)(2,1)S(1)}, u32[]{:S(2)}, u32[]{:S(2)}) %collective-permute-start.1) | collective-permute-done | bytes 1179680 | tf_op jit(solution)/shard_map/ppermute | solution.py:51
  32.5 1.5 %collective-permute-start.2 = (bf16[128,4608]{1,0:T(8,128)(2,1)S(1)}, bf16[128,4608]{1,0:T(8,128)(2,1)S(1)}, u32[]{:S(2)}, u32[]{:S(2)}) collective-permute-start(bf16[128,4608]{1,0:T(8,128)(2,1)S(1)} %collective-permute-done.1.pair.cot2), channel_id=1, source_target_pairs={{0,8},{1,9},{2,10},{3,11},{4,12},{5,13},{6,14},{7,15},{8,0},{9,1},... | collective-permute-start | bytes 3538952 | tf_op jit(solution)/shard_map/ppermute | solution.py:51
  34.1 0.1 collective-permute-start
  34.2 0.4 collective-permute-start.7
  34.6 3.3 %collective-permute-done.3.w1 = bf16[384,1536]{1,0:T(8,128)(2,1)S(1)} collective-permute-done((bf16[384,1536]{1,0:T(8,128)(2,1)}, bf16[384,1536]{1,0:T(8,128)(2,1)S(1)}, u32[]{:S(2)}, u32[]{:S(2)}) %collective-permute-start.3) | collective-permute-done | bytes 1179680 | tf_op jit(solution)/shard_map/ppermute | solution.py:51
  37.9 0.1 collective-permute-start.5
  38.0 0.0 collective-permute-done.4.w2
  38.0 2.7 %collective-permute-start.6 = (bf16[384,768]{1,0:T(8,128)(2,1)S(1)}, bf16[384,768]{1,0:T(8,128)(2,1)S(1)}, u32[]{:S(2)}, u32[]{:S(2)}) collective-permute-start(bf16[384,768]{1,0:T(8,128)(2,1)S(1)} %slice.27), channel_id=1, source_target_pairs={{0,3},{1,0},{2,1},{3,2},{4,7},{5,4},{6,5},{7,6},{8,11},{9,8},{10,9... | collective-permute-start | bytes 1769480 | tf_op jit(solution)/shard_map/ppermute | solution.py:51
  40.8 0.0 collective-permute-done.7.cot1
  40.8 0.0 collective-permute-done.2.psib.cot3
  40.8 4.8 %gradient.1 = (bf16[768,3072]{1,0:T(8,128)(2,1)S(1)}, bf16[48,3072]{1,0:T(8,128)(2,1)S(1)}, bf16[48,3072]{1,0:T(8,128)(2,1)S(1)}) custom-call(s32[4]{0:T(128)S(1)} %copy-done.5, bf16[128,3072]{1,0:T(8,128)(2,1)S(1)} %copy-done.3, bf16[128,3072]{1,0:T(8,128)(2,1)S(1)} %collective-permute-done.sib, bf16[128,4608]{1,0:T(8,128)(2,1)S(1)} %collective-permute-done.1.pair.cot2, ...), custom_call_target="tpu_custom_call" | custom-call | flops 2415919104 | bytes 13172736 | tf_op jit(solution)/shard_map/gradient/pallas_call | solution.py:69
  45.6 1.7 %collective-permute-start.8 = (bf16[48,3072]{1,0:T(8,128)(2,1)S(1)}, bf16[48,3072]{1,0:T(8,128)(2,1)S(1)}, u32[]{:S(2)}, u32[]{:S(2)}) collective-permute-start(bf16[48,3072]{1,0:T(8,128)(2,1)S(1)} %get-tuple-element.35), channel_id=1, source_target_pairs={{0,32},{1,33},{2,34},{3,35},{4,36},{5,37},{6,38},{7,39},{8,40},{9,... | collective-permute-start | bytes 884744 | tf_op jit(solution)/shard_map/ppermute | solution.py:51
  47.3 0.0 collective-permute-start.9
  47.3 4.5 %collective-permute-done.8.arrived = bf16[48,3072]{1,0:T(8,128)(2,1)S(1)} collective-permute-done((bf16[48,3072]{1,0:T(8,128)(2,1)S(1)}, bf16[48,3072]{1,0:T(8,128)(2,1)S(1)}, u32[]{:S(2)}, u32[]{:S(2)}) %collective-permute-start.8) | collective-permute-done | bytes 294944 | tf_op jit(solution)/shard_map/ppermute | solution.py:51
  51.8 0.6 hop.7
  52.4 1.7 %collective-permute-start.12 = (bf16[96,3072]{1,0:T(8,128)(2,1)S(1)}, bf16[96,3072]{1,0:T(8,128)(2,1)S(1)}, u32[]{:S(2)}, u32[]{:S(2)}) collective-permute-start(bf16[96,3072]{1,0:T(8,128)(2,1)S(1)} %hop.7), channel_id=1, source_target_pairs={{0,32},{1,33},{2,34},{3,35},{4,36},{5,37},{6,38},{7,39},{8,40},{9,... | collective-permute-start | bytes 1769480 | tf_op jit(solution)/shard_map/ppermute | solution.py:51
  54.1 0.6 hop.8
  54.8 2.7 %collective-permute-start.14 = (bf16[96,3072]{1,0:T(8,128)(2,1)S(1)}, bf16[96,3072]{1,0:T(8,128)(2,1)S(1)}, u32[]{:S(2)}, u32[]{:S(2)}) collective-permute-start(bf16[96,3072]{1,0:T(8,128)(2,1)S(1)} %hop.8), channel_id=1, source_target_pairs={{0,224},{1,225},{2,226},{3,227},{4,228},{5,229},{6,230},{7,231},{8... | collective-permute-start | bytes 1769480 | tf_op jit(solution)/shard_map/ppermute | solution.py:51
  57.5 4.1 %forward.1 = (f32[128,1536]{1,0:T(8,128)S(1)}, f32[128,1536]{1,0:T(8,128)S(1)}, bf16[256,1536]{1,0:T(8,128)(2,1)S(1)}) custom-call(s32[4]{0:T(128)S(1)} %copy-done.5, bf16[128,3072]{1,0:T(8,128)(2,1)S(1)} %copy-done.3, bf16[128,3072]{1,0:T(8,128)(2,1)S(1)} %collective-permute-done.sib, bf16[128,4608]{1,0:T(8,128)(2,1)S(1)} %collective-permute-done.1.pair.cot2, ...), custom_call_target="tpu_custom_call" | custom-call | flops 2415919104 | bytes 11010048 | tf_op jit(solution)/shard_map/forward/pallas_call | solution.py:69
  61.5 2.8 %collective-permute-start.10 = (bf16[256,1536]{1,0:T(8,128)(2,1)S(1)}, bf16[256,1536]{1,0:T(8,128)(2,1)S(1)}, u32[]{:S(2)}, u32[]{:S(2)}) collective-permute-start(bf16[256,1536]{1,0:T(8,128)(2,1)S(1)} %get-tuple-element.44), channel_id=1, source_target_pairs={{0,20},{1,21},{2,22},{3,23},{4,16},{5,17},{6,18},{7,19},{8,28},{9,... | collective-permute-start | bytes 2359304 | tf_op jit(solution)/shard_map/ppermute | solution.py:51
  64.4 3.0 %collective-permute-done.12.refs_0_ = bf16[96,3072]{1,0:T(8,128)(2,1)S(1)} collective-permute-done((bf16[96,3072]{1,0:T(8,128)(2,1)S(1)}, bf16[96,3072]{1,0:T(8,128)(2,1)S(1)}, u32[]{:S(2)}, u32[]{:S(2)}) %collective-permute-start.12) | collective-permute-done | bytes 589856 | tf_op jit(solution)/shard_map/ppermute | solution.py:51
  67.4 0.7 hop.9
  68.1 0.1 collective-permute-start.13
  68.2 1.5 %hop.10 = bf16[96,3072]{1,0:T(8,128)(2,1)} custom-call(s32[4]{0:T(128)S(1)} %copy-done.5, bf16[96,3072]{1,0:T(8,128)(2,1)S(1)} %collective-permute-done.14.refs_0_, bf16[768,3072]{1,0:T(8,128)(2,1)S(1)} %get-tuple-element.53.near.refs_1_.refs_2_), custom_call_target="tpu_custom_call" | custom-call | flops 589824 | bytes 5898240 | tf_op jit(solution)/shard_map/hop/pallas_call | solution.py:69
  69.7 2.4 %collective-permute-start.17 = (bf16[96,3072]{1,0:T(8,128)(2,1)}, bf16[96,3072]{1,0:T(8,128)(2,1)}, u32[]{:S(2)}, u32[]{:S(2)}) collective-permute-start(bf16[96,3072]{1,0:T(8,128)(2,1)} %hop.10), channel_id=1, source_target_pairs={{0,224},{1,225},{2,226},{3,227},{4,228},{5,229},{6,230},{7,231},{8... | collective-permute-start | bytes 1769480 | tf_op jit(solution)/shard_map/ppermute | solution.py:51
  72.1 4.9 %backward.1 = (f32[256,1536]{1,0:T(8,128)S(1)}, bf16[256,1536]{1,0:T(8,128)(2,1)}) custom-call(s32[4]{0:T(128)S(1)} %copy-done.5, bf16[128,3072]{1,0:T(8,128)(2,1)S(1)} %copy-done.4, bf16[128,3072]{1,0:T(8,128)(2,1)S(1)} %collective-permute-done.7.cot1, bf16[128,4608]{1,0:T(8,128)(2,1)S(1)} %copy-done.7, ...), custom_call_target="tpu_custom_call" | custom-call | flops 2415919104 | bytes 11010048 | tf_op jit(solution)/shard_map/backward/pallas_call | solution.py:69
  77.0 4.2 %collective-permute-start.15 = (bf16[256,1536]{1,0:T(8,128)(2,1)}, bf16[256,1536]{1,0:T(8,128)(2,1)S(1)}, u32[]{:S(2)}, u32[]{:S(2)}) collective-permute-start(bf16[256,1536]{1,0:T(8,128)(2,1)} %get-tuple-element.52), channel_id=1, source_target_pairs={{0,8},{1,9},{2,10},{3,11},{4,12},{5,13},{6,14},{7,15},{8,0},{9,1},... | collective-permute-start | bytes 2359304 | tf_op jit(solution)/shard_map/ppermute | solution.py:51
  81.2 0.2 convert_element_type.41
  81.4 1.2 fusion.1
  82.5 1.8 %collective-permute-start.11 = (bf16[128,1536]{1,0:T(8,128)(2,1)}, bf16[128,1536]{1,0:T(8,128)(2,1)}, u32[]{:S(2)}, u32[]{:S(2)}) collective-permute-start(bf16[128,1536]{1,0:T(8,128)(2,1)} %get-tuple-element.60), channel_id=1, source_target_pairs={{0,8},{1,9},{2,10},{3,11},{4,12},{5,13},{6,14},{7,15},{8,0},{9,1},... | collective-permute-start | bytes 1179656 | tf_op jit(solution)/shard_map/ppermute | solution.py:51
  84.3 2.3 %copy-done.1 = bf16[768,3072]{1,0:T(8,128)(2,1)S(1)} copy-done((bf16[768,3072]{1,0:T(8,128)(2,1)S(1)}, bf16[768,3072]{1,0:T(8,128)(2,1)}, u32[]{:S(2)}) %copy-start.1) | copy-done | bytes 4718616
  86.7 0.7 hop.11
  87.4 0.1 collective-permute-start.16
  87.5 2.0 %hop.12 = bf16[96,3072]{1,0:T(8,128)(2,1)S(1)} custom-call(s32[4]{0:T(128)S(1)} %copy-done.5, bf16[96,3072]{1,0:T(8,128)(2,1)} %collective-permute-done.17.refs_0_, bf16[768,3072]{1,0:T(8,128)(2,1)S(1)} %copy-done.1), custom_call_target="tpu_custom_call" | custom-call | flops 589824 | bytes 5898240 | tf_op jit(solution)/shard_map/hop/pallas_call | solution.py:69
  89.5 2.7 %collective-permute-start.18 = (bf16[96,3072]{1,0:T(8,128)(2,1)S(1)}, bf16[96,3072]{1,0:T(8,128)(2,1)S(1)}, u32[]{:S(2)}, u32[]{:S(2)}) collective-permute-start(bf16[96,3072]{1,0:T(8,128)(2,1)S(1)} %hop.12), channel_id=1, source_target_pairs={{0,224},{1,225},{2,226},{3,227},{4,228},{5,229},{6,230},{7,231},{8... | collective-permute-start | bytes 1769480 | tf_op jit(solution)/shard_map/ppermute | solution.py:51
  92.2 2.2 %maximum_select_fusion = bf16[128,3072]{1,0:T(8,128)(2,1)} fusion(bf16[128,1536]{1,0:T(8,128)(2,1)} %collective-permute-done.11, bf16[128,1536]{1,0:T(8,128)(2,1)S(1)} %copy-done.8, pred[]{:T(512)S(6)} %eq.11), kind=kLoop, calls=%fused_computation.5 | loop fusion | flops 3538944 | bytes 1572865 | tf_op jit(solution)/shard_map/jit(_where)/select_n | solution.py:321
  94.4 0.2 convert_add_fusion
  94.6 8.8 %collective-permute-done.16.refs_0_ = bf16[96,3072]{1,0:T(8,128)(2,1)S(1)} collective-permute-done((bf16[96,3072]{1,0:T(8,128)(2,1)S(1)}, bf16[96,3072]{1,0:T(8,128)(2,1)S(1)}, u32[]{:S(2)}, u32[]{:S(2)}) %collective-permute-start.16) | collective-permute-done | bytes 589856 | tf_op jit(solution)/shard_map/ppermute | solution.py:51
  103.4 2.6 %collective-permute-done.18.refs_1_ = bf16[96,3072]{1,0:T(8,128)(2,1)S(1)} collective-permute-done((bf16[96,3072]{1,0:T(8,128)(2,1)S(1)}, bf16[96,3072]{1,0:T(8,128)(2,1)S(1)}, u32[]{:S(2)}, u32[]{:S(2)}) %collective-permute-start.18) | collective-permute-done | bytes 589856 | tf_op jit(solution)/shard_map/ppermute | solution.py:51
  106.0 0.7 hop.13
  106.7 0.1 dynamic-slice_convert_fusion.2
  106.8 1.0 collective-permute-start.21
  107.8 0.5 collective-permute-start.20
  108.3 0.6 collective-permute-start.19
  108.9 0.1 fusion.2
  109.0 2.1 %collective-permute-start.24 = (bf16[128,1536]{1,0:T(8,128)(2,1)S(1)}, bf16[128,1536]{1,0:T(8,128)(2,1)S(1)}, u32[]{:S(2)}, u32[]{:S(2)}) collective-permute-start(bf16[128,1536]{1,0:T(8,128)(2,1)S(1)} %get-tuple-element.65), channel_id=1, source_target_pairs={{0,20},{1,21},{2,22},{3,23},{4,16},{5,17},{6,18},{7,19},{8,28},{9,... | collective-permute-start | bytes 1179656 | tf_op jit(solution)/shard_map/ppermute | solution.py:51
  111.0 0.4 collective-permute-done.21
  111.4 1.9 %collective-permute-done.20 = bf16[24,3072]{1,0:T(8,128)(2,1)S(1)} collective-permute-done((bf16[24,3072]{1,0:T(8,128)(2,1)S(1)}, bf16[24,3072]{1,0:T(8,128)(2,1)S(1)}, u32[]{:S(2)}, u32[]{:S(2)}) %collective-permute-start.20) | collective-permute-done | bytes 147488 | tf_op jit(solution)/shard_map/ppermute | solution.py:51
  113.4 4.7 %collective-permute-done.19 = bf16[24,3072]{1,0:T(8,128)(2,1)S(1)} collective-permute-done((bf16[24,3072]{1,0:T(8,128)(2,1)S(1)}, bf16[24,3072]{1,0:T(8,128)(2,1)S(1)}, u32[]{:S(2)}, u32[]{:S(2)}) %collective-permute-start.19) | collective-permute-done | bytes 147488 | tf_op jit(solution)/shard_map/ppermute | solution.py:51
  118.1 0.1 multiply_convert_fusion
  118.2 0.1 constant_dynamic-slice_fusion
  118.2 5.1 %collective-permute-start.22 = (bf16[12,3072]{1,0:T(8,128)(2,1)S(1)}, bf16[12,3072]{1,0:T(8,128)(2,1)S(1)}, u32[]{:S(2)}, u32[]{:S(2)}) collective-permute-start(bf16[12,3072]{1,0:T(8,128)(2,1)S(1)} %get-tuple-element.67), channel_id=1, source_target_pairs={{0,24},{1,26},{2,28},{3,30},{4,184},{5,186},{6,188},{7,190},{8,72}... | collective-permute-start | bytes 221192 | tf_op jit(solution)/shard_map/ppermute | solution.py:51
  123.4 2.8 %collective-permute-start.23 = (bf16[12,3072]{1,0:T(8,128)(2,1)S(1)}, bf16[12,3072]{1,0:T(8,128)(2,1)S(1)}, u32[]{:S(2)}, u32[]{:S(2)}) collective-permute-start(bf16[12,3072]{1,0:T(8,128)(2,1)S(1)} %get-tuple-element.66), channel_id=1, source_target_pairs={{0,25},{1,27},{2,29},{3,31},{4,185},{5,187},{6,189},{7,191},{8,73}... | collective-permute-start | bytes 221192 | tf_op jit(solution)/shard_map/ppermute | solution.py:51
  126.2 1.1 maximum_select_fusion.1
  127.3 4.5 %collective-permute-done.22 = bf16[12,3072]{1,0:T(8,128)(2,1)S(1)} collective-permute-done((bf16[12,3072]{1,0:T(8,128)(2,1)S(1)}, bf16[12,3072]{1,0:T(8,128)(2,1)S(1)}, u32[]{:S(2)}, u32[]{:S(2)}) %collective-permute-start.22) | collective-permute-done | bytes 73760 | tf_op jit(solution)/shard_map/ppermute | solution.py:51
  131.7 7.8 %collective-permute-done.23 = bf16[12,3072]{1,0:T(8,128)(2,1)S(1)} collective-permute-done((bf16[12,3072]{1,0:T(8,128)(2,1)S(1)}, bf16[12,3072]{1,0:T(8,128)(2,1)S(1)}, u32[]{:S(2)}, u32[]{:S(2)}) %collective-permute-start.23) | collective-permute-done | bytes 73760 | tf_op jit(solution)/shard_map/ppermute | solution.py:51
  139.6 0.7 add.84
  (39 shorter events, 0.2 us)
Async XLA Ops:
  0.6 3.6 %copy-start.9 = (f32[384,12]{0,1:T(8,128)S(1)}, f32[384,12]{0,1:T(8,128)}, u32[]{:S(2)}) copy-start(f32[384,12]{0,1:T(8,128)} %param.7) | copy-start | bytes 55300
  4.3 28.3 %collective-permute-start.1 = (bf16[128,4608]{1,0:T(8,128)(2,1)}, bf16[128,4608]{1,0:T(8,128)(2,1)S(1)}, u32[]{:S(2)}, u32[]{:S(2)}) collective-permute-start(bf16[128,4608]{1,0:T(8,128)(2,1)} %pack.1), channel_id=1, source_target_pairs={{0,20},{1,21},{2,22},{3,23},{4,16},{5,17},{6,18},{7,19},{8,28},{9,... | collective-permute-start | bytes 3538952 | tf_op jit(solution)/shard_map/ppermute | solution.py:51
  5.1 29.0 %copy-start.3 = (bf16[128,3072]{1,0:T(8,128)(2,1)S(1)}, bf16[128,3072]{1,0:T(8,128)(2,1)}, u32[]{:S(2)}) copy-start(bf16[128,3072]{1,0:T(8,128)(2,1)} %own.3) | copy-start | bytes 2359300
  5.1 29.1 %copy-start.4 = (bf16[128,3072]{1,0:T(8,128)(2,1)S(1)}, bf16[128,3072]{1,0:T(8,128)(2,1)}, u32[]{:S(2)}) copy-start(bf16[128,3072]{1,0:T(8,128)(2,1)} %cot0.3) | copy-start | bytes 2359300
  9.8 30.9 %copy-start.5 = (s32[4]{0:T(128)S(1)}, s32[4]{0:T(128)}, u32[]{:S(2)}) copy-start(s32[4]{0:T(128)} %pad_add_fusion.where) | copy-start | bytes 52
  9.8 28.0 %collective-permute-start.3 = (bf16[384,1536]{1,0:T(8,128)(2,1)}, bf16[384,1536]{1,0:T(8,128)(2,1)S(1)}, u32[]{:S(2)}, u32[]{:S(2)}) collective-permute-start(bf16[384,1536]{1,0:T(8,128)(2,1)} %dequantize.1.w0), channel_id=1, source_target_pairs={{0,1},{1,2},{2,3},{3,0},{4,5},{5,6},{6,7},{7,4},{8,9},{9,10},{10,1... | collective-permute-start | bytes 3538952 | tf_op jit(solution)/shard_map/ppermute | solution.py:51
  11.0 26.9 %collective-permute-start.4 = (bf16[384,1536]{1,0:T(8,128)(2,1)}, bf16[384,1536]{1,0:T(8,128)(2,1)S(1)}, u32[]{:S(2)}, u32[]{:S(2)}) collective-permute-start(bf16[384,1536]{1,0:T(8,128)(2,1)} %dequantize.1.w0), channel_id=1, source_target_pairs={{0,3},{1,0},{2,1},{3,2},{4,7},{5,4},{6,5},{7,6},{8,11},{9,8},{10,9... | collective-permute-start | bytes 3538952 | tf_op jit(solution)/shard_map/ppermute | solution.py:51
  32.5 25.0 %copy-start.6 = (bf16[128,4608]{1,0:T(8,128)(2,1)}, bf16[128,4608]{1,0:T(8,128)(2,1)S(1)}, u32[]{:S(2)}) copy-start(bf16[128,4608]{1,0:T(8,128)(2,1)S(1)} %collective-permute-done.1.pair.cot2) | copy-start | bytes 3538948
  32.5 8.2 %collective-permute-start.2 = (bf16[128,4608]{1,0:T(8,128)(2,1)S(1)}, bf16[128,4608]{1,0:T(8,128)(2,1)S(1)}, u32[]{:S(2)}, u32[]{:S(2)}) collective-permute-start(bf16[128,4608]{1,0:T(8,128)(2,1)S(1)} %collective-permute-done.1.pair.cot2), channel_id=1, source_target_pairs={{0,8},{1,9},{2,10},{3,11},{4,12},{5,13},{6,14},{7,15},{8,0},{9,1},... | collective-permute-start | bytes 3538952 | tf_op jit(solution)/shard_map/ppermute | solution.py:51
  34.1 6.7 %collective-permute-start = (bf16[128,3072]{1,0:T(8,128)(2,1)S(1)}, bf16[128,3072]{1,0:T(8,128)(2,1)S(1)}, u32[]{:S(2)}, u32[]{:S(2)}) collective-permute-start(bf16[128,3072]{1,0:T(8,128)(2,1)S(1)} %copy-done.3), channel_id=1, source_target_pairs={{0,8},{1,9},{2,10},{3,11},{4,12},{5,13},{6,14},{7,15},{8,0},{9,1},... | collective-permute-start | bytes 2359304 | tf_op jit(solution)/shard_map/ppermute | solution.py:51
  34.2 6.6 %collective-permute-start.7 = (bf16[128,3072]{1,0:T(8,128)(2,1)S(1)}, bf16[128,3072]{1,0:T(8,128)(2,1)S(1)}, u32[]{:S(2)}, u32[]{:S(2)}) collective-permute-start(bf16[128,3072]{1,0:T(8,128)(2,1)S(1)} %copy-done.4), channel_id=1, source_target_pairs={{0,8},{1,9},{2,10},{3,11},{4,12},{5,13},{6,14},{7,15},{8,0},{9,1},... | collective-permute-start | bytes 2359304 | tf_op jit(solution)/shard_map/ppermute | solution.py:51
  37.9 19.6 %collective-permute-start.5 = (bf16[384,768]{1,0:T(8,128)(2,1)S(1)}, bf16[384,768]{1,0:T(8,128)(2,1)S(1)}, u32[]{:S(2)}, u32[]{:S(2)}) collective-permute-start(bf16[384,768]{1,0:T(8,128)(2,1)S(1)} %slice.26), channel_id=1, source_target_pairs={{0,1},{1,2},{2,3},{3,0},{4,5},{5,6},{6,7},{7,4},{8,9},{9,10},{10,1... | collective-permute-start | bytes 1769480 | tf_op jit(solution)/shard_map/ppermute | solution.py:51
  38.0 19.4 %collective-permute-start.6 = (bf16[384,768]{1,0:T(8,128)(2,1)S(1)}, bf16[384,768]{1,0:T(8,128)(2,1)S(1)}, u32[]{:S(2)}, u32[]{:S(2)}) collective-permute-start(bf16[384,768]{1,0:T(8,128)(2,1)S(1)} %slice.27), channel_id=1, source_target_pairs={{0,3},{1,0},{2,1},{3,2},{4,7},{5,4},{6,5},{7,6},{8,11},{9,8},{10,9... | collective-permute-start | bytes 1769480 | tf_op jit(solution)/shard_map/ppermute | solution.py:51
  45.6 22.6 %copy-start = (bf16[768,3072]{1,0:T(8,128)(2,1)}, bf16[768,3072]{1,0:T(8,128)(2,1)S(1)}, u32[]{:S(2)}) copy-start(bf16[768,3072]{1,0:T(8,128)(2,1)S(1)} %get-tuple-element.53.near.refs_1_.refs_2_) | copy-start | bytes 14155780
  45.6 6.2 %collective-permute-start.8 = (bf16[48,3072]{1,0:T(8,128)(2,1)S(1)}, bf16[48,3072]{1,0:T(8,128)(2,1)S(1)}, u32[]{:S(2)}, u32[]{:S(2)}) collective-permute-start(bf16[48,3072]{1,0:T(8,128)(2,1)S(1)} %get-tuple-element.35), channel_id=1, source_target_pairs={{0,32},{1,33},{2,34},{3,35},{4,36},{5,37},{6,38},{7,39},{8,40},{9,... | collective-permute-start | bytes 884744 | tf_op jit(solution)/shard_map/ppermute | solution.py:51
  47.3 6.9 %collective-permute-start.9 = (bf16[48,3072]{1,0:T(8,128)(2,1)S(1)}, bf16[48,3072]{1,0:T(8,128)(2,1)S(1)}, u32[]{:S(2)}, u32[]{:S(2)}) collective-permute-start(bf16[48,3072]{1,0:T(8,128)(2,1)S(1)} %get-tuple-element.37), channel_id=1, source_target_pairs={{0,224},{1,225},{2,226},{3,227},{4,228},{5,229},{6,230},{7,231},{8... | collective-permute-start | bytes 884744 | tf_op jit(solution)/shard_map/ppermute | solution.py:51
  52.4 5.0 %copy-start.2 = (bf16[384,1536]{1,0:T(8,128)(2,1)S(1)}, bf16[384,1536]{1,0:T(8,128)(2,1)}, u32[]{:S(2)}) copy-start(bf16[384,1536]{1,0:T(8,128)(2,1)} %dequantize.1.w0) | copy-start | bytes 3538948
  52.4 14.9 %collective-permute-start.12 = (bf16[96,3072]{1,0:T(8,128)(2,1)S(1)}, bf16[96,3072]{1,0:T(8,128)(2,1)S(1)}, u32[]{:S(2)}, u32[]{:S(2)}) collective-permute-start(bf16[96,3072]{1,0:T(8,128)(2,1)S(1)} %hop.7), channel_id=1, source_target_pairs={{0,32},{1,33},{2,34},{3,35},{4,36},{5,37},{6,38},{7,39},{8,40},{9,... | collective-permute-start | bytes 1769480 | tf_op jit(solution)/shard_map/ppermute | solution.py:51
  54.8 13.4 %collective-permute-start.14 = (bf16[96,3072]{1,0:T(8,128)(2,1)S(1)}, bf16[96,3072]{1,0:T(8,128)(2,1)S(1)}, u32[]{:S(2)}, u32[]{:S(2)}) collective-permute-start(bf16[96,3072]{1,0:T(8,128)(2,1)S(1)} %hop.8), channel_id=1, source_target_pairs={{0,224},{1,225},{2,226},{3,227},{4,228},{5,229},{6,230},{7,231},{8... | collective-permute-start | bytes 1769480 | tf_op jit(solution)/shard_map/ppermute | solution.py:51
  61.5 19.6 %collective-permute-start.10 = (bf16[256,1536]{1,0:T(8,128)(2,1)S(1)}, bf16[256,1536]{1,0:T(8,128)(2,1)S(1)}, u32[]{:S(2)}, u32[]{:S(2)}) collective-permute-start(bf16[256,1536]{1,0:T(8,128)(2,1)S(1)} %get-tuple-element.44), channel_id=1, source_target_pairs={{0,20},{1,21},{2,22},{3,23},{4,16},{5,17},{6,18},{7,19},{8,28},{9,... | collective-permute-start | bytes 2359304 | tf_op jit(solution)/shard_map/ppermute | solution.py:51
  68.1 4.0 %copy-start.7 = (bf16[128,4608]{1,0:T(8,128)(2,1)S(1)}, bf16[128,4608]{1,0:T(8,128)(2,1)}, u32[]{:S(2)}) copy-start(bf16[128,4608]{1,0:T(8,128)(2,1)} %copy-done.6) | copy-start | bytes 3538948
  68.1 16.3 %collective-permute-start.13 = (bf16[96,3072]{1,0:T(8,128)(2,1)S(1)}, bf16[96,3072]{1,0:T(8,128)(2,1)S(1)}, u32[]{:S(2)}, u32[]{:S(2)}) collective-permute-start(bf16[96,3072]{1,0:T(8,128)(2,1)S(1)} %hop.9), channel_id=1, source_target_pairs={{0,32},{1,33},{2,34},{3,35},{4,36},{5,37},{6,38},{7,39},{8,40},{9,... | collective-permute-start | bytes 1769480 | tf_op jit(solution)/shard_map/ppermute | solution.py:51
  69.7 17.8 %collective-permute-start.17 = (bf16[96,3072]{1,0:T(8,128)(2,1)}, bf16[96,3072]{1,0:T(8,128)(2,1)}, u32[]{:S(2)}, u32[]{:S(2)}) collective-permute-start(bf16[96,3072]{1,0:T(8,128)(2,1)} %hop.10), channel_id=1, source_target_pairs={{0,224},{1,225},{2,226},{3,227},{4,228},{5,229},{6,230},{7,231},{8... | collective-permute-start | bytes 1769480 | tf_op jit(solution)/shard_map/ppermute | solution.py:51
  77.0 7.3 %collective-permute-start.15 = (bf16[256,1536]{1,0:T(8,128)(2,1)}, bf16[256,1536]{1,0:T(8,128)(2,1)S(1)}, u32[]{:S(2)}, u32[]{:S(2)}) collective-permute-start(bf16[256,1536]{1,0:T(8,128)(2,1)} %get-tuple-element.52), channel_id=1, source_target_pairs={{0,8},{1,9},{2,10},{3,11},{4,12},{5,13},{6,14},{7,15},{8,0},{9,1},... | collective-permute-start | bytes 2359304 | tf_op jit(solution)/shard_map/ppermute | solution.py:51
  82.5 9.7 %collective-permute-start.11 = (bf16[128,1536]{1,0:T(8,128)(2,1)}, bf16[128,1536]{1,0:T(8,128)(2,1)}, u32[]{:S(2)}, u32[]{:S(2)}) collective-permute-start(bf16[128,1536]{1,0:T(8,128)(2,1)} %get-tuple-element.60), channel_id=1, source_target_pairs={{0,8},{1,9},{2,10},{3,11},{4,12},{5,13},{6,14},{7,15},{8,0},{9,1},... | collective-permute-start | bytes 1179656 | tf_op jit(solution)/shard_map/ppermute | solution.py:51
  84.3 2.3 %copy-start.1 = (bf16[768,3072]{1,0:T(8,128)(2,1)S(1)}, bf16[768,3072]{1,0:T(8,128)(2,1)}, u32[]{:S(2)}) copy-start(bf16[768,3072]{1,0:T(8,128)(2,1)} %copy-done) | copy-start | bytes 14155780
  86.7 19.3 %slice-start = ((s8[4718592]{0:T(1024)(128)(4,1)}), s8[4194304]{0:T(1024)(128)(4,1)S(1)}, s32[]{:S(2)}) async-start(s8[4718592]{0:T(1024)(128)(4,1)} %bitcast.4), calls=%async_computation | async-start | bytes 8388608
  87.4 4.8 %copy-start.8 = (bf16[128,1536]{1,0:T(8,128)(2,1)S(1)}, bf16[128,1536]{1,0:T(8,128)(2,1)}, u32[]{:S(2)}) copy-start(bf16[128,1536]{1,0:T(8,128)(2,1)} %get-tuple-element.59) | copy-start | bytes 1179652
  87.4 18.6 %slice-start.1 = ((s8[4718592]{0:T(1024)(128)(4,1)}), s8[524288]{0:T(1024)(128)(4,1)S(1)}, s32[]{:S(2)}) async-start(s8[4718592]{0:T(1024)(128)(4,1)} %bitcast.4), calls=%async_computation.1 | async-start | bytes 1048576
  87.4 16.0 %collective-permute-start.16 = (bf16[96,3072]{1,0:T(8,128)(2,1)S(1)}, bf16[96,3072]{1,0:T(8,128)(2,1)S(1)}, u32[]{:S(2)}, u32[]{:S(2)}) collective-permute-start(bf16[96,3072]{1,0:T(8,128)(2,1)S(1)} %hop.11), channel_id=1, source_target_pairs={{0,32},{1,33},{2,34},{3,35},{4,36},{5,37},{6,38},{7,39},{8,40},{9,... | collective-permute-start | bytes 1769480 | tf_op jit(solution)/shard_map/ppermute | solution.py:51
  89.5 16.5 %collective-permute-start.18 = (bf16[96,3072]{1,0:T(8,128)(2,1)S(1)}, bf16[96,3072]{1,0:T(8,128)(2,1)S(1)}, u32[]{:S(2)}, u32[]{:S(2)}) collective-permute-start(bf16[96,3072]{1,0:T(8,128)(2,1)S(1)} %hop.12), channel_id=1, source_target_pairs={{0,224},{1,225},{2,226},{3,227},{4,228},{5,229},{6,230},{7,231},{8... | collective-permute-start | bytes 1769480 | tf_op jit(solution)/shard_map/ppermute | solution.py:51
  106.8 4.7 %collective-permute-start.21 = (bf16[24,3072]{1,0:T(8,128)(2,1)S(1)}, bf16[24,3072]{1,0:T(8,128)(2,1)S(1)}, u32[]{:S(2)}, u32[]{:S(2)}) collective-permute-start(bf16[24,3072]{1,0:T(8,128)(2,1)S(1)} %get-tuple-element.62), channel_id=1, source_target_pairs={{0,3},{1,0},{2,1},{3,2},{4,7},{5,4},{6,5},{7,6},{8,11},{9,8},{10,9... | collective-permute-start | bytes 442376 | tf_op jit(solution)/shard_map/ppermute | solution.py:51
  107.8 5.6 %collective-permute-start.20 = (bf16[24,3072]{1,0:T(8,128)(2,1)S(1)}, bf16[24,3072]{1,0:T(8,128)(2,1)S(1)}, u32[]{:S(2)}, u32[]{:S(2)}) collective-permute-start(bf16[24,3072]{1,0:T(8,128)(2,1)S(1)} %get-tuple-element.63), channel_id=1, source_target_pairs={{0,2},{1,3},{2,0},{3,1},{4,6},{5,7},{6,4},{7,5},{8,10},{9,11},{10,... | collective-permute-start | bytes 442376 | tf_op jit(solution)/shard_map/ppermute | solution.py:51
  108.3 9.8 %collective-permute-start.19 = (bf16[24,3072]{1,0:T(8,128)(2,1)S(1)}, bf16[24,3072]{1,0:T(8,128)(2,1)S(1)}, u32[]{:S(2)}, u32[]{:S(2)}) collective-permute-start(bf16[24,3072]{1,0:T(8,128)(2,1)S(1)} %get-tuple-element.61), channel_id=1, source_target_pairs={{0,1},{1,2},{2,3},{3,0},{4,5},{5,6},{6,7},{7,4},{8,9},{9,10},{10,1... | collective-permute-start | bytes 442376 | tf_op jit(solution)/shard_map/ppermute | solution.py:51
  109.0 17.2 %collective-permute-start.24 = (bf16[128,1536]{1,0:T(8,128)(2,1)S(1)}, bf16[128,1536]{1,0:T(8,128)(2,1)S(1)}, u32[]{:S(2)}, u32[]{:S(2)}) collective-permute-start(bf16[128,1536]{1,0:T(8,128)(2,1)S(1)} %get-tuple-element.65), channel_id=1, source_target_pairs={{0,20},{1,21},{2,22},{3,23},{4,16},{5,17},{6,18},{7,19},{8,28},{9,... | collective-permute-start | bytes 1179656 | tf_op jit(solution)/shard_map/ppermute | solution.py:51
  118.2 13.5 %collective-permute-start.22 = (bf16[12,3072]{1,0:T(8,128)(2,1)S(1)}, bf16[12,3072]{1,0:T(8,128)(2,1)S(1)}, u32[]{:S(2)}, u32[]{:S(2)}) collective-permute-start(bf16[12,3072]{1,0:T(8,128)(2,1)S(1)} %get-tuple-element.67), channel_id=1, source_target_pairs={{0,24},{1,26},{2,28},{3,30},{4,184},{5,186},{6,188},{7,190},{8,72}... | collective-permute-start | bytes 221192 | tf_op jit(solution)/shard_map/ppermute | solution.py:51
  123.4 16.2 %collective-permute-start.23 = (bf16[12,3072]{1,0:T(8,128)(2,1)S(1)}, bf16[12,3072]{1,0:T(8,128)(2,1)S(1)}, u32[]{:S(2)}, u32[]{:S(2)}) collective-permute-start(bf16[12,3072]{1,0:T(8,128)(2,1)S(1)} %get-tuple-element.66), channel_id=1, source_target_pairs={{0,25},{1,27},{2,29},{3,31},{4,185},{5,187},{6,189},{7,191},{8,73}... | collective-permute-start | bytes 221192 | tf_op jit(solution)/shard_map/ppermute | solution.py:51

commit v4 on v3

--- a/solution.py
+++ b/solution.py
@@ -1,4 +1,5 @@
 import functools
+import math
 
 import jax
 import jax.numpy as jnp
@@ -10,6 +11,7 @@
 AXES = ("z", "yl", "c", "yh", "x")
 SIZES = (8, 2, 2, 2, 4)
 BLOCK_STEPS = (0, 3, 1, 2)
+HOPS = (3, -3, 2, -2, 1, -1, 0)
 
 
 def table(move):
@@ -65,7 +67,7 @@
 
 def call(kernel, name, mib, where, grid, in_specs, out_specs, out_shape, scratch, flops, operands):
     moved = sum(v.size * v.dtype.itemsize for v in operands)
-    moved += sum(v.size * v.dtype.itemsize for v in jax.tree.leaves(out_shape))
+    moved += sum(math.prod(v.shape) * v.dtype.itemsize for v in jax.tree.leaves(out_shape))
     return pl.pallas_call(
         kernel,
         name=name,
@@ -87,11 +89,11 @@
 
 
 def dequantize_kernel(where, levels, scales, out):
-    c = where[0]
-    count = scales.shape[1] // 2
+    count = scales.shape[0] // 2
     width = out.shape[1] // count
+    mine = jnp.where(where[0] == 0, scales[:count], scales[count:]).T
     for b in range(count):
-        scale = jnp.where(c == 0, scales[:, b : b + 1], scales[:, count + b : count + b + 1])
+        scale = mine[:, b : b + 1]
         span = slice(b * width, (b + 1) * width)
         out[:, span] = bf16(f32(levels[:, span]) * scale)
 
@@ -107,7 +109,7 @@
         (3,),
         [
             pl.BlockSpec((size, nh), lambda i, where: (i, where[0])),
-            pl.BlockSpec((size, scales.shape[1]), lambda i, where: (i, 0)),
+            pl.BlockSpec((scales.shape[0], size), lambda i, where: (0, i)),
         ],
         pl.BlockSpec((size, nh), lambda i, where: (i, 0)),
         jax.ShapeDtypeStruct((row_count, nh), jnp.bfloat16),
@@ -117,36 +119,39 @@
     )
 
 
-def pack_kernel(where, tokens, cotangent, out):
-    kh = tokens.shape[1]
-    out[:, :kh] = tokens[...]
-    out[:, kh:] = cotangent[...]
-
-
-def pack(where, tokens, cotangent):
-    count, kh = tokens.shape[0], tokens.shape[1] // 2
-    width = kh + cotangent.shape[1]
-    return call(
+def pack_kernel(tokens, cotangent, out, sems):
+    kh = tokens.shape[1] // 2
+    start = pl.multiple_of((1 - lax.axis_index("yh")) * kh, 128)
+    copies = (
+        pltpu.make_async_copy(tokens.at[:, pl.ds(start, kh)], out.at[:, pl.ds(0, kh)], sems.at[0]),
+        pltpu.make_async_copy(cotangent, out.at[:, pl.ds(kh, cotangent.shape[1])], sems.at[1]),
+    )
+    for copy in copies:
+        copy.start()
+    for copy in copies:
+        copy.wait()
+
+
+def pack(tokens, cotangent):
+    shape = (tokens.shape[0], tokens.shape[1] // 2 + cotangent.shape[1])
+    return pl.pallas_call(
         pack_kernel,
-        "pack",
-        60,
-        where,
-        (1,),
-        [fixed((count, kh), lambda where: (0, 1 - where[1])), fixed(cotangent.shape)],
-        fixed((count, width)),
-        jax.ShapeDtypeStruct((count, width), jnp.bfloat16),
-        [],
-        0,
-        (tokens, cotangent),
-    )
+        name="pack",
+        in_specs=[pl.BlockSpec(memory_space=pl.ANY)] * 2,
+        out_specs=pl.BlockSpec(memory_space=pl.ANY),
+        out_shape=jax.ShapeDtypeStruct(shape, jnp.bfloat16),
+        scratch_shapes=[pltpu.SemaphoreType.DMA((2,))],
+        compiler_params=pltpu.CompilerParams(vmem_limit_bytes=60 * 2**20),
+    )(tokens, cotangent)
 
 
 def columns(ref, start, size):
     return ref[:, pl.ds(pl.multiple_of(start, 128), size)]
 
 
-def gradient_kernel(where, own, sib, pair, psib, cot0, cot1, cot2, cot3, out, up, down, lhs):
+def gradient_kernel(where, own, sib, pair, psib, cot0, cot1, cot2, cot3, *refs):
     c, yh = where[0], where[1]
+    *chunks, lhs, out = refs
     count, size = own.shape[0], lhs.shape[1]
 
     @pl.when(pl.program_id(0) == 0)
@@ -161,17 +166,19 @@
             lhs[...], rhs, (((0,), (0,)), ((), ())), preferred_element_type=jnp.float32
         )
     )
-    half = up.shape[0]
-    start = pl.multiple_of((where[3] + 4) % 8 * (2 * half), 2 * half)
-    up[...] = out[pl.ds(start, half)]
-    down[...] = out[pl.ds(start + half, half)]
+    height, start = size // 8, 0
+    for k, ref in zip((4, 4, *HOPS), chunks):
+        part = ref.shape[0]
+        row = (where[3] + 8 + k) % 8 * height + start
+        ref[...] = out[pl.ds(pl.multiple_of(row, 16), part)]
+        start = (start + part) % height
 
 
 def gradient(where, token_parts, cot_parts):
     count, outputs = cot_parts[0].shape
     kh = token_parts[0].shape[1] // 2
     size, width = kh // 2, outputs // 4
-    heights = (size, size // 16, size // 16)
+    heights = [size // 16] * 2 + [size // 8] * len(HOPS)
     return call(
         gradient_kernel,
         "gradient",
@@ -184,43 +191,37 @@
         + [pl.BlockSpec((count, width), lambda i, where: (0, i + 2))] * 2,
         [pl.BlockSpec((height, width), lambda i, where: (0, i)) for height in heights],
         [jax.ShapeDtypeStruct((height, outputs), jnp.bfloat16) for height in heights],
-        [pltpu.VMEM((4 * count, size), jnp.bfloat16)],
+        [pltpu.VMEM((4 * count, size), jnp.bfloat16), pltpu.VMEM((size, width), jnp.bfloat16)],
         8 * count * size * outputs,
         (*token_parts, *cot_parts),
     )
 
 
-def hop_kernel(where, *refs):
-    *arrived, near, out = refs
-    total = f32(near[...])
+def hop_kernel(*refs):
+    *arrived, part, out = refs
+    total = f32(part[...])
     for ref in arrived:
         total = total + f32(ref[...])
     out[...] = total.astype(out.dtype)
 
 
-def first_hop_kernel(where, arrived, near, out, *, upper):
+def first_hop_kernel(arrived, part, out, *, upper):
     half = arrived.shape[0]
     here, there = (slice(0, half), slice(half, 2 * half))[:: 1 if upper else -1]
-    out[here] = bf16(f32(near[here]) + f32(arrived[...]))
-    out[there] = near[there]
-
-
-def hop(where, part, k, kernel, kind, *arrived):
-    size, width = part.shape[0] // 8, part.shape[1]
-    return call(
+    out[here] = bf16(f32(part[here]) + f32(arrived[...]))
+    out[there] = part[there]
+
+
+def hop(part, *arrived, kernel=hop_kernel, kind=jnp.bfloat16):
+    return pl.pallas_call(
         kernel,
-        "hop",
-        8,
-        where,
-        (1,),
-        [fixed(v.shape) for v in arrived]
-        + [fixed((size, width), lambda where: ((where[3] + 8 + k) % 8, 0))],
-        fixed((size, width)),
-        jax.ShapeDtypeStruct((size, width), kind),
-        [],
-        2 * size * width,
-        (*arrived, part),
-    )
+        name="hop",
+        out_shape=jax.ShapeDtypeStruct(part.shape, kind),
+        compiler_params=pltpu.CompilerParams(vmem_limit_bytes=8 * 2**20),
+        cost_estimate=pl.CostEstimate(
+            flops=part.size, bytes_accessed=6 * part.size, transcendentals=0
+        ),
+    )(*arrived, part)
 
 
 def forward_kernel(where, own, sib, pair, psib, w0, w1, w2, w3, w4, mine, other, away, lhs):
@@ -338,10 +339,10 @@
     count = tokens.shape[0]
     factor = float(count * 256) ** -0.5
 
-    packed = pack(where, tokens, cotangent)
+    packed = pack(tokens, cotangent)
     pair = send(packed, PAIR)
 
-    levels, scales = after((levels, scales), packed)
+    levels, scales = after((levels, scales.T), packed)
     own = dequantize(where, levels, scales)
     left, right = send(own, X_UP), send(own, X_DOWN)
 
@@ -351,27 +352,24 @@
     token_parts = (tokens, token_sib, pair, cross)
     cot_parts = (cotangent, cot_sib, pair, cross)
 
-    grad, up, down = gradient(where, token_parts, cot_parts)
+    up, down, *grad = gradient(where, token_parts, cot_parts)
     half = own.shape[1] // 2
-    far_left, far_right = left[:, :half], right[:, half:]
-    blocks = (own, left, right, send(far_left, X_UP), send(far_right, X_DOWN))
+    blocks = (own, left, right, send(left[:, :half], X_UP), send(right[:, half:], X_DOWN))
     up, down = send(up, Z_UP), send(down, Z_DOWN)
-    up = hop(where, grad, 3, functools.partial(first_hop_kernel, upper=True), jnp.bfloat16, up)
-    down = hop(where, grad, -3, functools.partial(first_hop_kernel, upper=False), jnp.bfloat16, down)
+    up = hop(grad[0], up, kernel=functools.partial(first_hop_kernel, upper=True))
+    down = hop(grad[1], down, kernel=functools.partial(first_hop_kernel, upper=False))
     mine, other, away = forward_parts(where, token_parts, after(blocks, up, down))
     up, down = send(up, Z_UP), send(down, Z_DOWN)
     back = f32(send(away, PAIR))
     grad = after(grad, away)
-    up = hop(where, grad, 2, hop_kernel, jnp.bfloat16, up)
-    down = hop(where, grad, -2, hop_kernel, jnp.bfloat16, down)
+    up, down = hop(grad[2], up), hop(grad[3], down)
     part, give = backward_parts(where, cot_parts, after(blocks, up, down))
     up, down = send(up, Z_UP), send(down, Z_DOWN)
     give = send(give, CORE)
     grad = after(grad, give, back)
-    up = hop(where, grad, 1, hop_kernel, jnp.bfloat16, up)
-    down = hop(where, grad, -1, hop_kernel, jnp.bfloat16, down)
+    up, down = hop(grad[4], up), hop(grad[5], down)
     up, down = send(up, Z_UP), send(down, Z_DOWN)
-    total = hop(where, grad, 0, hop_kernel, jnp.float32, up, down)
+    total = hop(grad[6], up, down, kind=jnp.float32)
 
     part = part + f32(give)
     grad_input = joined(bf16(part[:count]), send(bf16(part[count:]), PAIR), yh)

time: 141 us -> 169 us (1.20)
  the two profiles are of different devices: /device:TPU:57 before, /device:TPU:24 now
where the time goes in v4:
time: 169 us; the launch traced here: 168 us
  Pallas kernels  59.9 us (35%)
  waiting for transfers between devices  58.9 us (35%)
  starting transfers between devices  41.8 us (25%)
  other arithmetic  6.07 us (4%)
    ppermute x25, waiting for transfers between devices, send(): return lax.ppermute(value, AXES, pairs)  58.9 us
    ppermute x25, starting transfers between devices, send(): return lax.ppermute(value, AXES, pairs)  41.8 us
    pallas_call x1, Pallas kernels, pack(): pl.pallas_call(pack_kernel, name='pack', in_specs=[pl.BlockSpec(memory_sp...  36.9 us
    pallas_call x4, Pallas kernels, call(): pl.pallas_call(kernel, name=name, grid_spec=pltpu.PrefetchScalarGridSpec(...  18.3 us
    pallas_call x7, Pallas kernels, hop(): pl.pallas_call(kernel, name='hop', out_shape=jax.ShapeDtypeStruct(part.sh...  4.66 us
  transfers between devices with their start and end apart: 25, of which 13 were waited for; matrix products, arithmetic and copies ran while one was open for 3% of the time, Pallas kernels for 14%

profile of v4, /device:TPU:24, one launch (start us, length us, event | category | flops | bytes accessed | tf_op | source)
XLA Modules:
  0.0 167.8 jit_solution(16395586885812400715)
XLA Ops:
  0.6 36.9 %pack.1 = bf16[128,4608]{1,0:T(8,128)(2,1)} custom-call(bf16[128,3072]{1,0:T(8,128)(2,1)} %own.3, bf16[128,3072]{1,0:T(8,128)(2,1)} %cot0.3), custom_call_target="tpu_custom_call" | custom-call | tf_op jit(solution)/shard_map/pack/pallas_call | solution.py:137
  37.5 2.0 %collective-permute-start.1 = (bf16[128,4608]{1,0:T(8,128)(2,1)}, bf16[128,4608]{1,0:T(8,128)(2,1)S(1)}, u32[]{:S(2)}, u32[]{:S(2)}) collective-permute-start(bf16[128,4608]{1,0:T(8,128)(2,1)} %pack.1), channel_id=1, source_target_pairs={{0,20},{1,21},{2,22},{3,23},{4,16},{5,17},{6,18},{7,19},{8,28},{9,... | collective-permute-start | bytes 3538952 | tf_op jit(solution)/shard_map/ppermute | solution.py:53
  39.5 0.6 pad_add_fusion.where
  40.1 4.3 %dequantize.1.w0 = bf16[384,1536]{1,0:T(8,128)(2,1)} custom-call(s32[4]{0:T(128)} %pad_add_fusion.where, bf16[384,3072]{1,0:T(8,128)(2,1)} %levels, f32[12,384]{1,0:T(8,128)} %bitcast.5), custom_call_target="tpu_custom_call" | custom-call | flops 589824 | bytes 3557376 | tf_op jit(solution)/shard_map/dequantize/pallas_call | solution.py:71
  44.4 0.0 collective-permute-start.3
  44.4 3.2 %collective-permute-start.4 = (bf16[384,1536]{1,0:T(8,128)(2,1)}, bf16[384,1536]{1,0:T(8,128)(2,1)S(1)}, u32[]{:S(2)}, u32[]{:S(2)}) collective-permute-start(bf16[384,1536]{1,0:T(8,128)(2,1)} %dequantize.1.w0), channel_id=1, source_target_pairs={{0,3},{1,0},{2,1},{3,2},{4,7},{5,4},{6,5},{7,6},{8,11},{9,8},{10,9... | collective-permute-start | bytes 3538952 | tf_op jit(solution)/shard_map/ppermute | solution.py:53
  47.7 19.1 %collective-permute-done.1.pair.cot2 = bf16[128,4608]{1,0:T(8,128)(2,1)S(1)} collective-permute-done((bf16[128,4608]{1,0:T(8,128)(2,1)}, bf16[128,4608]{1,0:T(8,128)(2,1)S(1)}, u32[]{:S(2)}, u32[]{:S(2)}) %collective-permute-start.1) | collective-permute-done | bytes 1179680 | tf_op jit(solution)/shard_map/ppermute | solution.py:53
  66.7 0.5 collective-permute-start
  67.2 0.1 collective-permute-start.7
  67.3 4.3 %collective-permute-done.3.w1 = bf16[384,1536]{1,0:T(8,128)(2,1)S(1)} collective-permute-done((bf16[384,1536]{1,0:T(8,128)(2,1)}, bf16[384,1536]{1,0:T(8,128)(2,1)S(1)}, u32[]{:S(2)}, u32[]{:S(2)}) %collective-permute-start.3) | collective-permute-done | bytes 1179680 | tf_op jit(solution)/shard_map/ppermute | solution.py:53
  71.7 0.4 collective-permute-start.5
  72.0 0.0 collective-permute-done.4.w2
  72.1 3.0 %collective-permute-start.6 = (bf16[384,768]{1,0:T(8,128)(2,1)S(1)}, bf16[384,768]{1,0:T(8,128)(2,1)S(1)}, u32[]{:S(2)}, u32[]{:S(2)}) collective-permute-start(bf16[384,768]{1,0:T(8,128)(2,1)S(1)} %slice.27), channel_id=1, source_target_pairs={{0,3},{1,0},{2,1},{3,2},{4,7},{5,4},{6,5},{7,6},{8,11},{9,8},{10,9... | collective-permute-start | bytes 1769480 | tf_op jit(solution)/shard_map/ppermute | solution.py:53
  75.1 0.0 collective-permute-done.sib
  75.1 5.2 %gradient.1 = (bf16[48,3072]{1,0:T(8,128)(2,1)S(1)}, bf16[48,3072]{1,0:T(8,128)(2,1)S(1)}, bf16[96,3072]{1,0:T(8,128)(2,1)S(1)}, bf16[96,3072]{1,0:T(8,128)(2,1)...) custom-call(s32[4]{0:T(128)S(1)} %copy-done.7, ...), custom_call_target="tpu_custom_call" | custom-call | flops 2415919104 | bytes 12582912 | tf_op jit(solution)/shard_map/gradient/pallas_call | solution.py:71
  80.3 5.9 %collective-permute-start.9 = (bf16[48,3072]{1,0:T(8,128)(2,1)S(1)}, bf16[48,3072]{1,0:T(8,128)(2,1)S(1)}, u32[]{:S(2)}, u32[]{:S(2)}) collective-permute-start(bf16[48,3072]{1,0:T(8,128)(2,1)S(1)} %get-tuple-element.49), channel_id=1, source_target_pairs={{0,224},{1,225},{2,226},{3,227},{4,228},{5,229},{6,230},{7,231},{8... | collective-permute-start | bytes 884744 | tf_op jit(solution)/shard_map/ppermute | solution.py:53
  86.3 0.0 collective-permute-start.8
  86.3 4.6 %collective-permute-done.9.arrived = bf16[48,3072]{1,0:T(8,128)(2,1)S(1)} collective-permute-done((bf16[48,3072]{1,0:T(8,128)(2,1)S(1)}, bf16[48,3072]{1,0:T(8,128)(2,1)S(1)}, u32[]{:S(2)}, u32[]{:S(2)}) %collective-permute-start.9) | collective-permute-done | bytes 294944 | tf_op jit(solution)/shard_map/ppermute | solution.py:53
  90.9 0.1 hop.8
  91.0 3.8 %collective-permute-start.14 = (bf16[96,3072]{1,0:T(8,128)(2,1)S(1)}, bf16[96,3072]{1,0:T(8,128)(2,1)S(1)}, u32[]{:S(2)}, u32[]{:S(2)}) collective-permute-start(bf16[96,3072]{1,0:T(8,128)(2,1)S(1)} %hop.8), channel_id=1, source_target_pairs={{0,224},{1,225},{2,226},{3,227},{4,228},{5,229},{6,230},{7,231},{8... | collective-permute-start | bytes 1769480 | tf_op jit(solution)/shard_map/ppermute | solution.py:53
  94.7 0.1 hop.7
  94.8 0.1 collective-permute-start.12
  94.9 0.0 collective-permute-done.5.w3
  95.0 4.0 %forward.1 = (f32[128,1536]{1,0:T(8,128)S(1)}, f32[128,1536]{1,0:T(8,128)S(1)}, bf16[256,1536]{1,0:T(8,128)(2,1)S(1)}) custom-call(s32[4]{0:T(128)S(1)} %copy-done.7, bf16[128,3072]{1,0:T(8,128)(2,1)S(1)} %copy-done.1, bf16[128,3072]{1,0:T(8,128)(2,1)S(1)} %collective-permute-done.sib, bf16[128,4608]{1,0:T(8,128)(2,1)S(1)} %collective-permute-done.1.pair.cot2, ...), custom_call_target="tpu_custom_call" | custom-call | flops 2415919104 | bytes 11010048 | tf_op jit(solution)/shard_map/forward/pallas_call | solution.py:71
  99.0 3.1 %collective-permute-start.10 = (bf16[256,1536]{1,0:T(8,128)(2,1)S(1)}, bf16[256,1536]{1,0:T(8,128)(2,1)S(1)}, u32[]{:S(2)}, u32[]{:S(2)}) collective-permute-start(bf16[256,1536]{1,0:T(8,128)(2,1)S(1)} %get-tuple-element.57), channel_id=1, source_target_pairs={{0,20},{1,21},{2,22},{3,23},{4,16},{5,17},{6,18},{7,19},{8,28},{9,... | collective-permute-start | bytes 2359304 | tf_op jit(solution)/shard_map/ppermute | solution.py:53
  102.1 2.7 %collective-permute-done.14.refs_0_ = bf16[96,3072]{1,0:T(8,128)(2,1)S(1)} collective-permute-done((bf16[96,3072]{1,0:T(8,128)(2,1)S(1)}, bf16[96,3072]{1,0:T(8,128)(2,1)S(1)}, u32[]{:S(2)}, u32[]{:S(2)}) %collective-permute-start.14) | collective-permute-done | bytes 589856 | tf_op jit(solution)/shard_map/ppermute | solution.py:53
  104.7 1.0 hop.10
  105.7 3.7 %collective-permute-start.17 = (bf16[96,3072]{1,0:T(8,128)(2,1)}, bf16[96,3072]{1,0:T(8,128)(2,1)}, u32[]{:S(2)}, u32[]{:S(2)}) collective-permute-start(bf16[96,3072]{1,0:T(8,128)(2,1)} %hop.10), channel_id=1, source_target_pairs={{0,224},{1,225},{2,226},{3,227},{4,228},{5,229},{6,230},{7,231},{8... | collective-permute-start | bytes 1769480 | tf_op jit(solution)/shard_map/ppermute | solution.py:53
  109.4 0.0 collective-permute-done.12.refs_0_
  109.4 1.0 hop.9
  110.4 4.9 %backward.1 = (f32[256,1536]{1,0:T(8,128)S(1)}, bf16[256,1536]{1,0:T(8,128)(2,1)}) custom-call(s32[4]{0:T(128)S(1)} %copy-done.7, bf16[128,3072]{1,0:T(8,128)(2,1)S(1)} %copy-done.2, bf16[128,3072]{1,0:T(8,128)(2,1)S(1)} %collective-permute-done.7.cot1, bf16[128,4608]{1,0:T(8,128)(2,1)S(1)} %copy-done.9, ...), custom_call_target="tpu_custom_call" | custom-call | flops 2415919104 | bytes 11010048 | tf_op jit(solution)/shard_map/backward/pallas_call | solution.py:71
  115.3 0.0 collective-permute-start.15
  115.3 1.6 collective-permute-done.10
  116.9 0.2 convert_element_type.41
  117.1 1.0 fusion.1
  118.1 0.7 collective-permute-done.17.refs_0_
  118.8 1.2 hop.12
  120.0 3.8 %collective-permute-start.18 = (bf16[96,3072]{1,0:T(8,128)(2,1)S(1)}, bf16[96,3072]{1,0:T(8,128)(2,1)S(1)}, u32[]{:S(2)}, u32[]{:S(2)}) collective-permute-start(bf16[96,3072]{1,0:T(8,128)(2,1)S(1)} %hop.12), channel_id=1, source_target_pairs={{0,224},{1,225},{2,226},{3,227},{4,228},{5,229},{6,230},{7,231},{8... | collective-permute-start | bytes 1769480 | tf_op jit(solution)/shard_map/ppermute | solution.py:53
  123.8 0.0 collective-permute-done.13.refs_0_
  123.8 1.2 hop.11
  125.0 0.1 collective-permute-start.16
  125.1 0.0 collective-permute-done.11
  125.1 1.1 maximum_select_fusion
  126.2 1.4 convert_add_fusion
  127.5 8.0 %collective-permute-done.18.refs_1_ = bf16[96,3072]{1,0:T(8,128)(2,1)S(1)} collective-permute-done((bf16[96,3072]{1,0:T(8,128)(2,1)S(1)}, bf16[96,3072]{1,0:T(8,128)(2,1)S(1)}, u32[]{:S(2)}, u32[]{:S(2)}) %collective-permute-start.18) | collective-permute-done | bytes 589856 | tf_op jit(solution)/shard_map/ppermute | solution.py:53
  135.6 4.7 %collective-permute-done.16.refs_0_ = bf16[96,3072]{1,0:T(8,128)(2,1)S(1)} collective-permute-done((bf16[96,3072]{1,0:T(8,128)(2,1)S(1)}, bf16[96,3072]{1,0:T(8,128)(2,1)S(1)}, u32[]{:S(2)}, u32[]{:S(2)}) %collective-permute-start.16) | collective-permute-done | bytes 589856 | tf_op jit(solution)/shard_map/ppermute | solution.py:53
  140.3 0.2 hop.13
  140.5 0.1 dynamic-slice_convert_fusion.2
  140.5 1.2 collective-permute-start.19
  141.8 2.7 %collective-permute-start.20 = (bf16[24,3072]{1,0:T(8,128)(2,1)S(1)}, bf16[24,3072]{1,0:T(8,128)(2,1)S(1)}, u32[]{:S(2)}, u32[]{:S(2)}) collective-permute-start(bf16[24,3072]{1,0:T(8,128)(2,1)S(1)} %get-tuple-element.87), channel_id=1, source_target_pairs={{0,2},{1,3},{2,0},{3,1},{4,6},{5,7},{6,4},{7,5},{8,10},{9,11},{10,... | collective-permute-start | bytes 442376 | tf_op jit(solution)/shard_map/ppermute | solution.py:53
  144.5 1.4 collective-permute-start.21
  145.9 0.1 fusion.2
  146.0 0.7 collective-permute-start.24
  146.7 0.3 collective-permute-done.19
  147.0 2.2 %collective-permute-done.20 = bf16[24,3072]{1,0:T(8,128)(2,1)S(1)} collective-permute-done((bf16[24,3072]{1,0:T(8,128)(2,1)S(1)}, bf16[24,3072]{1,0:T(8,128)(2,1)S(1)}, u32[]{:S(2)}, u32[]{:S(2)}) %collective-permute-start.20) | collective-permute-done | bytes 147488 | tf_op jit(solution)/shard_map/ppermute | solution.py:53
  149.2 0.4 collective-permute-done.21
  149.6 0.1 multiply_convert_fusion
  149.7 0.1 constant_dynamic-slice_fusion
  149.8 1.9 %collective-permute-start.22 = (bf16[12,3072]{1,0:T(8,128)(2,1)S(1)}, bf16[12,3072]{1,0:T(8,128)(2,1)S(1)}, u32[]{:S(2)}, u32[]{:S(2)}) collective-permute-start(bf16[12,3072]{1,0:T(8,128)(2,1)S(1)} %get-tuple-element.91), channel_id=1, source_target_pairs={{0,24},{1,26},{2,28},{3,30},{4,184},{5,186},{6,188},{7,190},{8,72}... | collective-permute-start | bytes 221192 | tf_op jit(solution)/shard_map/ppermute | solution.py:53
  151.7 4.0 %collective-permute-start.23 = (bf16[12,3072]{1,0:T(8,128)(2,1)S(1)}, bf16[12,3072]{1,0:T(8,128)(2,1)S(1)}, u32[]{:S(2)}, u32[]{:S(2)}) collective-permute-start(bf16[12,3072]{1,0:T(8,128)(2,1)S(1)} %get-tuple-element.90), channel_id=1, source_target_pairs={{0,25},{1,27},{2,29},{3,31},{4,185},{5,187},{6,189},{7,191},{8,73}... | collective-permute-start | bytes 221192 | tf_op jit(solution)/shard_map/ppermute | solution.py:53
  155.8 1.1 maximum_select_fusion.1
  156.9 8.9 %collective-permute-done.22 = bf16[12,3072]{1,0:T(8,128)(2,1)S(1)} collective-permute-done((bf16[12,3072]{1,0:T(8,128)(2,1)S(1)}, bf16[12,3072]{1,0:T(8,128)(2,1)S(1)}, u32[]{:S(2)}, u32[]{:S(2)}) %collective-permute-start.22) | collective-permute-done | bytes 73760 | tf_op jit(solution)/shard_map/ppermute | solution.py:53
  165.8 1.3 collective-permute-done.23
  167.1 0.7 add.84
  (33 shorter events, 0.2 us)
Async XLA Ops:
  37.5 29.2 %collective-permute-start.1 = (bf16[128,4608]{1,0:T(8,128)(2,1)}, bf16[128,4608]{1,0:T(8,128)(2,1)S(1)}, u32[]{:S(2)}, u32[]{:S(2)}) collective-permute-start(bf16[128,4608]{1,0:T(8,128)(2,1)} %pack.1), channel_id=1, source_target_pairs={{0,20},{1,21},{2,22},{3,23},{4,16},{5,17},{6,18},{7,19},{8,28},{9,... | collective-permute-start | bytes 3538952 | tf_op jit(solution)/shard_map/ppermute | solution.py:53
  40.1 26.6 %copy-start.1 = (bf16[128,3072]{1,0:T(8,128)(2,1)S(1)}, bf16[128,3072]{1,0:T(8,128)(2,1)}, u32[]{:S(2)}) copy-start(bf16[128,3072]{1,0:T(8,128)(2,1)} %own.3) | copy-start | bytes 2359300
  40.1 27.1 %copy-start.2 = (bf16[128,3072]{1,0:T(8,128)(2,1)S(1)}, bf16[128,3072]{1,0:T(8,128)(2,1)}, u32[]{:S(2)}) copy-start(bf16[128,3072]{1,0:T(8,128)(2,1)} %cot0.3) | copy-start | bytes 2359300
  44.4 30.7 %copy-start.7 = (s32[4]{0:T(128)S(1)}, s32[4]{0:T(128)}, u32[]{:S(2)}) copy-start(s32[4]{0:T(128)} %pad_add_fusion.where) | copy-start | bytes 52
  44.4 27.2 %collective-permute-start.3 = (bf16[384,1536]{1,0:T(8,128)(2,1)}, bf16[384,1536]{1,0:T(8,128)(2,1)S(1)}, u32[]{:S(2)}, u32[]{:S(2)}) collective-permute-start(bf16[384,1536]{1,0:T(8,128)(2,1)} %dequantize.1.w0), channel_id=1, source_target_pairs={{0,1},{1,2},{2,3},{3,0},{4,5},{5,6},{6,7},{7,4},{8,9},{9,10},{10,1... | collective-permute-start | bytes 3538952 | tf_op jit(solution)/shard_map/ppermute | solution.py:53
  44.4 27.6 %collective-permute-start.4 = (bf16[384,1536]{1,0:T(8,128)(2,1)}, bf16[384,1536]{1,0:T(8,128)(2,1)S(1)}, u32[]{:S(2)}, u32[]{:S(2)}) collective-permute-start(bf16[384,1536]{1,0:T(8,128)(2,1)} %dequantize.1.w0), channel_id=1, source_target_pairs={{0,3},{1,0},{2,1},{3,2},{4,7},{5,4},{6,5},{7,6},{8,11},{9,8},{10,9... | collective-permute-start | bytes 3538952 | tf_op jit(solution)/shard_map/ppermute | solution.py:53
  66.7 28.2 %copy-start.8 = (bf16[128,4608]{1,0:T(8,128)(2,1)}, bf16[128,4608]{1,0:T(8,128)(2,1)S(1)}, u32[]{:S(2)}) copy-start(bf16[128,4608]{1,0:T(8,128)(2,1)S(1)} %collective-permute-done.1.pair.cot2) | copy-start | bytes 3538948
  66.7 8.4 %collective-permute-start.2 = (bf16[128,4608]{1,0:T(8,128)(2,1)S(1)}, bf16[128,4608]{1,0:T(8,128)(2,1)S(1)}, u32[]{:S(2)}, u32[]{:S(2)}) collective-permute-start(bf16[128,4608]{1,0:T(8,128)(2,1)S(1)} %collective-permute-done.1.pair.cot2), channel_id=1, source_target_pairs={{0,8},{1,9},{2,10},{3,11},{4,12},{5,13},{6,14},{7,15},{8,0},{9,1},... | collective-permute-start | bytes 3538952 | tf_op jit(solution)/shard_map/ppermute | solution.py:53
  66.7 8.4 %collective-permute-start = (bf16[128,3072]{1,0:T(8,128)(2,1)S(1)}, bf16[128,3072]{1,0:T(8,128)(2,1)S(1)}, u32[]{:S(2)}, u32[]{:S(2)}) collective-permute-start(bf16[128,3072]{1,0:T(8,128)(2,1)S(1)} %copy-done.1), channel_id=1, source_target_pairs={{0,8},{1,9},{2,10},{3,11},{4,12},{5,13},{6,14},{7,15},{8,0},{9,1},... | collective-permute-start | bytes 2359304 | tf_op jit(solution)/shard_map/ppermute | solution.py:53
  67.2 7.9 %collective-permute-start.7 = (bf16[128,3072]{1,0:T(8,128)(2,1)S(1)}, bf16[128,3072]{1,0:T(8,128)(2,1)S(1)}, u32[]{:S(2)}, u32[]{:S(2)}) collective-permute-start(bf16[128,3072]{1,0:T(8,128)(2,1)S(1)} %copy-done.2), channel_id=1, source_target_pairs={{0,8},{1,9},{2,10},{3,11},{4,12},{5,13},{6,14},{7,15},{8,0},{9,1},... | collective-permute-start | bytes 2359304 | tf_op jit(solution)/shard_map/ppermute | solution.py:53
  71.7 23.2 %collective-permute-start.5 = (bf16[384,768]{1,0:T(8,128)(2,1)S(1)}, bf16[384,768]{1,0:T(8,128)(2,1)S(1)}, u32[]{:S(2)}, u32[]{:S(2)}) collective-permute-start(bf16[384,768]{1,0:T(8,128)(2,1)S(1)} %slice.26), channel_id=1, source_target_pairs={{0,1},{1,2},{2,3},{3,0},{4,5},{5,6},{6,7},{7,4},{8,9},{9,10},{10,1... | collective-permute-start | bytes 1769480 | tf_op jit(solution)/shard_map/ppermute | solution.py:53
  72.1 22.9 %collective-permute-start.6 = (bf16[384,768]{1,0:T(8,128)(2,1)S(1)}, bf16[384,768]{1,0:T(8,128)(2,1)S(1)}, u32[]{:S(2)}, u32[]{:S(2)}) collective-permute-start(bf16[384,768]{1,0:T(8,128)(2,1)S(1)} %slice.27), channel_id=1, source_target_pairs={{0,3},{1,0},{2,1},{3,2},{4,7},{5,4},{6,5},{7,6},{8,11},{9,8},{10,9... | collective-permute-start | bytes 1769480 | tf_op jit(solution)/shard_map/ppermute | solution.py:53
  80.3 14.6 %copy-start.3 = (bf16[96,3072]{1,0:T(8,128)(2,1)}, bf16[96,3072]{1,0:T(8,128)(2,1)S(1)}, u32[]{:S(2)}) copy-start(bf16[96,3072]{1,0:T(8,128)(2,1)S(1)} %get-tuple-element.76.refs_1_) | copy-start | bytes 1769476
  80.3 14.6 %copy-start.5 = (bf16[96,3072]{1,0:T(8,128)(2,1)}, bf16[96,3072]{1,0:T(8,128)(2,1)S(1)}, u32[]{:S(2)}) copy-start(bf16[96,3072]{1,0:T(8,128)(2,1)S(1)} %get-tuple-element.77.refs_2_) | copy-start | bytes 1769476
  80.3 14.6 %copy-start = (bf16[384,1536]{1,0:T(8,128)(2,1)S(1)}, bf16[384,1536]{1,0:T(8,128)(2,1)}, u32[]{:S(2)}) copy-start(bf16[384,1536]{1,0:T(8,128)(2,1)} %dequantize.1.w0) | copy-start | bytes 3538948
  80.3 10.5 %collective-permute-start.9 = (bf16[48,3072]{1,0:T(8,128)(2,1)S(1)}, bf16[48,3072]{1,0:T(8,128)(2,1)S(1)}, u32[]{:S(2)}, u32[]{:S(2)}) collective-permute-start(bf16[48,3072]{1,0:T(8,128)(2,1)S(1)} %get-tuple-element.49), channel_id=1, source_target_pairs={{0,224},{1,225},{2,226},{3,227},{4,228},{5,229},{6,230},{7,231},{8... | collective-permute-start | bytes 884744 | tf_op jit(solution)/shard_map/ppermute | solution.py:53
  86.3 8.5 %collective-permute-start.8 = (bf16[48,3072]{1,0:T(8,128)(2,1)S(1)}, bf16[48,3072]{1,0:T(8,128)(2,1)S(1)}, u32[]{:S(2)}, u32[]{:S(2)}) collective-permute-start(bf16[48,3072]{1,0:T(8,128)(2,1)S(1)} %get-tuple-element.47), channel_id=1, source_target_pairs={{0,32},{1,33},{2,34},{3,35},{4,36},{5,37},{6,38},{7,39},{8,40},{9,... | collective-permute-start | bytes 884744 | tf_op jit(solution)/shard_map/ppermute | solution.py:53
  91.0 13.8 %collective-permute-start.14 = (bf16[96,3072]{1,0:T(8,128)(2,1)S(1)}, bf16[96,3072]{1,0:T(8,128)(2,1)S(1)}, u32[]{:S(2)}, u32[]{:S(2)}) collective-permute-start(bf16[96,3072]{1,0:T(8,128)(2,1)S(1)} %hop.8), channel_id=1, source_target_pairs={{0,224},{1,225},{2,226},{3,227},{4,228},{5,229},{6,230},{7,231},{8... | collective-permute-start | bytes 1769480 | tf_op jit(solution)/shard_map/ppermute | solution.py:53
  94.8 14.6 %collective-permute-start.12 = (bf16[96,3072]{1,0:T(8,128)(2,1)S(1)}, bf16[96,3072]{1,0:T(8,128)(2,1)S(1)}, u32[]{:S(2)}, u32[]{:S(2)}) collective-permute-start(bf16[96,3072]{1,0:T(8,128)(2,1)S(1)} %hop.7), channel_id=1, source_target_pairs={{0,32},{1,33},{2,34},{3,35},{4,36},{5,37},{6,38},{7,39},{8,40},{9,... | collective-permute-start | bytes 1769480 | tf_op jit(solution)/shard_map/ppermute | solution.py:53
  99.0 17.9 %collective-permute-start.10 = (bf16[256,1536]{1,0:T(8,128)(2,1)S(1)}, bf16[256,1536]{1,0:T(8,128)(2,1)S(1)}, u32[]{:S(2)}, u32[]{:S(2)}) collective-permute-start(bf16[256,1536]{1,0:T(8,128)(2,1)S(1)} %get-tuple-element.57), channel_id=1, source_target_pairs={{0,20},{1,21},{2,22},{3,23},{4,16},{5,17},{6,18},{7,19},{8,28},{9,... | collective-permute-start | bytes 2359304 | tf_op jit(solution)/shard_map/ppermute | solution.py:53
  102.1 8.3 %copy-start.9 = (bf16[128,4608]{1,0:T(8,128)(2,1)S(1)}, bf16[128,4608]{1,0:T(8,128)(2,1)}, u32[]{:S(2)}) copy-start(bf16[128,4608]{1,0:T(8,128)(2,1)} %copy-done.8) | copy-start | bytes 3538948
  105.7 13.1 %collective-permute-start.17 = (bf16[96,3072]{1,0:T(8,128)(2,1)}, bf16[96,3072]{1,0:T(8,128)(2,1)}, u32[]{:S(2)}, u32[]{:S(2)}) collective-permute-start(bf16[96,3072]{1,0:T(8,128)(2,1)} %hop.10), channel_id=1, source_target_pairs={{0,224},{1,225},{2,226},{3,227},{4,228},{5,229},{6,230},{7,231},{8... | collective-permute-start | bytes 1769480 | tf_op jit(solution)/shard_map/ppermute | solution.py:53
  110.4 13.4 %collective-permute-start.13 = (bf16[96,3072]{1,0:T(8,128)(2,1)}, bf16[96,3072]{1,0:T(8,128)(2,1)}, u32[]{:S(2)}, u32[]{:S(2)}) collective-permute-start(bf16[96,3072]{1,0:T(8,128)(2,1)} %hop.9), channel_id=1, source_target_pairs={{0,32},{1,33},{2,34},{3,35},{4,36},{5,37},{6,38},{7,39},{8,40},{9,... | collective-permute-start | bytes 1769480 | tf_op jit(solution)/shard_map/ppermute | solution.py:53
  115.3 2.8 %collective-permute-start.15 = (bf16[256,1536]{1,0:T(8,128)(2,1)}, bf16[256,1536]{1,0:T(8,128)(2,1)}, u32[]{:S(2)}, u32[]{:S(2)}) collective-permute-start(bf16[256,1536]{1,0:T(8,128)(2,1)} %get-tuple-element.74), channel_id=1, source_target_pairs={{0,8},{1,9},{2,10},{3,11},{4,12},{5,13},{6,14},{7,15},{8,0},{9,1},... | collective-permute-start | bytes 2359304 | tf_op jit(solution)/shard_map/ppermute | solution.py:53
  117.1 1.7 %copy-start.4 = (bf16[96,3072]{1,0:T(8,128)(2,1)S(1)}, bf16[96,3072]{1,0:T(8,128)(2,1)}, u32[]{:S(2)}) copy-start(bf16[96,3072]{1,0:T(8,128)(2,1)} %copy-done.3) | copy-start | bytes 1769476
  118.1 7.0 %collective-permute-start.11 = (bf16[128,1536]{1,0:T(8,128)(2,1)}, bf16[128,1536]{1,0:T(8,128)(2,1)S(1)}, u32[]{:S(2)}, u32[]{:S(2)}) collective-permute-start(bf16[128,1536]{1,0:T(8,128)(2,1)} %get-tuple-element.84), channel_id=1, source_target_pairs={{0,8},{1,9},{2,10},{3,11},{4,12},{5,13},{6,14},{7,15},{8,0},{9,1},... | collective-permute-start | bytes 1179656 | tf_op jit(solution)/shard_map/ppermute | solution.py:53
  120.0 15.5 %collective-permute-start.18 = (bf16[96,3072]{1,0:T(8,128)(2,1)S(1)}, bf16[96,3072]{1,0:T(8,128)(2,1)S(1)}, u32[]{:S(2)}, u32[]{:S(2)}) collective-permute-start(bf16[96,3072]{1,0:T(8,128)(2,1)S(1)} %hop.12), channel_id=1, source_target_pairs={{0,224},{1,225},{2,226},{3,227},{4,228},{5,229},{6,230},{7,231},{8... | collective-permute-start | bytes 1769480 | tf_op jit(solution)/shard_map/ppermute | solution.py:53
  125.0 15.3 %collective-permute-start.16 = (bf16[96,3072]{1,0:T(8,128)(2,1)S(1)}, bf16[96,3072]{1,0:T(8,128)(2,1)S(1)}, u32[]{:S(2)}, u32[]{:S(2)}) collective-permute-start(bf16[96,3072]{1,0:T(8,128)(2,1)S(1)} %hop.11), channel_id=1, source_target_pairs={{0,32},{1,33},{2,34},{3,35},{4,36},{5,37},{6,38},{7,39},{8,40},{9,... | collective-permute-start | bytes 1769480 | tf_op jit(solution)/shard_map/ppermute | solution.py:53
  126.2 14.1 %copy-start.6 = (bf16[96,3072]{1,0:T(8,128)(2,1)S(1)}, bf16[96,3072]{1,0:T(8,128)(2,1)}, u32[]{:S(2)}) copy-start(bf16[96,3072]{1,0:T(8,128)(2,1)} %copy-done.5) | copy-start | bytes 1769476
  140.5 6.4 %collective-permute-start.19 = (bf16[24,3072]{1,0:T(8,128)(2,1)S(1)}, bf16[24,3072]{1,0:T(8,128)(2,1)S(1)}, u32[]{:S(2)}, u32[]{:S(2)}) collective-permute-start(bf16[24,3072]{1,0:T(8,128)(2,1)S(1)} %get-tuple-element.85), channel_id=1, source_target_pairs={{0,1},{1,2},{2,3},{3,0},{4,5},{5,6},{6,7},{7,4},{8,9},{9,10},{10,1... | collective-permute-start | bytes 442376 | tf_op jit(solution)/shard_map/ppermute | solution.py:53
  141.8 7.4 %collective-permute-start.20 = (bf16[24,3072]{1,0:T(8,128)(2,1)S(1)}, bf16[24,3072]{1,0:T(8,128)(2,1)S(1)}, u32[]{:S(2)}, u32[]{:S(2)}) collective-permute-start(bf16[24,3072]{1,0:T(8,128)(2,1)S(1)} %get-tuple-element.87), channel_id=1, source_target_pairs={{0,2},{1,3},{2,0},{3,1},{4,6},{5,7},{6,4},{7,5},{8,10},{9,11},{10,... | collective-permute-start | bytes 442376 | tf_op jit(solution)/shard_map/ppermute | solution.py:53
  144.5 5.1 %collective-permute-start.21 = (bf16[24,3072]{1,0:T(8,128)(2,1)S(1)}, bf16[24,3072]{1,0:T(8,128)(2,1)S(1)}, u32[]{:S(2)}, u32[]{:S(2)}) collective-permute-start(bf16[24,3072]{1,0:T(8,128)(2,1)S(1)} %get-tuple-element.86), channel_id=1, source_target_pairs={{0,3},{1,0},{2,1},{3,2},{4,7},{5,4},{6,5},{7,6},{8,11},{9,8},{10,9... | collective-permute-start | bytes 442376 | tf_op jit(solution)/shard_map/ppermute | solution.py:53
  146.0 9.8 %collective-permute-start.24 = (bf16[128,1536]{1,0:T(8,128)(2,1)S(1)}, bf16[128,1536]{1,0:T(8,128)(2,1)S(1)}, u32[]{:S(2)}, u32[]{:S(2)}) collective-permute-start(bf16[128,1536]{1,0:T(8,128)(2,1)S(1)} %get-tuple-element.89), channel_id=1, source_target_pairs={{0,20},{1,21},{2,22},{3,23},{4,16},{5,17},{6,18},{7,19},{8,28},{9,... | collective-permute-start | bytes 1179656 | tf_op jit(solution)/shard_map/ppermute | solution.py:53
  149.8 16.0 %collective-permute-start.22 = (bf16[12,3072]{1,0:T(8,128)(2,1)S(1)}, bf16[12,3072]{1,0:T(8,128)(2,1)S(1)}, u32[]{:S(2)}, u32[]{:S(2)}) collective-permute-start(bf16[12,3072]{1,0:T(8,128)(2,1)S(1)} %get-tuple-element.91), channel_id=1, source_target_pairs={{0,24},{1,26},{2,28},{3,30},{4,184},{5,186},{6,188},{7,190},{8,72}... | collective-permute-start | bytes 221192 | tf_op jit(solution)/shard_map/ppermute | solution.py:53
  151.7 15.3 %collective-permute-start.23 = (bf16[12,3072]{1,0:T(8,128)(2,1)S(1)}, bf16[12,3072]{1,0:T(8,128)(2,1)S(1)}, u32[]{:S(2)}, u32[]{:S(2)}) collective-permute-start(bf16[12,3072]{1,0:T(8,128)(2,1)S(1)} %get-tuple-element.90), channel_id=1, source_target_pairs={{0,25},{1,27},{2,29},{3,31},{4,185},{5,187},{6,189},{7,191},{8,73}... | collective-permute-start | bytes 221192 | tf_op jit(solution)/shard_map/ppermute | solution.py:53

commit v5 on v4

--- a/solution.py
+++ b/solution.py
@@ -104,7 +104,7 @@
     return call(
         dequantize_kernel,
         "dequantize",
-        60,
+        12,
         where,
         (3,),
         [
@@ -138,7 +138,7 @@
         pack_kernel,
         name="pack",
         in_specs=[pl.BlockSpec(memory_space=pl.ANY)] * 2,
-        out_specs=pl.BlockSpec(memory_space=pl.ANY),
+        out_specs=pl.BlockSpec(memory_space=pltpu.VMEM),
         out_shape=jax.ShapeDtypeStruct(shape, jnp.bfloat16),
         scratch_shapes=[pltpu.SemaphoreType.DMA((2,))],
         compiler_params=pltpu.CompilerParams(vmem_limit_bytes=60 * 2**20),
@@ -352,23 +352,24 @@
     token_parts = (tokens, token_sib, pair, cross)
     cot_parts = (cotangent, cot_sib, pair, cross)
 
-    up, down, *grad = gradient(where, token_parts, cot_parts)
+    up, down, *grad = gradient(where, token_parts, after(cot_parts, left, right))
     half = own.shape[1] // 2
-    blocks = (own, left, right, send(left[:, :half], X_UP), send(right[:, half:], X_DOWN))
     up, down = send(up, Z_UP), send(down, Z_DOWN)
     up = hop(grad[0], up, kernel=functools.partial(first_hop_kernel, upper=True))
     down = hop(grad[1], down, kernel=functools.partial(first_hop_kernel, upper=False))
+    left, right = after((left, right), up, down)
+    blocks = (own, left, right, send(left[:, :half], X_UP), send(right[:, half:], X_DOWN))
+    up, down = send(up, Z_UP), send(down, Z_DOWN)
+    up, down = hop(grad[2], up), hop(grad[3], down)
     mine, other, away = forward_parts(where, token_parts, after(blocks, up, down))
     up, down = send(up, Z_UP), send(down, Z_DOWN)
     back = f32(send(away, PAIR))
     grad = after(grad, away)
-    up, down = hop(grad[2], up), hop(grad[3], down)
+    up, down = hop(grad[4], up), hop(grad[5], down)
     part, give = backward_parts(where, cot_parts, after(blocks, up, down))
     up, down = send(up, Z_UP), send(down, Z_DOWN)
     give = send(give, CORE)
-    grad = after(grad, give, back)
-    up, down = hop(grad[4], up), hop(grad[5], down)
-    up, down = send(up, Z_UP), send(down, Z_DOWN)
+    grad = after(grad, part)
     total = hop(grad[6], up, down, kind=jnp.float32)
 
     part = part + f32(give)

time: 169 us -> 140 us (0.83)
  Pallas kernels: 59.9 us -> 22.9 us
  waiting for transfers between devices: 58.9 us -> 67.2 us
  starting transfers between devices: 41.8 us -> 40 us
    pallas_call x1, Pallas kernels: 36.9 us -> 2.45 us  [pack(): pl.pallas_call(pack_kernel, name='pack', in_specs=[pl.BlockSpec(memory_sp...]
    ppermute x25, waiting for transfers between devices: 58.9 us -> 67.2 us  [send(): return lax.ppermute(value, AXES, pairs)]
    pallas_call x7, Pallas kernels: 4.66 us -> 2.17 us  [hop(): pl.pallas_call(kernel, name='hop', out_shape=jax.ShapeDtypeStruct(part.sh...]
    ppermute x25, starting transfers between devices: 41.8 us -> 40 us  [send(): return lax.ppermute(value, AXES, pairs)]
  transfers between devices with their start and end apart: 25 -> 25, of which waited for: 13 -> 14; matrix products, arithmetic and copies ran while one was open for 3% -> 3% of each run, Pallas kernels for 14% -> 10%
where the time goes in v5:
time: 140 us; the launch traced here: 138 us
  waiting for transfers between devices  67.2 us (48%)
  starting transfers between devices  40 us (29%)
  Pallas kernels  22.9 us (16%)
  other arithmetic  6.73 us (5%)
    ppermute x25, waiting for transfers between devices, send(): return lax.ppermute(value, AXES, pairs)  67.2 us
    ppermute x25, starting transfers between devices, send(): return lax.ppermute(value, AXES, pairs)  40 us
    pallas_call x4, Pallas kernels, call(): pl.pallas_call(kernel, name=name, grid_spec=pltpu.PrefetchScalarGridSpec(...  18.3 us
    select_n x2, other arithmetic, joined(): jnp.where(flag == 0, jnp.concatenate([here, there], axis=1), jnp.concaten...  3.24 us
  transfers between devices with their start and end apart: 25, of which 14 were waited for; matrix products, arithmetic and copies ran while one was open for 3% of the time, Pallas kernels for 10%

profile of v5, /device:TPU:24, one launch (start us, length us, event | category | flops | bytes accessed | tf_op | source)
XLA Modules:
  0.0 137.9 jit_solution(11903094966651192327)
XLA Ops:
  0.7 2.5 %pack.1 = bf16[128,4608]{1,0:T(8,128)(2,1)} custom-call(bf16[128,3072]{1,0:T(8,128)(2,1)} %own.3, bf16[128,3072]{1,0:T(8,128)(2,1)} %cot0.2), custom_call_target="tpu_custom_call" | custom-call | tf_op jit(solution)/shard_map/pack/pallas_call | solution.py:137
  3.1 2.0 %collective-permute-start.1 = (bf16[128,4608]{1,0:T(8,128)(2,1)}, bf16[128,4608]{1,0:T(8,128)(2,1)}, u32[]{:S(2)}, u32[]{:S(2)}) collective-permute-start(bf16[128,4608]{1,0:T(8,128)(2,1)} %pack.1), channel_id=1, source_target_pairs={{0,20},{1,21},{2,22},{3,23},{4,16},{5,17},{6,18},{7,19},{8,28},{9,... | collective-permute-start | bytes 3538952 | tf_op jit(solution)/shard_map/ppermute | solution.py:53
  5.2 0.1 pad_add_fusion.where
  5.2 0.0 copy-start.1
  5.3 1.6 %dequantize.1.w0 = bf16[384,1536]{1,0:T(8,128)(2,1)S(1)} custom-call(s32[4]{0:T(128)S(1)} %pad_add_fusion.where, bf16[384,3072]{1,0:T(8,128)(2,1)S(1)} %copy-done, f32[12,384]{1,0:T(8,128)S(1)} %bitcast.5), custom_call_target="tpu_custom_call" | custom-call | flops 589824 | bytes 3557376 | tf_op jit(solution)/shard_map/dequantize/pallas_call | solution.py:71
  6.8 0.1 collective-permute-start.3
  6.9 3.2 %collective-permute-start.4 = (bf16[384,1536]{1,0:T(8,128)(2,1)S(1)}, bf16[384,1536]{1,0:T(8,128)(2,1)S(1)}, u32[]{:S(2)}, u32[]{:S(2)}) collective-permute-start(bf16[384,1536]{1,0:T(8,128)(2,1)S(1)} %dequantize.1.w0), channel_id=1, source_target_pairs={{0,3},{1,0},{2,1},{3,2},{4,7},{5,4},{6,5},{7,6},{8,11},{9,8},{10,9... | collective-permute-start | bytes 3538952 | tf_op jit(solution)/shard_map/ppermute | solution.py:53
  10.2 22.3 %collective-permute-done.1.pair.cot2 = bf16[128,4608]{1,0:T(8,128)(2,1)} collective-permute-done((bf16[128,4608]{1,0:T(8,128)(2,1)}, bf16[128,4608]{1,0:T(8,128)(2,1)}, u32[]{:S(2)}, u32[]{:S(2)}) %collective-permute-start.1) | collective-permute-done | bytes 1179680 | tf_op jit(solution)/shard_map/ppermute | solution.py:53
  32.4 0.5 collective-permute-start.5
  32.9 0.1 collective-permute-start
  33.0 3.0 %collective-permute-done.5.cot1 = bf16[128,3072]{1,0:T(8,128)(2,1)S(1)} collective-permute-done((bf16[128,3072]{1,0:T(8,128)(2,1)S(1)}, bf16[128,3072]{1,0:T(8,128)(2,1)S(1)}, u32[]{:S(2)}, u32[]{:S(2)}) %collective-permute-start.5) | collective-permute-done | bytes 786464 | tf_op jit(solution)/shard_map/ppermute | solution.py:53
  36.0 0.0 collective-permute-done.4.w2
  36.0 1.1 collective-permute-done.2.psib.cot3
  37.1 0.4 collective-permute-done.sib
  37.5 6.0 %gradient.1 = (bf16[48,3072]{1,0:T(8,128)(2,1)S(1)}, bf16[48,3072]{1,0:T(8,128)(2,1)S(1)}, bf16[96,3072]{1,0:T(8,128)(2,1)S(1)}, bf16[96,3072]{1,0:T(8,128)(2,1)...) custom-call(s32[4]{0:T(128)S(1)} %pad_add_fusion.where, ...), custom_call_target="tpu_custom_call" | custom-call | flops 2415919104 | bytes 12582912 | tf_op jit(solution)/shard_map/gradient/pallas_call | solution.py:71
  43.6 5.9 %collective-permute-start.7 = (bf16[48,3072]{1,0:T(8,128)(2,1)S(1)}, bf16[48,3072]{1,0:T(8,128)(2,1)S(1)}, u32[]{:S(2)}, u32[]{:S(2)}) collective-permute-start(bf16[48,3072]{1,0:T(8,128)(2,1)S(1)} %get-tuple-element.55), channel_id=1, source_target_pairs={{0,224},{1,225},{2,226},{3,227},{4,228},{5,229},{6,230},{7,231},{8... | collective-permute-start | bytes 884744 | tf_op jit(solution)/shard_map/ppermute | solution.py:53
  49.5 0.0 collective-permute-start.6
  49.5 6.6 %collective-permute-done.7.arrived = bf16[48,3072]{1,0:T(8,128)(2,1)S(1)} collective-permute-done((bf16[48,3072]{1,0:T(8,128)(2,1)S(1)}, bf16[48,3072]{1,0:T(8,128)(2,1)S(1)}, u32[]{:S(2)}, u32[]{:S(2)}) %collective-permute-start.7) | collective-permute-done | bytes 294944 | tf_op jit(solution)/shard_map/ppermute | solution.py:53
  56.1 0.1 hop.8
  56.2 3.8 %collective-permute-start.11 = (bf16[96,3072]{1,0:T(8,128)(2,1)S(1)}, bf16[96,3072]{1,0:T(8,128)(2,1)S(1)}, u32[]{:S(2)}, u32[]{:S(2)}) collective-permute-start(bf16[96,3072]{1,0:T(8,128)(2,1)S(1)} %hop.8), channel_id=1, source_target_pairs={{0,224},{1,225},{2,226},{3,227},{4,228},{5,229},{6,230},{7,231},{8... | collective-permute-start | bytes 1769480 | tf_op jit(solution)/shard_map/ppermute | solution.py:53
  59.9 0.0 collective-permute-done.6.arrived
  59.9 0.1 hop.7
  60.0 0.1 collective-permute-start.10
  60.1 1.6 %collective-permute-start.8 = (bf16[384,768]{1,0:T(8,128)(2,1)S(1)}, bf16[384,768]{1,0:T(8,128)(2,1)S(1)}, u32[]{:S(2)}, u32[]{:S(2)}) collective-permute-start(bf16[384,768]{1,0:T(8,128)(2,1)S(1)} %slice.20), channel_id=1, source_target_pairs={{0,1},{1,2},{2,3},{3,0},{4,5},{5,6},{6,7},{7,4},{8,9},{9,10},{10,1... | collective-permute-start | bytes 1769480 | tf_op jit(solution)/shard_map/ppermute | solution.py:53
  61.8 1.8 %collective-permute-start.9 = (bf16[384,768]{1,0:T(8,128)(2,1)S(1)}, bf16[384,768]{1,0:T(8,128)(2,1)S(1)}, u32[]{:S(2)}, u32[]{:S(2)}) collective-permute-start(bf16[384,768]{1,0:T(8,128)(2,1)S(1)} %slice.21), channel_id=1, source_target_pairs={{0,3},{1,0},{2,1},{3,2},{4,7},{5,4},{6,5},{7,6},{8,11},{9,8},{10,9... | collective-permute-start | bytes 1769480 | tf_op jit(solution)/shard_map/ppermute | solution.py:53
  63.6 8.4 %collective-permute-done.11.refs_0_ = bf16[96,3072]{1,0:T(8,128)(2,1)S(1)} collective-permute-done((bf16[96,3072]{1,0:T(8,128)(2,1)S(1)}, bf16[96,3072]{1,0:T(8,128)(2,1)S(1)}, u32[]{:S(2)}, u32[]{:S(2)}) %collective-permute-start.11) | collective-permute-done | bytes 589856 | tf_op jit(solution)/shard_map/ppermute | solution.py:53
  72.0 0.2 hop.10
  72.1 3.8 %collective-permute-start.16 = (bf16[96,3072]{1,0:T(8,128)(2,1)S(1)}, bf16[96,3072]{1,0:T(8,128)(2,1)S(1)}, u32[]{:S(2)}, u32[]{:S(2)}) collective-permute-start(bf16[96,3072]{1,0:T(8,128)(2,1)S(1)} %hop.10), channel_id=1, source_target_pairs={{0,224},{1,225},{2,226},{3,227},{4,228},{5,229},{6,230},{7,231},{8... | collective-permute-start | bytes 1769480 | tf_op jit(solution)/shard_map/ppermute | solution.py:53
  75.9 0.0 collective-permute-done.10.refs_0_
  75.9 0.2 hop.9
  76.1 0.3 collective-permute-start.14
  76.3 0.0 collective-permute-done.8.w3
  76.4 4.8 %forward.1 = (f32[128,1536]{1,0:T(8,128)S(1)}, f32[128,1536]{1,0:T(8,128)S(1)}, bf16[256,1536]{1,0:T(8,128)(2,1)S(1)}) custom-call(s32[4]{0:T(128)S(1)} %pad_add_fusion.where, bf16[128,3072]{1,0:T(8,128)(2,1)S(1)} %copy-done.1, bf16[128,3072]{1,0:T(8,128)(2,1)S(1)} %collective-permute-done.sib, bf16[128,4608]{1,0:T(8,128)(2,1)} %collective-permute-done.1.pair.cot2, ...), custom_call_target="tpu_custom_call" | custom-call | flops 2415919104 | bytes 11010048 | tf_op jit(solution)/shard_map/forward/pallas_call | solution.py:71
  81.2 0.4 collective-permute-start.12
  81.6 5.5 %collective-permute-done.16.refs_0_ = bf16[96,3072]{1,0:T(8,128)(2,1)S(1)} collective-permute-done((bf16[96,3072]{1,0:T(8,128)(2,1)S(1)}, bf16[96,3072]{1,0:T(8,128)(2,1)S(1)}, u32[]{:S(2)}, u32[]{:S(2)}) %collective-permute-start.16) | collective-permute-done | bytes 589856 | tf_op jit(solution)/shard_map/ppermute | solution.py:53
  87.0 0.1 hop.12
  87.2 3.8 %collective-permute-start.17 = (bf16[96,3072]{1,0:T(8,128)(2,1)S(1)}, bf16[96,3072]{1,0:T(8,128)(2,1)}, u32[]{:S(2)}, u32[]{:S(2)}) collective-permute-start(bf16[96,3072]{1,0:T(8,128)(2,1)S(1)} %hop.12), channel_id=1, source_target_pairs={{0,224},{1,225},{2,226},{3,227},{4,228},{5,229},{6,230},{7,231},{8... | collective-permute-start | bytes 1769480 | tf_op jit(solution)/shard_map/ppermute | solution.py:53
  90.9 0.1 hop.11
  91.1 0.1 collective-permute-start.15
  91.2 5.8 %backward.1 = (f32[256,1536]{1,0:T(8,128)S(1)}, bf16[256,1536]{1,0:T(8,128)(2,1)}) custom-call(s32[4]{0:T(128)S(1)} %pad_add_fusion.where, bf16[128,3072]{1,0:T(8,128)(2,1)S(1)} %copy-done.2, bf16[128,3072]{1,0:T(8,128)(2,1)S(1)} %collective-permute-done.5.cot1, bf16[128,4608]{1,0:T(8,128)(2,1)} %collective-permute-done.1.pair.cot2, ...), custom_call_target="tpu_custom_call" | custom-call | flops 2415919104 | bytes 11010048 | tf_op jit(solution)/shard_map/backward/pallas_call | solution.py:71
  97.0 3.0 %collective-permute-done.12 = bf16[256,1536]{1,0:T(8,128)(2,1)S(1)} collective-permute-done((bf16[256,1536]{1,0:T(8,128)(2,1)S(1)}, bf16[256,1536]{1,0:T(8,128)(2,1)S(1)}, u32[]{:S(2)}, u32[]{:S(2)}) %collective-permute-start.12) | collective-permute-done | bytes 786464 | tf_op jit(solution)/shard_map/ppermute | solution.py:53
  100.1 0.2 convert_element_type.41
  100.2 1.1 fusion.1
  101.4 3.5 %collective-permute-done.15.refs_0_ = bf16[96,3072]{1,0:T(8,128)(2,1)} collective-permute-done((bf16[96,3072]{1,0:T(8,128)(2,1)S(1)}, bf16[96,3072]{1,0:T(8,128)(2,1)}, u32[]{:S(2)}, u32[]{:S(2)}) %collective-permute-start.15) | collective-permute-done | bytes 589856 | tf_op jit(solution)/shard_map/ppermute | solution.py:53
  104.9 1.4 %hop.13 = f32[96,3072]{1,0:T(8,128)S(1)} custom-call(bf16[96,3072]{1,0:T(8,128)(2,1)} %collective-permute-done.15.refs_0_, bf16[96,3072]{1,0:T(8,128)(2,1)} %collective-permute-done.17.refs_1_, bf16[96,3072]{1,0:T(8,128)(2,1)S(1)} %get-tuple-element.81.refs_2_), custom_call_target="tpu_custom_call" | custom-call | flops 294912 | bytes 1769472 | tf_op jit(solution)/shard_map/hop/pallas_call | solution.py:216
  106.4 2.2 %maximum_select_fusion = bf16[128,3072]{1,0:T(8,128)(2,1)} fusion(bf16[128,1536]{1,0:T(8,128)(2,1)} %collective-permute-done.13, bf16[128,1536]{1,0:T(8,128)(2,1)S(1)} %copy-done.4, pred[]{:T(512)S(6)} %eq.11), kind=kLoop, calls=%fused_computation.5 | loop fusion | flops 3538944 | bytes 1572865 | tf_op jit(solution)/shard_map/jit(_where)/select_n | solution.py:322
  108.5 1.3 convert_add_fusion
  109.9 0.1 dynamic-slice_convert_fusion.2
  109.9 1.6 %collective-permute-start.19 = (bf16[24,3072]{1,0:T(8,128)(2,1)S(1)}, bf16[24,3072]{1,0:T(8,128)(2,1)S(1)}, u32[]{:S(2)}, u32[]{:S(2)}) collective-permute-start(bf16[24,3072]{1,0:T(8,128)(2,1)S(1)} %get-tuple-element.89), channel_id=1, source_target_pairs={{0,1},{1,2},{2,3},{3,0},{4,5},{5,6},{6,7},{7,4},{8,9},{9,10},{10,1... | collective-permute-start | bytes 442376 | tf_op jit(solution)/shard_map/ppermute | solution.py:53
  111.5 2.7 %collective-permute-start.20 = (bf16[24,3072]{1,0:T(8,128)(2,1)S(1)}, bf16[24,3072]{1,0:T(8,128)(2,1)S(1)}, u32[]{:S(2)}, u32[]{:S(2)}) collective-permute-start(bf16[24,3072]{1,0:T(8,128)(2,1)S(1)} %get-tuple-element.91), channel_id=1, source_target_pairs={{0,2},{1,3},{2,0},{3,1},{4,6},{5,7},{6,4},{7,5},{8,10},{9,11},{10,... | collective-permute-start | bytes 442376 | tf_op jit(solution)/shard_map/ppermute | solution.py:53
  114.2 1.5 %collective-permute-start.21 = (bf16[24,3072]{1,0:T(8,128)(2,1)S(1)}, bf16[24,3072]{1,0:T(8,128)(2,1)S(1)}, u32[]{:S(2)}, u32[]{:S(2)}) collective-permute-start(bf16[24,3072]{1,0:T(8,128)(2,1)S(1)} %get-tuple-element.90), channel_id=1, source_target_pairs={{0,3},{1,0},{2,1},{3,2},{4,7},{5,4},{6,5},{7,6},{8,11},{9,8},{10,9... | collective-permute-start | bytes 442376 | tf_op jit(solution)/shard_map/ppermute | solution.py:53
  115.7 0.1 fusion.2
  115.7 0.4 collective-permute-start.24
  116.1 0.6 collective-permute-done.19
  116.7 2.2 %collective-permute-done.20 = bf16[24,3072]{1,0:T(8,128)(2,1)S(1)} collective-permute-done((bf16[24,3072]{1,0:T(8,128)(2,1)S(1)}, bf16[24,3072]{1,0:T(8,128)(2,1)S(1)}, u32[]{:S(2)}, u32[]{:S(2)}) %collective-permute-start.20) | collective-permute-done | bytes 147488 | tf_op jit(solution)/shard_map/ppermute | solution.py:53
  118.9 0.4 collective-permute-done.21
  119.4 0.1 multiply_convert_fusion
  119.4 0.1 constant_dynamic-slice_fusion
  119.5 1.9 %collective-permute-start.22 = (bf16[12,3072]{1,0:T(8,128)(2,1)S(1)}, bf16[12,3072]{1,0:T(8,128)(2,1)S(1)}, u32[]{:S(2)}, u32[]{:S(2)}) collective-permute-start(bf16[12,3072]{1,0:T(8,128)(2,1)S(1)} %get-tuple-element.95), channel_id=1, source_target_pairs={{0,24},{1,26},{2,28},{3,30},{4,184},{5,186},{6,188},{7,190},{8,72}... | collective-permute-start | bytes 221192 | tf_op jit(solution)/shard_map/ppermute | solution.py:53
  121.4 4.5 %collective-permute-start.23 = (bf16[12,3072]{1,0:T(8,128)(2,1)S(1)}, bf16[12,3072]{1,0:T(8,128)(2,1)S(1)}, u32[]{:S(2)}, u32[]{:S(2)}) collective-permute-start(bf16[12,3072]{1,0:T(8,128)(2,1)S(1)} %get-tuple-element.94), channel_id=1, source_target_pairs={{0,25},{1,27},{2,29},{3,31},{4,185},{5,187},{6,189},{7,191},{8,73}... | collective-permute-start | bytes 221192 | tf_op jit(solution)/shard_map/ppermute | solution.py:53
  126.0 7.8 %collective-permute-done.22 = bf16[12,3072]{1,0:T(8,128)(2,1)S(1)} collective-permute-done((bf16[12,3072]{1,0:T(8,128)(2,1)S(1)}, bf16[12,3072]{1,0:T(8,128)(2,1)S(1)}, u32[]{:S(2)}, u32[]{:S(2)}) %collective-permute-start.22) | collective-permute-done | bytes 73760 | tf_op jit(solution)/shard_map/ppermute | solution.py:53
  133.9 2.3 %collective-permute-done.23 = bf16[12,3072]{1,0:T(8,128)(2,1)S(1)} collective-permute-done((bf16[12,3072]{1,0:T(8,128)(2,1)S(1)}, bf16[12,3072]{1,0:T(8,128)(2,1)S(1)}, u32[]{:S(2)}, u32[]{:S(2)}) %collective-permute-start.23) | collective-permute-done | bytes 73760 | tf_op jit(solution)/shard_map/ppermute | solution.py:53
  136.2 1.1 maximum_select_fusion.1
  137.2 0.7 add.84
  (23 shorter events, 0.2 us)
Async XLA Ops:
  0.6 4.6 %copy-start.3 = (f32[384,12]{0,1:T(8,128)S(1)}, f32[384,12]{0,1:T(8,128)}, u32[]{:S(2)}) copy-start(f32[384,12]{0,1:T(8,128)} %param.7) | copy-start | bytes 55300
  0.6 4.6 %copy-start = (bf16[384,3072]{1,0:T(8,128)(2,1)S(1)}, bf16[384,3072]{1,0:T(8,128)(2,1)}, u32[]{:S(2)}) copy-start(bf16[384,3072]{1,0:T(8,128)(2,1)} %levels) | copy-start | bytes 7077892
  3.1 29.3 %collective-permute-start.1 = (bf16[128,4608]{1,0:T(8,128)(2,1)}, bf16[128,4608]{1,0:T(8,128)(2,1)}, u32[]{:S(2)}, u32[]{:S(2)}) collective-permute-start(bf16[128,4608]{1,0:T(8,128)(2,1)} %pack.1), channel_id=1, source_target_pairs={{0,20},{1,21},{2,22},{3,23},{4,16},{5,17},{6,18},{7,19},{8,28},{9,... | collective-permute-start | bytes 3538952 | tf_op jit(solution)/shard_map/ppermute | solution.py:53
  5.2 27.2 %copy-start.2 = (bf16[128,3072]{1,0:T(8,128)(2,1)S(1)}, bf16[128,3072]{1,0:T(8,128)(2,1)}, u32[]{:S(2)}) copy-start(bf16[128,3072]{1,0:T(8,128)(2,1)} %cot0.2) | copy-start | bytes 2359300
  5.2 27.7 %copy-start.1 = (bf16[128,3072]{1,0:T(8,128)(2,1)S(1)}, bf16[128,3072]{1,0:T(8,128)(2,1)}, u32[]{:S(2)}) copy-start(bf16[128,3072]{1,0:T(8,128)(2,1)} %own.3) | copy-start | bytes 2359300
  6.8 29.2 %collective-permute-start.3 = (bf16[384,1536]{1,0:T(8,128)(2,1)S(1)}, bf16[384,1536]{1,0:T(8,128)(2,1)S(1)}, u32[]{:S(2)}, u32[]{:S(2)}) collective-permute-start(bf16[384,1536]{1,0:T(8,128)(2,1)S(1)} %dequantize.1.w0), channel_id=1, source_target_pairs={{0,1},{1,2},{2,3},{3,0},{4,5},{5,6},{6,7},{7,4},{8,9},{9,10},{10,1... | collective-permute-start | bytes 3538952 | tf_op jit(solution)/shard_map/ppermute | solution.py:53
  6.9 29.1 %collective-permute-start.4 = (bf16[384,1536]{1,0:T(8,128)(2,1)S(1)}, bf16[384,1536]{1,0:T(8,128)(2,1)S(1)}, u32[]{:S(2)}, u32[]{:S(2)}) collective-permute-start(bf16[384,1536]{1,0:T(8,128)(2,1)S(1)} %dequantize.1.w0), channel_id=1, source_target_pairs={{0,3},{1,0},{2,1},{3,2},{4,7},{5,4},{6,5},{7,6},{8,11},{9,8},{10,9... | collective-permute-start | bytes 3538952 | tf_op jit(solution)/shard_map/ppermute | solution.py:53
  32.4 4.7 %collective-permute-start.2 = (bf16[128,4608]{1,0:T(8,128)(2,1)}, bf16[128,4608]{1,0:T(8,128)(2,1)S(1)}, u32[]{:S(2)}, u32[]{:S(2)}) collective-permute-start(bf16[128,4608]{1,0:T(8,128)(2,1)} %collective-permute-done.1.pair.cot2), channel_id=1, source_target_pairs={{0,8},{1,9},{2,10},{3,11},{4,12},{5,13},{6,14},{7,15},{8,0},{9,1},... | collective-permute-start | bytes 3538952 | tf_op jit(solution)/shard_map/ppermute | solution.py:53
  32.4 3.6 %collective-permute-start.5 = (bf16[128,3072]{1,0:T(8,128)(2,1)S(1)}, bf16[128,3072]{1,0:T(8,128)(2,1)S(1)}, u32[]{:S(2)}, u32[]{:S(2)}) collective-permute-start(bf16[128,3072]{1,0:T(8,128)(2,1)S(1)} %copy-done.2), channel_id=1, source_target_pairs={{0,8},{1,9},{2,10},{3,11},{4,12},{5,13},{6,14},{7,15},{8,0},{9,1},... | collective-permute-start | bytes 2359304 | tf_op jit(solution)/shard_map/ppermute | solution.py:53
  32.9 4.6 %collective-permute-start = (bf16[128,3072]{1,0:T(8,128)(2,1)S(1)}, bf16[128,3072]{1,0:T(8,128)(2,1)S(1)}, u32[]{:S(2)}, u32[]{:S(2)}) collective-permute-start(bf16[128,3072]{1,0:T(8,128)(2,1)S(1)} %copy-done.1), channel_id=1, source_target_pairs={{0,8},{1,9},{2,10},{3,11},{4,12},{5,13},{6,14},{7,15},{8,0},{9,1},... | collective-permute-start | bytes 2359304 | tf_op jit(solution)/shard_map/ppermute | solution.py:53
  43.6 12.5 %collective-permute-start.7 = (bf16[48,3072]{1,0:T(8,128)(2,1)S(1)}, bf16[48,3072]{1,0:T(8,128)(2,1)S(1)}, u32[]{:S(2)}, u32[]{:S(2)}) collective-permute-start(bf16[48,3072]{1,0:T(8,128)(2,1)S(1)} %get-tuple-element.55), channel_id=1, source_target_pairs={{0,224},{1,225},{2,226},{3,227},{4,228},{5,229},{6,230},{7,231},{8... | collective-permute-start | bytes 884744 | tf_op jit(solution)/shard_map/ppermute | solution.py:53
  49.5 10.4 %collective-permute-start.6 = (bf16[48,3072]{1,0:T(8,128)(2,1)S(1)}, bf16[48,3072]{1,0:T(8,128)(2,1)S(1)}, u32[]{:S(2)}, u32[]{:S(2)}) collective-permute-start(bf16[48,3072]{1,0:T(8,128)(2,1)S(1)} %get-tuple-element.53), channel_id=1, source_target_pairs={{0,32},{1,33},{2,34},{3,35},{4,36},{5,37},{6,38},{7,39},{8,40},{9,... | collective-permute-start | bytes 884744 | tf_op jit(solution)/shard_map/ppermute | solution.py:53
  56.2 15.8 %collective-permute-start.11 = (bf16[96,3072]{1,0:T(8,128)(2,1)S(1)}, bf16[96,3072]{1,0:T(8,128)(2,1)S(1)}, u32[]{:S(2)}, u32[]{:S(2)}) collective-permute-start(bf16[96,3072]{1,0:T(8,128)(2,1)S(1)} %hop.8), channel_id=1, source_target_pairs={{0,224},{1,225},{2,226},{3,227},{4,228},{5,229},{6,230},{7,231},{8... | collective-permute-start | bytes 1769480 | tf_op jit(solution)/shard_map/ppermute | solution.py:53
  60.0 15.9 %collective-permute-start.10 = (bf16[96,3072]{1,0:T(8,128)(2,1)S(1)}, bf16[96,3072]{1,0:T(8,128)(2,1)S(1)}, u32[]{:S(2)}, u32[]{:S(2)}) collective-permute-start(bf16[96,3072]{1,0:T(8,128)(2,1)S(1)} %hop.7), channel_id=1, source_target_pairs={{0,32},{1,33},{2,34},{3,35},{4,36},{5,37},{6,38},{7,39},{8,40},{9,... | collective-permute-start | bytes 1769480 | tf_op jit(solution)/shard_map/ppermute | solution.py:53
  60.1 16.2 %collective-permute-start.8 = (bf16[384,768]{1,0:T(8,128)(2,1)S(1)}, bf16[384,768]{1,0:T(8,128)(2,1)S(1)}, u32[]{:S(2)}, u32[]{:S(2)}) collective-permute-start(bf16[384,768]{1,0:T(8,128)(2,1)S(1)} %slice.20), channel_id=1, source_target_pairs={{0,1},{1,2},{2,3},{3,0},{4,5},{5,6},{6,7},{7,4},{8,9},{9,10},{10,1... | collective-permute-start | bytes 1769480 | tf_op jit(solution)/shard_map/ppermute | solution.py:53
  61.8 14.6 %collective-permute-start.9 = (bf16[384,768]{1,0:T(8,128)(2,1)S(1)}, bf16[384,768]{1,0:T(8,128)(2,1)S(1)}, u32[]{:S(2)}, u32[]{:S(2)}) collective-permute-start(bf16[384,768]{1,0:T(8,128)(2,1)S(1)} %slice.21), channel_id=1, source_target_pairs={{0,3},{1,0},{2,1},{3,2},{4,7},{5,4},{6,5},{7,6},{8,11},{9,8},{10,9... | collective-permute-start | bytes 1769480 | tf_op jit(solution)/shard_map/ppermute | solution.py:53
  72.1 14.9 %collective-permute-start.16 = (bf16[96,3072]{1,0:T(8,128)(2,1)S(1)}, bf16[96,3072]{1,0:T(8,128)(2,1)S(1)}, u32[]{:S(2)}, u32[]{:S(2)}) collective-permute-start(bf16[96,3072]{1,0:T(8,128)(2,1)S(1)} %hop.10), channel_id=1, source_target_pairs={{0,224},{1,225},{2,226},{3,227},{4,228},{5,229},{6,230},{7,231},{8... | collective-permute-start | bytes 1769480 | tf_op jit(solution)/shard_map/ppermute | solution.py:53
  76.1 14.9 %collective-permute-start.14 = (bf16[96,3072]{1,0:T(8,128)(2,1)S(1)}, bf16[96,3072]{1,0:T(8,128)(2,1)S(1)}, u32[]{:S(2)}, u32[]{:S(2)}) collective-permute-start(bf16[96,3072]{1,0:T(8,128)(2,1)S(1)} %hop.9), channel_id=1, source_target_pairs={{0,32},{1,33},{2,34},{3,35},{4,36},{5,37},{6,38},{7,39},{8,40},{9,... | collective-permute-start | bytes 1769480 | tf_op jit(solution)/shard_map/ppermute | solution.py:53
  81.2 18.8 %collective-permute-start.12 = (bf16[256,1536]{1,0:T(8,128)(2,1)S(1)}, bf16[256,1536]{1,0:T(8,128)(2,1)S(1)}, u32[]{:S(2)}, u32[]{:S(2)}) collective-permute-start(bf16[256,1536]{1,0:T(8,128)(2,1)S(1)} %get-tuple-element.67), channel_id=1, source_target_pairs={{0,20},{1,21},{2,22},{3,23},{4,16},{5,17},{6,18},{7,19},{8,28},{9,... | collective-permute-start | bytes 2359304 | tf_op jit(solution)/shard_map/ppermute | solution.py:53
  87.2 14.2 %collective-permute-start.17 = (bf16[96,3072]{1,0:T(8,128)(2,1)S(1)}, bf16[96,3072]{1,0:T(8,128)(2,1)}, u32[]{:S(2)}, u32[]{:S(2)}) collective-permute-start(bf16[96,3072]{1,0:T(8,128)(2,1)S(1)} %hop.12), channel_id=1, source_target_pairs={{0,224},{1,225},{2,226},{3,227},{4,228},{5,229},{6,230},{7,231},{8... | collective-permute-start | bytes 1769480 | tf_op jit(solution)/shard_map/ppermute | solution.py:53
  91.1 13.8 %collective-permute-start.15 = (bf16[96,3072]{1,0:T(8,128)(2,1)S(1)}, bf16[96,3072]{1,0:T(8,128)(2,1)}, u32[]{:S(2)}, u32[]{:S(2)}) collective-permute-start(bf16[96,3072]{1,0:T(8,128)(2,1)S(1)} %hop.11), channel_id=1, source_target_pairs={{0,32},{1,33},{2,34},{3,35},{4,36},{5,37},{6,38},{7,39},{8,40},{9,... | collective-permute-start | bytes 1769480 | tf_op jit(solution)/shard_map/ppermute | solution.py:53
  97.0 11.5 %collective-permute-start.18 = (bf16[256,1536]{1,0:T(8,128)(2,1)}, bf16[256,1536]{1,0:T(8,128)(2,1)}, u32[]{:S(2)}, u32[]{:S(2)}) collective-permute-start(bf16[256,1536]{1,0:T(8,128)(2,1)} %get-tuple-element.82), channel_id=1, source_target_pairs={{0,8},{1,9},{2,10},{3,11},{4,12},{5,13},{6,14},{7,15},{8,0},{9,1},... | collective-permute-start | bytes 2359304 | tf_op jit(solution)/shard_map/ppermute | solution.py:53
  101.3 5.0 %collective-permute-start.13 = (bf16[128,1536]{1,0:T(8,128)(2,1)}, bf16[128,1536]{1,0:T(8,128)(2,1)}, u32[]{:S(2)}, u32[]{:S(2)}) collective-permute-start(bf16[128,1536]{1,0:T(8,128)(2,1)} %get-tuple-element.88), channel_id=1, source_target_pairs={{0,8},{1,9},{2,10},{3,11},{4,12},{5,13},{6,14},{7,15},{8,0},{9,1},... | collective-permute-start | bytes 1179656 | tf_op jit(solution)/shard_map/ppermute | solution.py:53
  101.3 5.0 %copy-start.4 = (bf16[128,1536]{1,0:T(8,128)(2,1)S(1)}, bf16[128,1536]{1,0:T(8,128)(2,1)}, u32[]{:S(2)}) copy-start(bf16[128,1536]{1,0:T(8,128)(2,1)} %get-tuple-element.87) | copy-start | bytes 1179652
  109.9 6.8 %collective-permute-start.19 = (bf16[24,3072]{1,0:T(8,128)(2,1)S(1)}, bf16[24,3072]{1,0:T(8,128)(2,1)S(1)}, u32[]{:S(2)}, u32[]{:S(2)}) collective-permute-start(bf16[24,3072]{1,0:T(8,128)(2,1)S(1)} %get-tuple-element.89), channel_id=1, source_target_pairs={{0,1},{1,2},{2,3},{3,0},{4,5},{5,6},{6,7},{7,4},{8,9},{9,10},{10,1... | collective-permute-start | bytes 442376 | tf_op jit(solution)/shard_map/ppermute | solution.py:53
  111.5 7.4 %collective-permute-start.20 = (bf16[24,3072]{1,0:T(8,128)(2,1)S(1)}, bf16[24,3072]{1,0:T(8,128)(2,1)S(1)}, u32[]{:S(2)}, u32[]{:S(2)}) collective-permute-start(bf16[24,3072]{1,0:T(8,128)(2,1)S(1)} %get-tuple-element.91), channel_id=1, source_target_pairs={{0,2},{1,3},{2,0},{3,1},{4,6},{5,7},{6,4},{7,5},{8,10},{9,11},{10,... | collective-permute-start | bytes 442376 | tf_op jit(solution)/shard_map/ppermute | solution.py:53
  114.2 5.1 %collective-permute-start.21 = (bf16[24,3072]{1,0:T(8,128)(2,1)S(1)}, bf16[24,3072]{1,0:T(8,128)(2,1)S(1)}, u32[]{:S(2)}, u32[]{:S(2)}) collective-permute-start(bf16[24,3072]{1,0:T(8,128)(2,1)S(1)} %get-tuple-element.90), channel_id=1, source_target_pairs={{0,3},{1,0},{2,1},{3,2},{4,7},{5,4},{6,5},{7,6},{8,11},{9,8},{10,9... | collective-permute-start | bytes 442376 | tf_op jit(solution)/shard_map/ppermute | solution.py:53
  115.7 20.4 %collective-permute-start.24 = (bf16[128,1536]{1,0:T(8,128)(2,1)S(1)}, bf16[128,1536]{1,0:T(8,128)(2,1)S(1)}, u32[]{:S(2)}, u32[]{:S(2)}) collective-permute-start(bf16[128,1536]{1,0:T(8,128)(2,1)S(1)} %get-tuple-element.93), channel_id=1, source_target_pairs={{0,20},{1,21},{2,22},{3,23},{4,16},{5,17},{6,18},{7,19},{8,28},{9,... | collective-permute-start | bytes 1179656 | tf_op jit(solution)/shard_map/ppermute | solution.py:53
  119.5 14.3 %collective-permute-start.22 = (bf16[12,3072]{1,0:T(8,128)(2,1)S(1)}, bf16[12,3072]{1,0:T(8,128)(2,1)S(1)}, u32[]{:S(2)}, u32[]{:S(2)}) collective-permute-start(bf16[12,3072]{1,0:T(8,128)(2,1)S(1)} %get-tuple-element.95), channel_id=1, source_target_pairs={{0,24},{1,26},{2,28},{3,30},{4,184},{5,186},{6,188},{7,190},{8,72}... | collective-permute-start | bytes 221192 | tf_op jit(solution)/shard_map/ppermute | solution.py:53
  121.4 14.7 %collective-permute-start.23 = (bf16[12,3072]{1,0:T(8,128)(2,1)S(1)}, bf16[12,3072]{1,0:T(8,128)(2,1)S(1)}, u32[]{:S(2)}, u32[]{:S(2)}) collective-permute-start(bf16[12,3072]{1,0:T(8,128)(2,1)S(1)} %get-tuple-element.94), channel_id=1, source_target_pairs={{0,25},{1,27},{2,29},{3,31},{4,185},{5,187},{6,189},{7,191},{8,73}... | collective-permute-start | bytes 221192 | tf_op jit(solution)/shard_map/ppermute | solution.py:53

commit v6 on v5

--- a/solution.py
+++ b/solution.py
@@ -35,11 +35,12 @@
 
 def owner(z, yl, c, yh, x, message):
     chunk = window(z, c, yh)
-    return 4 * yh + 2 * c + chunk // 4, chunk % 4 // 2, chunk % 2, x // 2, x % 2 * 2 + (yl ^ message)
+    return 4 * yh + 2 * c + chunk // 4, chunk % 4 // 2, chunk % 2, yl ^ message, x
 
 
 X_UP = table(lambda z, yl, c, yh, x: (z, yl, c, yh, x + 1))
 X_DOWN = table(lambda z, yl, c, yh, x: (z, yl, c, yh, x - 1))
+X_STEPS = [table(lambda z, yl, c, yh, x: (z, yl, c, yh, x + dx)) for dx in (1, 2, 3)]
 Z_UP = table(lambda z, yl, c, yh, x: (z + 1, yl, c, yh, x))
 Z_DOWN = table(lambda z, yl, c, yh, x: (z - 1, yl, c, yh, x))
 CORE = table(lambda z, yl, c, yh, x: (z, yl, c + 1, yh, x))
@@ -224,6 +225,64 @@
     )(*arrived, part)
 
 
+def last_hop_kernel(where, up, down, part, own, *refs):
+    *pieces, total = refs
+    size = own.shape[0]
+    for x in range(4):
+        for yh in range(2):
+            here = slice((yh * 4 + x) * (size // 2), (yh * 4 + x + 1) * (size // 2))
+            there = slice((x * 2 + yh) * (size // 2), (x * 2 + yh + 1) * (size // 2))
+            total[there] = f32(part[here]) + f32(up[here]) + f32(down[here])
+    for dx, ref in enumerate((own, *pieces)):
+        start = pl.multiple_of((where[2] + dx) % 4 * size, 8)
+        ref[...] = total[pl.ds(start, size)].astype(ref.dtype)
+
+
+def last_hop(where, part, up, down):
+    size, outputs = part.shape
+    width = outputs // 2
+    kinds = (jnp.float32, *[jnp.bfloat16] * 3)
+    return call(
+        last_hop_kernel,
+        "last_hop",
+        8,
+        where,
+        (2,),
+        [pl.BlockSpec((size, width), lambda i, where: (0, i))] * 3,
+        [pl.BlockSpec((size // 4, width), lambda i, where: (0, i)) for _ in kinds],
+        [jax.ShapeDtypeStruct((size // 4, outputs), kind) for kind in kinds],
+        [pltpu.VMEM((size, width), jnp.float32)],
+        2 * part.size,
+        (up, down, part),
+    )
+
+
+def sum_kernel(where, own, one, two, three, same, other, total, *, factor):
+    size = same.shape[0]
+    total[...] = (own[...] + f32(one[...]) + f32(two[...]) + f32(three[...])) * factor
+    first, second = bf16(total[:size]), bf16(total[size:])
+    yl = where[4]
+    same[...] = jnp.where(yl == 0, first, second)
+    other[...] = jnp.where(yl == 0, second, first)
+
+
+def sum_over_x(where, factor, own, *arrived):
+    size, outputs = own.shape
+    return call(
+        functools.partial(sum_kernel, factor=factor),
+        "sum_over_x",
+        8,
+        where,
+        (1,),
+        [fixed(own.shape)] * 4,
+        [fixed((size // 2, outputs))] * 2,
+        [jax.ShapeDtypeStruct((size // 2, outputs), jnp.bfloat16)] * 2,
+        [pltpu.VMEM((size, outputs), jnp.float32)],
+        4 * own.size,
+        (own, *arrived),
+    )
+
+
 def forward_kernel(where, own, sib, pair, psib, w0, w1, w2, w3, w4, mine, other, away, lhs):
     yh, x = where[1], where[2]
     count, shard = own.shape[0], w0.shape[0]
@@ -314,28 +373,15 @@
     )
 
 
-def rows(value, start, size):
-    return lax.dynamic_slice_in_dim(value, start, size, 0)
-
-
 def joined(here, there, flag):
     return jnp.where(
         flag == 0, jnp.concatenate([here, there], axis=1), jnp.concatenate([there, here], axis=1)
     )
 
 
-def reduce_over_x(part, x):
-    size = part.shape[0] // 4
-    total = rows(part, x * size, size)
-    for dx in range(1, 4):
-        to = table(lambda z, yl, c, yh, x: (z, yl, c, yh, x + dx))
-        total = total + f32(send(bf16(rows(part, (x + dx) % 4 * size, size)), to))
-    return total
-
-
 def on_device(tokens, cotangent, levels, scales):
     z, yl, c, yh, x = (lax.axis_index(name) for name in AXES)
-    where = jnp.stack([c, yh, x, window(z, c, yh)]).astype(jnp.int32)
+    where = jnp.stack([c, yh, x, window(z, c, yh), yl]).astype(jnp.int32)
     count = tokens.shape[0]
     factor = float(count * 256) ** -0.5
 
@@ -369,19 +415,21 @@
     part, give = backward_parts(where, cot_parts, after(blocks, up, down))
     up, down = send(up, Z_UP), send(down, Z_DOWN)
     give = send(give, CORE)
-    grad = after(grad, part)
-    total = hop(grad[6], up, down, kind=jnp.float32)
-
+    own_piece, *pieces = last_hop(where, after(grad[6], part), up, down)
+    arrived = [send(piece, to) for piece, to in zip(pieces, X_STEPS)]
+    back = after(back, own_piece)
+    here = bf16(mine + back[:count])
+    there = send(bf16(other + back[count:]), CORE)
+    part, give = after((part, give), own_piece)
     part = part + f32(give)
-    grad_input = joined(bf16(part[:count]), send(bf16(part[count:]), PAIR), yh)
-    there = send(bf16(other + back[count:]), CORE)
-    forward = joined(bf16(mine + back[:count]), there, c)
-
-    total = bf16(reduce_over_x(after(total, forward, part), x) * factor)
-    size = total.shape[0] // 2
-    got = [f32(send(rows(total, (yl ^ m) * size, size), OWNERS[m])) for m in range(2)]
-    got, grad_input = after((got, grad_input))
-    return forward, grad_input, got[0] + got[1]
+    grad_here, grad_away = bf16(part[:count]), bf16(part[count:])
+    grad_there = send(grad_away, PAIR)
+    same, swapped = sum_over_x(where, factor, own_piece, *after(arrived, grad_away))
+    got = send(same, OWNERS[0]), send(swapped, OWNERS[1])
+    forward = joined(after(here, same), there, c)
+    grad_input = joined(after(grad_here, same), grad_there, yh)
+    one, two = after(got, forward, grad_input)
+    return forward, grad_input, f32(one) + f32(two)
 
 
 def solution(mesh):

time: 140 us -> 131 us (0.936); the launches traced: 138 us -> 131 us
  waiting for transfers between devices: 67.2 us -> 63.8 us
  other arithmetic: 6.73 us -> 3.46 us
    ppermute x25, waiting for transfers between devices: 67.2 us -> 63.8 us  [send(): return lax.ppermute(value, AXES, pairs)]
    pallas_call x7 -> x6, Pallas kernels: 2.17 us -> 0.7 us  [hop(): pl.pallas_call(kernel, name='hop', out_shape=jax.ShapeDtypeStruct(part.sh...]
    pallas_call x4 -> x6, Pallas kernels: 18.3 us -> 19.3 us  [call(): pl.pallas_call(kernel, name=name, grid_spec=pltpu.PrefetchScalarGridSpec(...]
  transfers between devices with their start and end apart: 25 -> 25, of which waited for: 14 -> 15; matrix products, arithmetic and copies ran while one was open for 3% -> 2% of each run, Pallas kernels for 10% -> 11%
where the time goes in v6:
time: 131 us
  waiting for transfers between devices  63.8 us (49%)
  starting transfers between devices  40.2 us (31%)
  Pallas kernels  22.4 us (17%)
  other arithmetic  3.46 us (3%)
    ppermute x25, waiting for transfers between devices, send(): return lax.ppermute(value, AXES, pairs)  63.8 us
    ppermute x25, starting transfers between devices, send(): return lax.ppermute(value, AXES, pairs)  40.2 us
    pallas_call x6, Pallas kernels, call(): pl.pallas_call(kernel, name=name, grid_spec=pltpu.PrefetchScalarGridSpec(...  19.3 us
  transfers between devices with their start and end apart: 25, of which 15 were waited for; matrix products, arithmetic and copies ran while one was open for 2% of the time, Pallas kernels for 11%

profile of v6, /device:TPU:24, one launch (start us, length us, event | category | flops | bytes accessed | tf_op | source)
XLA Modules:
  0.0 131.0 jit_solution(13293819179292834369)
XLA Ops:
  0.7 2.5 %pack.1 = bf16[128,4608]{1,0:T(8,128)(2,1)} custom-call(bf16[128,3072]{1,0:T(8,128)(2,1)} %own.3, bf16[128,3072]{1,0:T(8,128)(2,1)} %cot0.2), custom_call_target="tpu_custom_call" | custom-call | tf_op jit(solution)/shard_map/pack/pallas_call | solution.py:138
  3.1 2.0 %collective-permute-start.1 = (bf16[128,4608]{1,0:T(8,128)(2,1)}, bf16[128,4608]{1,0:T(8,128)(2,1)}, u32[]{:S(2)}, u32[]{:S(2)}) collective-permute-start(bf16[128,4608]{1,0:T(8,128)(2,1)} %pack.1), channel_id=1, source_target_pairs={{0,20},{1,21},{2,22},{3,23},{4,16},{5,17},{6,18},{7,19},{8,28},{9,... | collective-permute-start | bytes 3538952 | tf_op jit(solution)/shard_map/ppermute | solution.py:54
  5.2 0.1 stack.23.where
  5.3 0.0 copy-start.1
  5.3 1.6 %dequantize.1.w0 = bf16[384,1536]{1,0:T(8,128)(2,1)S(1)} custom-call(s32[5]{0:T(128)S(1)} %stack.23.where, bf16[384,3072]{1,0:T(8,128)(2,1)S(1)} %copy-done, f32[12,384]{1,0:T(8,128)S(1)} %bitcast.6), custom_call_target="tpu_custom_call" | custom-call | flops 589824 | bytes 3557376 | tf_op jit(solution)/shard_map/dequantize/pallas_call | solution.py:72
  6.9 1.1 collective-permute-start.4
  8.0 1.0 collective-permute-start.3
  9.0 23.5 %collective-permute-done.1.pair.cot2 = bf16[128,4608]{1,0:T(8,128)(2,1)} collective-permute-done((bf16[128,4608]{1,0:T(8,128)(2,1)}, bf16[128,4608]{1,0:T(8,128)(2,1)}, u32[]{:S(2)}, u32[]{:S(2)}) %collective-permute-start.1) | collective-permute-done | bytes 1179680 | tf_op jit(solution)/shard_map/ppermute | solution.py:54
  32.4 0.0 collective-permute-start.2
  32.4 0.5 collective-permute-start.5
  33.0 0.1 collective-permute-start
  33.0 3.0 %collective-permute-done.5.cot1 = bf16[128,3072]{1,0:T(8,128)(2,1)S(1)} collective-permute-done((bf16[128,3072]{1,0:T(8,128)(2,1)S(1)}, bf16[128,3072]{1,0:T(8,128)(2,1)S(1)}, u32[]{:S(2)}, u32[]{:S(2)}) %collective-permute-start.5) | collective-permute-done | bytes 786464 | tf_op jit(solution)/shard_map/ppermute | solution.py:54
  36.0 0.0 collective-permute-done.4.w2
  36.0 0.4 collective-permute-done.3.w1
  36.4 0.7 collective-permute-done.2.psib.cot3
  37.1 0.4 collective-permute-done.sib
  37.5 6.0 %gradient.1 = (bf16[48,3072]{1,0:T(8,128)(2,1)S(1)}, bf16[48,3072]{1,0:T(8,128)(2,1)S(1)}, bf16[96,3072]{1,0:T(8,128)(2,1)S(1)}, bf16[96,3072]{1,0:T(8,128)(2,1)...) custom-call(s32[5]{0:T(128)S(1)} %stack.23.where, ...), custom_call_target="tpu_custom_call" | custom-call | flops 2415919104 | bytes 12582912 | tf_op jit(solution)/shard_map/gradient/pallas_call | solution.py:72
  43.6 5.9 %collective-permute-start.7 = (bf16[48,3072]{1,0:T(8,128)(2,1)S(1)}, bf16[48,3072]{1,0:T(8,128)(2,1)S(1)}, u32[]{:S(2)}, u32[]{:S(2)}) collective-permute-start(bf16[48,3072]{1,0:T(8,128)(2,1)S(1)} %get-tuple-element.67), channel_id=1, source_target_pairs={{0,224},{1,225},{2,226},{3,227},{4,228},{5,229},{6,230},{7,231},{8... | collective-permute-start | bytes 884744 | tf_op jit(solution)/shard_map/ppermute | solution.py:54
  49.5 6.6 %collective-permute-done.7.arrived = bf16[48,3072]{1,0:T(8,128)(2,1)S(1)} collective-permute-done((bf16[48,3072]{1,0:T(8,128)(2,1)S(1)}, bf16[48,3072]{1,0:T(8,128)(2,1)S(1)}, u32[]{:S(2)}, u32[]{:S(2)}) %collective-permute-start.7) | collective-permute-done | bytes 294944 | tf_op jit(solution)/shard_map/ppermute | solution.py:54
  56.1 0.1 hop.7
  56.2 3.8 %collective-permute-start.11 = (bf16[96,3072]{1,0:T(8,128)(2,1)S(1)}, bf16[96,3072]{1,0:T(8,128)(2,1)S(1)}, u32[]{:S(2)}, u32[]{:S(2)}) collective-permute-start(bf16[96,3072]{1,0:T(8,128)(2,1)S(1)} %hop.7), channel_id=1, source_target_pairs={{0,224},{1,225},{2,226},{3,227},{4,228},{5,229},{6,230},{7,231},{8... | collective-permute-start | bytes 1769480 | tf_op jit(solution)/shard_map/ppermute | solution.py:54
  59.9 0.0 collective-permute-done.6.arrived
  59.9 0.1 hop.6
  60.0 0.1 collective-permute-start.10
  60.2 2.8 %collective-permute-start.9 = (bf16[384,768]{1,0:T(8,128)(2,1)S(1)}, bf16[384,768]{1,0:T(8,128)(2,1)S(1)}, u32[]{:S(2)}, u32[]{:S(2)}) collective-permute-start(bf16[384,768]{1,0:T(8,128)(2,1)S(1)} %slice.21), channel_id=1, source_target_pairs={{0,3},{1,0},{2,1},{3,2},{4,7},{5,4},{6,5},{7,6},{8,11},{9,8},{10,9... | collective-permute-start | bytes 1769480 | tf_op jit(solution)/shard_map/ppermute | solution.py:54
  63.0 8.9 %collective-permute-done.11.refs_0_ = bf16[96,3072]{1,0:T(8,128)(2,1)S(1)} collective-permute-done((bf16[96,3072]{1,0:T(8,128)(2,1)S(1)}, bf16[96,3072]{1,0:T(8,128)(2,1)S(1)}, u32[]{:S(2)}, u32[]{:S(2)}) %collective-permute-start.11) | collective-permute-done | bytes 589856 | tf_op jit(solution)/shard_map/ppermute | solution.py:54
  72.0 0.1 hop.9
  72.1 3.8 %collective-permute-start.15 = (bf16[96,3072]{1,0:T(8,128)(2,1)S(1)}, bf16[96,3072]{1,0:T(8,128)(2,1)S(1)}, u32[]{:S(2)}, u32[]{:S(2)}) collective-permute-start(bf16[96,3072]{1,0:T(8,128)(2,1)S(1)} %hop.9), channel_id=1, source_target_pairs={{0,224},{1,225},{2,226},{3,227},{4,228},{5,229},{6,230},{7,231},{8... | collective-permute-start | bytes 1769480 | tf_op jit(solution)/shard_map/ppermute | solution.py:54
  75.9 0.0 collective-permute-done.10.refs_0_
  75.9 0.1 hop.8
  76.0 0.3 collective-permute-start.13
  76.3 1.9 %collective-permute-done.8.w3 = bf16[384,768]{1,0:T(8,128)(2,1)S(1)} collective-permute-done((bf16[384,768]{1,0:T(8,128)(2,1)S(1)}, bf16[384,768]{1,0:T(8,128)(2,1)S(1)}, u32[]{:S(2)}, u32[]{:S(2)}) %collective-permute-start.8) | collective-permute-done | bytes 589856 | tf_op jit(solution)/shard_map/ppermute | solution.py:54
  78.2 4.8 %forward.1 = (f32[128,1536]{1,0:T(8,128)S(1)}, f32[128,1536]{1,0:T(8,128)S(1)}, bf16[256,1536]{1,0:T(8,128)(2,1)S(1)}) custom-call(s32[5]{0:T(128)S(1)} %stack.23.where, bf16[128,3072]{1,0:T(8,128)(2,1)S(1)} %copy-done.1, bf16[128,3072]{1,0:T(8,128)(2,1)S(1)} %collective-permute-done.sib, bf16[128,4608]{1,0:T(8,128)(2,1)} %collective-permute-done.1.pair.cot2, ...), custom_call_target="tpu_custom_call" | custom-call | flops 2415919104 | bytes 11010048 | tf_op jit(solution)/shard_map/forward/pallas_call | solution.py:72
  83.1 0.4 collective-permute-start.12
  83.4 3.6 %collective-permute-done.15.refs_0_ = bf16[96,3072]{1,0:T(8,128)(2,1)S(1)} collective-permute-done((bf16[96,3072]{1,0:T(8,128)(2,1)S(1)}, bf16[96,3072]{1,0:T(8,128)(2,1)S(1)}, u32[]{:S(2)}, u32[]{:S(2)}) %collective-permute-start.15) | collective-permute-done | bytes 589856 | tf_op jit(solution)/shard_map/ppermute | solution.py:54
  87.0 0.1 hop.11
  87.2 3.8 %collective-permute-start.16 = (bf16[96,3072]{1,0:T(8,128)(2,1)S(1)}, bf16[96,3072]{1,0:T(8,128)(2,1)S(1)}, u32[]{:S(2)}, u32[]{:S(2)}) collective-permute-start(bf16[96,3072]{1,0:T(8,128)(2,1)S(1)} %hop.11), channel_id=1, source_target_pairs={{0,224},{1,225},{2,226},{3,227},{4,228},{5,229},{6,230},{7,231},{8... | collective-permute-start | bytes 1769480 | tf_op jit(solution)/shard_map/ppermute | solution.py:54
  90.9 0.1 hop.10
  91.1 0.1 collective-permute-start.14
  91.2 5.0 %backward.1 = (f32[256,1536]{1,0:T(8,128)S(1)}, bf16[256,1536]{1,0:T(8,128)(2,1)S(1)}) custom-call(s32[5]{0:T(128)S(1)} %stack.23.where, bf16[128,3072]{1,0:T(8,128)(2,1)S(1)} %copy-done.2, bf16[128,3072]{1,0:T(8,128)(2,1)S(1)} %collective-permute-done.5.cot1, bf16[128,4608]{1,0:T(8,128)(2,1)} %collective-permute-done.1.pair.cot2, ...), custom_call_target="tpu_custom_call" | custom-call | flops 2415919104 | bytes 11010048 | tf_op jit(solution)/shard_map/backward/pallas_call | solution.py:72
  96.2 0.1 collective-permute-start.20
  96.3 5.4 %collective-permute-done.12 = bf16[256,1536]{1,0:T(8,128)(2,1)S(1)} collective-permute-done((bf16[256,1536]{1,0:T(8,128)(2,1)S(1)}, bf16[256,1536]{1,0:T(8,128)(2,1)S(1)}, u32[]{:S(2)}, u32[]{:S(2)}) %collective-permute-start.12) | collective-permute-done | bytes 786464 | tf_op jit(solution)/shard_map/ppermute | solution.py:54
  101.6 0.2 convert_element_type.20
  101.8 0.0 collective-permute-done.16.down
  101.8 2.9 %collective-permute-done.14.up = bf16[96,3072]{1,0:T(8,128)(2,1)S(1)} collective-permute-done((bf16[96,3072]{1,0:T(8,128)(2,1)S(1)}, bf16[96,3072]{1,0:T(8,128)(2,1)S(1)}, u32[]{:S(2)}, u32[]{:S(2)}) %collective-permute-start.14) | collective-permute-done | bytes 589856 | tf_op jit(solution)/shard_map/ppermute | solution.py:54
  104.8 1.2 last_hop.1
  105.9 1.6 %collective-permute-start.17 = (bf16[24,3072]{1,0:T(8,128)(2,1)S(1)}, bf16[24,3072]{1,0:T(8,128)(2,1)S(1)}, u32[]{:S(2)}, u32[]{:S(2)}) collective-permute-start(bf16[24,3072]{1,0:T(8,128)(2,1)S(1)} %get-tuple-element.95), channel_id=1, source_target_pairs={{0,1},{1,2},{2,3},{3,0},{4,5},{5,6},{6,7},{7,4},{8,9},{9,10},{10,1... | collective-permute-start | bytes 442376 | tf_op jit(solution)/shard_map/ppermute | solution.py:54
  107.5 2.7 %collective-permute-start.18 = (bf16[24,3072]{1,0:T(8,128)(2,1)S(1)}, bf16[24,3072]{1,0:T(8,128)(2,1)S(1)}, u32[]{:S(2)}, u32[]{:S(2)}) collective-permute-start(bf16[24,3072]{1,0:T(8,128)(2,1)S(1)} %get-tuple-element.96), channel_id=1, source_target_pairs={{0,2},{1,3},{2,0},{3,1},{4,6},{5,7},{6,4},{7,5},{8,10},{9,11},{10,... | collective-permute-start | bytes 442376 | tf_op jit(solution)/shard_map/ppermute | solution.py:54
  110.2 1.5 %collective-permute-start.19 = (bf16[24,3072]{1,0:T(8,128)(2,1)S(1)}, bf16[24,3072]{1,0:T(8,128)(2,1)S(1)}, u32[]{:S(2)}, u32[]{:S(2)}) collective-permute-start(bf16[24,3072]{1,0:T(8,128)(2,1)S(1)} %get-tuple-element.97), channel_id=1, source_target_pairs={{0,3},{1,0},{2,1},{3,2},{4,7},{5,4},{6,5},{7,6},{8,11},{9,8},{10,9... | collective-permute-start | bytes 442376 | tf_op jit(solution)/shard_map/ppermute | solution.py:54
  111.7 0.3 add_convert_fusion.2
  112.0 0.1 collective-permute-start.21
  112.1 0.2 add_convert_fusion
  112.3 0.1 fusion
  112.3 0.4 collective-permute-start.22
  112.7 2.2 %collective-permute-done.18.two = bf16[24,3072]{1,0:T(8,128)(2,1)S(1)} collective-permute-done((bf16[24,3072]{1,0:T(8,128)(2,1)S(1)}, bf16[24,3072]{1,0:T(8,128)(2,1)S(1)}, u32[]{:S(2)}, u32[]{:S(2)}) %collective-permute-start.18) | collective-permute-done | bytes 147488 | tf_op jit(solution)/shard_map/ppermute | solution.py:54
  114.9 0.4 collective-permute-done.19.three
  115.4 0.7 sum_over_x.1
  116.1 1.9 %collective-permute-start.23 = (bf16[12,3072]{1,0:T(8,128)(2,1)S(1)}, bf16[12,3072]{1,0:T(8,128)(2,1)S(1)}, u32[]{:S(2)}, u32[]{:S(2)}) collective-permute-start(bf16[12,3072]{1,0:T(8,128)(2,1)S(1)} %get-tuple-element.104), channel_id=1, source_target_pairs={{0,24},{1,25},{2,26},{3,27},{4,184},{5,185},{6,186},{7,187},{8,72}... | collective-permute-start | bytes 221192 | tf_op jit(solution)/shard_map/ppermute | solution.py:54
  118.0 6.3 %collective-permute-start.24 = (bf16[12,3072]{1,0:T(8,128)(2,1)S(1)}, bf16[12,3072]{1,0:T(8,128)(2,1)S(1)}, u32[]{:S(2)}, u32[]{:S(2)}) collective-permute-start(bf16[12,3072]{1,0:T(8,128)(2,1)S(1)} %get-tuple-element.108), channel_id=1, source_target_pairs={{0,28},{1,29},{2,30},{3,31},{4,188},{5,189},{6,190},{7,191},{8,76}... | collective-permute-start | bytes 221192 | tf_op jit(solution)/shard_map/ppermute | solution.py:54
  124.3 1.1 maximum_select_fusion
  125.4 0.8 collective-permute-done.22
  126.2 1.1 maximum_select_fusion.1
  127.3 3.0 %collective-permute-done.24 = bf16[12,3072]{1,0:T(8,128)(2,1)S(1)} collective-permute-done((bf16[12,3072]{1,0:T(8,128)(2,1)S(1)}, bf16[12,3072]{1,0:T(8,128)(2,1)S(1)}, u32[]{:S(2)}, u32[]{:S(2)}) %collective-permute-start.24) | collective-permute-done | bytes 73760 | tf_op jit(solution)/shard_map/ppermute | solution.py:54
  130.3 0.7 convert_add_fusion
  (17 shorter events, 0.1 us)
Async XLA Ops:
  0.6 4.6 %copy-start.3 = (f32[384,12]{0,1:T(8,128)S(1)}, f32[384,12]{0,1:T(8,128)}, u32[]{:S(2)}) copy-start(f32[384,12]{0,1:T(8,128)} %param.7) | copy-start | bytes 55300
  0.6 4.6 %copy-start = (bf16[384,3072]{1,0:T(8,128)(2,1)S(1)}, bf16[384,3072]{1,0:T(8,128)(2,1)}, u32[]{:S(2)}) copy-start(bf16[384,3072]{1,0:T(8,128)(2,1)} %levels) | copy-start | bytes 7077892
  3.1 29.3 %collective-permute-start.1 = (bf16[128,4608]{1,0:T(8,128)(2,1)}, bf16[128,4608]{1,0:T(8,128)(2,1)}, u32[]{:S(2)}, u32[]{:S(2)}) collective-permute-start(bf16[128,4608]{1,0:T(8,128)(2,1)} %pack.1), channel_id=1, source_target_pairs={{0,20},{1,21},{2,22},{3,23},{4,16},{5,17},{6,18},{7,19},{8,28},{9,... | collective-permute-start | bytes 3538952 | tf_op jit(solution)/shard_map/ppermute | solution.py:54
  5.3 27.2 %copy-start.2 = (bf16[128,3072]{1,0:T(8,128)(2,1)S(1)}, bf16[128,3072]{1,0:T(8,128)(2,1)}, u32[]{:S(2)}) copy-start(bf16[128,3072]{1,0:T(8,128)(2,1)} %cot0.2) | copy-start | bytes 2359300
  5.3 27.7 %copy-start.1 = (bf16[128,3072]{1,0:T(8,128)(2,1)S(1)}, bf16[128,3072]{1,0:T(8,128)(2,1)}, u32[]{:S(2)}) copy-start(bf16[128,3072]{1,0:T(8,128)(2,1)} %own.3) | copy-start | bytes 2359300
  6.9 29.2 %collective-permute-start.4 = (bf16[384,1536]{1,0:T(8,128)(2,1)S(1)}, bf16[384,1536]{1,0:T(8,128)(2,1)S(1)}, u32[]{:S(2)}, u32[]{:S(2)}) collective-permute-start(bf16[384,1536]{1,0:T(8,128)(2,1)S(1)} %dequantize.1.w0), channel_id=1, source_target_pairs={{0,3},{1,0},{2,1},{3,2},{4,7},{5,4},{6,5},{7,6},{8,11},{9,8},{10,9... | collective-permute-start | bytes 3538952 | tf_op jit(solution)/shard_map/ppermute | solution.py:54
  8.0 28.5 %collective-permute-start.3 = (bf16[384,1536]{1,0:T(8,128)(2,1)S(1)}, bf16[384,1536]{1,0:T(8,128)(2,1)S(1)}, u32[]{:S(2)}, u32[]{:S(2)}) collective-permute-start(bf16[384,1536]{1,0:T(8,128)(2,1)S(1)} %dequantize.1.w0), channel_id=1, source_target_pairs={{0,1},{1,2},{2,3},{3,0},{4,5},{5,6},{6,7},{7,4},{8,9},{9,10},{10,1... | collective-permute-start | bytes 3538952 | tf_op jit(solution)/shard_map/ppermute | solution.py:54
  32.4 4.7 %collective-permute-start.2 = (bf16[128,4608]{1,0:T(8,128)(2,1)}, bf16[128,4608]{1,0:T(8,128)(2,1)S(1)}, u32[]{:S(2)}, u32[]{:S(2)}) collective-permute-start(bf16[128,4608]{1,0:T(8,128)(2,1)} %collective-permute-done.1.pair.cot2), channel_id=1, source_target_pairs={{0,8},{1,9},{2,10},{3,11},{4,12},{5,13},{6,14},{7,15},{8,0},{9,1},... | collective-permute-start | bytes 3538952 | tf_op jit(solution)/shard_map/ppermute | solution.py:54
  32.4 3.6 %collective-permute-start.5 = (bf16[128,3072]{1,0:T(8,128)(2,1)S(1)}, bf16[128,3072]{1,0:T(8,128)(2,1)S(1)}, u32[]{:S(2)}, u32[]{:S(2)}) collective-permute-start(bf16[128,3072]{1,0:T(8,128)(2,1)S(1)} %copy-done.2), channel_id=1, source_target_pairs={{0,8},{1,9},{2,10},{3,11},{4,12},{5,13},{6,14},{7,15},{8,0},{9,1},... | collective-permute-start | bytes 2359304 | tf_op jit(solution)/shard_map/ppermute | solution.py:54
  33.0 4.6 %collective-permute-start = (bf16[128,3072]{1,0:T(8,128)(2,1)S(1)}, bf16[128,3072]{1,0:T(8,128)(2,1)S(1)}, u32[]{:S(2)}, u32[]{:S(2)}) collective-permute-start(bf16[128,3072]{1,0:T(8,128)(2,1)S(1)} %copy-done.1), channel_id=1, source_target_pairs={{0,8},{1,9},{2,10},{3,11},{4,12},{5,13},{6,14},{7,15},{8,0},{9,1},... | collective-permute-start | bytes 2359304 | tf_op jit(solution)/shard_map/ppermute | solution.py:54
  43.6 12.5 %collective-permute-start.7 = (bf16[48,3072]{1,0:T(8,128)(2,1)S(1)}, bf16[48,3072]{1,0:T(8,128)(2,1)S(1)}, u32[]{:S(2)}, u32[]{:S(2)}) collective-permute-start(bf16[48,3072]{1,0:T(8,128)(2,1)S(1)} %get-tuple-element.67), channel_id=1, source_target_pairs={{0,224},{1,225},{2,226},{3,227},{4,228},{5,229},{6,230},{7,231},{8... | collective-permute-start | bytes 884744 | tf_op jit(solution)/shard_map/ppermute | solution.py:54
  49.5 10.4 %collective-permute-start.6 = (bf16[48,3072]{1,0:T(8,128)(2,1)S(1)}, bf16[48,3072]{1,0:T(8,128)(2,1)S(1)}, u32[]{:S(2)}, u32[]{:S(2)}) collective-permute-start(bf16[48,3072]{1,0:T(8,128)(2,1)S(1)} %get-tuple-element.65), channel_id=1, source_target_pairs={{0,32},{1,33},{2,34},{3,35},{4,36},{5,37},{6,38},{7,39},{8,40},{9,... | collective-permute-start | bytes 884744 | tf_op jit(solution)/shard_map/ppermute | solution.py:54
  56.2 15.8 %collective-permute-start.11 = (bf16[96,3072]{1,0:T(8,128)(2,1)S(1)}, bf16[96,3072]{1,0:T(8,128)(2,1)S(1)}, u32[]{:S(2)}, u32[]{:S(2)}) collective-permute-start(bf16[96,3072]{1,0:T(8,128)(2,1)S(1)} %hop.7), channel_id=1, source_target_pairs={{0,224},{1,225},{2,226},{3,227},{4,228},{5,229},{6,230},{7,231},{8... | collective-permute-start | bytes 1769480 | tf_op jit(solution)/shard_map/ppermute | solution.py:54
  60.0 15.9 %collective-permute-start.10 = (bf16[96,3072]{1,0:T(8,128)(2,1)S(1)}, bf16[96,3072]{1,0:T(8,128)(2,1)S(1)}, u32[]{:S(2)}, u32[]{:S(2)}) collective-permute-start(bf16[96,3072]{1,0:T(8,128)(2,1)S(1)} %hop.6), channel_id=1, source_target_pairs={{0,32},{1,33},{2,34},{3,35},{4,36},{5,37},{6,38},{7,39},{8,40},{9,... | collective-permute-start | bytes 1769480 | tf_op jit(solution)/shard_map/ppermute | solution.py:54
  60.2 16.1 %collective-permute-start.9 = (bf16[384,768]{1,0:T(8,128)(2,1)S(1)}, bf16[384,768]{1,0:T(8,128)(2,1)S(1)}, u32[]{:S(2)}, u32[]{:S(2)}) collective-permute-start(bf16[384,768]{1,0:T(8,128)(2,1)S(1)} %slice.21), channel_id=1, source_target_pairs={{0,3},{1,0},{2,1},{3,2},{4,7},{5,4},{6,5},{7,6},{8,11},{9,8},{10,9... | collective-permute-start | bytes 1769480 | tf_op jit(solution)/shard_map/ppermute | solution.py:54
  63.0 15.2 %collective-permute-start.8 = (bf16[384,768]{1,0:T(8,128)(2,1)S(1)}, bf16[384,768]{1,0:T(8,128)(2,1)S(1)}, u32[]{:S(2)}, u32[]{:S(2)}) collective-permute-start(bf16[384,768]{1,0:T(8,128)(2,1)S(1)} %slice.20), channel_id=1, source_target_pairs={{0,1},{1,2},{2,3},{3,0},{4,5},{5,6},{6,7},{7,4},{8,9},{9,10},{10,1... | collective-permute-start | bytes 1769480 | tf_op jit(solution)/shard_map/ppermute | solution.py:54
  72.1 14.9 %collective-permute-start.15 = (bf16[96,3072]{1,0:T(8,128)(2,1)S(1)}, bf16[96,3072]{1,0:T(8,128)(2,1)S(1)}, u32[]{:S(2)}, u32[]{:S(2)}) collective-permute-start(bf16[96,3072]{1,0:T(8,128)(2,1)S(1)} %hop.9), channel_id=1, source_target_pairs={{0,224},{1,225},{2,226},{3,227},{4,228},{5,229},{6,230},{7,231},{8... | collective-permute-start | bytes 1769480 | tf_op jit(solution)/shard_map/ppermute | solution.py:54
  76.0 14.9 %collective-permute-start.13 = (bf16[96,3072]{1,0:T(8,128)(2,1)S(1)}, bf16[96,3072]{1,0:T(8,128)(2,1)S(1)}, u32[]{:S(2)}, u32[]{:S(2)}) collective-permute-start(bf16[96,3072]{1,0:T(8,128)(2,1)S(1)} %hop.8), channel_id=1, source_target_pairs={{0,32},{1,33},{2,34},{3,35},{4,36},{5,37},{6,38},{7,39},{8,40},{9,... | collective-permute-start | bytes 1769480 | tf_op jit(solution)/shard_map/ppermute | solution.py:54
  83.1 18.6 %collective-permute-start.12 = (bf16[256,1536]{1,0:T(8,128)(2,1)S(1)}, bf16[256,1536]{1,0:T(8,128)(2,1)S(1)}, u32[]{:S(2)}, u32[]{:S(2)}) collective-permute-start(bf16[256,1536]{1,0:T(8,128)(2,1)S(1)} %get-tuple-element.79), channel_id=1, source_target_pairs={{0,20},{1,21},{2,22},{3,23},{4,16},{5,17},{6,18},{7,19},{8,28},{9,... | collective-permute-start | bytes 2359304 | tf_op jit(solution)/shard_map/ppermute | solution.py:54
  87.2 14.7 %collective-permute-start.16 = (bf16[96,3072]{1,0:T(8,128)(2,1)S(1)}, bf16[96,3072]{1,0:T(8,128)(2,1)S(1)}, u32[]{:S(2)}, u32[]{:S(2)}) collective-permute-start(bf16[96,3072]{1,0:T(8,128)(2,1)S(1)} %hop.11), channel_id=1, source_target_pairs={{0,224},{1,225},{2,226},{3,227},{4,228},{5,229},{6,230},{7,231},{8... | collective-permute-start | bytes 1769480 | tf_op jit(solution)/shard_map/ppermute | solution.py:54
  91.1 13.7 %collective-permute-start.14 = (bf16[96,3072]{1,0:T(8,128)(2,1)S(1)}, bf16[96,3072]{1,0:T(8,128)(2,1)S(1)}, u32[]{:S(2)}, u32[]{:S(2)}) collective-permute-start(bf16[96,3072]{1,0:T(8,128)(2,1)S(1)} %hop.10), channel_id=1, source_target_pairs={{0,32},{1,33},{2,34},{3,35},{4,36},{5,37},{6,38},{7,39},{8,40},{9,... | collective-permute-start | bytes 1769480 | tf_op jit(solution)/shard_map/ppermute | solution.py:54
  96.2 15.9 %collective-permute-start.20 = (bf16[256,1536]{1,0:T(8,128)(2,1)S(1)}, bf16[256,1536]{1,0:T(8,128)(2,1)S(1)}, u32[]{:S(2)}, u32[]{:S(2)}) collective-permute-start(bf16[256,1536]{1,0:T(8,128)(2,1)S(1)} %get-tuple-element.98), channel_id=1, source_target_pairs={{0,8},{1,9},{2,10},{3,11},{4,12},{5,13},{6,14},{7,15},{8,0},{9,1},... | collective-permute-start | bytes 2359304 | tf_op jit(solution)/shard_map/ppermute | solution.py:54
  105.9 6.8 %collective-permute-start.17 = (bf16[24,3072]{1,0:T(8,128)(2,1)S(1)}, bf16[24,3072]{1,0:T(8,128)(2,1)S(1)}, u32[]{:S(2)}, u32[]{:S(2)}) collective-permute-start(bf16[24,3072]{1,0:T(8,128)(2,1)S(1)} %get-tuple-element.95), channel_id=1, source_target_pairs={{0,1},{1,2},{2,3},{3,0},{4,5},{5,6},{6,7},{7,4},{8,9},{9,10},{10,1... | collective-permute-start | bytes 442376 | tf_op jit(solution)/shard_map/ppermute | solution.py:54
  107.5 7.4 %collective-permute-start.18 = (bf16[24,3072]{1,0:T(8,128)(2,1)S(1)}, bf16[24,3072]{1,0:T(8,128)(2,1)S(1)}, u32[]{:S(2)}, u32[]{:S(2)}) collective-permute-start(bf16[24,3072]{1,0:T(8,128)(2,1)S(1)} %get-tuple-element.96), channel_id=1, source_target_pairs={{0,2},{1,3},{2,0},{3,1},{4,6},{5,7},{6,4},{7,5},{8,10},{9,11},{10,... | collective-permute-start | bytes 442376 | tf_op jit(solution)/shard_map/ppermute | solution.py:54
  110.2 5.1 %collective-permute-start.19 = (bf16[24,3072]{1,0:T(8,128)(2,1)S(1)}, bf16[24,3072]{1,0:T(8,128)(2,1)S(1)}, u32[]{:S(2)}, u32[]{:S(2)}) collective-permute-start(bf16[24,3072]{1,0:T(8,128)(2,1)S(1)} %get-tuple-element.97), channel_id=1, source_target_pairs={{0,3},{1,0},{2,1},{3,2},{4,7},{5,4},{6,5},{7,6},{8,11},{9,8},{10,9... | collective-permute-start | bytes 442376 | tf_op jit(solution)/shard_map/ppermute | solution.py:54
  112.0 12.4 %collective-permute-start.21 = (bf16[128,1536]{1,0:T(8,128)(2,1)S(1)}, bf16[128,1536]{1,0:T(8,128)(2,1)S(1)}, u32[]{:S(2)}, u32[]{:S(2)}) collective-permute-start(bf16[128,1536]{1,0:T(8,128)(2,1)S(1)} %get-tuple-element.112), channel_id=1, source_target_pairs={{0,8},{1,9},{2,10},{3,11},{4,12},{5,13},{6,14},{7,15},{8,0},{9,1},... | collective-permute-start | bytes 1179656 | tf_op jit(solution)/shard_map/ppermute | solution.py:54
  112.3 13.9 %collective-permute-start.22 = (bf16[128,1536]{1,0:T(8,128)(2,1)S(1)}, bf16[128,1536]{1,0:T(8,128)(2,1)S(1)}, u32[]{:S(2)}, u32[]{:S(2)}) collective-permute-start(bf16[128,1536]{1,0:T(8,128)(2,1)S(1)} %get-tuple-element.114), channel_id=1, source_target_pairs={{0,20},{1,21},{2,22},{3,23},{4,16},{5,17},{6,18},{7,19},{8,28},{9,... | collective-permute-start | bytes 1179656 | tf_op jit(solution)/shard_map/ppermute | solution.py:54
  116.1 14.2 %collective-permute-start.23 = (bf16[12,3072]{1,0:T(8,128)(2,1)S(1)}, bf16[12,3072]{1,0:T(8,128)(2,1)S(1)}, u32[]{:S(2)}, u32[]{:S(2)}) collective-permute-start(bf16[12,3072]{1,0:T(8,128)(2,1)S(1)} %get-tuple-element.104), channel_id=1, source_target_pairs={{0,24},{1,25},{2,26},{3,27},{4,184},{5,185},{6,186},{7,187},{8,72}... | collective-permute-start | bytes 221192 | tf_op jit(solution)/shard_map/ppermute | solution.py:54
  118.0 12.3 %collective-permute-start.24 = (bf16[12,3072]{1,0:T(8,128)(2,1)S(1)}, bf16[12,3072]{1,0:T(8,128)(2,1)S(1)}, u32[]{:S(2)}, u32[]{:S(2)}) collective-permute-start(bf16[12,3072]{1,0:T(8,128)(2,1)S(1)} %get-tuple-element.108), channel_id=1, source_target_pairs={{0,28},{1,29},{2,30},{3,31},{4,188},{5,189},{6,190},{7,191},{8,76}... | collective-permute-start | bytes 221192 | tf_op jit(solution)/shard_map/ppermute | solution.py:54

commit v7 on v6

--- a/solution.py
+++ b/solution.py
@@ -120,80 +120,70 @@
     )
 
 
-def pack_kernel(tokens, cotangent, out, sems):
-    kh = tokens.shape[1] // 2
-    start = pl.multiple_of((1 - lax.axis_index("yh")) * kh, 128)
-    copies = (
-        pltpu.make_async_copy(tokens.at[:, pl.ds(start, kh)], out.at[:, pl.ds(0, kh)], sems.at[0]),
-        pltpu.make_async_copy(cotangent, out.at[:, pl.ds(kh, cotangent.shape[1])], sems.at[1]),
-    )
-    for copy in copies:
-        copy.start()
-    for copy in copies:
-        copy.wait()
-
-
-def pack(tokens, cotangent):
-    shape = (tokens.shape[0], tokens.shape[1] // 2 + cotangent.shape[1])
-    return pl.pallas_call(
-        pack_kernel,
-        name="pack",
-        in_specs=[pl.BlockSpec(memory_space=pl.ANY)] * 2,
-        out_specs=pl.BlockSpec(memory_space=pltpu.VMEM),
-        out_shape=jax.ShapeDtypeStruct(shape, jnp.bfloat16),
-        scratch_shapes=[pltpu.SemaphoreType.DMA((2,))],
-        compiler_params=pltpu.CompilerParams(vmem_limit_bytes=60 * 2**20),
-    )(tokens, cotangent)
-
-
 def columns(ref, start, size):
     return ref[:, pl.ds(pl.multiple_of(start, 128), size)]
 
 
-def gradient_kernel(where, own, sib, pair, psib, cot0, cot1, cot2, cot3, *refs):
-    c, yh = where[0], where[1]
-    *chunks, lhs, out = refs
-    count, size = own.shape[0], lhs.shape[1]
+def product(parts, starts, cots, lhs):
+    count, size = parts[0].shape[0], lhs.shape[1]
 
     @pl.when(pl.program_id(0) == 0)
     def _():
-        for r, (ref, base) in enumerate(((own, yh), (sib, yh), (pair, 0), (psib, 0))):
-            start = base * 2 * size + c * size
+        for r, (ref, start) in enumerate(zip(parts, starts)):
             lhs[r * count : (r + 1) * count] = columns(ref, start, size)
 
-    rhs = jnp.concatenate([cot0[...], cot1[...], cot2[...], cot3[...]])
-    out[...] = bf16(
+    rhs = jnp.concatenate([cot[...] for cot in cots])
+    return bf16(
         lax.dot_general(
             lhs[...], rhs, (((0,), (0,)), ((), ())), preferred_element_type=jnp.float32
         )
     )
-    height, start = size // 8, 0
-    for k, ref in zip((4, 4, *HOPS), chunks):
-        part = ref.shape[0]
-        row = (where[3] + 8 + k) % 8 * height + start
-        ref[...] = out[pl.ds(pl.multiple_of(row, 16), part)]
-        start = (start + part) % height
-
-
-def gradient(where, token_parts, cot_parts):
+
+
+def gradient_kernel(where, own, sib, pair, psib, cot0, cot1, cot2, cot3, *refs):
+    *chunks, lhs, out = refs
+    c, yh = where[0], where[1]
+    size = lhs.shape[1]
+    starts = [base * 2 * size + c * size for base in (yh, yh, 0, 0)]
+    out[...] = product((own, sib, pair, psib), starts, (cot0, cot1, cot2, cot3), lhs)
+    height = size // 8
+    for k, ref in zip(HOPS, chunks):
+        row = pl.multiple_of((where[3] + 8 + k) % 8 * height, 16)
+        ref[...] = out[pl.ds(row, height)]
+
+
+def far_kernel(where, own, sib, pair, psib, cot0, cot1, cot2, cot3, up, down, lhs, out):
+    c, yh = where[0], where[1]
+    window, half = lhs.shape[1], up.shape[0]
+    size, chunk, tile = 3 * window, 2 * half, window // 2
+    row = (where[3] + 4) % 8 * chunk
+    first = jnp.minimum(row // tile * tile, size - window)
+    starts = [base * 2 * size + c * size + first for base in (yh, yh, 0, 0)]
+    out[...] = product((own, sib, pair, psib), starts, (cot0, cot1, cot2, cot3), lhs)
+    skip = pl.multiple_of(row - first, 16)
+    up[...] = out[pl.ds(skip, half)]
+    down[...] = out[pl.ds(skip + half, half)]
+
+
+def gradient(where, token_parts, cot_parts, far):
     count, outputs = cot_parts[0].shape
     kh = token_parts[0].shape[1] // 2
     size, width = kh // 2, outputs // 4
-    heights = [size // 16] * 2 + [size // 8] * len(HOPS)
-    return call(
-        gradient_kernel,
-        "gradient",
+    window = size // 3 if far else size
+    heights = [size // 16] * 2 if far else [size // 8] * len(HOPS)
+    return call(
+        far_kernel if far else gradient_kernel,
+        "far" if far else "gradient",
         24,
         where,
         (4,),
         [fixed(v.shape) for v in token_parts[:2]]
         + [fixed((count, kh))] * 2
-        + [pl.BlockSpec((count, width), lambda i, where: (0, i))] * 2
-        + [pl.BlockSpec((count, width), lambda i, where: (0, i + 2))] * 2,
+        + [pl.BlockSpec((count, width), lambda i, where: (0, i))] * 4,
         [pl.BlockSpec((height, width), lambda i, where: (0, i)) for height in heights],
         [jax.ShapeDtypeStruct((height, outputs), jnp.bfloat16) for height in heights],
-        [pltpu.VMEM((4 * count, size), jnp.bfloat16), pltpu.VMEM((size, width), jnp.bfloat16)],
-        8 * count * size * outputs,
+        [pltpu.VMEM((4 * count, window), jnp.bfloat16), pltpu.VMEM((window, width), jnp.bfloat16)],
+        8 * count * window * outputs,
         (*token_parts, *cot_parts),
     )
 
@@ -361,8 +351,7 @@
         28,
         where,
         (3,),
-        [fixed((count, nh), lambda where: (0, where[0]))] * 2
-        + [fixed((count, nh), lambda where: (0, 1 + where[0]))] * 2
+        [fixed((count, nh), lambda where: (0, where[0]))] * 4
         + [pl.BlockSpec((size, nh), lambda i, where: (i, 0))] * 3
         + [pl.BlockSpec((size, nh // 2), lambda i, where: (i, 0))] * 2,
         [fixed((2 * count, 4 * shard))] * 2,
@@ -385,20 +374,21 @@
     count = tokens.shape[0]
     factor = float(count * 256) ** -0.5
 
-    packed = pack(tokens, cotangent)
-    pair = send(packed, PAIR)
-
-    levels, scales = after((levels, scales.T), packed)
-    own = dequantize(where, levels, scales)
+    cot_pair = send(cotangent, PAIR)
+    kh = tokens.shape[1] // 2
+
+    own = dequantize(where, levels, scales.T)
     left, right = send(own, X_UP), send(own, X_DOWN)
 
-    cot_own, token_own = after((cotangent, tokens), own)
+    token_out = lax.dynamic_slice_in_dim(after(tokens, own), (1 - yh) * kh, kh, 1)
+    token_pair = send(token_out, PAIR)
+    cot_own, token_own = after((cotangent, tokens), token_out)
     cot_sib, token_sib = send(cot_own, CORE), send(token_own, CORE)
-    cross = send(pair, CORE)
-    token_parts = (tokens, token_sib, pair, cross)
-    cot_parts = (cotangent, cot_sib, pair, cross)
-
-    up, down, *grad = gradient(where, token_parts, after(cot_parts, left, right))
+    token_parts = (tokens, token_sib, token_pair, send(token_pair, CORE))
+    cot_parts = (cotangent, cot_sib, cot_pair, send(cot_pair, CORE))
+
+    up, down = gradient(where, token_parts, after(cot_parts, left, right), True)
+    grad = gradient(where, token_parts, after(cot_parts, up), False)
     half = own.shape[1] // 2
     up, down = send(up, Z_UP), send(down, Z_DOWN)
     up = hop(grad[0], up, kernel=functools.partial(first_hop_kernel, upper=True))

time: 131 us -> 122 us (0.931)
  waiting for transfers between devices: 63.8 us -> 45.2 us
  starting transfers between devices: 40.2 us -> 44.8 us
  local copies, waits for them, and re-layouts: 0.24 us -> 4.78 us
    ppermute x25 -> x27, waiting for transfers between devices: 63.8 us -> 45.2 us  [send(): return lax.ppermute(value, AXES, pairs)]
    ppermute x25 -> x27, starting transfers between devices: 40.2 us -> 44.8 us  [send(): return lax.ppermute(value, AXES, pairs)]
    pallas_call x1 -> x0, Pallas kernels: 2.46 us -> none  [pack(): pl.pallas_call(pack_kernel, name='pack', in_specs=[pl.BlockSpec(memory_sp...]
    unnamed x8, local copies, waits for them, and re-layouts: 0.02 us -> 2.41 us
    pallas_call x6 -> x7, Pallas kernels: 19.3 us -> 21 us  [call(): pl.pallas_call(kernel, name=name, grid_spec=pltpu.PrefetchScalarGridSpec(...]
  transfers between devices with their start and end apart: 25 -> 27, of which waited for: 15 -> 12; matrix products, arithmetic and copies ran while one was open for 2% -> 5% of each run, Pallas kernels for 11% -> 16%
where the time goes in v7:
time: 122 us; the launch traced here: 121 us
  waiting for transfers between devices  45.2 us (37%)
  starting transfers between devices  44.8 us (37%)
  Pallas kernels  21.7 us (18%)
  local copies, waits for them, and re-layouts  4.78 us (4%)
  other arithmetic  4.12 us (3%)
    ppermute x27, waiting for transfers between devices, send(): return lax.ppermute(value, AXES, pairs)  45.2 us
    ppermute x27, starting transfers between devices, send(): return lax.ppermute(value, AXES, pairs)  44.8 us
    pallas_call x7, Pallas kernels, call(): pl.pallas_call(kernel, name=name, grid_spec=pltpu.PrefetchScalarGridSpec(...  21 us
  transfers between devices with their start and end apart: 27, of which 12 were waited for; matrix products, arithmetic and copies ran while one was open for 5% of the time, Pallas kernels for 16%

profile of v7, /device:TPU:24, one launch (start us, length us, event | category | flops | bytes accessed | tf_op | source)
XLA Modules:
  0.0 121.5 jit_solution(1899405852313408953)
XLA Ops:
  0.6 2.0 %collective-permute-start.6 = (bf16[128,3072]{1,0:T(8,128)(2,1)}, bf16[128,3072]{1,0:T(8,128)(2,1)S(1)}, u32[]{:S(2)}, u32[]{:S(2)}) collective-permute-start(bf16[128,3072]{1,0:T(8,128)(2,1)} %cot0.3), channel_id=1, source_target_pairs={{0,20},{1,21},{2,22},{3,23},{4,16},{5,17},{6,18},{7,19},{8,28},{9,... | collective-permute-start | bytes 2359304 | tf_op jit(solution)/shard_map/ppermute | solution.py:54
  2.7 0.1 stack.23.where
  2.8 1.7 %copy-done = bf16[384,3072]{1,0:T(8,128)(2,1)S(1)} copy-done((bf16[384,3072]{1,0:T(8,128)(2,1)S(1)}, bf16[384,3072]{1,0:T(8,128)(2,1)}, u32[]{:S(2)}) %copy-start) | copy-done | bytes 2359320
  4.4 0.7 copy-done.3
  5.2 1.6 %dequantize.1.w0 = bf16[384,1536]{1,0:T(8,128)(2,1)S(1)} custom-call(s32[5]{0:T(128)S(1)} %stack.23.where, bf16[384,3072]{1,0:T(8,128)(2,1)S(1)} %copy-done, f32[12,384]{1,0:T(8,128)S(1)} %bitcast.6), custom_call_target="tpu_custom_call" | custom-call | flops 589824 | bytes 3557376 | tf_op jit(solution)/shard_map/dequantize/pallas_call | solution.py:72
  6.8 1.1 collective-permute-start.4
  7.9 1.0 collective-permute-start.3
  8.9 2.1 %collective-permute-start.1 = (bf16[128,1536]{1,0:T(8,128)(2,1)S(1)}, bf16[128,1536]{1,0:T(8,128)(2,1)S(1)}, u32[]{:S(2)}, u32[]{:S(2)}) collective-permute-start(bf16[128,1536]{1,0:T(8,128)(2,1)S(1)} %constant_dynamic-slice_fusion), channel_id=1, source_target_pairs={{0,20},{1,21},{2,22},{3,23},{4,16},{5,17},{6,18},{7,19},{8,28},{9,... | collective-permute-start | bytes 1179656 | tf_op jit(solution)/shard_map/ppermute | solution.py:54
  11.0 0.0 collective-permute-start.5
  11.0 11.6 %collective-permute-done.6.cot2 = bf16[128,3072]{1,0:T(8,128)(2,1)S(1)} collective-permute-done((bf16[128,3072]{1,0:T(8,128)(2,1)}, bf16[128,3072]{1,0:T(8,128)(2,1)S(1)}, u32[]{:S(2)}, u32[]{:S(2)}) %collective-permute-start.6) | collective-permute-done | bytes 786464 | tf_op jit(solution)/shard_map/ppermute | solution.py:54
  22.6 0.0 collective-permute-start.7
  22.6 7.3 %collective-permute-done.1.pair = bf16[128,1536]{1,0:T(8,128)(2,1)S(1)} collective-permute-done((bf16[128,1536]{1,0:T(8,128)(2,1)S(1)}, bf16[128,1536]{1,0:T(8,128)(2,1)S(1)}, u32[]{:S(2)}, u32[]{:S(2)}) %collective-permute-start.1) | collective-permute-done | bytes 393248 | tf_op jit(solution)/shard_map/ppermute | solution.py:54
  29.8 0.0 collective-permute-start
  29.8 0.0 collective-permute-done.5.cot1
  29.9 0.5 collective-permute-start.2
  30.4 2.5 %collective-permute-done.4.w2 = bf16[384,1536]{1,0:T(8,128)(2,1)} collective-permute-done((bf16[384,1536]{1,0:T(8,128)(2,1)S(1)}, bf16[384,1536]{1,0:T(8,128)(2,1)}, u32[]{:S(2)}, u32[]{:S(2)}) %collective-permute-start.4) | collective-permute-done | bytes 1179680 | tf_op jit(solution)/shard_map/ppermute | solution.py:54
  32.9 3.5 %collective-permute-done.3.w1 = bf16[384,1536]{1,0:T(8,128)(2,1)} collective-permute-done((bf16[384,1536]{1,0:T(8,128)(2,1)S(1)}, bf16[384,1536]{1,0:T(8,128)(2,1)}, u32[]{:S(2)}, u32[]{:S(2)}) %collective-permute-start.3) | collective-permute-done | bytes 1179680 | tf_op jit(solution)/shard_map/ppermute | solution.py:54
  36.4 0.0 collective-permute-done.7.cot3
  36.4 2.7 %far.1 = (bf16[48,3072]{1,0:T(8,128)(2,1)S(1)}, bf16[48,3072]{1,0:T(8,128)(2,1)S(1)}) custom-call(s32[5]{0:T(128)S(1)} %stack.23.where, bf16[128,3072]{1,0:T(8,128)(2,1)S(1)} %copy-done.1, bf16[128,3072]{1,0:T(8,128)(2,1)S(1)} %collective-permute-done.sib, bf16[128,1536]{1,0:T(8,128)(2,1)S(1)} %collective-permute-done.1.pair, ...), custom_call_target="tpu_custom_call" | custom-call | flops 805306368 | bytes 6094848 | tf_op jit(solution)/shard_map/far/pallas_call | solution.py:72
  39.1 5.9 %collective-permute-start.9 = (bf16[48,3072]{1,0:T(8,128)(2,1)S(1)}, bf16[48,3072]{1,0:T(8,128)(2,1)S(1)}, u32[]{:S(2)}, u32[]{:S(2)}) collective-permute-start(bf16[48,3072]{1,0:T(8,128)(2,1)S(1)} %get-tuple-element.73), channel_id=1, source_target_pairs={{0,224},{1,225},{2,226},{3,227},{4,228},{5,229},{6,230},{7,231},{8... | collective-permute-start | bytes 884744 | tf_op jit(solution)/shard_map/ppermute | solution.py:54
  45.1 4.9 %gradient.1 = (bf16[96,3072]{1,0:T(8,128)(2,1)S(1)}, bf16[96,3072]{1,0:T(8,128)(2,1)S(1)}, bf16[96,3072]{1,0:T(8,128)(2,1)S(1)}, bf16[96,3072]{1,0:T(8,128)(2,1)...) custom-call(s32[5]{0:T(128)S(1)} %stack.23.where, ...), custom_call_target="tpu_custom_call" | custom-call | flops 2415919104 | bytes 9633792 | tf_op jit(solution)/shard_map/gradient/pallas_call | solution.py:72
  50.0 0.1 hop.7
  50.1 3.7 %collective-permute-start.13 = (bf16[96,3072]{1,0:T(8,128)(2,1)S(1)}, bf16[96,3072]{1,0:T(8,128)(2,1)S(1)}, u32[]{:S(2)}, u32[]{:S(2)}) collective-permute-start(bf16[96,3072]{1,0:T(8,128)(2,1)S(1)} %hop.7), channel_id=1, source_target_pairs={{0,224},{1,225},{2,226},{3,227},{4,228},{5,229},{6,230},{7,231},{8... | collective-permute-start | bytes 1769480 | tf_op jit(solution)/shard_map/ppermute | solution.py:54
  53.8 0.1 hop.6
  53.9 0.1 collective-permute-start.12
  54.0 1.1 slice.20
  55.1 1.1 slice.21
  56.2 0.8 collective-permute-start.11
  57.0 1.3 %collective-permute-start.10 = (bf16[384,768]{1,0:T(8,128)(2,1)S(1)}, bf16[384,768]{1,0:T(8,128)(2,1)S(1)}, u32[]{:S(2)}, u32[]{:S(2)}) collective-permute-start(bf16[384,768]{1,0:T(8,128)(2,1)S(1)} %slice.20), channel_id=1, source_target_pairs={{0,1},{1,2},{2,3},{3,0},{4,5},{5,6},{6,7},{7,4},{8,9},{9,10},{10,1... | collective-permute-start | bytes 1769480 | tf_op jit(solution)/shard_map/ppermute | solution.py:54
  58.3 5.8 %collective-permute-done.13.refs_0_ = bf16[96,3072]{1,0:T(8,128)(2,1)S(1)} collective-permute-done((bf16[96,3072]{1,0:T(8,128)(2,1)S(1)}, bf16[96,3072]{1,0:T(8,128)(2,1)S(1)}, u32[]{:S(2)}, u32[]{:S(2)}) %collective-permute-start.13) | collective-permute-done | bytes 589856 | tf_op jit(solution)/shard_map/ppermute | solution.py:54
  64.1 0.1 hop.9
  64.2 3.9 %collective-permute-start.17 = (bf16[96,3072]{1,0:T(8,128)(2,1)S(1)}, bf16[96,3072]{1,0:T(8,128)(2,1)S(1)}, u32[]{:S(2)}, u32[]{:S(2)}) collective-permute-start(bf16[96,3072]{1,0:T(8,128)(2,1)S(1)} %hop.9), channel_id=1, source_target_pairs={{0,224},{1,225},{2,226},{3,227},{4,228},{5,229},{6,230},{7,231},{8... | collective-permute-start | bytes 1769480 | tf_op jit(solution)/shard_map/ppermute | solution.py:54
  68.2 0.1 hop.8
  68.3 0.1 collective-permute-start.15
  68.4 0.3 collective-permute-done.11.w4
  68.7 2.1 %collective-permute-done.10.w3 = bf16[384,768]{1,0:T(8,128)(2,1)S(1)} collective-permute-done((bf16[384,768]{1,0:T(8,128)(2,1)S(1)}, bf16[384,768]{1,0:T(8,128)(2,1)S(1)}, u32[]{:S(2)}, u32[]{:S(2)}) %collective-permute-start.10) | collective-permute-done | bytes 589856 | tf_op jit(solution)/shard_map/ppermute | solution.py:54
  70.8 5.0 %forward.1 = (f32[128,1536]{1,0:T(8,128)S(1)}, f32[128,1536]{1,0:T(8,128)S(1)}, bf16[256,1536]{1,0:T(8,128)(2,1)S(1)}) custom-call(s32[5]{0:T(128)S(1)} %stack.23.where, bf16[128,3072]{1,0:T(8,128)(2,1)S(1)} %copy-done.1, bf16[128,3072]{1,0:T(8,128)(2,1)S(1)} %collective-permute-done.sib, bf16[128,1536]{1,0:T(8,128)(2,1)S(1)} %collective-permute-done.1.pair, ...), custom_call_target="tpu_custom_call" | custom-call | flops 2415919104 | bytes 9437184 | tf_op jit(solution)/shard_map/forward/pallas_call | solution.py:72
  75.8 2.6 %collective-permute-start.14 = (bf16[256,1536]{1,0:T(8,128)(2,1)S(1)}, bf16[256,1536]{1,0:T(8,128)(2,1)S(1)}, u32[]{:S(2)}, u32[]{:S(2)}) collective-permute-start(bf16[256,1536]{1,0:T(8,128)(2,1)S(1)} %get-tuple-element.85), channel_id=1, source_target_pairs={{0,20},{1,21},{2,22},{3,23},{4,16},{5,17},{6,18},{7,19},{8,28},{9,... | collective-permute-start | bytes 2359304 | tf_op jit(solution)/shard_map/ppermute | solution.py:54
  78.3 0.1 hop.11
  78.5 3.1 %collective-permute-start.18 = (bf16[96,3072]{1,0:T(8,128)(2,1)S(1)}, bf16[96,3072]{1,0:T(8,128)(2,1)S(1)}, u32[]{:S(2)}, u32[]{:S(2)}) collective-permute-start(bf16[96,3072]{1,0:T(8,128)(2,1)S(1)} %hop.11), channel_id=1, source_target_pairs={{0,224},{1,225},{2,226},{3,227},{4,228},{5,229},{6,230},{7,231},{8... | collective-permute-start | bytes 1769480 | tf_op jit(solution)/shard_map/ppermute | solution.py:54
  81.6 0.1 hop.10
  81.7 0.1 collective-permute-start.16
  81.8 5.1 %backward.1 = (f32[256,1536]{1,0:T(8,128)S(1)}, bf16[256,1536]{1,0:T(8,128)(2,1)S(1)}) custom-call(s32[5]{0:T(128)S(1)} %stack.23.where, bf16[128,3072]{1,0:T(8,128)(2,1)S(1)} %copy-done.2, bf16[128,3072]{1,0:T(8,128)(2,1)S(1)} %collective-permute-done.5.cot1, bf16[128,3072]{1,0:T(8,128)(2,1)S(1)} %collective-permute-done.6.cot2, ...), custom_call_target="tpu_custom_call" | custom-call | flops 2415919104 | bytes 10223616 | tf_op jit(solution)/shard_map/backward/pallas_call | solution.py:72
  86.9 0.1 collective-permute-start.22
  87.0 6.0 %collective-permute-done.14 = bf16[256,1536]{1,0:T(8,128)(2,1)S(1)} collective-permute-done((bf16[256,1536]{1,0:T(8,128)(2,1)S(1)}, bf16[256,1536]{1,0:T(8,128)(2,1)S(1)}, u32[]{:S(2)}, u32[]{:S(2)}) %collective-permute-start.14) | collective-permute-done | bytes 786464 | tf_op jit(solution)/shard_map/ppermute | solution.py:54
  93.0 0.2 convert_element_type.20
  93.2 0.6 collective-permute-done.16.up
  93.8 1.2 last_hop.1
  95.0 0.3 collective-permute-start.19
  95.3 4.8 %collective-permute-start.20 = (bf16[24,3072]{1,0:T(8,128)(2,1)S(1)}, bf16[24,3072]{1,0:T(8,128)(2,1)S(1)}, u32[]{:S(2)}, u32[]{:S(2)}) collective-permute-start(bf16[24,3072]{1,0:T(8,128)(2,1)S(1)} %get-tuple-element.102), channel_id=1, source_target_pairs={{0,2},{1,3},{2,0},{3,1},{4,6},{5,7},{6,4},{7,5},{8,10},{9,11},{10,... | collective-permute-start | bytes 442376 | tf_op jit(solution)/shard_map/ppermute | solution.py:54
  100.1 2.5 %collective-permute-start.21 = (bf16[24,3072]{1,0:T(8,128)(2,1)S(1)}, bf16[24,3072]{1,0:T(8,128)(2,1)S(1)}, u32[]{:S(2)}, u32[]{:S(2)}) collective-permute-start(bf16[24,3072]{1,0:T(8,128)(2,1)S(1)} %get-tuple-element.103), channel_id=1, source_target_pairs={{0,3},{1,0},{2,1},{3,2},{4,7},{5,4},{6,5},{7,6},{8,11},{9,8},{10,9... | collective-permute-start | bytes 442376 | tf_op jit(solution)/shard_map/ppermute | solution.py:54
  102.7 0.9 add_convert_fusion.2
  103.6 0.2 add_convert_fusion
  103.8 0.1 fusion
  103.9 0.1 collective-permute-start.24
  104.0 0.8 collective-permute-done.20.two
  104.7 0.6 collective-permute-done.21.three
  105.3 0.7 sum_over_x.1
  106.0 1.9 %collective-permute-start.25 = (bf16[12,3072]{1,0:T(8,128)(2,1)S(1)}, bf16[12,3072]{1,0:T(8,128)(2,1)S(1)}, u32[]{:S(2)}, u32[]{:S(2)}) collective-permute-start(bf16[12,3072]{1,0:T(8,128)(2,1)S(1)} %get-tuple-element.110), channel_id=1, source_target_pairs={{0,24},{1,25},{2,26},{3,27},{4,184},{5,185},{6,186},{7,187},{8,72}... | collective-permute-start | bytes 221192 | tf_op jit(solution)/shard_map/ppermute | solution.py:54
  107.9 6.6 %collective-permute-start.26 = (bf16[12,3072]{1,0:T(8,128)(2,1)S(1)}, bf16[12,3072]{1,0:T(8,128)(2,1)S(1)}, u32[]{:S(2)}, u32[]{:S(2)}) collective-permute-start(bf16[12,3072]{1,0:T(8,128)(2,1)S(1)} %get-tuple-element.114), channel_id=1, source_target_pairs={{0,28},{1,29},{2,30},{3,31},{4,188},{5,189},{6,190},{7,191},{8,76}... | collective-permute-start | bytes 221192 | tf_op jit(solution)/shard_map/ppermute | solution.py:54
  114.5 1.1 maximum_select_fusion
  115.6 4.1 %collective-permute-done.24 = bf16[128,1536]{1,0:T(8,128)(2,1)S(1)} collective-permute-done((bf16[128,1536]{1,0:T(8,128)(2,1)S(1)}, bf16[128,1536]{1,0:T(8,128)(2,1)S(1)}, u32[]{:S(2)}, u32[]{:S(2)}) %collective-permute-start.24) | collective-permute-done | bytes 393248 | tf_op jit(solution)/shard_map/ppermute | solution.py:54
  119.7 1.1 maximum_select_fusion.1
  120.8 0.7 convert_add_fusion
  (22 shorter events, 0.1 us)
Async XLA Ops:
  0.6 21.9 %collective-permute-start.6 = (bf16[128,3072]{1,0:T(8,128)(2,1)}, bf16[128,3072]{1,0:T(8,128)(2,1)S(1)}, u32[]{:S(2)}, u32[]{:S(2)}) collective-permute-start(bf16[128,3072]{1,0:T(8,128)(2,1)} %cot0.3), channel_id=1, source_target_pairs={{0,20},{1,21},{2,22},{3,23},{4,16},{5,17},{6,18},{7,19},{8,28},{9,... | collective-permute-start | bytes 2359304 | tf_op jit(solution)/shard_map/ppermute | solution.py:54
  2.8 1.7 %copy-start = (bf16[384,3072]{1,0:T(8,128)(2,1)S(1)}, bf16[384,3072]{1,0:T(8,128)(2,1)}, u32[]{:S(2)}) copy-start(bf16[384,3072]{1,0:T(8,128)(2,1)} %levels.1) | copy-start | bytes 7077892
  4.4 0.7 copy-start.3
  5.2 3.7 %copy-start.1 = (bf16[128,3072]{1,0:T(8,128)(2,1)S(1)}, bf16[128,3072]{1,0:T(8,128)(2,1)}, u32[]{:S(2)}) copy-start(bf16[128,3072]{1,0:T(8,128)(2,1)} %own.5) | copy-start | bytes 2359300
  5.2 5.8 %copy-start.2 = (bf16[128,3072]{1,0:T(8,128)(2,1)S(1)}, bf16[128,3072]{1,0:T(8,128)(2,1)}, u32[]{:S(2)}) copy-start(bf16[128,3072]{1,0:T(8,128)(2,1)} %cot0.3) | copy-start | bytes 2359300
  6.8 26.1 %collective-permute-start.4 = (bf16[384,1536]{1,0:T(8,128)(2,1)S(1)}, bf16[384,1536]{1,0:T(8,128)(2,1)}, u32[]{:S(2)}, u32[]{:S(2)}) collective-permute-start(bf16[384,1536]{1,0:T(8,128)(2,1)S(1)} %dequantize.1.w0), channel_id=1, source_target_pairs={{0,3},{1,0},{2,1},{3,2},{4,7},{5,4},{6,5},{7,6},{8,11},{9,8},{10,9... | collective-permute-start | bytes 3538952 | tf_op jit(solution)/shard_map/ppermute | solution.py:54
  7.9 28.6 %collective-permute-start.3 = (bf16[384,1536]{1,0:T(8,128)(2,1)S(1)}, bf16[384,1536]{1,0:T(8,128)(2,1)}, u32[]{:S(2)}, u32[]{:S(2)}) collective-permute-start(bf16[384,1536]{1,0:T(8,128)(2,1)S(1)} %dequantize.1.w0), channel_id=1, source_target_pairs={{0,1},{1,2},{2,3},{3,0},{4,5},{5,6},{6,7},{7,4},{8,9},{9,10},{10,1... | collective-permute-start | bytes 3538952 | tf_op jit(solution)/shard_map/ppermute | solution.py:54
  8.9 21.0 %collective-permute-start.1 = (bf16[128,1536]{1,0:T(8,128)(2,1)S(1)}, bf16[128,1536]{1,0:T(8,128)(2,1)S(1)}, u32[]{:S(2)}, u32[]{:S(2)}) collective-permute-start(bf16[128,1536]{1,0:T(8,128)(2,1)S(1)} %constant_dynamic-slice_fusion), channel_id=1, source_target_pairs={{0,20},{1,21},{2,22},{3,23},{4,16},{5,17},{6,18},{7,19},{8,28},{9,... | collective-permute-start | bytes 1179656 | tf_op jit(solution)/shard_map/ppermute | solution.py:54
  11.0 18.9 %collective-permute-start.5 = (bf16[128,3072]{1,0:T(8,128)(2,1)S(1)}, bf16[128,3072]{1,0:T(8,128)(2,1)S(1)}, u32[]{:S(2)}, u32[]{:S(2)}) collective-permute-start(bf16[128,3072]{1,0:T(8,128)(2,1)S(1)} %copy-done.2), channel_id=1, source_target_pairs={{0,8},{1,9},{2,10},{3,11},{4,12},{5,13},{6,14},{7,15},{8,0},{9,1},... | collective-permute-start | bytes 2359304 | tf_op jit(solution)/shard_map/ppermute | solution.py:54
  22.6 13.9 %collective-permute-start.7 = (bf16[128,3072]{1,0:T(8,128)(2,1)S(1)}, bf16[128,3072]{1,0:T(8,128)(2,1)S(1)}, u32[]{:S(2)}, u32[]{:S(2)}) collective-permute-start(bf16[128,3072]{1,0:T(8,128)(2,1)S(1)} %collective-permute-done.6.cot2), channel_id=1, source_target_pairs={{0,8},{1,9},{2,10},{3,11},{4,12},{5,13},{6,14},{7,15},{8,0},{9,1},... | collective-permute-start | bytes 2359304 | tf_op jit(solution)/shard_map/ppermute | solution.py:54
  29.8 6.6 %collective-permute-start = (bf16[128,3072]{1,0:T(8,128)(2,1)S(1)}, bf16[128,3072]{1,0:T(8,128)(2,1)S(1)}, u32[]{:S(2)}, u32[]{:S(2)}) collective-permute-start(bf16[128,3072]{1,0:T(8,128)(2,1)S(1)} %copy-done.1), channel_id=1, source_target_pairs={{0,8},{1,9},{2,10},{3,11},{4,12},{5,13},{6,14},{7,15},{8,0},{9,1},... | collective-permute-start | bytes 2359304 | tf_op jit(solution)/shard_map/ppermute | solution.py:54
  29.9 6.6 %collective-permute-start.2 = (bf16[128,1536]{1,0:T(8,128)(2,1)S(1)}, bf16[128,1536]{1,0:T(8,128)(2,1)S(1)}, u32[]{:S(2)}, u32[]{:S(2)}) collective-permute-start(bf16[128,1536]{1,0:T(8,128)(2,1)S(1)} %collective-permute-done.1.pair), channel_id=1, source_target_pairs={{0,8},{1,9},{2,10},{3,11},{4,12},{5,13},{6,14},{7,15},{8,0},{9,1},... | collective-permute-start | bytes 1179656 | tf_op jit(solution)/shard_map/ppermute | solution.py:54
  39.1 10.8 %collective-permute-start.9 = (bf16[48,3072]{1,0:T(8,128)(2,1)S(1)}, bf16[48,3072]{1,0:T(8,128)(2,1)S(1)}, u32[]{:S(2)}, u32[]{:S(2)}) collective-permute-start(bf16[48,3072]{1,0:T(8,128)(2,1)S(1)} %get-tuple-element.73), channel_id=1, source_target_pairs={{0,224},{1,225},{2,226},{3,227},{4,228},{5,229},{6,230},{7,231},{8... | collective-permute-start | bytes 884744 | tf_op jit(solution)/shard_map/ppermute | solution.py:54
  45.1 8.7 %collective-permute-start.8 = (bf16[48,3072]{1,0:T(8,128)(2,1)S(1)}, bf16[48,3072]{1,0:T(8,128)(2,1)S(1)}, u32[]{:S(2)}, u32[]{:S(2)}) collective-permute-start(bf16[48,3072]{1,0:T(8,128)(2,1)S(1)} %get-tuple-element.67), channel_id=1, source_target_pairs={{0,32},{1,33},{2,34},{3,35},{4,36},{5,37},{6,38},{7,39},{8,40},{9,... | collective-permute-start | bytes 884744 | tf_op jit(solution)/shard_map/ppermute | solution.py:54
  50.1 14.0 %collective-permute-start.13 = (bf16[96,3072]{1,0:T(8,128)(2,1)S(1)}, bf16[96,3072]{1,0:T(8,128)(2,1)S(1)}, u32[]{:S(2)}, u32[]{:S(2)}) collective-permute-start(bf16[96,3072]{1,0:T(8,128)(2,1)S(1)} %hop.7), channel_id=1, source_target_pairs={{0,224},{1,225},{2,226},{3,227},{4,228},{5,229},{6,230},{7,231},{8... | collective-permute-start | bytes 1769480 | tf_op jit(solution)/shard_map/ppermute | solution.py:54
  53.9 14.3 %collective-permute-start.12 = (bf16[96,3072]{1,0:T(8,128)(2,1)S(1)}, bf16[96,3072]{1,0:T(8,128)(2,1)S(1)}, u32[]{:S(2)}, u32[]{:S(2)}) collective-permute-start(bf16[96,3072]{1,0:T(8,128)(2,1)S(1)} %hop.6), channel_id=1, source_target_pairs={{0,32},{1,33},{2,34},{3,35},{4,36},{5,37},{6,38},{7,39},{8,40},{9,... | collective-permute-start | bytes 1769480 | tf_op jit(solution)/shard_map/ppermute | solution.py:54
  56.2 12.6 %collective-permute-start.11 = (bf16[384,768]{1,0:T(8,128)(2,1)S(1)}, bf16[384,768]{1,0:T(8,128)(2,1)S(1)}, u32[]{:S(2)}, u32[]{:S(2)}) collective-permute-start(bf16[384,768]{1,0:T(8,128)(2,1)S(1)} %slice.21), channel_id=1, source_target_pairs={{0,3},{1,0},{2,1},{3,2},{4,7},{5,4},{6,5},{7,6},{8,11},{9,8},{10,9... | collective-permute-start | bytes 1769480 | tf_op jit(solution)/shard_map/ppermute | solution.py:54
  57.0 13.8 %collective-permute-start.10 = (bf16[384,768]{1,0:T(8,128)(2,1)S(1)}, bf16[384,768]{1,0:T(8,128)(2,1)S(1)}, u32[]{:S(2)}, u32[]{:S(2)}) collective-permute-start(bf16[384,768]{1,0:T(8,128)(2,1)S(1)} %slice.20), channel_id=1, source_target_pairs={{0,1},{1,2},{2,3},{3,0},{4,5},{5,6},{6,7},{7,4},{8,9},{9,10},{10,1... | collective-permute-start | bytes 1769480 | tf_op jit(solution)/shard_map/ppermute | solution.py:54
  64.2 14.1 %collective-permute-start.17 = (bf16[96,3072]{1,0:T(8,128)(2,1)S(1)}, bf16[96,3072]{1,0:T(8,128)(2,1)S(1)}, u32[]{:S(2)}, u32[]{:S(2)}) collective-permute-start(bf16[96,3072]{1,0:T(8,128)(2,1)S(1)} %hop.9), channel_id=1, source_target_pairs={{0,224},{1,225},{2,226},{3,227},{4,228},{5,229},{6,230},{7,231},{8... | collective-permute-start | bytes 1769480 | tf_op jit(solution)/shard_map/ppermute | solution.py:54
  68.3 13.3 %collective-permute-start.15 = (bf16[96,3072]{1,0:T(8,128)(2,1)S(1)}, bf16[96,3072]{1,0:T(8,128)(2,1)S(1)}, u32[]{:S(2)}, u32[]{:S(2)}) collective-permute-start(bf16[96,3072]{1,0:T(8,128)(2,1)S(1)} %hop.8), channel_id=1, source_target_pairs={{0,32},{1,33},{2,34},{3,35},{4,36},{5,37},{6,38},{7,39},{8,40},{9,... | collective-permute-start | bytes 1769480 | tf_op jit(solution)/shard_map/ppermute | solution.py:54
  75.8 17.2 %collective-permute-start.14 = (bf16[256,1536]{1,0:T(8,128)(2,1)S(1)}, bf16[256,1536]{1,0:T(8,128)(2,1)S(1)}, u32[]{:S(2)}, u32[]{:S(2)}) collective-permute-start(bf16[256,1536]{1,0:T(8,128)(2,1)S(1)} %get-tuple-element.85), channel_id=1, source_target_pairs={{0,20},{1,21},{2,22},{3,23},{4,16},{5,17},{6,18},{7,19},{8,28},{9,... | collective-permute-start | bytes 2359304 | tf_op jit(solution)/shard_map/ppermute | solution.py:54
  78.5 14.7 %collective-permute-start.18 = (bf16[96,3072]{1,0:T(8,128)(2,1)S(1)}, bf16[96,3072]{1,0:T(8,128)(2,1)S(1)}, u32[]{:S(2)}, u32[]{:S(2)}) collective-permute-start(bf16[96,3072]{1,0:T(8,128)(2,1)S(1)} %hop.11), channel_id=1, source_target_pairs={{0,224},{1,225},{2,226},{3,227},{4,228},{5,229},{6,230},{7,231},{8... | collective-permute-start | bytes 1769480 | tf_op jit(solution)/shard_map/ppermute | solution.py:54
  81.7 12.1 %collective-permute-start.16 = (bf16[96,3072]{1,0:T(8,128)(2,1)S(1)}, bf16[96,3072]{1,0:T(8,128)(2,1)S(1)}, u32[]{:S(2)}, u32[]{:S(2)}) collective-permute-start(bf16[96,3072]{1,0:T(8,128)(2,1)S(1)} %hop.10), channel_id=1, source_target_pairs={{0,32},{1,33},{2,34},{3,35},{4,36},{5,37},{6,38},{7,39},{8,40},{9,... | collective-permute-start | bytes 1769480 | tf_op jit(solution)/shard_map/ppermute | solution.py:54
  86.9 16.7 %collective-permute-start.22 = (bf16[256,1536]{1,0:T(8,128)(2,1)S(1)}, bf16[256,1536]{1,0:T(8,128)(2,1)S(1)}, u32[]{:S(2)}, u32[]{:S(2)}) collective-permute-start(bf16[256,1536]{1,0:T(8,128)(2,1)S(1)} %get-tuple-element.104), channel_id=1, source_target_pairs={{0,8},{1,9},{2,10},{3,11},{4,12},{5,13},{6,14},{7,15},{8,0},{9,1},... | collective-permute-start | bytes 2359304 | tf_op jit(solution)/shard_map/ppermute | solution.py:54
  95.0 9.0 %collective-permute-start.19 = (bf16[24,3072]{1,0:T(8,128)(2,1)S(1)}, bf16[24,3072]{1,0:T(8,128)(2,1)S(1)}, u32[]{:S(2)}, u32[]{:S(2)}) collective-permute-start(bf16[24,3072]{1,0:T(8,128)(2,1)S(1)} %get-tuple-element.101), channel_id=1, source_target_pairs={{0,1},{1,2},{2,3},{3,0},{4,5},{5,6},{6,7},{7,4},{8,9},{9,10},{10,1... | collective-permute-start | bytes 442376 | tf_op jit(solution)/shard_map/ppermute | solution.py:54
  95.3 9.4 %collective-permute-start.20 = (bf16[24,3072]{1,0:T(8,128)(2,1)S(1)}, bf16[24,3072]{1,0:T(8,128)(2,1)S(1)}, u32[]{:S(2)}, u32[]{:S(2)}) collective-permute-start(bf16[24,3072]{1,0:T(8,128)(2,1)S(1)} %get-tuple-element.102), channel_id=1, source_target_pairs={{0,2},{1,3},{2,0},{3,1},{4,6},{5,7},{6,4},{7,5},{8,10},{9,11},{10,... | collective-permute-start | bytes 442376 | tf_op jit(solution)/shard_map/ppermute | solution.py:54
  100.1 5.2 %collective-permute-start.21 = (bf16[24,3072]{1,0:T(8,128)(2,1)S(1)}, bf16[24,3072]{1,0:T(8,128)(2,1)S(1)}, u32[]{:S(2)}, u32[]{:S(2)}) collective-permute-start(bf16[24,3072]{1,0:T(8,128)(2,1)S(1)} %get-tuple-element.103), channel_id=1, source_target_pairs={{0,3},{1,0},{2,1},{3,2},{4,7},{5,4},{6,5},{7,6},{8,11},{9,8},{10,9... | collective-permute-start | bytes 442376 | tf_op jit(solution)/shard_map/ppermute | solution.py:54
  103.6 10.9 %collective-permute-start.23 = (bf16[128,1536]{1,0:T(8,128)(2,1)}, bf16[128,1536]{1,0:T(8,128)(2,1)S(1)}, u32[]{:S(2)}, u32[]{:S(2)}) collective-permute-start(bf16[128,1536]{1,0:T(8,128)(2,1)} %get-tuple-element.118), channel_id=1, source_target_pairs={{0,8},{1,9},{2,10},{3,11},{4,12},{5,13},{6,14},{7,15},{8,0},{9,1},... | collective-permute-start | bytes 1179656 | tf_op jit(solution)/shard_map/ppermute | solution.py:54
  103.9 15.9 %collective-permute-start.24 = (bf16[128,1536]{1,0:T(8,128)(2,1)S(1)}, bf16[128,1536]{1,0:T(8,128)(2,1)S(1)}, u32[]{:S(2)}, u32[]{:S(2)}) collective-permute-start(bf16[128,1536]{1,0:T(8,128)(2,1)S(1)} %get-tuple-element.120), channel_id=1, source_target_pairs={{0,20},{1,21},{2,22},{3,23},{4,16},{5,17},{6,18},{7,19},{8,28},{9,... | collective-permute-start | bytes 1179656 | tf_op jit(solution)/shard_map/ppermute | solution.py:54
  106.0 14.8 %collective-permute-start.25 = (bf16[12,3072]{1,0:T(8,128)(2,1)S(1)}, bf16[12,3072]{1,0:T(8,128)(2,1)S(1)}, u32[]{:S(2)}, u32[]{:S(2)}) collective-permute-start(bf16[12,3072]{1,0:T(8,128)(2,1)S(1)} %get-tuple-element.110), channel_id=1, source_target_pairs={{0,24},{1,25},{2,26},{3,27},{4,184},{5,185},{6,186},{7,187},{8,72}... | collective-permute-start | bytes 221192 | tf_op jit(solution)/shard_map/ppermute | solution.py:54
  107.9 12.8 %collective-permute-start.26 = (bf16[12,3072]{1,0:T(8,128)(2,1)S(1)}, bf16[12,3072]{1,0:T(8,128)(2,1)S(1)}, u32[]{:S(2)}, u32[]{:S(2)}) collective-permute-start(bf16[12,3072]{1,0:T(8,128)(2,1)S(1)} %get-tuple-element.114), channel_id=1, source_target_pairs={{0,28},{1,29},{2,30},{3,31},{4,188},{5,189},{6,190},{7,191},{8,76}... | collective-permute-start | bytes 221192 | tf_op jit(solution)/shard_map/ppermute | solution.py:54

commit v8 on v7

--- a/solution.py
+++ b/solution.py
@@ -387,8 +387,8 @@
     token_parts = (tokens, token_sib, token_pair, send(token_pair, CORE))
     cot_parts = (cotangent, cot_sib, cot_pair, send(cot_pair, CORE))
 
-    up, down = gradient(where, token_parts, after(cot_parts, left, right), True)
-    grad = gradient(where, token_parts, after(cot_parts, up), False)
+    up, down = gradient(where, token_parts, cot_parts, True)
+    grad = gradient(where, token_parts, after(cot_parts, up, left, right), False)
     half = own.shape[1] // 2
     up, down = send(up, Z_UP), send(down, Z_DOWN)
     up = hop(grad[0], up, kernel=functools.partial(first_hop_kernel, upper=True))

time: 122 us -> 144 us (1.18)
  waiting for transfers between devices: 45.2 us -> 74.2 us
  starting transfers between devices: 44.8 us -> 41 us
  local copies, waits for them, and re-layouts: 4.78 us -> 2.66 us
  Pallas kernels: 21.7 us -> 19.7 us
    ppermute x27, waiting for transfers between devices: 45.2 us -> 74.2 us  [send(): return lax.ppermute(value, AXES, pairs)]
    ppermute x27, starting transfers between devices: 44.8 us -> 41 us  [send(): return lax.ppermute(value, AXES, pairs)]
    pallas_call x7, Pallas kernels: 21 us -> 19 us  [call(): pl.pallas_call(kernel, name=name, grid_spec=pltpu.PrefetchScalarGridSpec(...]
  transfers between devices with their start and end apart: 27 -> 27, of which waited for: 12 -> 14; matrix products, arithmetic and copies ran while one was open for 5% -> 3% of each run, Pallas kernels for 16% -> 14%
where the time goes in v8:
time: 144 us
  waiting for transfers between devices  74.2 us (52%)
  starting transfers between devices  41 us (28%)
  Pallas kernels  19.7 us (14%)
  other arithmetic  5.26 us (4%)
  local copies, waits for them, and re-layouts  2.66 us (2%)
    ppermute x27, waiting for transfers between devices, send(): return lax.ppermute(value, AXES, pairs)  74.2 us
    ppermute x27, starting transfers between devices, send(): return lax.ppermute(value, AXES, pairs)  41 us
    pallas_call x7, Pallas kernels, call(): pl.pallas_call(kernel, name=name, grid_spec=pltpu.PrefetchScalarGridSpec(...  19 us
    select_n x2, other arithmetic, joined(): jnp.where(flag == 0, jnp.concatenate([here, there], axis=1), jnp.concaten...  3.24 us
  transfers between devices with their start and end apart: 27, of which 14 were waited for; matrix products, arithmetic and copies ran while one was open for 3% of the time, Pallas kernels for 14%

profile of v8, /device:TPU:24, one launch (start us, length us, event | category | flops | bytes accessed | tf_op | source)
XLA Modules:
  0.0 143.7 jit_solution(4414735705521659139)
XLA Ops:
  0.6 2.0 %collective-permute-start.6 = (bf16[128,3072]{1,0:T(8,128)(2,1)}, bf16[128,3072]{1,0:T(8,128)(2,1)S(1)}, u32[]{:S(2)}, u32[]{:S(2)}) collective-permute-start(bf16[128,3072]{1,0:T(8,128)(2,1)} %cot0.4), channel_id=1, source_target_pairs={{0,20},{1,21},{2,22},{3,23},{4,16},{5,17},{6,18},{7,19},{8,28},{9,... | collective-permute-start | bytes 2359304 | tf_op jit(solution)/shard_map/ppermute | solution.py:54
  2.7 0.1 stack.23.where
  2.8 1.7 %copy-done = bf16[384,3072]{1,0:T(8,128)(2,1)S(1)} copy-done((bf16[384,3072]{1,0:T(8,128)(2,1)S(1)}, bf16[384,3072]{1,0:T(8,128)(2,1)}, u32[]{:S(2)}) %copy-start) | copy-done | bytes 2359320
  4.4 0.7 copy-done.3
  5.2 1.6 %dequantize.1.w0 = bf16[384,1536]{1,0:T(8,128)(2,1)S(1)} custom-call(s32[5]{0:T(128)S(1)} %stack.23.where, bf16[384,3072]{1,0:T(8,128)(2,1)S(1)} %copy-done, f32[12,384]{1,0:T(8,128)S(1)} %bitcast.6), custom_call_target="tpu_custom_call" | custom-call | flops 589824 | bytes 3557376 | tf_op jit(solution)/shard_map/dequantize/pallas_call | solution.py:72
  6.8 1.4 collective-permute-start.1
  8.2 21.7 %collective-permute-done.1.pair = bf16[128,1536]{1,0:T(8,128)(2,1)S(1)} collective-permute-done((bf16[128,1536]{1,0:T(8,128)(2,1)S(1)}, bf16[128,1536]{1,0:T(8,128)(2,1)S(1)}, u32[]{:S(2)}, u32[]{:S(2)}) %collective-permute-start.1) | collective-permute-done | bytes 393248 | tf_op jit(solution)/shard_map/ppermute | solution.py:54
  29.8 0.0 collective-permute-start.2
  29.8 2.8 %collective-permute-start.4 = (bf16[384,1536]{1,0:T(8,128)(2,1)S(1)}, bf16[384,1536]{1,0:T(8,128)(2,1)S(1)}, u32[]{:S(2)}, u32[]{:S(2)}) collective-permute-start(bf16[384,1536]{1,0:T(8,128)(2,1)S(1)} %dequantize.1.w0), channel_id=1, source_target_pairs={{0,3},{1,0},{2,1},{3,2},{4,7},{5,4},{6,5},{7,6},{8,11},{9,8},{10,9... | collective-permute-start | bytes 3538952 | tf_op jit(solution)/shard_map/ppermute | solution.py:54
  32.6 0.2 collective-permute-start
  32.8 0.0 collective-permute-done.6.cot2
  32.8 0.3 collective-permute-start.5
  33.1 0.0 collective-permute-done.2.psib
  33.1 0.2 collective-permute-start.7
  33.4 1.5 %collective-permute-done.sib = bf16[128,3072]{1,0:T(8,128)(2,1)S(1)} collective-permute-done((bf16[128,3072]{1,0:T(8,128)(2,1)S(1)}, bf16[128,3072]{1,0:T(8,128)(2,1)S(1)}, u32[]{:S(2)}, u32[]{:S(2)}) %collective-permute-start) | collective-permute-done | bytes 786464 | tf_op jit(solution)/shard_map/ppermute | solution.py:54
  34.9 1.1 collective-permute-done.5.cot1
  36.0 1.1 collective-permute-done.7.cot3
  37.1 2.7 %far.1 = (bf16[48,3072]{1,0:T(8,128)(2,1)S(1)}, bf16[48,3072]{1,0:T(8,128)(2,1)S(1)}) custom-call(s32[5]{0:T(128)S(1)} %stack.23.where, bf16[128,3072]{1,0:T(8,128)(2,1)S(1)} %copy-done.1, bf16[128,3072]{1,0:T(8,128)(2,1)S(1)} %collective-permute-done.sib, bf16[128,1536]{1,0:T(8,128)(2,1)S(1)} %collective-permute-done.1.pair, ...), custom_call_target="tpu_custom_call" | custom-call | flops 805306368 | bytes 6094848 | tf_op jit(solution)/shard_map/far/pallas_call | solution.py:72
  39.8 5.9 %collective-permute-start.9 = (bf16[48,3072]{1,0:T(8,128)(2,1)S(1)}, bf16[48,3072]{1,0:T(8,128)(2,1)S(1)}, u32[]{:S(2)}, u32[]{:S(2)}) collective-permute-start(bf16[48,3072]{1,0:T(8,128)(2,1)S(1)} %get-tuple-element.65), channel_id=1, source_target_pairs={{0,224},{1,225},{2,226},{3,227},{4,228},{5,229},{6,230},{7,231},{8... | collective-permute-start | bytes 884744 | tf_op jit(solution)/shard_map/ppermute | solution.py:54
  45.8 0.0 collective-permute-start.8
  45.8 12.7 %collective-permute-done.4.w2 = bf16[384,1536]{1,0:T(8,128)(2,1)S(1)} collective-permute-done((bf16[384,1536]{1,0:T(8,128)(2,1)S(1)}, bf16[384,1536]{1,0:T(8,128)(2,1)S(1)}, u32[]{:S(2)}, u32[]{:S(2)}) %collective-permute-start.4) | collective-permute-done | bytes 1179680 | tf_op jit(solution)/shard_map/ppermute | solution.py:54
  58.5 3.4 %collective-permute-done.3.w1 = bf16[384,1536]{1,0:T(8,128)(2,1)S(1)} collective-permute-done((bf16[384,1536]{1,0:T(8,128)(2,1)S(1)}, bf16[384,1536]{1,0:T(8,128)(2,1)S(1)}, u32[]{:S(2)}, u32[]{:S(2)}) %collective-permute-start.3) | collective-permute-done | bytes 1179680 | tf_op jit(solution)/shard_map/ppermute | solution.py:54
  61.9 4.9 %gradient.1 = (bf16[96,3072]{1,0:T(8,128)(2,1)S(1)}, bf16[96,3072]{1,0:T(8,128)(2,1)S(1)}, bf16[96,3072]{1,0:T(8,128)(2,1)S(1)}, bf16[96,3072]{1,0:T(8,128)(2,1)...) custom-call(s32[5]{0:T(128)S(1)} %stack.23.where, ...), custom_call_target="tpu_custom_call" | custom-call | flops 2415919104 | bytes 9633792 | tf_op jit(solution)/shard_map/gradient/pallas_call | solution.py:72
  66.8 0.1 hop.7
  66.9 5.9 %collective-permute-start.13 = (bf16[96,3072]{1,0:T(8,128)(2,1)S(1)}, bf16[96,3072]{1,0:T(8,128)(2,1)S(1)}, u32[]{:S(2)}, u32[]{:S(2)}) collective-permute-start(bf16[96,3072]{1,0:T(8,128)(2,1)S(1)} %hop.7), channel_id=1, source_target_pairs={{0,224},{1,225},{2,226},{3,227},{4,228},{5,229},{6,230},{7,231},{8... | collective-permute-start | bytes 1769480 | tf_op jit(solution)/shard_map/ppermute | solution.py:54
  72.8 0.1 hop.6
  72.9 0.1 collective-permute-start.12
  73.1 0.4 collective-permute-start.11
  73.5 1.7 %collective-permute-start.10 = (bf16[384,768]{1,0:T(8,128)(2,1)S(1)}, bf16[384,768]{1,0:T(8,128)(2,1)S(1)}, u32[]{:S(2)}, u32[]{:S(2)}) collective-permute-start(bf16[384,768]{1,0:T(8,128)(2,1)S(1)} %slice.20), channel_id=1, source_target_pairs={{0,1},{1,2},{2,3},{3,0},{4,5},{5,6},{6,7},{7,4},{8,9},{9,10},{10,1... | collective-permute-start | bytes 1769480 | tf_op jit(solution)/shard_map/ppermute | solution.py:54
  75.2 9.8 %collective-permute-done.13.refs_0_ = bf16[96,3072]{1,0:T(8,128)(2,1)S(1)} collective-permute-done((bf16[96,3072]{1,0:T(8,128)(2,1)S(1)}, bf16[96,3072]{1,0:T(8,128)(2,1)S(1)}, u32[]{:S(2)}, u32[]{:S(2)}) %collective-permute-start.13) | collective-permute-done | bytes 589856 | tf_op jit(solution)/shard_map/ppermute | solution.py:54
  85.0 0.1 hop.9
  85.1 3.9 %collective-permute-start.17 = (bf16[96,3072]{1,0:T(8,128)(2,1)S(1)}, bf16[96,3072]{1,0:T(8,128)(2,1)S(1)}, u32[]{:S(2)}, u32[]{:S(2)}) collective-permute-start(bf16[96,3072]{1,0:T(8,128)(2,1)S(1)} %hop.9), channel_id=1, source_target_pairs={{0,224},{1,225},{2,226},{3,227},{4,228},{5,229},{6,230},{7,231},{8... | collective-permute-start | bytes 1769480 | tf_op jit(solution)/shard_map/ppermute | solution.py:54
  89.1 0.1 hop.8
  89.2 0.1 collective-permute-start.15
  89.3 4.0 %forward.1 = (f32[128,1536]{1,0:T(8,128)S(1)}, f32[128,1536]{1,0:T(8,128)S(1)}, bf16[256,1536]{1,0:T(8,128)(2,1)S(1)}) custom-call(s32[5]{0:T(128)S(1)} %stack.23.where, bf16[128,3072]{1,0:T(8,128)(2,1)S(1)} %copy-done.1, bf16[128,3072]{1,0:T(8,128)(2,1)S(1)} %collective-permute-done.sib, bf16[128,1536]{1,0:T(8,128)(2,1)S(1)} %collective-permute-done.1.pair, ...), custom_call_target="tpu_custom_call" | custom-call | flops 2415919104 | bytes 9437184 | tf_op jit(solution)/shard_map/forward/pallas_call | solution.py:72
  93.3 0.4 collective-permute-start.14
  93.7 6.6 %collective-permute-done.17.refs_0_ = bf16[96,3072]{1,0:T(8,128)(2,1)S(1)} collective-permute-done((bf16[96,3072]{1,0:T(8,128)(2,1)S(1)}, bf16[96,3072]{1,0:T(8,128)(2,1)S(1)}, u32[]{:S(2)}, u32[]{:S(2)}) %collective-permute-start.17) | collective-permute-done | bytes 589856 | tf_op jit(solution)/shard_map/ppermute | solution.py:54
  100.3 0.1 hop.11
  100.5 3.8 %collective-permute-start.18 = (bf16[96,3072]{1,0:T(8,128)(2,1)S(1)}, bf16[96,3072]{1,0:T(8,128)(2,1)S(1)}, u32[]{:S(2)}, u32[]{:S(2)}) collective-permute-start(bf16[96,3072]{1,0:T(8,128)(2,1)S(1)} %hop.11), channel_id=1, source_target_pairs={{0,224},{1,225},{2,226},{3,227},{4,228},{5,229},{6,230},{7,231},{8... | collective-permute-start | bytes 1769480 | tf_op jit(solution)/shard_map/ppermute | solution.py:54
  104.2 0.1 hop.10
  104.4 0.1 collective-permute-start.16
  104.5 4.0 %backward.1 = (f32[256,1536]{1,0:T(8,128)S(1)}, bf16[256,1536]{1,0:T(8,128)(2,1)S(1)}) custom-call(s32[5]{0:T(128)S(1)} %stack.23.where, bf16[128,3072]{1,0:T(8,128)(2,1)S(1)} %copy-done.2, bf16[128,3072]{1,0:T(8,128)(2,1)S(1)} %collective-permute-done.5.cot1, bf16[128,3072]{1,0:T(8,128)(2,1)S(1)} %collective-permute-done.6.cot2, ...), custom_call_target="tpu_custom_call" | custom-call | flops 2415919104 | bytes 10223616 | tf_op jit(solution)/shard_map/backward/pallas_call | solution.py:72
  108.5 0.1 collective-permute-start.22
  108.6 3.6 %collective-permute-done.14 = bf16[256,1536]{1,0:T(8,128)(2,1)S(1)} collective-permute-done((bf16[256,1536]{1,0:T(8,128)(2,1)S(1)}, bf16[256,1536]{1,0:T(8,128)(2,1)S(1)}, u32[]{:S(2)}, u32[]{:S(2)}) %collective-permute-start.14) | collective-permute-done | bytes 786464 | tf_op jit(solution)/shard_map/ppermute | solution.py:54
  112.3 0.2 convert_element_type.20
  112.4 2.1 %collective-permute-done.18.down = bf16[96,3072]{1,0:T(8,128)(2,1)S(1)} collective-permute-done((bf16[96,3072]{1,0:T(8,128)(2,1)S(1)}, bf16[96,3072]{1,0:T(8,128)(2,1)S(1)}, u32[]{:S(2)}, u32[]{:S(2)}) %collective-permute-start.18) | collective-permute-done | bytes 589856 | tf_op jit(solution)/shard_map/ppermute | solution.py:54
  114.5 3.6 %collective-permute-done.16.up = bf16[96,3072]{1,0:T(8,128)(2,1)S(1)} collective-permute-done((bf16[96,3072]{1,0:T(8,128)(2,1)S(1)}, bf16[96,3072]{1,0:T(8,128)(2,1)S(1)}, u32[]{:S(2)}, u32[]{:S(2)}) %collective-permute-start.16) | collective-permute-done | bytes 589856 | tf_op jit(solution)/shard_map/ppermute | solution.py:54
  118.2 1.2 last_hop.1
  119.3 0.2 collective-permute-start.19
  119.5 2.7 %collective-permute-start.20 = (bf16[24,3072]{1,0:T(8,128)(2,1)S(1)}, bf16[24,3072]{1,0:T(8,128)(2,1)S(1)}, u32[]{:S(2)}, u32[]{:S(2)}) collective-permute-start(bf16[24,3072]{1,0:T(8,128)(2,1)S(1)} %get-tuple-element.94), channel_id=1, source_target_pairs={{0,2},{1,3},{2,0},{3,1},{4,6},{5,7},{6,4},{7,5},{8,10},{9,11},{10,... | collective-permute-start | bytes 442376 | tf_op jit(solution)/shard_map/ppermute | solution.py:54
  122.2 0.5 collective-permute-start.21
  122.7 0.9 add_convert_fusion.2
  123.6 0.2 add_convert_fusion
  123.8 0.1 fusion
  123.9 0.4 collective-permute-start.24
  124.2 3.1 %collective-permute-done.19.one = bf16[24,3072]{1,0:T(8,128)(2,1)S(1)} collective-permute-done((bf16[24,3072]{1,0:T(8,128)(2,1)S(1)}, bf16[24,3072]{1,0:T(8,128)(2,1)S(1)}, u32[]{:S(2)}, u32[]{:S(2)}) %collective-permute-start.19) | collective-permute-done | bytes 147488 | tf_op jit(solution)/shard_map/ppermute | solution.py:54
  127.3 0.9 collective-permute-done.21.three
  128.2 0.7 sum_over_x.1
  128.9 1.9 %collective-permute-start.25 = (bf16[12,3072]{1,0:T(8,128)(2,1)S(1)}, bf16[12,3072]{1,0:T(8,128)(2,1)S(1)}, u32[]{:S(2)}, u32[]{:S(2)}) collective-permute-start(bf16[12,3072]{1,0:T(8,128)(2,1)S(1)} %get-tuple-element.102), channel_id=1, source_target_pairs={{0,24},{1,25},{2,26},{3,27},{4,184},{5,185},{6,186},{7,187},{8,72}... | collective-permute-start | bytes 221192 | tf_op jit(solution)/shard_map/ppermute | solution.py:54
  130.9 6.1 %collective-permute-start.26 = (bf16[12,3072]{1,0:T(8,128)(2,1)S(1)}, bf16[12,3072]{1,0:T(8,128)(2,1)S(1)}, u32[]{:S(2)}, u32[]{:S(2)}) collective-permute-start(bf16[12,3072]{1,0:T(8,128)(2,1)S(1)} %get-tuple-element.106), channel_id=1, source_target_pairs={{0,28},{1,29},{2,30},{3,31},{4,188},{5,189},{6,190},{7,191},{8,76}... | collective-permute-start | bytes 221192 | tf_op jit(solution)/shard_map/ppermute | solution.py:54
  137.0 2.2 %maximum_select_fusion = bf16[128,3072]{1,0:T(8,128)(2,1)} fusion(bf16[128,1536]{1,0:T(8,128)(2,1)} %collective-permute-done.23, bf16[128,1536]{1,0:T(8,128)(2,1)S(1)} %get-tuple-element.103, pred[]{:T(512)S(6)} %eq.8), kind=kLoop, calls=%fused_computation.1 | loop fusion | flops 3538944 | bytes 1572865 | tf_op jit(solution)/shard_map/jit(_where)/select_n | solution.py:366
  139.2 1.1 maximum_select_fusion.1
  140.2 2.8 %collective-permute-done.26 = bf16[12,3072]{1,0:T(8,128)(2,1)S(1)} collective-permute-done((bf16[12,3072]{1,0:T(8,128)(2,1)S(1)}, bf16[12,3072]{1,0:T(8,128)(2,1)S(1)}, u32[]{:S(2)}, u32[]{:S(2)}) %collective-permute-start.26) | collective-permute-done | bytes 73760 | tf_op jit(solution)/shard_map/ppermute | solution.py:54
  143.0 0.7 convert_add_fusion
  (22 shorter events, 0.2 us)
Async XLA Ops:
  0.6 32.2 %collective-permute-start.6 = (bf16[128,3072]{1,0:T(8,128)(2,1)}, bf16[128,3072]{1,0:T(8,128)(2,1)S(1)}, u32[]{:S(2)}, u32[]{:S(2)}) collective-permute-start(bf16[128,3072]{1,0:T(8,128)(2,1)} %cot0.4), channel_id=1, source_target_pairs={{0,20},{1,21},{2,22},{3,23},{4,16},{5,17},{6,18},{7,19},{8,28},{9,... | collective-permute-start | bytes 2359304 | tf_op jit(solution)/shard_map/ppermute | solution.py:54
  2.8 1.7 %copy-start = (bf16[384,3072]{1,0:T(8,128)(2,1)S(1)}, bf16[384,3072]{1,0:T(8,128)(2,1)}, u32[]{:S(2)}) copy-start(bf16[384,3072]{1,0:T(8,128)(2,1)} %levels.1) | copy-start | bytes 7077892
  4.4 0.7 copy-start.3
  5.2 1.6 %copy-start.1 = (bf16[128,3072]{1,0:T(8,128)(2,1)S(1)}, bf16[128,3072]{1,0:T(8,128)(2,1)}, u32[]{:S(2)}) copy-start(bf16[128,3072]{1,0:T(8,128)(2,1)} %own.5) | copy-start | bytes 2359300
  5.2 27.7 %copy-start.2 = (bf16[128,3072]{1,0:T(8,128)(2,1)S(1)}, bf16[128,3072]{1,0:T(8,128)(2,1)}, u32[]{:S(2)}) copy-start(bf16[128,3072]{1,0:T(8,128)(2,1)} %cot0.4) | copy-start | bytes 2359300
  6.8 23.0 %collective-permute-start.1 = (bf16[128,1536]{1,0:T(8,128)(2,1)S(1)}, bf16[128,1536]{1,0:T(8,128)(2,1)S(1)}, u32[]{:S(2)}, u32[]{:S(2)}) collective-permute-start(bf16[128,1536]{1,0:T(8,128)(2,1)S(1)} %constant_dynamic-slice_fusion), channel_id=1, source_target_pairs={{0,20},{1,21},{2,22},{3,23},{4,16},{5,17},{6,18},{7,19},{8,28},{9,... | collective-permute-start | bytes 1179656 | tf_op jit(solution)/shard_map/ppermute | solution.py:54
  29.8 3.3 %collective-permute-start.2 = (bf16[128,1536]{1,0:T(8,128)(2,1)S(1)}, bf16[128,1536]{1,0:T(8,128)(2,1)S(1)}, u32[]{:S(2)}, u32[]{:S(2)}) collective-permute-start(bf16[128,1536]{1,0:T(8,128)(2,1)S(1)} %collective-permute-done.1.pair), channel_id=1, source_target_pairs={{0,8},{1,9},{2,10},{3,11},{4,12},{5,13},{6,14},{7,15},{8,0},{9,1},... | collective-permute-start | bytes 1179656 | tf_op jit(solution)/shard_map/ppermute | solution.py:54
  29.8 28.7 %collective-permute-start.4 = (bf16[384,1536]{1,0:T(8,128)(2,1)S(1)}, bf16[384,1536]{1,0:T(8,128)(2,1)S(1)}, u32[]{:S(2)}, u32[]{:S(2)}) collective-permute-start(bf16[384,1536]{1,0:T(8,128)(2,1)S(1)} %dequantize.1.w0), channel_id=1, source_target_pairs={{0,3},{1,0},{2,1},{3,2},{4,7},{5,4},{6,5},{7,6},{8,11},{9,8},{10,9... | collective-permute-start | bytes 3538952 | tf_op jit(solution)/shard_map/ppermute | solution.py:54
  32.6 29.3 %collective-permute-start.3 = (bf16[384,1536]{1,0:T(8,128)(2,1)S(1)}, bf16[384,1536]{1,0:T(8,128)(2,1)S(1)}, u32[]{:S(2)}, u32[]{:S(2)}) collective-permute-start(bf16[384,1536]{1,0:T(8,128)(2,1)S(1)} %dequantize.1.w0), channel_id=1, source_target_pairs={{0,1},{1,2},{2,3},{3,0},{4,5},{5,6},{6,7},{7,4},{8,9},{9,10},{10,1... | collective-permute-start | bytes 3538952 | tf_op jit(solution)/shard_map/ppermute | solution.py:54
  32.6 2.3 %collective-permute-start = (bf16[128,3072]{1,0:T(8,128)(2,1)S(1)}, bf16[128,3072]{1,0:T(8,128)(2,1)S(1)}, u32[]{:S(2)}, u32[]{:S(2)}) collective-permute-start(bf16[128,3072]{1,0:T(8,128)(2,1)S(1)} %copy-done.1), channel_id=1, source_target_pairs={{0,8},{1,9},{2,10},{3,11},{4,12},{5,13},{6,14},{7,15},{8,0},{9,1},... | collective-permute-start | bytes 2359304 | tf_op jit(solution)/shard_map/ppermute | solution.py:54
  32.8 3.2 %collective-permute-start.5 = (bf16[128,3072]{1,0:T(8,128)(2,1)S(1)}, bf16[128,3072]{1,0:T(8,128)(2,1)S(1)}, u32[]{:S(2)}, u32[]{:S(2)}) collective-permute-start(bf16[128,3072]{1,0:T(8,128)(2,1)S(1)} %copy-done.2), channel_id=1, source_target_pairs={{0,8},{1,9},{2,10},{3,11},{4,12},{5,13},{6,14},{7,15},{8,0},{9,1},... | collective-permute-start | bytes 2359304 | tf_op jit(solution)/shard_map/ppermute | solution.py:54
  33.1 4.0 %collective-permute-start.7 = (bf16[128,3072]{1,0:T(8,128)(2,1)S(1)}, bf16[128,3072]{1,0:T(8,128)(2,1)S(1)}, u32[]{:S(2)}, u32[]{:S(2)}) collective-permute-start(bf16[128,3072]{1,0:T(8,128)(2,1)S(1)} %collective-permute-done.6.cot2), channel_id=1, source_target_pairs={{0,8},{1,9},{2,10},{3,11},{4,12},{5,13},{6,14},{7,15},{8,0},{9,1},... | collective-permute-start | bytes 2359304 | tf_op jit(solution)/shard_map/ppermute | solution.py:54
  39.8 27.0 %collective-permute-start.9 = (bf16[48,3072]{1,0:T(8,128)(2,1)S(1)}, bf16[48,3072]{1,0:T(8,128)(2,1)S(1)}, u32[]{:S(2)}, u32[]{:S(2)}) collective-permute-start(bf16[48,3072]{1,0:T(8,128)(2,1)S(1)} %get-tuple-element.65), channel_id=1, source_target_pairs={{0,224},{1,225},{2,226},{3,227},{4,228},{5,229},{6,230},{7,231},{8... | collective-permute-start | bytes 884744 | tf_op jit(solution)/shard_map/ppermute | solution.py:54
  45.8 27.1 %collective-permute-start.8 = (bf16[48,3072]{1,0:T(8,128)(2,1)S(1)}, bf16[48,3072]{1,0:T(8,128)(2,1)S(1)}, u32[]{:S(2)}, u32[]{:S(2)}) collective-permute-start(bf16[48,3072]{1,0:T(8,128)(2,1)S(1)} %get-tuple-element.59), channel_id=1, source_target_pairs={{0,32},{1,33},{2,34},{3,35},{4,36},{5,37},{6,38},{7,39},{8,40},{9,... | collective-permute-start | bytes 884744 | tf_op jit(solution)/shard_map/ppermute | solution.py:54
  66.9 18.1 %collective-permute-start.13 = (bf16[96,3072]{1,0:T(8,128)(2,1)S(1)}, bf16[96,3072]{1,0:T(8,128)(2,1)S(1)}, u32[]{:S(2)}, u32[]{:S(2)}) collective-permute-start(bf16[96,3072]{1,0:T(8,128)(2,1)S(1)} %hop.7), channel_id=1, source_target_pairs={{0,224},{1,225},{2,226},{3,227},{4,228},{5,229},{6,230},{7,231},{8... | collective-permute-start | bytes 1769480 | tf_op jit(solution)/shard_map/ppermute | solution.py:54
  72.9 16.2 %collective-permute-start.12 = (bf16[96,3072]{1,0:T(8,128)(2,1)S(1)}, bf16[96,3072]{1,0:T(8,128)(2,1)S(1)}, u32[]{:S(2)}, u32[]{:S(2)}) collective-permute-start(bf16[96,3072]{1,0:T(8,128)(2,1)S(1)} %hop.6), channel_id=1, source_target_pairs={{0,32},{1,33},{2,34},{3,35},{4,36},{5,37},{6,38},{7,39},{8,40},{9,... | collective-permute-start | bytes 1769480 | tf_op jit(solution)/shard_map/ppermute | solution.py:54
  73.1 16.2 %collective-permute-start.11 = (bf16[384,768]{1,0:T(8,128)(2,1)S(1)}, bf16[384,768]{1,0:T(8,128)(2,1)S(1)}, u32[]{:S(2)}, u32[]{:S(2)}) collective-permute-start(bf16[384,768]{1,0:T(8,128)(2,1)S(1)} %slice.21), channel_id=1, source_target_pairs={{0,3},{1,0},{2,1},{3,2},{4,7},{5,4},{6,5},{7,6},{8,11},{9,8},{10,9... | collective-permute-start | bytes 1769480 | tf_op jit(solution)/shard_map/ppermute | solution.py:54
  73.5 15.9 %collective-permute-start.10 = (bf16[384,768]{1,0:T(8,128)(2,1)S(1)}, bf16[384,768]{1,0:T(8,128)(2,1)S(1)}, u32[]{:S(2)}, u32[]{:S(2)}) collective-permute-start(bf16[384,768]{1,0:T(8,128)(2,1)S(1)} %slice.20), channel_id=1, source_target_pairs={{0,1},{1,2},{2,3},{3,0},{4,5},{5,6},{6,7},{7,4},{8,9},{9,10},{10,1... | collective-permute-start | bytes 1769480 | tf_op jit(solution)/shard_map/ppermute | solution.py:54
  85.1 15.2 %collective-permute-start.17 = (bf16[96,3072]{1,0:T(8,128)(2,1)S(1)}, bf16[96,3072]{1,0:T(8,128)(2,1)S(1)}, u32[]{:S(2)}, u32[]{:S(2)}) collective-permute-start(bf16[96,3072]{1,0:T(8,128)(2,1)S(1)} %hop.9), channel_id=1, source_target_pairs={{0,224},{1,225},{2,226},{3,227},{4,228},{5,229},{6,230},{7,231},{8... | collective-permute-start | bytes 1769480 | tf_op jit(solution)/shard_map/ppermute | solution.py:54
  89.2 15.0 %collective-permute-start.15 = (bf16[96,3072]{1,0:T(8,128)(2,1)S(1)}, bf16[96,3072]{1,0:T(8,128)(2,1)S(1)}, u32[]{:S(2)}, u32[]{:S(2)}) collective-permute-start(bf16[96,3072]{1,0:T(8,128)(2,1)S(1)} %hop.8), channel_id=1, source_target_pairs={{0,32},{1,33},{2,34},{3,35},{4,36},{5,37},{6,38},{7,39},{8,40},{9,... | collective-permute-start | bytes 1769480 | tf_op jit(solution)/shard_map/ppermute | solution.py:54
  93.3 18.9 %collective-permute-start.14 = (bf16[256,1536]{1,0:T(8,128)(2,1)S(1)}, bf16[256,1536]{1,0:T(8,128)(2,1)S(1)}, u32[]{:S(2)}, u32[]{:S(2)}) collective-permute-start(bf16[256,1536]{1,0:T(8,128)(2,1)S(1)} %get-tuple-element.77), channel_id=1, source_target_pairs={{0,20},{1,21},{2,22},{3,23},{4,16},{5,17},{6,18},{7,19},{8,28},{9,... | collective-permute-start | bytes 2359304 | tf_op jit(solution)/shard_map/ppermute | solution.py:54
  100.5 14.1 %collective-permute-start.18 = (bf16[96,3072]{1,0:T(8,128)(2,1)S(1)}, bf16[96,3072]{1,0:T(8,128)(2,1)S(1)}, u32[]{:S(2)}, u32[]{:S(2)}) collective-permute-start(bf16[96,3072]{1,0:T(8,128)(2,1)S(1)} %hop.11), channel_id=1, source_target_pairs={{0,224},{1,225},{2,226},{3,227},{4,228},{5,229},{6,230},{7,231},{8... | collective-permute-start | bytes 1769480 | tf_op jit(solution)/shard_map/ppermute | solution.py:54
  104.4 13.8 %collective-permute-start.16 = (bf16[96,3072]{1,0:T(8,128)(2,1)S(1)}, bf16[96,3072]{1,0:T(8,128)(2,1)S(1)}, u32[]{:S(2)}, u32[]{:S(2)}) collective-permute-start(bf16[96,3072]{1,0:T(8,128)(2,1)S(1)} %hop.10), channel_id=1, source_target_pairs={{0,32},{1,33},{2,34},{3,35},{4,36},{5,37},{6,38},{7,39},{8,40},{9,... | collective-permute-start | bytes 1769480 | tf_op jit(solution)/shard_map/ppermute | solution.py:54
  108.5 15.1 %collective-permute-start.22 = (bf16[256,1536]{1,0:T(8,128)(2,1)S(1)}, bf16[256,1536]{1,0:T(8,128)(2,1)S(1)}, u32[]{:S(2)}, u32[]{:S(2)}) collective-permute-start(bf16[256,1536]{1,0:T(8,128)(2,1)S(1)} %get-tuple-element.96), channel_id=1, source_target_pairs={{0,8},{1,9},{2,10},{3,11},{4,12},{5,13},{6,14},{7,15},{8,0},{9,1},... | collective-permute-start | bytes 2359304 | tf_op jit(solution)/shard_map/ppermute | solution.py:54
  119.3 8.0 %collective-permute-start.19 = (bf16[24,3072]{1,0:T(8,128)(2,1)S(1)}, bf16[24,3072]{1,0:T(8,128)(2,1)S(1)}, u32[]{:S(2)}, u32[]{:S(2)}) collective-permute-start(bf16[24,3072]{1,0:T(8,128)(2,1)S(1)} %get-tuple-element.93), channel_id=1, source_target_pairs={{0,1},{1,2},{2,3},{3,0},{4,5},{5,6},{6,7},{7,4},{8,9},{9,10},{10,1... | collective-permute-start | bytes 442376 | tf_op jit(solution)/shard_map/ppermute | solution.py:54
  119.5 7.8 %collective-permute-start.20 = (bf16[24,3072]{1,0:T(8,128)(2,1)S(1)}, bf16[24,3072]{1,0:T(8,128)(2,1)S(1)}, u32[]{:S(2)}, u32[]{:S(2)}) collective-permute-start(bf16[24,3072]{1,0:T(8,128)(2,1)S(1)} %get-tuple-element.94), channel_id=1, source_target_pairs={{0,2},{1,3},{2,0},{3,1},{4,6},{5,7},{6,4},{7,5},{8,10},{9,11},{10,... | collective-permute-start | bytes 442376 | tf_op jit(solution)/shard_map/ppermute | solution.py:54
  122.2 6.1 %collective-permute-start.21 = (bf16[24,3072]{1,0:T(8,128)(2,1)S(1)}, bf16[24,3072]{1,0:T(8,128)(2,1)S(1)}, u32[]{:S(2)}, u32[]{:S(2)}) collective-permute-start(bf16[24,3072]{1,0:T(8,128)(2,1)S(1)} %get-tuple-element.95), channel_id=1, source_target_pairs={{0,3},{1,0},{2,1},{3,2},{4,7},{5,4},{6,5},{7,6},{8,11},{9,8},{10,9... | collective-permute-start | bytes 442376 | tf_op jit(solution)/shard_map/ppermute | solution.py:54
  123.6 13.4 %collective-permute-start.23 = (bf16[128,1536]{1,0:T(8,128)(2,1)}, bf16[128,1536]{1,0:T(8,128)(2,1)}, u32[]{:S(2)}, u32[]{:S(2)}) collective-permute-start(bf16[128,1536]{1,0:T(8,128)(2,1)} %get-tuple-element.110), channel_id=1, source_target_pairs={{0,8},{1,9},{2,10},{3,11},{4,12},{5,13},{6,14},{7,15},{8,0},{9,1},... | collective-permute-start | bytes 1179656 | tf_op jit(solution)/shard_map/ppermute | solution.py:54
  123.9 15.3 %collective-permute-start.24 = (bf16[128,1536]{1,0:T(8,128)(2,1)S(1)}, bf16[128,1536]{1,0:T(8,128)(2,1)S(1)}, u32[]{:S(2)}, u32[]{:S(2)}) collective-permute-start(bf16[128,1536]{1,0:T(8,128)(2,1)S(1)} %get-tuple-element.112), channel_id=1, source_target_pairs={{0,20},{1,21},{2,22},{3,23},{4,16},{5,17},{6,18},{7,19},{8,28},{9,... | collective-permute-start | bytes 1179656 | tf_op jit(solution)/shard_map/ppermute | solution.py:54
  128.9 14.1 %collective-permute-start.25 = (bf16[12,3072]{1,0:T(8,128)(2,1)S(1)}, bf16[12,3072]{1,0:T(8,128)(2,1)S(1)}, u32[]{:S(2)}, u32[]{:S(2)}) collective-permute-start(bf16[12,3072]{1,0:T(8,128)(2,1)S(1)} %get-tuple-element.102), channel_id=1, source_target_pairs={{0,24},{1,25},{2,26},{3,27},{4,184},{5,185},{6,186},{7,187},{8,72}... | collective-permute-start | bytes 221192 | tf_op jit(solution)/shard_map/ppermute | solution.py:54
  130.9 12.2 %collective-permute-start.26 = (bf16[12,3072]{1,0:T(8,128)(2,1)S(1)}, bf16[12,3072]{1,0:T(8,128)(2,1)S(1)}, u32[]{:S(2)}, u32[]{:S(2)}) collective-permute-start(bf16[12,3072]{1,0:T(8,128)(2,1)S(1)} %get-tuple-element.106), channel_id=1, source_target_pairs={{0,28},{1,29},{2,30},{3,31},{4,188},{5,189},{6,190},{7,191},{8,76}... | collective-permute-start | bytes 221192 | tf_op jit(solution)/shard_map/ppermute | solution.py:54

commit v9 on v8

--- a/solution.py
+++ b/solution.py
@@ -387,7 +387,7 @@
     token_parts = (tokens, token_sib, token_pair, send(token_pair, CORE))
     cot_parts = (cotangent, cot_sib, cot_pair, send(cot_pair, CORE))
 
-    up, down = gradient(where, token_parts, cot_parts, True)
+    up, down = gradient(where, token_parts, after(cot_parts, cotangent), True)
     grad = gradient(where, token_parts, after(cot_parts, up, left, right), False)
     half = own.shape[1] // 2
     up, down = send(up, Z_UP), send(down, Z_DOWN)

time: 144 us -> 124 us (0.86)
  waiting for transfers between devices: 74.2 us -> 52.5 us
    ppermute x27, waiting for transfers between devices: 74.2 us -> 52.5 us  [send(): return lax.ppermute(value, AXES, pairs)]
  transfers between devices with their start and end apart: 27 -> 27, of which waited for: 14 -> 15; matrix products, arithmetic and copies ran while one was open for 3% -> 4% of each run, Pallas kernels for 14% -> 16%
where the time goes in v9:
time: 124 us; the launch traced here: 123 us
  waiting for transfers between devices  52.5 us (42%)
  starting transfers between devices  42 us (34%)
  Pallas kernels  19.7 us (16%)
  other arithmetic  5.26 us (4%)
  local copies, waits for them, and re-layouts  2.66 us (2%)
    ppermute x27, waiting for transfers between devices, send(): return lax.ppermute(value, AXES, pairs)  52.5 us
    ppermute x27, starting transfers between devices, send(): return lax.ppermute(value, AXES, pairs)  42 us
    pallas_call x7, Pallas kernels, call(): pl.pallas_call(kernel, name=name, grid_spec=pltpu.PrefetchScalarGridSpec(...  19 us
    select_n x2, other arithmetic, joined(): jnp.where(flag == 0, jnp.concatenate([here, there], axis=1), jnp.concaten...  3.24 us
  transfers between devices with their start and end apart: 27, of which 15 were waited for; matrix products, arithmetic and copies ran while one was open for 4% of the time, Pallas kernels for 16%

profile of v9, /device:TPU:24, one launch (start us, length us, event | category | flops | bytes accessed | tf_op | source)
XLA Modules:
  0.0 123.0 jit_solution(8877748757813989262)
XLA Ops:
  0.6 2.0 %collective-permute-start.6 = (bf16[128,3072]{1,0:T(8,128)(2,1)}, bf16[128,3072]{1,0:T(8,128)(2,1)S(1)}, u32[]{:S(2)}, u32[]{:S(2)}) collective-permute-start(bf16[128,3072]{1,0:T(8,128)(2,1)} %cot0.3), channel_id=1, source_target_pairs={{0,20},{1,21},{2,22},{3,23},{4,16},{5,17},{6,18},{7,19},{8,28},{9,... | collective-permute-start | bytes 2359304 | tf_op jit(solution)/shard_map/ppermute | solution.py:54
  2.7 0.1 stack.23.where
  2.8 1.7 %copy-done = bf16[384,3072]{1,0:T(8,128)(2,1)S(1)} copy-done((bf16[384,3072]{1,0:T(8,128)(2,1)S(1)}, bf16[384,3072]{1,0:T(8,128)(2,1)}, u32[]{:S(2)}) %copy-start) | copy-done | bytes 2359320
  4.4 0.7 copy-done.3
  5.2 1.6 %dequantize.1.w0 = bf16[384,1536]{1,0:T(8,128)(2,1)S(1)} custom-call(s32[5]{0:T(128)S(1)} %stack.23.where, bf16[384,3072]{1,0:T(8,128)(2,1)S(1)} %copy-done, f32[12,384]{1,0:T(8,128)S(1)} %bitcast.6), custom_call_target="tpu_custom_call" | custom-call | flops 589824 | bytes 3557376 | tf_op jit(solution)/shard_map/dequantize/pallas_call | solution.py:72
  6.8 1.4 %collective-permute-start.1 = (bf16[128,1536]{1,0:T(8,128)(2,1)S(1)}, bf16[128,1536]{1,0:T(8,128)(2,1)S(1)}, u32[]{:S(2)}, u32[]{:S(2)}) collective-permute-start(bf16[128,1536]{1,0:T(8,128)(2,1)S(1)} %constant_dynamic-slice_fusion), channel_id=1, source_target_pairs={{0,20},{1,21},{2,22},{3,23},{4,16},{5,17},{6,18},{7,19},{8,28},{9,... | collective-permute-start | bytes 1179656 | tf_op jit(solution)/shard_map/ppermute | solution.py:54
  8.2 2.8 %collective-permute-start.4 = (bf16[384,1536]{1,0:T(8,128)(2,1)S(1)}, bf16[384,1536]{1,0:T(8,128)(2,1)S(1)}, u32[]{:S(2)}, u32[]{:S(2)}) collective-permute-start(bf16[384,1536]{1,0:T(8,128)(2,1)S(1)} %dequantize.1.w0), channel_id=1, source_target_pairs={{0,3},{1,0},{2,1},{3,2},{4,7},{5,4},{6,5},{7,6},{8,11},{9,8},{10,9... | collective-permute-start | bytes 3538952 | tf_op jit(solution)/shard_map/ppermute | solution.py:54
  10.9 0.0 collective-permute-start.3
  10.9 11.6 %collective-permute-done.6.cot2 = bf16[128,3072]{1,0:T(8,128)(2,1)S(1)} collective-permute-done((bf16[128,3072]{1,0:T(8,128)(2,1)}, bf16[128,3072]{1,0:T(8,128)(2,1)S(1)}, u32[]{:S(2)}, u32[]{:S(2)}) %collective-permute-start.6) | collective-permute-done | bytes 786464 | tf_op jit(solution)/shard_map/ppermute | solution.py:54
  22.6 0.0 collective-permute-start.7
  22.6 7.3 %collective-permute-done.1.pair = bf16[128,1536]{1,0:T(8,128)(2,1)S(1)} collective-permute-done((bf16[128,1536]{1,0:T(8,128)(2,1)S(1)}, bf16[128,1536]{1,0:T(8,128)(2,1)S(1)}, u32[]{:S(2)}, u32[]{:S(2)}) %collective-permute-start.1) | collective-permute-done | bytes 393248 | tf_op jit(solution)/shard_map/ppermute | solution.py:54
  29.8 0.0 collective-permute-start
  29.8 0.0 collective-permute-done.5.cot1
  29.9 0.5 collective-permute-start.2
  30.4 0.0 collective-permute-done.7.cot3
  30.4 2.3 %collective-permute-done.2.psib = bf16[128,1536]{1,0:T(8,128)(2,1)S(1)} collective-permute-done((bf16[128,1536]{1,0:T(8,128)(2,1)S(1)}, bf16[128,1536]{1,0:T(8,128)(2,1)S(1)}, u32[]{:S(2)}, u32[]{:S(2)}) %collective-permute-start.2) | collective-permute-done | bytes 393248 | tf_op jit(solution)/shard_map/ppermute | solution.py:54
  32.7 2.7 %far.1 = (bf16[48,3072]{1,0:T(8,128)(2,1)S(1)}, bf16[48,3072]{1,0:T(8,128)(2,1)S(1)}) custom-call(s32[5]{0:T(128)S(1)} %stack.23.where, bf16[128,3072]{1,0:T(8,128)(2,1)S(1)} %copy-done.1, bf16[128,3072]{1,0:T(8,128)(2,1)S(1)} %collective-permute-done.sib, bf16[128,1536]{1,0:T(8,128)(2,1)S(1)} %collective-permute-done.1.pair, ...), custom_call_target="tpu_custom_call" | custom-call | flops 805306368 | bytes 6094848 | tf_op jit(solution)/shard_map/far/pallas_call | solution.py:72
  35.4 5.9 %collective-permute-start.9 = (bf16[48,3072]{1,0:T(8,128)(2,1)S(1)}, bf16[48,3072]{1,0:T(8,128)(2,1)S(1)}, u32[]{:S(2)}, u32[]{:S(2)}) collective-permute-start(bf16[48,3072]{1,0:T(8,128)(2,1)S(1)} %get-tuple-element.73), channel_id=1, source_target_pairs={{0,224},{1,225},{2,226},{3,227},{4,228},{5,229},{6,230},{7,231},{8... | collective-permute-start | bytes 884744 | tf_op jit(solution)/shard_map/ppermute | solution.py:54
  41.3 0.0 collective-permute-done.4.w2
  41.3 4.9 %gradient.1 = (bf16[96,3072]{1,0:T(8,128)(2,1)S(1)}, bf16[96,3072]{1,0:T(8,128)(2,1)S(1)}, bf16[96,3072]{1,0:T(8,128)(2,1)S(1)}, bf16[96,3072]{1,0:T(8,128)(2,1)...) custom-call(s32[5]{0:T(128)S(1)} %stack.23.where, ...), custom_call_target="tpu_custom_call" | custom-call | flops 2415919104 | bytes 9633792 | tf_op jit(solution)/shard_map/gradient/pallas_call | solution.py:72
  46.2 1.7 %collective-permute-done.9.arrived = bf16[48,3072]{1,0:T(8,128)(2,1)S(1)} collective-permute-done((bf16[48,3072]{1,0:T(8,128)(2,1)S(1)}, bf16[48,3072]{1,0:T(8,128)(2,1)S(1)}, u32[]{:S(2)}, u32[]{:S(2)}) %collective-permute-start.9) | collective-permute-done | bytes 294944 | tf_op jit(solution)/shard_map/ppermute | solution.py:54
  47.9 0.1 hop.7
  48.0 3.8 %collective-permute-start.13 = (bf16[96,3072]{1,0:T(8,128)(2,1)S(1)}, bf16[96,3072]{1,0:T(8,128)(2,1)S(1)}, u32[]{:S(2)}, u32[]{:S(2)}) collective-permute-start(bf16[96,3072]{1,0:T(8,128)(2,1)S(1)} %hop.7), channel_id=1, source_target_pairs={{0,224},{1,225},{2,226},{3,227},{4,228},{5,229},{6,230},{7,231},{8... | collective-permute-start | bytes 1769480 | tf_op jit(solution)/shard_map/ppermute | solution.py:54
  51.8 0.1 hop.6
  51.8 0.1 collective-permute-start.12
  52.0 2.8 %collective-permute-start.11 = (bf16[384,768]{1,0:T(8,128)(2,1)S(1)}, bf16[384,768]{1,0:T(8,128)(2,1)S(1)}, u32[]{:S(2)}, u32[]{:S(2)}) collective-permute-start(bf16[384,768]{1,0:T(8,128)(2,1)S(1)} %slice.21), channel_id=1, source_target_pairs={{0,3},{1,0},{2,1},{3,2},{4,7},{5,4},{6,5},{7,6},{8,11},{9,8},{10,9... | collective-permute-start | bytes 1769480 | tf_op jit(solution)/shard_map/ppermute | solution.py:54
  54.9 8.9 %collective-permute-done.13.refs_0_ = bf16[96,3072]{1,0:T(8,128)(2,1)S(1)} collective-permute-done((bf16[96,3072]{1,0:T(8,128)(2,1)S(1)}, bf16[96,3072]{1,0:T(8,128)(2,1)S(1)}, u32[]{:S(2)}, u32[]{:S(2)}) %collective-permute-start.13) | collective-permute-done | bytes 589856 | tf_op jit(solution)/shard_map/ppermute | solution.py:54
  63.8 0.1 hop.9
  63.9 3.9 %collective-permute-start.17 = (bf16[96,3072]{1,0:T(8,128)(2,1)S(1)}, bf16[96,3072]{1,0:T(8,128)(2,1)S(1)}, u32[]{:S(2)}, u32[]{:S(2)}) collective-permute-start(bf16[96,3072]{1,0:T(8,128)(2,1)S(1)} %hop.9), channel_id=1, source_target_pairs={{0,224},{1,225},{2,226},{3,227},{4,228},{5,229},{6,230},{7,231},{8... | collective-permute-start | bytes 1769480 | tf_op jit(solution)/shard_map/ppermute | solution.py:54
  67.9 0.1 hop.8
  68.0 0.1 collective-permute-start.15
  68.1 1.9 %collective-permute-done.10.w3 = bf16[384,768]{1,0:T(8,128)(2,1)S(1)} collective-permute-done((bf16[384,768]{1,0:T(8,128)(2,1)S(1)}, bf16[384,768]{1,0:T(8,128)(2,1)S(1)}, u32[]{:S(2)}, u32[]{:S(2)}) %collective-permute-start.10) | collective-permute-done | bytes 589856 | tf_op jit(solution)/shard_map/ppermute | solution.py:54
  70.0 4.0 %forward.1 = (f32[128,1536]{1,0:T(8,128)S(1)}, f32[128,1536]{1,0:T(8,128)S(1)}, bf16[256,1536]{1,0:T(8,128)(2,1)S(1)}) custom-call(s32[5]{0:T(128)S(1)} %stack.23.where, bf16[128,3072]{1,0:T(8,128)(2,1)S(1)} %copy-done.1, bf16[128,3072]{1,0:T(8,128)(2,1)S(1)} %collective-permute-done.sib, bf16[128,1536]{1,0:T(8,128)(2,1)S(1)} %collective-permute-done.1.pair, ...), custom_call_target="tpu_custom_call" | custom-call | flops 2415919104 | bytes 9437184 | tf_op jit(solution)/shard_map/forward/pallas_call | solution.py:72
  74.0 0.4 collective-permute-start.14
  74.4 4.6 %collective-permute-done.17.refs_0_ = bf16[96,3072]{1,0:T(8,128)(2,1)S(1)} collective-permute-done((bf16[96,3072]{1,0:T(8,128)(2,1)S(1)}, bf16[96,3072]{1,0:T(8,128)(2,1)S(1)}, u32[]{:S(2)}, u32[]{:S(2)}) %collective-permute-start.17) | collective-permute-done | bytes 589856 | tf_op jit(solution)/shard_map/ppermute | solution.py:54
  79.0 0.1 hop.11
  79.2 3.8 %collective-permute-start.18 = (bf16[96,3072]{1,0:T(8,128)(2,1)S(1)}, bf16[96,3072]{1,0:T(8,128)(2,1)S(1)}, u32[]{:S(2)}, u32[]{:S(2)}) collective-permute-start(bf16[96,3072]{1,0:T(8,128)(2,1)S(1)} %hop.11), channel_id=1, source_target_pairs={{0,224},{1,225},{2,226},{3,227},{4,228},{5,229},{6,230},{7,231},{8... | collective-permute-start | bytes 1769480 | tf_op jit(solution)/shard_map/ppermute | solution.py:54
  82.9 0.1 hop.10
  83.1 0.1 collective-permute-start.16
  83.2 4.1 %backward.1 = (f32[256,1536]{1,0:T(8,128)S(1)}, bf16[256,1536]{1,0:T(8,128)(2,1)S(1)}) custom-call(s32[5]{0:T(128)S(1)} %stack.23.where, bf16[128,3072]{1,0:T(8,128)(2,1)S(1)} %copy-done.2, bf16[128,3072]{1,0:T(8,128)(2,1)S(1)} %collective-permute-done.5.cot1, bf16[128,3072]{1,0:T(8,128)(2,1)S(1)} %collective-permute-done.6.cot2, ...), custom_call_target="tpu_custom_call" | custom-call | flops 2415919104 | bytes 10223616 | tf_op jit(solution)/shard_map/backward/pallas_call | solution.py:72
  87.2 0.1 collective-permute-start.22
  87.3 5.3 %collective-permute-done.14 = bf16[256,1536]{1,0:T(8,128)(2,1)S(1)} collective-permute-done((bf16[256,1536]{1,0:T(8,128)(2,1)S(1)}, bf16[256,1536]{1,0:T(8,128)(2,1)S(1)}, u32[]{:S(2)}, u32[]{:S(2)}) %collective-permute-start.14) | collective-permute-done | bytes 786464 | tf_op jit(solution)/shard_map/ppermute | solution.py:54
  92.6 0.2 convert_element_type.20
  92.8 0.4 collective-permute-done.18.down
  93.1 3.6 %collective-permute-done.16.up = bf16[96,3072]{1,0:T(8,128)(2,1)S(1)} collective-permute-done((bf16[96,3072]{1,0:T(8,128)(2,1)S(1)}, bf16[96,3072]{1,0:T(8,128)(2,1)S(1)}, u32[]{:S(2)}, u32[]{:S(2)}) %collective-permute-start.16) | collective-permute-done | bytes 589856 | tf_op jit(solution)/shard_map/ppermute | solution.py:54
  96.8 1.2 last_hop.1
  97.9 1.6 %collective-permute-start.19 = (bf16[24,3072]{1,0:T(8,128)(2,1)S(1)}, bf16[24,3072]{1,0:T(8,128)(2,1)S(1)}, u32[]{:S(2)}, u32[]{:S(2)}) collective-permute-start(bf16[24,3072]{1,0:T(8,128)(2,1)S(1)} %get-tuple-element.101), channel_id=1, source_target_pairs={{0,1},{1,2},{2,3},{3,0},{4,5},{5,6},{6,7},{7,4},{8,9},{9,10},{10,1... | collective-permute-start | bytes 442376 | tf_op jit(solution)/shard_map/ppermute | solution.py:54
  99.5 2.7 %collective-permute-start.20 = (bf16[24,3072]{1,0:T(8,128)(2,1)S(1)}, bf16[24,3072]{1,0:T(8,128)(2,1)S(1)}, u32[]{:S(2)}, u32[]{:S(2)}) collective-permute-start(bf16[24,3072]{1,0:T(8,128)(2,1)S(1)} %get-tuple-element.102), channel_id=1, source_target_pairs={{0,2},{1,3},{2,0},{3,1},{4,6},{5,7},{6,4},{7,5},{8,10},{9,11},{10,... | collective-permute-start | bytes 442376 | tf_op jit(solution)/shard_map/ppermute | solution.py:54
  102.2 1.5 %collective-permute-start.21 = (bf16[24,3072]{1,0:T(8,128)(2,1)S(1)}, bf16[24,3072]{1,0:T(8,128)(2,1)S(1)}, u32[]{:S(2)}, u32[]{:S(2)}) collective-permute-start(bf16[24,3072]{1,0:T(8,128)(2,1)S(1)} %get-tuple-element.103), channel_id=1, source_target_pairs={{0,3},{1,0},{2,1},{3,2},{4,7},{5,4},{6,5},{7,6},{8,11},{9,8},{10,9... | collective-permute-start | bytes 442376 | tf_op jit(solution)/shard_map/ppermute | solution.py:54
  103.7 0.9 add_convert_fusion.2
  104.6 0.2 add_convert_fusion
  104.9 0.1 fusion
  104.9 0.4 collective-permute-start.24
  105.3 1.6 %collective-permute-done.20.two = bf16[24,3072]{1,0:T(8,128)(2,1)S(1)} collective-permute-done((bf16[24,3072]{1,0:T(8,128)(2,1)S(1)}, bf16[24,3072]{1,0:T(8,128)(2,1)S(1)}, u32[]{:S(2)}, u32[]{:S(2)}) %collective-permute-start.20) | collective-permute-done | bytes 147488 | tf_op jit(solution)/shard_map/ppermute | solution.py:54
  106.9 0.4 collective-permute-done.21.three
  107.4 0.7 sum_over_x.1
  108.1 1.9 %collective-permute-start.25 = (bf16[12,3072]{1,0:T(8,128)(2,1)S(1)}, bf16[12,3072]{1,0:T(8,128)(2,1)S(1)}, u32[]{:S(2)}, u32[]{:S(2)}) collective-permute-start(bf16[12,3072]{1,0:T(8,128)(2,1)S(1)} %get-tuple-element.110), channel_id=1, source_target_pairs={{0,24},{1,25},{2,26},{3,27},{4,184},{5,185},{6,186},{7,187},{8,72}... | collective-permute-start | bytes 221192 | tf_op jit(solution)/shard_map/ppermute | solution.py:54
  110.0 6.3 %collective-permute-start.26 = (bf16[12,3072]{1,0:T(8,128)(2,1)S(1)}, bf16[12,3072]{1,0:T(8,128)(2,1)S(1)}, u32[]{:S(2)}, u32[]{:S(2)}) collective-permute-start(bf16[12,3072]{1,0:T(8,128)(2,1)S(1)} %get-tuple-element.114), channel_id=1, source_target_pairs={{0,28},{1,29},{2,30},{3,31},{4,188},{5,189},{6,190},{7,191},{8,76}... | collective-permute-start | bytes 221192 | tf_op jit(solution)/shard_map/ppermute | solution.py:54
  116.3 2.2 %maximum_select_fusion = bf16[128,3072]{1,0:T(8,128)(2,1)} fusion(bf16[128,1536]{1,0:T(8,128)(2,1)} %collective-permute-done.23, bf16[128,1536]{1,0:T(8,128)(2,1)S(1)} %get-tuple-element.111, pred[]{:T(512)S(6)} %eq.8), kind=kLoop, calls=%fused_computation.1 | loop fusion | flops 3538944 | bytes 1572865 | tf_op jit(solution)/shard_map/jit(_where)/select_n | solution.py:366
  118.5 1.4 %collective-permute-done.24 = bf16[128,1536]{1,0:T(8,128)(2,1)S(1)} collective-permute-done((bf16[128,1536]{1,0:T(8,128)(2,1)S(1)}, bf16[128,1536]{1,0:T(8,128)(2,1)S(1)}, u32[]{:S(2)}, u32[]{:S(2)}) %collective-permute-start.24) | collective-permute-done | bytes 393248 | tf_op jit(solution)/shard_map/ppermute | solution.py:54
  120.0 1.1 maximum_select_fusion.1
  121.0 1.1 collective-permute-done.26
  122.1 0.2 collective-permute-done.25
  122.3 0.7 convert_add_fusion
  (22 shorter events, 0.2 us)
Async XLA Ops:
  0.6 21.9 %collective-permute-start.6 = (bf16[128,3072]{1,0:T(8,128)(2,1)}, bf16[128,3072]{1,0:T(8,128)(2,1)S(1)}, u32[]{:S(2)}, u32[]{:S(2)}) collective-permute-start(bf16[128,3072]{1,0:T(8,128)(2,1)} %cot0.3), channel_id=1, source_target_pairs={{0,20},{1,21},{2,22},{3,23},{4,16},{5,17},{6,18},{7,19},{8,28},{9,... | collective-permute-start | bytes 2359304 | tf_op jit(solution)/shard_map/ppermute | solution.py:54
  2.8 1.7 %copy-start = (bf16[384,3072]{1,0:T(8,128)(2,1)S(1)}, bf16[384,3072]{1,0:T(8,128)(2,1)}, u32[]{:S(2)}) copy-start(bf16[384,3072]{1,0:T(8,128)(2,1)} %levels.1) | copy-start | bytes 7077892
  4.4 0.7 copy-start.3
  5.2 1.6 %copy-start.1 = (bf16[128,3072]{1,0:T(8,128)(2,1)S(1)}, bf16[128,3072]{1,0:T(8,128)(2,1)}, u32[]{:S(2)}) copy-start(bf16[128,3072]{1,0:T(8,128)(2,1)} %own.5) | copy-start | bytes 2359300
  5.2 3.0 %copy-start.2 = (bf16[128,3072]{1,0:T(8,128)(2,1)S(1)}, bf16[128,3072]{1,0:T(8,128)(2,1)}, u32[]{:S(2)}) copy-start(bf16[128,3072]{1,0:T(8,128)(2,1)} %cot0.3) | copy-start | bytes 2359300
  6.8 23.0 %collective-permute-start.1 = (bf16[128,1536]{1,0:T(8,128)(2,1)S(1)}, bf16[128,1536]{1,0:T(8,128)(2,1)S(1)}, u32[]{:S(2)}, u32[]{:S(2)}) collective-permute-start(bf16[128,1536]{1,0:T(8,128)(2,1)S(1)} %constant_dynamic-slice_fusion), channel_id=1, source_target_pairs={{0,20},{1,21},{2,22},{3,23},{4,16},{5,17},{6,18},{7,19},{8,28},{9,... | collective-permute-start | bytes 1179656 | tf_op jit(solution)/shard_map/ppermute | solution.py:54
  8.2 21.7 %collective-permute-start.5 = (bf16[128,3072]{1,0:T(8,128)(2,1)S(1)}, bf16[128,3072]{1,0:T(8,128)(2,1)S(1)}, u32[]{:S(2)}, u32[]{:S(2)}) collective-permute-start(bf16[128,3072]{1,0:T(8,128)(2,1)S(1)} %copy-done.2), channel_id=1, source_target_pairs={{0,8},{1,9},{2,10},{3,11},{4,12},{5,13},{6,14},{7,15},{8,0},{9,1},... | collective-permute-start | bytes 2359304 | tf_op jit(solution)/shard_map/ppermute | solution.py:54
  8.2 33.2 %collective-permute-start.4 = (bf16[384,1536]{1,0:T(8,128)(2,1)S(1)}, bf16[384,1536]{1,0:T(8,128)(2,1)S(1)}, u32[]{:S(2)}, u32[]{:S(2)}) collective-permute-start(bf16[384,1536]{1,0:T(8,128)(2,1)S(1)} %dequantize.1.w0), channel_id=1, source_target_pairs={{0,3},{1,0},{2,1},{3,2},{4,7},{5,4},{6,5},{7,6},{8,11},{9,8},{10,9... | collective-permute-start | bytes 3538952 | tf_op jit(solution)/shard_map/ppermute | solution.py:54
  10.9 30.4 %collective-permute-start.3 = (bf16[384,1536]{1,0:T(8,128)(2,1)S(1)}, bf16[384,1536]{1,0:T(8,128)(2,1)S(1)}, u32[]{:S(2)}, u32[]{:S(2)}) collective-permute-start(bf16[384,1536]{1,0:T(8,128)(2,1)S(1)} %dequantize.1.w0), channel_id=1, source_target_pairs={{0,1},{1,2},{2,3},{3,0},{4,5},{5,6},{6,7},{7,4},{8,9},{9,10},{10,1... | collective-permute-start | bytes 3538952 | tf_op jit(solution)/shard_map/ppermute | solution.py:54
  22.6 7.8 %collective-permute-start.7 = (bf16[128,3072]{1,0:T(8,128)(2,1)S(1)}, bf16[128,3072]{1,0:T(8,128)(2,1)S(1)}, u32[]{:S(2)}, u32[]{:S(2)}) collective-permute-start(bf16[128,3072]{1,0:T(8,128)(2,1)S(1)} %collective-permute-done.6.cot2), channel_id=1, source_target_pairs={{0,8},{1,9},{2,10},{3,11},{4,12},{5,13},{6,14},{7,15},{8,0},{9,1},... | collective-permute-start | bytes 2359304 | tf_op jit(solution)/shard_map/ppermute | solution.py:54
  29.8 2.9 %collective-permute-start = (bf16[128,3072]{1,0:T(8,128)(2,1)S(1)}, bf16[128,3072]{1,0:T(8,128)(2,1)S(1)}, u32[]{:S(2)}, u32[]{:S(2)}) collective-permute-start(bf16[128,3072]{1,0:T(8,128)(2,1)S(1)} %copy-done.1), channel_id=1, source_target_pairs={{0,8},{1,9},{2,10},{3,11},{4,12},{5,13},{6,14},{7,15},{8,0},{9,1},... | collective-permute-start | bytes 2359304 | tf_op jit(solution)/shard_map/ppermute | solution.py:54
  29.9 2.8 %collective-permute-start.2 = (bf16[128,1536]{1,0:T(8,128)(2,1)S(1)}, bf16[128,1536]{1,0:T(8,128)(2,1)S(1)}, u32[]{:S(2)}, u32[]{:S(2)}) collective-permute-start(bf16[128,1536]{1,0:T(8,128)(2,1)S(1)} %collective-permute-done.1.pair), channel_id=1, source_target_pairs={{0,8},{1,9},{2,10},{3,11},{4,12},{5,13},{6,14},{7,15},{8,0},{9,1},... | collective-permute-start | bytes 1179656 | tf_op jit(solution)/shard_map/ppermute | solution.py:54
  35.4 12.5 %collective-permute-start.9 = (bf16[48,3072]{1,0:T(8,128)(2,1)S(1)}, bf16[48,3072]{1,0:T(8,128)(2,1)S(1)}, u32[]{:S(2)}, u32[]{:S(2)}) collective-permute-start(bf16[48,3072]{1,0:T(8,128)(2,1)S(1)} %get-tuple-element.73), channel_id=1, source_target_pairs={{0,224},{1,225},{2,226},{3,227},{4,228},{5,229},{6,230},{7,231},{8... | collective-permute-start | bytes 884744 | tf_op jit(solution)/shard_map/ppermute | solution.py:54
  41.3 10.4 %collective-permute-start.8 = (bf16[48,3072]{1,0:T(8,128)(2,1)S(1)}, bf16[48,3072]{1,0:T(8,128)(2,1)S(1)}, u32[]{:S(2)}, u32[]{:S(2)}) collective-permute-start(bf16[48,3072]{1,0:T(8,128)(2,1)S(1)} %get-tuple-element.67), channel_id=1, source_target_pairs={{0,32},{1,33},{2,34},{3,35},{4,36},{5,37},{6,38},{7,39},{8,40},{9,... | collective-permute-start | bytes 884744 | tf_op jit(solution)/shard_map/ppermute | solution.py:54
  48.0 15.8 %collective-permute-start.13 = (bf16[96,3072]{1,0:T(8,128)(2,1)S(1)}, bf16[96,3072]{1,0:T(8,128)(2,1)S(1)}, u32[]{:S(2)}, u32[]{:S(2)}) collective-permute-start(bf16[96,3072]{1,0:T(8,128)(2,1)S(1)} %hop.7), channel_id=1, source_target_pairs={{0,224},{1,225},{2,226},{3,227},{4,228},{5,229},{6,230},{7,231},{8... | collective-permute-start | bytes 1769480 | tf_op jit(solution)/shard_map/ppermute | solution.py:54
  51.8 16.1 %collective-permute-start.12 = (bf16[96,3072]{1,0:T(8,128)(2,1)S(1)}, bf16[96,3072]{1,0:T(8,128)(2,1)S(1)}, u32[]{:S(2)}, u32[]{:S(2)}) collective-permute-start(bf16[96,3072]{1,0:T(8,128)(2,1)S(1)} %hop.6), channel_id=1, source_target_pairs={{0,32},{1,33},{2,34},{3,35},{4,36},{5,37},{6,38},{7,39},{8,40},{9,... | collective-permute-start | bytes 1769480 | tf_op jit(solution)/shard_map/ppermute | solution.py:54
  52.0 16.1 %collective-permute-start.11 = (bf16[384,768]{1,0:T(8,128)(2,1)S(1)}, bf16[384,768]{1,0:T(8,128)(2,1)S(1)}, u32[]{:S(2)}, u32[]{:S(2)}) collective-permute-start(bf16[384,768]{1,0:T(8,128)(2,1)S(1)} %slice.21), channel_id=1, source_target_pairs={{0,3},{1,0},{2,1},{3,2},{4,7},{5,4},{6,5},{7,6},{8,11},{9,8},{10,9... | collective-permute-start | bytes 1769480 | tf_op jit(solution)/shard_map/ppermute | solution.py:54
  54.9 15.2 %collective-permute-start.10 = (bf16[384,768]{1,0:T(8,128)(2,1)S(1)}, bf16[384,768]{1,0:T(8,128)(2,1)S(1)}, u32[]{:S(2)}, u32[]{:S(2)}) collective-permute-start(bf16[384,768]{1,0:T(8,128)(2,1)S(1)} %slice.20), channel_id=1, source_target_pairs={{0,1},{1,2},{2,3},{3,0},{4,5},{5,6},{6,7},{7,4},{8,9},{9,10},{10,1... | collective-permute-start | bytes 1769480 | tf_op jit(solution)/shard_map/ppermute | solution.py:54
  63.9 15.1 %collective-permute-start.17 = (bf16[96,3072]{1,0:T(8,128)(2,1)S(1)}, bf16[96,3072]{1,0:T(8,128)(2,1)S(1)}, u32[]{:S(2)}, u32[]{:S(2)}) collective-permute-start(bf16[96,3072]{1,0:T(8,128)(2,1)S(1)} %hop.9), channel_id=1, source_target_pairs={{0,224},{1,225},{2,226},{3,227},{4,228},{5,229},{6,230},{7,231},{8... | collective-permute-start | bytes 1769480 | tf_op jit(solution)/shard_map/ppermute | solution.py:54
  68.0 14.9 %collective-permute-start.15 = (bf16[96,3072]{1,0:T(8,128)(2,1)S(1)}, bf16[96,3072]{1,0:T(8,128)(2,1)S(1)}, u32[]{:S(2)}, u32[]{:S(2)}) collective-permute-start(bf16[96,3072]{1,0:T(8,128)(2,1)S(1)} %hop.8), channel_id=1, source_target_pairs={{0,32},{1,33},{2,34},{3,35},{4,36},{5,37},{6,38},{7,39},{8,40},{9,... | collective-permute-start | bytes 1769480 | tf_op jit(solution)/shard_map/ppermute | solution.py:54
  74.0 18.6 %collective-permute-start.14 = (bf16[256,1536]{1,0:T(8,128)(2,1)S(1)}, bf16[256,1536]{1,0:T(8,128)(2,1)S(1)}, u32[]{:S(2)}, u32[]{:S(2)}) collective-permute-start(bf16[256,1536]{1,0:T(8,128)(2,1)S(1)} %get-tuple-element.85), channel_id=1, source_target_pairs={{0,20},{1,21},{2,22},{3,23},{4,16},{5,17},{6,18},{7,19},{8,28},{9,... | collective-permute-start | bytes 2359304 | tf_op jit(solution)/shard_map/ppermute | solution.py:54
  79.2 14.0 %collective-permute-start.18 = (bf16[96,3072]{1,0:T(8,128)(2,1)S(1)}, bf16[96,3072]{1,0:T(8,128)(2,1)S(1)}, u32[]{:S(2)}, u32[]{:S(2)}) collective-permute-start(bf16[96,3072]{1,0:T(8,128)(2,1)S(1)} %hop.11), channel_id=1, source_target_pairs={{0,224},{1,225},{2,226},{3,227},{4,228},{5,229},{6,230},{7,231},{8... | collective-permute-start | bytes 1769480 | tf_op jit(solution)/shard_map/ppermute | solution.py:54
  83.1 13.7 %collective-permute-start.16 = (bf16[96,3072]{1,0:T(8,128)(2,1)S(1)}, bf16[96,3072]{1,0:T(8,128)(2,1)S(1)}, u32[]{:S(2)}, u32[]{:S(2)}) collective-permute-start(bf16[96,3072]{1,0:T(8,128)(2,1)S(1)} %hop.10), channel_id=1, source_target_pairs={{0,32},{1,33},{2,34},{3,35},{4,36},{5,37},{6,38},{7,39},{8,40},{9,... | collective-permute-start | bytes 1769480 | tf_op jit(solution)/shard_map/ppermute | solution.py:54
  87.2 17.4 %collective-permute-start.22 = (bf16[256,1536]{1,0:T(8,128)(2,1)S(1)}, bf16[256,1536]{1,0:T(8,128)(2,1)S(1)}, u32[]{:S(2)}, u32[]{:S(2)}) collective-permute-start(bf16[256,1536]{1,0:T(8,128)(2,1)S(1)} %get-tuple-element.104), channel_id=1, source_target_pairs={{0,8},{1,9},{2,10},{3,11},{4,12},{5,13},{6,14},{7,15},{8,0},{9,1},... | collective-permute-start | bytes 2359304 | tf_op jit(solution)/shard_map/ppermute | solution.py:54
  97.9 7.3 %collective-permute-start.19 = (bf16[24,3072]{1,0:T(8,128)(2,1)S(1)}, bf16[24,3072]{1,0:T(8,128)(2,1)S(1)}, u32[]{:S(2)}, u32[]{:S(2)}) collective-permute-start(bf16[24,3072]{1,0:T(8,128)(2,1)S(1)} %get-tuple-element.101), channel_id=1, source_target_pairs={{0,1},{1,2},{2,3},{3,0},{4,5},{5,6},{6,7},{7,4},{8,9},{9,10},{10,1... | collective-permute-start | bytes 442376 | tf_op jit(solution)/shard_map/ppermute | solution.py:54
  99.5 7.4 %collective-permute-start.20 = (bf16[24,3072]{1,0:T(8,128)(2,1)S(1)}, bf16[24,3072]{1,0:T(8,128)(2,1)S(1)}, u32[]{:S(2)}, u32[]{:S(2)}) collective-permute-start(bf16[24,3072]{1,0:T(8,128)(2,1)S(1)} %get-tuple-element.102), channel_id=1, source_target_pairs={{0,2},{1,3},{2,0},{3,1},{4,6},{5,7},{6,4},{7,5},{8,10},{9,11},{10,... | collective-permute-start | bytes 442376 | tf_op jit(solution)/shard_map/ppermute | solution.py:54
  102.2 5.1 %collective-permute-start.21 = (bf16[24,3072]{1,0:T(8,128)(2,1)S(1)}, bf16[24,3072]{1,0:T(8,128)(2,1)S(1)}, u32[]{:S(2)}, u32[]{:S(2)}) collective-permute-start(bf16[24,3072]{1,0:T(8,128)(2,1)S(1)} %get-tuple-element.103), channel_id=1, source_target_pairs={{0,3},{1,0},{2,1},{3,2},{4,7},{5,4},{6,5},{7,6},{8,11},{9,8},{10,9... | collective-permute-start | bytes 442376 | tf_op jit(solution)/shard_map/ppermute | solution.py:54
  104.6 11.7 %collective-permute-start.23 = (bf16[128,1536]{1,0:T(8,128)(2,1)}, bf16[128,1536]{1,0:T(8,128)(2,1)}, u32[]{:S(2)}, u32[]{:S(2)}) collective-permute-start(bf16[128,1536]{1,0:T(8,128)(2,1)} %get-tuple-element.118), channel_id=1, source_target_pairs={{0,8},{1,9},{2,10},{3,11},{4,12},{5,13},{6,14},{7,15},{8,0},{9,1},... | collective-permute-start | bytes 1179656 | tf_op jit(solution)/shard_map/ppermute | solution.py:54
  104.9 15.0 %collective-permute-start.24 = (bf16[128,1536]{1,0:T(8,128)(2,1)S(1)}, bf16[128,1536]{1,0:T(8,128)(2,1)S(1)}, u32[]{:S(2)}, u32[]{:S(2)}) collective-permute-start(bf16[128,1536]{1,0:T(8,128)(2,1)S(1)} %get-tuple-element.120), channel_id=1, source_target_pairs={{0,20},{1,21},{2,22},{3,23},{4,16},{5,17},{6,18},{7,19},{8,28},{9,... | collective-permute-start | bytes 1179656 | tf_op jit(solution)/shard_map/ppermute | solution.py:54
  108.1 14.2 %collective-permute-start.25 = (bf16[12,3072]{1,0:T(8,128)(2,1)S(1)}, bf16[12,3072]{1,0:T(8,128)(2,1)S(1)}, u32[]{:S(2)}, u32[]{:S(2)}) collective-permute-start(bf16[12,3072]{1,0:T(8,128)(2,1)S(1)} %get-tuple-element.110), channel_id=1, source_target_pairs={{0,24},{1,25},{2,26},{3,27},{4,184},{5,185},{6,186},{7,187},{8,72}... | collective-permute-start | bytes 221192 | tf_op jit(solution)/shard_map/ppermute | solution.py:54
  110.0 12.1 %collective-permute-start.26 = (bf16[12,3072]{1,0:T(8,128)(2,1)S(1)}, bf16[12,3072]{1,0:T(8,128)(2,1)S(1)}, u32[]{:S(2)}, u32[]{:S(2)}) collective-permute-start(bf16[12,3072]{1,0:T(8,128)(2,1)S(1)} %get-tuple-element.114), channel_id=1, source_target_pairs={{0,28},{1,29},{2,30},{3,31},{4,188},{5,189},{6,190},{7,191},{8,76}... | collective-permute-start | bytes 221192 | tf_op jit(solution)/shard_map/ppermute | solution.py:54

commit v10 on v7

--- a/solution.py
+++ b/solution.py
@@ -105,7 +105,7 @@
     return call(
         dequantize_kernel,
         "dequantize",
-        12,
+        60,
         where,
         (3,),
         [

time: 122 us -> 122 us (level)
  local copies, waits for them, and re-layouts: 4.78 us -> 1.85 us
  Pallas kernels: 21.7 us -> 24.2 us
  waiting for transfers between devices: 45.2 us -> 47 us
    pallas_call x7, Pallas kernels: 21 us -> 23.4 us  [call(): pl.pallas_call(kernel, name=name, grid_spec=pltpu.PrefetchScalarGridSpec(...]
    unnamed x8, local copies, waits for them, and re-layouts: 2.41 us -> 0.01 us
    ppermute x27, waiting for transfers between devices: 45.2 us -> 47 us  [send(): return lax.ppermute(value, AXES, pairs)]
  transfers between devices with their start and end apart: 27 -> 27, of which waited for: 12 -> 12; matrix products, arithmetic and copies ran while one was open for 5% -> 4% of each run, Pallas kernels for 16% -> 18%
where the time goes in v10:
time: 122 us
  waiting for transfers between devices  47 us (39%)
  starting transfers between devices  43.7 us (36%)
  Pallas kernels  24.2 us (20%)
  other arithmetic  4.11 us (3%)
  local copies, waits for them, and re-layouts  1.85 us (2%)
    ppermute x27, waiting for transfers between devices, send(): return lax.ppermute(value, AXES, pairs)  47 us
    ppermute x27, starting transfers between devices, send(): return lax.ppermute(value, AXES, pairs)  43.7 us
    pallas_call x7, Pallas kernels, call(): pl.pallas_call(kernel, name=name, grid_spec=pltpu.PrefetchScalarGridSpec(...  23.4 us
  transfers between devices with their start and end apart: 27, of which 12 were waited for; matrix products, arithmetic and copies ran while one was open for 4% of the time, Pallas kernels for 18%

profile of v10, /device:TPU:24, one launch (start us, length us, event | category | flops | bytes accessed | tf_op | source)
XLA Modules:
  0.0 121.7 jit_solution(13491548486179476924)
XLA Ops:
  0.6 2.0 %collective-permute-start.6 = (bf16[128,3072]{1,0:T(8,128)(2,1)}, bf16[128,3072]{1,0:T(8,128)(2,1)S(1)}, u32[]{:S(2)}, u32[]{:S(2)}) collective-permute-start(bf16[128,3072]{1,0:T(8,128)(2,1)} %cot0.3), channel_id=1, source_target_pairs={{0,20},{1,21},{2,22},{3,23},{4,16},{5,17},{6,18},{7,19},{8,28},{9,... | collective-permute-start | bytes 2359304 | tf_op jit(solution)/shard_map/ppermute | solution.py:54
  2.7 0.6 stack.23.where
  3.3 4.3 %dequantize.1.w0 = bf16[384,1536]{1,0:T(8,128)(2,1)} custom-call(s32[5]{0:T(128)} %stack.23.where, bf16[384,3072]{1,0:T(8,128)(2,1)} %levels.1, f32[12,384]{1,0:T(8,128)} %bitcast.6), custom_call_target="tpu_custom_call" | custom-call | flops 589824 | bytes 3557376 | tf_op jit(solution)/shard_map/dequantize/pallas_call | solution.py:72
  7.6 1.0 collective-permute-start.4
  8.6 1.0 collective-permute-start.3
  9.7 2.1 %collective-permute-start.1 = (bf16[128,1536]{1,0:T(8,128)(2,1)S(1)}, bf16[128,1536]{1,0:T(8,128)(2,1)S(1)}, u32[]{:S(2)}, u32[]{:S(2)}) collective-permute-start(bf16[128,1536]{1,0:T(8,128)(2,1)S(1)} %constant_dynamic-slice_fusion), channel_id=1, source_target_pairs={{0,20},{1,21},{2,22},{3,23},{4,16},{5,17},{6,18},{7,19},{8,28},{9,... | collective-permute-start | bytes 1179656 | tf_op jit(solution)/shard_map/ppermute | solution.py:54
  11.8 0.0 collective-permute-start.5
  11.8 10.8 %collective-permute-done.6.cot2 = bf16[128,3072]{1,0:T(8,128)(2,1)S(1)} collective-permute-done((bf16[128,3072]{1,0:T(8,128)(2,1)}, bf16[128,3072]{1,0:T(8,128)(2,1)S(1)}, u32[]{:S(2)}, u32[]{:S(2)}) %collective-permute-start.6) | collective-permute-done | bytes 786464 | tf_op jit(solution)/shard_map/ppermute | solution.py:54
  22.6 0.0 collective-permute-start.7
  22.6 7.3 %collective-permute-done.1.pair = bf16[128,1536]{1,0:T(8,128)(2,1)S(1)} collective-permute-done((bf16[128,1536]{1,0:T(8,128)(2,1)S(1)}, bf16[128,1536]{1,0:T(8,128)(2,1)S(1)}, u32[]{:S(2)}, u32[]{:S(2)}) %collective-permute-start.1) | collective-permute-done | bytes 393248 | tf_op jit(solution)/shard_map/ppermute | solution.py:54
  29.8 0.0 collective-permute-start
  29.9 0.5 collective-permute-start.2
  30.4 3.6 %collective-permute-done.4.w2 = bf16[384,1536]{1,0:T(8,128)(2,1)S(1)} collective-permute-done((bf16[384,1536]{1,0:T(8,128)(2,1)}, bf16[384,1536]{1,0:T(8,128)(2,1)S(1)}, u32[]{:S(2)}, u32[]{:S(2)}) %collective-permute-start.4) | collective-permute-done | bytes 1179680 | tf_op jit(solution)/shard_map/ppermute | solution.py:54
  34.0 3.4 %collective-permute-done.3.w1 = bf16[384,1536]{1,0:T(8,128)(2,1)} collective-permute-done((bf16[384,1536]{1,0:T(8,128)(2,1)}, bf16[384,1536]{1,0:T(8,128)(2,1)}, u32[]{:S(2)}, u32[]{:S(2)}) %collective-permute-start.3) | collective-permute-done | bytes 1179680 | tf_op jit(solution)/shard_map/ppermute | solution.py:54
  37.4 0.0 collective-permute-done.7.cot3
  37.4 0.0 collective-permute-done.2.psib
  37.4 0.0 collective-permute-done.sib
  37.4 2.7 %far.1 = (bf16[48,3072]{1,0:T(8,128)(2,1)S(1)}, bf16[48,3072]{1,0:T(8,128)(2,1)S(1)}) custom-call(s32[5]{0:T(128)S(1)} %copy-done.3, bf16[128,3072]{1,0:T(8,128)(2,1)S(1)} %copy-done, bf16[128,3072]{1,0:T(8,128)(2,1)S(1)} %collective-permute-done.sib, bf16[128,1536]{1,0:T(8,128)(2,1)S(1)} %collective-permute-done.1.pair, ...), custom_call_target="tpu_custom_call" | custom-call | flops 805306368 | bytes 6094848 | tf_op jit(solution)/shard_map/far/pallas_call | solution.py:72
  40.1 5.9 %collective-permute-start.9 = (bf16[48,3072]{1,0:T(8,128)(2,1)S(1)}, bf16[48,3072]{1,0:T(8,128)(2,1)S(1)}, u32[]{:S(2)}, u32[]{:S(2)}) collective-permute-start(bf16[48,3072]{1,0:T(8,128)(2,1)S(1)} %get-tuple-element.73), channel_id=1, source_target_pairs={{0,224},{1,225},{2,226},{3,227},{4,228},{5,229},{6,230},{7,231},{8... | collective-permute-start | bytes 884744 | tf_op jit(solution)/shard_map/ppermute | solution.py:54
  46.1 4.9 %gradient.1 = (bf16[96,3072]{1,0:T(8,128)(2,1)S(1)}, bf16[96,3072]{1,0:T(8,128)(2,1)S(1)}, bf16[96,3072]{1,0:T(8,128)(2,1)S(1)}, bf16[96,3072]{1,0:T(8,128)(2,1)...) custom-call(s32[5]{0:T(128)S(1)} %copy-done.3, ...), custom_call_target="tpu_custom_call" | custom-call | flops 2415919104 | bytes 9633792 | tf_op jit(solution)/shard_map/gradient/pallas_call | solution.py:72
  51.0 0.0 collective-permute-done.9.arrived
  51.0 0.1 hop.7
  51.0 3.7 %collective-permute-start.13 = (bf16[96,3072]{1,0:T(8,128)(2,1)S(1)}, bf16[96,3072]{1,0:T(8,128)(2,1)S(1)}, u32[]{:S(2)}, u32[]{:S(2)}) collective-permute-start(bf16[96,3072]{1,0:T(8,128)(2,1)S(1)} %hop.7), channel_id=1, source_target_pairs={{0,224},{1,225},{2,226},{3,227},{4,228},{5,229},{6,230},{7,231},{8... | collective-permute-start | bytes 1769480 | tf_op jit(solution)/shard_map/ppermute | solution.py:54
  54.8 0.0 collective-permute-done.8.arrived
  54.8 0.1 hop.6
  54.9 0.1 collective-permute-start.12
  55.0 1.1 slice.20
  56.1 0.6 collective-permute-start.11
  56.7 1.5 %collective-permute-start.10 = (bf16[384,768]{1,0:T(8,128)(2,1)S(1)}, bf16[384,768]{1,0:T(8,128)(2,1)S(1)}, u32[]{:S(2)}, u32[]{:S(2)}) collective-permute-start(bf16[384,768]{1,0:T(8,128)(2,1)S(1)} %slice.20), channel_id=1, source_target_pairs={{0,1},{1,2},{2,3},{3,0},{4,5},{5,6},{6,7},{7,4},{8,9},{9,10},{10,1... | collective-permute-start | bytes 1769480 | tf_op jit(solution)/shard_map/ppermute | solution.py:54
  58.2 6.8 %collective-permute-done.13.refs_0_ = bf16[96,3072]{1,0:T(8,128)(2,1)S(1)} collective-permute-done((bf16[96,3072]{1,0:T(8,128)(2,1)S(1)}, bf16[96,3072]{1,0:T(8,128)(2,1)S(1)}, u32[]{:S(2)}, u32[]{:S(2)}) %collective-permute-start.13) | collective-permute-done | bytes 589856 | tf_op jit(solution)/shard_map/ppermute | solution.py:54
  65.1 0.1 hop.9
  65.2 3.9 %collective-permute-start.17 = (bf16[96,3072]{1,0:T(8,128)(2,1)S(1)}, bf16[96,3072]{1,0:T(8,128)(2,1)S(1)}, u32[]{:S(2)}, u32[]{:S(2)}) collective-permute-start(bf16[96,3072]{1,0:T(8,128)(2,1)S(1)} %hop.9), channel_id=1, source_target_pairs={{0,224},{1,225},{2,226},{3,227},{4,228},{5,229},{6,230},{7,231},{8... | collective-permute-start | bytes 1769480 | tf_op jit(solution)/shard_map/ppermute | solution.py:54
  69.2 0.1 hop.8
  69.3 0.1 collective-permute-start.15
  69.4 1.0 collective-permute-done.10.w3
  70.4 4.8 %forward.1 = (f32[128,1536]{1,0:T(8,128)S(1)}, f32[128,1536]{1,0:T(8,128)S(1)}, bf16[256,1536]{1,0:T(8,128)(2,1)S(1)}) custom-call(s32[5]{0:T(128)S(1)} %copy-done.3, bf16[128,3072]{1,0:T(8,128)(2,1)S(1)} %copy-done, bf16[128,3072]{1,0:T(8,128)(2,1)S(1)} %collective-permute-done.sib, bf16[128,1536]{1,0:T(8,128)(2,1)S(1)} %collective-permute-done.1.pair, ...), custom_call_target="tpu_custom_call" | custom-call | flops 2415919104 | bytes 9437184 | tf_op jit(solution)/shard_map/forward/pallas_call | solution.py:72
  75.2 2.8 %collective-permute-start.14 = (bf16[256,1536]{1,0:T(8,128)(2,1)S(1)}, bf16[256,1536]{1,0:T(8,128)(2,1)S(1)}, u32[]{:S(2)}, u32[]{:S(2)}) collective-permute-start(bf16[256,1536]{1,0:T(8,128)(2,1)S(1)} %get-tuple-element.85), channel_id=1, source_target_pairs={{0,20},{1,21},{2,22},{3,23},{4,16},{5,17},{6,18},{7,19},{8,28},{9,... | collective-permute-start | bytes 2359304 | tf_op jit(solution)/shard_map/ppermute | solution.py:54
  78.0 0.8 collective-permute-done.17.refs_0_
  78.7 0.2 hop.11
  78.9 3.8 %collective-permute-start.18 = (bf16[96,3072]{1,0:T(8,128)(2,1)S(1)}, bf16[96,3072]{1,0:T(8,128)(2,1)S(1)}, u32[]{:S(2)}, u32[]{:S(2)}) collective-permute-start(bf16[96,3072]{1,0:T(8,128)(2,1)S(1)} %hop.11), channel_id=1, source_target_pairs={{0,224},{1,225},{2,226},{3,227},{4,228},{5,229},{6,230},{7,231},{8... | collective-permute-start | bytes 1769480 | tf_op jit(solution)/shard_map/ppermute | solution.py:54
  82.6 0.1 hop.10
  82.8 0.1 collective-permute-start.16
  82.9 4.9 %backward.1 = (f32[256,1536]{1,0:T(8,128)S(1)}, bf16[256,1536]{1,0:T(8,128)(2,1)S(1)}) custom-call(s32[5]{0:T(128)S(1)} %copy-done.3, bf16[128,3072]{1,0:T(8,128)(2,1)S(1)} %copy-done.2, bf16[128,3072]{1,0:T(8,128)(2,1)S(1)} %collective-permute-done.5.cot1, bf16[128,3072]{1,0:T(8,128)(2,1)S(1)} %collective-permute-done.6.cot2, ...), custom_call_target="tpu_custom_call" | custom-call | flops 2415919104 | bytes 10223616 | tf_op jit(solution)/shard_map/backward/pallas_call | solution.py:72
  87.8 0.1 collective-permute-start.22
  87.9 4.3 %collective-permute-done.14 = bf16[256,1536]{1,0:T(8,128)(2,1)S(1)} collective-permute-done((bf16[256,1536]{1,0:T(8,128)(2,1)S(1)}, bf16[256,1536]{1,0:T(8,128)(2,1)S(1)}, u32[]{:S(2)}, u32[]{:S(2)}) %collective-permute-start.14) | collective-permute-done | bytes 786464 | tf_op jit(solution)/shard_map/ppermute | solution.py:54
  92.3 0.2 convert_element_type.20
  92.5 2.3 %collective-permute-done.16.up = bf16[96,3072]{1,0:T(8,128)(2,1)S(1)} collective-permute-done((bf16[96,3072]{1,0:T(8,128)(2,1)S(1)}, bf16[96,3072]{1,0:T(8,128)(2,1)S(1)}, u32[]{:S(2)}, u32[]{:S(2)}) %collective-permute-start.16) | collective-permute-done | bytes 589856 | tf_op jit(solution)/shard_map/ppermute | solution.py:54
  94.8 1.2 last_hop.1
  95.9 0.1 collective-permute-start.19
  96.1 2.5 %collective-permute-start.20 = (bf16[24,3072]{1,0:T(8,128)(2,1)S(1)}, bf16[24,3072]{1,0:T(8,128)(2,1)S(1)}, u32[]{:S(2)}, u32[]{:S(2)}) collective-permute-start(bf16[24,3072]{1,0:T(8,128)(2,1)S(1)} %get-tuple-element.102), channel_id=1, source_target_pairs={{0,2},{1,3},{2,0},{3,1},{4,6},{5,7},{6,4},{7,5},{8,10},{9,11},{10,... | collective-permute-start | bytes 442376 | tf_op jit(solution)/shard_map/ppermute | solution.py:54
  98.6 1.0 collective-permute-start.21
  99.6 0.9 add_convert_fusion.2
  100.5 0.2 add_convert_fusion
  100.7 0.1 fusion
  100.8 2.4 %collective-permute-start.24 = (bf16[128,1536]{1,0:T(8,128)(2,1)S(1)}, bf16[128,1536]{1,0:T(8,128)(2,1)S(1)}, u32[]{:S(2)}, u32[]{:S(2)}) collective-permute-start(bf16[128,1536]{1,0:T(8,128)(2,1)S(1)} %get-tuple-element.120), channel_id=1, source_target_pairs={{0,20},{1,21},{2,22},{3,23},{4,16},{5,17},{6,18},{7,19},{8,28},{9,... | collective-permute-start | bytes 1179656 | tf_op jit(solution)/shard_map/ppermute | solution.py:54
  103.2 0.7 collective-permute-done.19.one
  104.0 0.9 collective-permute-done.21.three
  104.8 0.7 sum_over_x.1
  105.5 1.9 %collective-permute-start.25 = (bf16[12,3072]{1,0:T(8,128)(2,1)S(1)}, bf16[12,3072]{1,0:T(8,128)(2,1)S(1)}, u32[]{:S(2)}, u32[]{:S(2)}) collective-permute-start(bf16[12,3072]{1,0:T(8,128)(2,1)S(1)} %get-tuple-element.110), channel_id=1, source_target_pairs={{0,24},{1,25},{2,26},{3,27},{4,184},{5,185},{6,186},{7,187},{8,72}... | collective-permute-start | bytes 221192 | tf_op jit(solution)/shard_map/ppermute | solution.py:54
  107.4 6.4 %collective-permute-start.26 = (bf16[12,3072]{1,0:T(8,128)(2,1)S(1)}, bf16[12,3072]{1,0:T(8,128)(2,1)S(1)}, u32[]{:S(2)}, u32[]{:S(2)}) collective-permute-start(bf16[12,3072]{1,0:T(8,128)(2,1)S(1)} %get-tuple-element.114), channel_id=1, source_target_pairs={{0,28},{1,29},{2,30},{3,31},{4,188},{5,189},{6,190},{7,191},{8,76}... | collective-permute-start | bytes 221192 | tf_op jit(solution)/shard_map/ppermute | solution.py:54
  113.8 1.1 maximum_select_fusion
  114.9 1.1 maximum_select_fusion.1
  116.0 5.0 %collective-permute-done.26 = bf16[12,3072]{1,0:T(8,128)(2,1)S(1)} collective-permute-done((bf16[12,3072]{1,0:T(8,128)(2,1)S(1)}, bf16[12,3072]{1,0:T(8,128)(2,1)S(1)}, u32[]{:S(2)}, u32[]{:S(2)}) %collective-permute-start.26) | collective-permute-done | bytes 73760 | tf_op jit(solution)/shard_map/ppermute | solution.py:54
  121.0 0.7 convert_add_fusion
  (22 shorter events, 0.1 us)
Async XLA Ops:
  0.6 21.9 %collective-permute-start.6 = (bf16[128,3072]{1,0:T(8,128)(2,1)}, bf16[128,3072]{1,0:T(8,128)(2,1)S(1)}, u32[]{:S(2)}, u32[]{:S(2)}) collective-permute-start(bf16[128,3072]{1,0:T(8,128)(2,1)} %cot0.3), channel_id=1, source_target_pairs={{0,20},{1,21},{2,22},{3,23},{4,16},{5,17},{6,18},{7,19},{8,28},{9,... | collective-permute-start | bytes 2359304 | tf_op jit(solution)/shard_map/ppermute | solution.py:54
  3.3 6.3 %copy-start = (bf16[128,3072]{1,0:T(8,128)(2,1)S(1)}, bf16[128,3072]{1,0:T(8,128)(2,1)}, u32[]{:S(2)}) copy-start(bf16[128,3072]{1,0:T(8,128)(2,1)} %own.5) | copy-start | bytes 2359300
  3.3 8.5 %copy-start.2 = (bf16[128,3072]{1,0:T(8,128)(2,1)S(1)}, bf16[128,3072]{1,0:T(8,128)(2,1)}, u32[]{:S(2)}) copy-start(bf16[128,3072]{1,0:T(8,128)(2,1)} %cot0.3) | copy-start | bytes 2359300
  3.3 34.1 %copy-start.3 = (s32[5]{0:T(128)S(1)}, s32[5]{0:T(128)}, u32[]{:S(2)}) copy-start(s32[5]{0:T(128)} %stack.23.where) | copy-start | bytes 64
  7.6 26.4 %collective-permute-start.4 = (bf16[384,1536]{1,0:T(8,128)(2,1)}, bf16[384,1536]{1,0:T(8,128)(2,1)S(1)}, u32[]{:S(2)}, u32[]{:S(2)}) collective-permute-start(bf16[384,1536]{1,0:T(8,128)(2,1)} %dequantize.1.w0), channel_id=1, source_target_pairs={{0,3},{1,0},{2,1},{3,2},{4,7},{5,4},{6,5},{7,6},{8,11},{9,8},{10,9... | collective-permute-start | bytes 3538952 | tf_op jit(solution)/shard_map/ppermute | solution.py:54
  8.6 28.8 %collective-permute-start.3 = (bf16[384,1536]{1,0:T(8,128)(2,1)}, bf16[384,1536]{1,0:T(8,128)(2,1)}, u32[]{:S(2)}, u32[]{:S(2)}) collective-permute-start(bf16[384,1536]{1,0:T(8,128)(2,1)} %dequantize.1.w0), channel_id=1, source_target_pairs={{0,1},{1,2},{2,3},{3,0},{4,5},{5,6},{6,7},{7,4},{8,9},{9,10},{10,1... | collective-permute-start | bytes 3538952 | tf_op jit(solution)/shard_map/ppermute | solution.py:54
  9.7 20.2 %collective-permute-start.1 = (bf16[128,1536]{1,0:T(8,128)(2,1)S(1)}, bf16[128,1536]{1,0:T(8,128)(2,1)S(1)}, u32[]{:S(2)}, u32[]{:S(2)}) collective-permute-start(bf16[128,1536]{1,0:T(8,128)(2,1)S(1)} %constant_dynamic-slice_fusion), channel_id=1, source_target_pairs={{0,20},{1,21},{2,22},{3,23},{4,16},{5,17},{6,18},{7,19},{8,28},{9,... | collective-permute-start | bytes 1179656 | tf_op jit(solution)/shard_map/ppermute | solution.py:54
  11.8 18.1 %collective-permute-start.5 = (bf16[128,3072]{1,0:T(8,128)(2,1)S(1)}, bf16[128,3072]{1,0:T(8,128)(2,1)S(1)}, u32[]{:S(2)}, u32[]{:S(2)}) collective-permute-start(bf16[128,3072]{1,0:T(8,128)(2,1)S(1)} %copy-done.2), channel_id=1, source_target_pairs={{0,8},{1,9},{2,10},{3,11},{4,12},{5,13},{6,14},{7,15},{8,0},{9,1},... | collective-permute-start | bytes 2359304 | tf_op jit(solution)/shard_map/ppermute | solution.py:54
  22.6 14.8 %collective-permute-start.7 = (bf16[128,3072]{1,0:T(8,128)(2,1)S(1)}, bf16[128,3072]{1,0:T(8,128)(2,1)S(1)}, u32[]{:S(2)}, u32[]{:S(2)}) collective-permute-start(bf16[128,3072]{1,0:T(8,128)(2,1)S(1)} %collective-permute-done.6.cot2), channel_id=1, source_target_pairs={{0,8},{1,9},{2,10},{3,11},{4,12},{5,13},{6,14},{7,15},{8,0},{9,1},... | collective-permute-start | bytes 2359304 | tf_op jit(solution)/shard_map/ppermute | solution.py:54
  29.8 7.5 %collective-permute-start = (bf16[128,3072]{1,0:T(8,128)(2,1)S(1)}, bf16[128,3072]{1,0:T(8,128)(2,1)S(1)}, u32[]{:S(2)}, u32[]{:S(2)}) collective-permute-start(bf16[128,3072]{1,0:T(8,128)(2,1)S(1)} %copy-done), channel_id=1, source_target_pairs={{0,8},{1,9},{2,10},{3,11},{4,12},{5,13},{6,14},{7,15},{8,0},{9,1},... | collective-permute-start | bytes 2359304 | tf_op jit(solution)/shard_map/ppermute | solution.py:54
  29.9 7.5 %collective-permute-start.2 = (bf16[128,1536]{1,0:T(8,128)(2,1)S(1)}, bf16[128,1536]{1,0:T(8,128)(2,1)S(1)}, u32[]{:S(2)}, u32[]{:S(2)}) collective-permute-start(bf16[128,1536]{1,0:T(8,128)(2,1)S(1)} %collective-permute-done.1.pair), channel_id=1, source_target_pairs={{0,8},{1,9},{2,10},{3,11},{4,12},{5,13},{6,14},{7,15},{8,0},{9,1},... | collective-permute-start | bytes 1179656 | tf_op jit(solution)/shard_map/ppermute | solution.py:54
  40.1 10.8 %collective-permute-start.9 = (bf16[48,3072]{1,0:T(8,128)(2,1)S(1)}, bf16[48,3072]{1,0:T(8,128)(2,1)S(1)}, u32[]{:S(2)}, u32[]{:S(2)}) collective-permute-start(bf16[48,3072]{1,0:T(8,128)(2,1)S(1)} %get-tuple-element.73), channel_id=1, source_target_pairs={{0,224},{1,225},{2,226},{3,227},{4,228},{5,229},{6,230},{7,231},{8... | collective-permute-start | bytes 884744 | tf_op jit(solution)/shard_map/ppermute | solution.py:54
  46.1 8.7 %collective-permute-start.8 = (bf16[48,3072]{1,0:T(8,128)(2,1)S(1)}, bf16[48,3072]{1,0:T(8,128)(2,1)S(1)}, u32[]{:S(2)}, u32[]{:S(2)}) collective-permute-start(bf16[48,3072]{1,0:T(8,128)(2,1)S(1)} %get-tuple-element.67), channel_id=1, source_target_pairs={{0,32},{1,33},{2,34},{3,35},{4,36},{5,37},{6,38},{7,39},{8,40},{9,... | collective-permute-start | bytes 884744 | tf_op jit(solution)/shard_map/ppermute | solution.py:54
  51.0 14.0 %collective-permute-start.13 = (bf16[96,3072]{1,0:T(8,128)(2,1)S(1)}, bf16[96,3072]{1,0:T(8,128)(2,1)S(1)}, u32[]{:S(2)}, u32[]{:S(2)}) collective-permute-start(bf16[96,3072]{1,0:T(8,128)(2,1)S(1)} %hop.7), channel_id=1, source_target_pairs={{0,224},{1,225},{2,226},{3,227},{4,228},{5,229},{6,230},{7,231},{8... | collective-permute-start | bytes 1769480 | tf_op jit(solution)/shard_map/ppermute | solution.py:54
  54.9 14.3 %collective-permute-start.12 = (bf16[96,3072]{1,0:T(8,128)(2,1)S(1)}, bf16[96,3072]{1,0:T(8,128)(2,1)S(1)}, u32[]{:S(2)}, u32[]{:S(2)}) collective-permute-start(bf16[96,3072]{1,0:T(8,128)(2,1)S(1)} %hop.6), channel_id=1, source_target_pairs={{0,32},{1,33},{2,34},{3,35},{4,36},{5,37},{6,38},{7,39},{8,40},{9,... | collective-permute-start | bytes 1769480 | tf_op jit(solution)/shard_map/ppermute | solution.py:54
  56.1 13.3 %collective-permute-start.11 = (bf16[384,768]{1,0:T(8,128)(2,1)S(1)}, bf16[384,768]{1,0:T(8,128)(2,1)S(1)}, u32[]{:S(2)}, u32[]{:S(2)}) collective-permute-start(bf16[384,768]{1,0:T(8,128)(2,1)S(1)} %slice.21), channel_id=1, source_target_pairs={{0,3},{1,0},{2,1},{3,2},{4,7},{5,4},{6,5},{7,6},{8,11},{9,8},{10,9... | collective-permute-start | bytes 1769480 | tf_op jit(solution)/shard_map/ppermute | solution.py:54
  56.7 13.7 %collective-permute-start.10 = (bf16[384,768]{1,0:T(8,128)(2,1)S(1)}, bf16[384,768]{1,0:T(8,128)(2,1)S(1)}, u32[]{:S(2)}, u32[]{:S(2)}) collective-permute-start(bf16[384,768]{1,0:T(8,128)(2,1)S(1)} %slice.20), channel_id=1, source_target_pairs={{0,1},{1,2},{2,3},{3,0},{4,5},{5,6},{6,7},{7,4},{8,9},{9,10},{10,1... | collective-permute-start | bytes 1769480 | tf_op jit(solution)/shard_map/ppermute | solution.py:54
  65.1 5.3 %copy-start.1 = (bf16[384,1536]{1,0:T(8,128)(2,1)S(1)}, bf16[384,1536]{1,0:T(8,128)(2,1)}, u32[]{:S(2)}) copy-start(bf16[384,1536]{1,0:T(8,128)(2,1)} %dequantize.1.w0) | copy-start | bytes 3538948
  65.2 13.5 %collective-permute-start.17 = (bf16[96,3072]{1,0:T(8,128)(2,1)S(1)}, bf16[96,3072]{1,0:T(8,128)(2,1)S(1)}, u32[]{:S(2)}, u32[]{:S(2)}) collective-permute-start(bf16[96,3072]{1,0:T(8,128)(2,1)S(1)} %hop.9), channel_id=1, source_target_pairs={{0,224},{1,225},{2,226},{3,227},{4,228},{5,229},{6,230},{7,231},{8... | collective-permute-start | bytes 1769480 | tf_op jit(solution)/shard_map/ppermute | solution.py:54
  69.3 13.4 %collective-permute-start.15 = (bf16[96,3072]{1,0:T(8,128)(2,1)S(1)}, bf16[96,3072]{1,0:T(8,128)(2,1)S(1)}, u32[]{:S(2)}, u32[]{:S(2)}) collective-permute-start(bf16[96,3072]{1,0:T(8,128)(2,1)S(1)} %hop.8), channel_id=1, source_target_pairs={{0,32},{1,33},{2,34},{3,35},{4,36},{5,37},{6,38},{7,39},{8,40},{9,... | collective-permute-start | bytes 1769480 | tf_op jit(solution)/shard_map/ppermute | solution.py:54
  75.2 17.1 %collective-permute-start.14 = (bf16[256,1536]{1,0:T(8,128)(2,1)S(1)}, bf16[256,1536]{1,0:T(8,128)(2,1)S(1)}, u32[]{:S(2)}, u32[]{:S(2)}) collective-permute-start(bf16[256,1536]{1,0:T(8,128)(2,1)S(1)} %get-tuple-element.85), channel_id=1, source_target_pairs={{0,20},{1,21},{2,22},{3,23},{4,16},{5,17},{6,18},{7,19},{8,28},{9,... | collective-permute-start | bytes 2359304 | tf_op jit(solution)/shard_map/ppermute | solution.py:54
  78.9 13.6 %collective-permute-start.18 = (bf16[96,3072]{1,0:T(8,128)(2,1)S(1)}, bf16[96,3072]{1,0:T(8,128)(2,1)S(1)}, u32[]{:S(2)}, u32[]{:S(2)}) collective-permute-start(bf16[96,3072]{1,0:T(8,128)(2,1)S(1)} %hop.11), channel_id=1, source_target_pairs={{0,224},{1,225},{2,226},{3,227},{4,228},{5,229},{6,230},{7,231},{8... | collective-permute-start | bytes 1769480 | tf_op jit(solution)/shard_map/ppermute | solution.py:54
  82.8 12.0 %collective-permute-start.16 = (bf16[96,3072]{1,0:T(8,128)(2,1)S(1)}, bf16[96,3072]{1,0:T(8,128)(2,1)S(1)}, u32[]{:S(2)}, u32[]{:S(2)}) collective-permute-start(bf16[96,3072]{1,0:T(8,128)(2,1)S(1)} %hop.10), channel_id=1, source_target_pairs={{0,32},{1,33},{2,34},{3,35},{4,36},{5,37},{6,38},{7,39},{8,40},{9,... | collective-permute-start | bytes 1769480 | tf_op jit(solution)/shard_map/ppermute | solution.py:54
  87.8 12.7 %collective-permute-start.22 = (bf16[256,1536]{1,0:T(8,128)(2,1)S(1)}, bf16[256,1536]{1,0:T(8,128)(2,1)S(1)}, u32[]{:S(2)}, u32[]{:S(2)}) collective-permute-start(bf16[256,1536]{1,0:T(8,128)(2,1)S(1)} %get-tuple-element.104), channel_id=1, source_target_pairs={{0,8},{1,9},{2,10},{3,11},{4,12},{5,13},{6,14},{7,15},{8,0},{9,1},... | collective-permute-start | bytes 2359304 | tf_op jit(solution)/shard_map/ppermute | solution.py:54
  95.9 8.0 %collective-permute-start.19 = (bf16[24,3072]{1,0:T(8,128)(2,1)S(1)}, bf16[24,3072]{1,0:T(8,128)(2,1)S(1)}, u32[]{:S(2)}, u32[]{:S(2)}) collective-permute-start(bf16[24,3072]{1,0:T(8,128)(2,1)S(1)} %get-tuple-element.101), channel_id=1, source_target_pairs={{0,1},{1,2},{2,3},{3,0},{4,5},{5,6},{6,7},{7,4},{8,9},{9,10},{10,1... | collective-permute-start | bytes 442376 | tf_op jit(solution)/shard_map/ppermute | solution.py:54
  96.1 7.9 %collective-permute-start.20 = (bf16[24,3072]{1,0:T(8,128)(2,1)S(1)}, bf16[24,3072]{1,0:T(8,128)(2,1)S(1)}, u32[]{:S(2)}, u32[]{:S(2)}) collective-permute-start(bf16[24,3072]{1,0:T(8,128)(2,1)S(1)} %get-tuple-element.102), channel_id=1, source_target_pairs={{0,2},{1,3},{2,0},{3,1},{4,6},{5,7},{6,4},{7,5},{8,10},{9,11},{10,... | collective-permute-start | bytes 442376 | tf_op jit(solution)/shard_map/ppermute | solution.py:54
  98.6 6.2 %collective-permute-start.21 = (bf16[24,3072]{1,0:T(8,128)(2,1)S(1)}, bf16[24,3072]{1,0:T(8,128)(2,1)S(1)}, u32[]{:S(2)}, u32[]{:S(2)}) collective-permute-start(bf16[24,3072]{1,0:T(8,128)(2,1)S(1)} %get-tuple-element.103), channel_id=1, source_target_pairs={{0,3},{1,0},{2,1},{3,2},{4,7},{5,4},{6,5},{7,6},{8,11},{9,8},{10,9... | collective-permute-start | bytes 442376 | tf_op jit(solution)/shard_map/ppermute | solution.py:54
  100.5 13.3 %collective-permute-start.23 = (bf16[128,1536]{1,0:T(8,128)(2,1)}, bf16[128,1536]{1,0:T(8,128)(2,1)S(1)}, u32[]{:S(2)}, u32[]{:S(2)}) collective-permute-start(bf16[128,1536]{1,0:T(8,128)(2,1)} %get-tuple-element.118), channel_id=1, source_target_pairs={{0,8},{1,9},{2,10},{3,11},{4,12},{5,13},{6,14},{7,15},{8,0},{9,1},... | collective-permute-start | bytes 1179656 | tf_op jit(solution)/shard_map/ppermute | solution.py:54
  100.8 14.1 %collective-permute-start.24 = (bf16[128,1536]{1,0:T(8,128)(2,1)S(1)}, bf16[128,1536]{1,0:T(8,128)(2,1)S(1)}, u32[]{:S(2)}, u32[]{:S(2)}) collective-permute-start(bf16[128,1536]{1,0:T(8,128)(2,1)S(1)} %get-tuple-element.120), channel_id=1, source_target_pairs={{0,20},{1,21},{2,22},{3,23},{4,16},{5,17},{6,18},{7,19},{8,28},{9,... | collective-permute-start | bytes 1179656 | tf_op jit(solution)/shard_map/ppermute | solution.py:54
  105.5 15.5 %collective-permute-start.25 = (bf16[12,3072]{1,0:T(8,128)(2,1)S(1)}, bf16[12,3072]{1,0:T(8,128)(2,1)S(1)}, u32[]{:S(2)}, u32[]{:S(2)}) collective-permute-start(bf16[12,3072]{1,0:T(8,128)(2,1)S(1)} %get-tuple-element.110), channel_id=1, source_target_pairs={{0,24},{1,25},{2,26},{3,27},{4,184},{5,185},{6,186},{7,187},{8,72}... | collective-permute-start | bytes 221192 | tf_op jit(solution)/shard_map/ppermute | solution.py:54
  107.4 13.6 %collective-permute-start.26 = (bf16[12,3072]{1,0:T(8,128)(2,1)S(1)}, bf16[12,3072]{1,0:T(8,128)(2,1)S(1)}, u32[]{:S(2)}, u32[]{:S(2)}) collective-permute-start(bf16[12,3072]{1,0:T(8,128)(2,1)S(1)} %get-tuple-element.114), channel_id=1, source_target_pairs={{0,28},{1,29},{2,30},{3,31},{4,188},{5,189},{6,190},{7,191},{8,76}... | collective-permute-start | bytes 221192 | tf_op jit(solution)/shard_map/ppermute | solution.py:54

commit v11 on v10

--- a/solution.py
+++ b/solution.py
@@ -218,11 +218,12 @@
 def last_hop_kernel(where, up, down, part, own, *refs):
     *pieces, total = refs
     size = own.shape[0]
+    sums = f32(part[...]) + f32(up[...]) + f32(down[...])
     for x in range(4):
         for yh in range(2):
             here = slice((yh * 4 + x) * (size // 2), (yh * 4 + x + 1) * (size // 2))
             there = slice((x * 2 + yh) * (size // 2), (x * 2 + yh + 1) * (size // 2))
-            total[there] = f32(part[here]) + f32(up[here]) + f32(down[here])
+            total[there] = sums[here]
     for dx, ref in enumerate((own, *pieces)):
         start = pl.multiple_of((where[2] + dx) % 4 * size, 8)
         ref[...] = total[pl.ds(start, size)].astype(ref.dtype)

time: 122 us -> 122 us (level)
  no operation moved by 1% of the time
where the time goes in v11:
time: 122 us
  waiting for transfers between devices  47 us (39%)
  starting transfers between devices  43.7 us (36%)
  Pallas kernels  24.2 us (20%)
  other arithmetic  4.11 us (3%)
  local copies, waits for them, and re-layouts  1.85 us (2%)
    ppermute x27, waiting for transfers between devices, send(): return lax.ppermute(value, AXES, pairs)  47 us
    ppermute x27, starting transfers between devices, send(): return lax.ppermute(value, AXES, pairs)  43.7 us
    pallas_call x7, Pallas kernels, call(): pl.pallas_call(kernel, name=name, grid_spec=pltpu.PrefetchScalarGridSpec(...  23.5 us
  transfers between devices with their start and end apart: 27, of which 12 were waited for; matrix products, arithmetic and copies ran while one was open for 4% of the time, Pallas kernels for 18%

profile of v11, /device:TPU:24, one launch (start us, length us, event | category | flops | bytes accessed | tf_op | source)
XLA Modules:
  0.0 121.8 jit_solution(3600587870553675785)
XLA Ops:
  0.6 2.0 %collective-permute-start.6 = (bf16[128,3072]{1,0:T(8,128)(2,1)}, bf16[128,3072]{1,0:T(8,128)(2,1)S(1)}, u32[]{:S(2)}, u32[]{:S(2)}) collective-permute-start(bf16[128,3072]{1,0:T(8,128)(2,1)} %cot0.3), channel_id=1, source_target_pairs={{0,20},{1,21},{2,22},{3,23},{4,16},{5,17},{6,18},{7,19},{8,28},{9,... | collective-permute-start | bytes 2359304 | tf_op jit(solution)/shard_map/ppermute | solution.py:54
  2.7 0.6 stack.23.where
  3.3 4.3 %dequantize.1.w0 = bf16[384,1536]{1,0:T(8,128)(2,1)} custom-call(s32[5]{0:T(128)} %stack.23.where, bf16[384,3072]{1,0:T(8,128)(2,1)} %levels.1, f32[12,384]{1,0:T(8,128)} %bitcast.6), custom_call_target="tpu_custom_call" | custom-call | flops 589824 | bytes 3557376 | tf_op jit(solution)/shard_map/dequantize/pallas_call | solution.py:72
  7.6 1.0 collective-permute-start.4
  8.6 1.0 collective-permute-start.3
  9.7 2.1 %collective-permute-start.1 = (bf16[128,1536]{1,0:T(8,128)(2,1)S(1)}, bf16[128,1536]{1,0:T(8,128)(2,1)S(1)}, u32[]{:S(2)}, u32[]{:S(2)}) collective-permute-start(bf16[128,1536]{1,0:T(8,128)(2,1)S(1)} %constant_dynamic-slice_fusion), channel_id=1, source_target_pairs={{0,20},{1,21},{2,22},{3,23},{4,16},{5,17},{6,18},{7,19},{8,28},{9,... | collective-permute-start | bytes 1179656 | tf_op jit(solution)/shard_map/ppermute | solution.py:54
  11.8 0.0 collective-permute-start.5
  11.8 10.8 %collective-permute-done.6.cot2 = bf16[128,3072]{1,0:T(8,128)(2,1)S(1)} collective-permute-done((bf16[128,3072]{1,0:T(8,128)(2,1)}, bf16[128,3072]{1,0:T(8,128)(2,1)S(1)}, u32[]{:S(2)}, u32[]{:S(2)}) %collective-permute-start.6) | collective-permute-done | bytes 786464 | tf_op jit(solution)/shard_map/ppermute | solution.py:54
  22.6 0.0 collective-permute-start.7
  22.6 7.3 %collective-permute-done.1.pair = bf16[128,1536]{1,0:T(8,128)(2,1)S(1)} collective-permute-done((bf16[128,1536]{1,0:T(8,128)(2,1)S(1)}, bf16[128,1536]{1,0:T(8,128)(2,1)S(1)}, u32[]{:S(2)}, u32[]{:S(2)}) %collective-permute-start.1) | collective-permute-done | bytes 393248 | tf_op jit(solution)/shard_map/ppermute | solution.py:54
  29.8 0.0 collective-permute-start
  29.9 0.5 collective-permute-start.2
  30.4 3.6 %collective-permute-done.4.w2 = bf16[384,1536]{1,0:T(8,128)(2,1)S(1)} collective-permute-done((bf16[384,1536]{1,0:T(8,128)(2,1)}, bf16[384,1536]{1,0:T(8,128)(2,1)S(1)}, u32[]{:S(2)}, u32[]{:S(2)}) %collective-permute-start.4) | collective-permute-done | bytes 1179680 | tf_op jit(solution)/shard_map/ppermute | solution.py:54
  34.0 3.4 %collective-permute-done.3.w1 = bf16[384,1536]{1,0:T(8,128)(2,1)} collective-permute-done((bf16[384,1536]{1,0:T(8,128)(2,1)}, bf16[384,1536]{1,0:T(8,128)(2,1)}, u32[]{:S(2)}, u32[]{:S(2)}) %collective-permute-start.3) | collective-permute-done | bytes 1179680 | tf_op jit(solution)/shard_map/ppermute | solution.py:54
  37.4 0.0 collective-permute-done.7.cot3
  37.4 0.0 collective-permute-done.2.psib
  37.4 0.0 collective-permute-done.sib
  37.4 2.7 %far.1 = (bf16[48,3072]{1,0:T(8,128)(2,1)S(1)}, bf16[48,3072]{1,0:T(8,128)(2,1)S(1)}) custom-call(s32[5]{0:T(128)S(1)} %copy-done.3, bf16[128,3072]{1,0:T(8,128)(2,1)S(1)} %copy-done, bf16[128,3072]{1,0:T(8,128)(2,1)S(1)} %collective-permute-done.sib, bf16[128,1536]{1,0:T(8,128)(2,1)S(1)} %collective-permute-done.1.pair, ...), custom_call_target="tpu_custom_call" | custom-call | flops 805306368 | bytes 6094848 | tf_op jit(solution)/shard_map/far/pallas_call | solution.py:72
  40.1 5.9 %collective-permute-start.9 = (bf16[48,3072]{1,0:T(8,128)(2,1)S(1)}, bf16[48,3072]{1,0:T(8,128)(2,1)S(1)}, u32[]{:S(2)}, u32[]{:S(2)}) collective-permute-start(bf16[48,3072]{1,0:T(8,128)(2,1)S(1)} %get-tuple-element.73), channel_id=1, source_target_pairs={{0,224},{1,225},{2,226},{3,227},{4,228},{5,229},{6,230},{7,231},{8... | collective-permute-start | bytes 884744 | tf_op jit(solution)/shard_map/ppermute | solution.py:54
  46.1 4.9 %gradient.1 = (bf16[96,3072]{1,0:T(8,128)(2,1)S(1)}, bf16[96,3072]{1,0:T(8,128)(2,1)S(1)}, bf16[96,3072]{1,0:T(8,128)(2,1)S(1)}, bf16[96,3072]{1,0:T(8,128)(2,1)...) custom-call(s32[5]{0:T(128)S(1)} %copy-done.3, ...), custom_call_target="tpu_custom_call" | custom-call | flops 2415919104 | bytes 9633792 | tf_op jit(solution)/shard_map/gradient/pallas_call | solution.py:72
  51.0 0.0 collective-permute-done.9.arrived
  51.0 0.1 hop.7
  51.0 3.7 %collective-permute-start.13 = (bf16[96,3072]{1,0:T(8,128)(2,1)S(1)}, bf16[96,3072]{1,0:T(8,128)(2,1)S(1)}, u32[]{:S(2)}, u32[]{:S(2)}) collective-permute-start(bf16[96,3072]{1,0:T(8,128)(2,1)S(1)} %hop.7), channel_id=1, source_target_pairs={{0,224},{1,225},{2,226},{3,227},{4,228},{5,229},{6,230},{7,231},{8... | collective-permute-start | bytes 1769480 | tf_op jit(solution)/shard_map/ppermute | solution.py:54
  54.8 0.0 collective-permute-done.8.arrived
  54.8 0.1 hop.6
  54.9 0.1 collective-permute-start.12
  55.0 1.1 slice.20
  56.1 0.6 collective-permute-start.11
  56.7 1.5 %collective-permute-start.10 = (bf16[384,768]{1,0:T(8,128)(2,1)S(1)}, bf16[384,768]{1,0:T(8,128)(2,1)S(1)}, u32[]{:S(2)}, u32[]{:S(2)}) collective-permute-start(bf16[384,768]{1,0:T(8,128)(2,1)S(1)} %slice.20), channel_id=1, source_target_pairs={{0,1},{1,2},{2,3},{3,0},{4,5},{5,6},{6,7},{7,4},{8,9},{9,10},{10,1... | collective-permute-start | bytes 1769480 | tf_op jit(solution)/shard_map/ppermute | solution.py:54
  58.2 6.8 %collective-permute-done.13.refs_0_ = bf16[96,3072]{1,0:T(8,128)(2,1)S(1)} collective-permute-done((bf16[96,3072]{1,0:T(8,128)(2,1)S(1)}, bf16[96,3072]{1,0:T(8,128)(2,1)S(1)}, u32[]{:S(2)}, u32[]{:S(2)}) %collective-permute-start.13) | collective-permute-done | bytes 589856 | tf_op jit(solution)/shard_map/ppermute | solution.py:54
  65.1 0.1 hop.9
  65.2 3.9 %collective-permute-start.17 = (bf16[96,3072]{1,0:T(8,128)(2,1)S(1)}, bf16[96,3072]{1,0:T(8,128)(2,1)S(1)}, u32[]{:S(2)}, u32[]{:S(2)}) collective-permute-start(bf16[96,3072]{1,0:T(8,128)(2,1)S(1)} %hop.9), channel_id=1, source_target_pairs={{0,224},{1,225},{2,226},{3,227},{4,228},{5,229},{6,230},{7,231},{8... | collective-permute-start | bytes 1769480 | tf_op jit(solution)/shard_map/ppermute | solution.py:54
  69.2 0.1 hop.8
  69.3 0.1 collective-permute-start.15
  69.4 1.0 collective-permute-done.10.w3
  70.4 4.8 %forward.1 = (f32[128,1536]{1,0:T(8,128)S(1)}, f32[128,1536]{1,0:T(8,128)S(1)}, bf16[256,1536]{1,0:T(8,128)(2,1)S(1)}) custom-call(s32[5]{0:T(128)S(1)} %copy-done.3, bf16[128,3072]{1,0:T(8,128)(2,1)S(1)} %copy-done, bf16[128,3072]{1,0:T(8,128)(2,1)S(1)} %collective-permute-done.sib, bf16[128,1536]{1,0:T(8,128)(2,1)S(1)} %collective-permute-done.1.pair, ...), custom_call_target="tpu_custom_call" | custom-call | flops 2415919104 | bytes 9437184 | tf_op jit(solution)/shard_map/forward/pallas_call | solution.py:72
  75.2 2.8 %collective-permute-start.14 = (bf16[256,1536]{1,0:T(8,128)(2,1)S(1)}, bf16[256,1536]{1,0:T(8,128)(2,1)S(1)}, u32[]{:S(2)}, u32[]{:S(2)}) collective-permute-start(bf16[256,1536]{1,0:T(8,128)(2,1)S(1)} %get-tuple-element.85), channel_id=1, source_target_pairs={{0,20},{1,21},{2,22},{3,23},{4,16},{5,17},{6,18},{7,19},{8,28},{9,... | collective-permute-start | bytes 2359304 | tf_op jit(solution)/shard_map/ppermute | solution.py:54
  78.0 0.8 collective-permute-done.17.refs_0_
  78.7 0.2 hop.11
  78.9 3.8 %collective-permute-start.18 = (bf16[96,3072]{1,0:T(8,128)(2,1)S(1)}, bf16[96,3072]{1,0:T(8,128)(2,1)S(1)}, u32[]{:S(2)}, u32[]{:S(2)}) collective-permute-start(bf16[96,3072]{1,0:T(8,128)(2,1)S(1)} %hop.11), channel_id=1, source_target_pairs={{0,224},{1,225},{2,226},{3,227},{4,228},{5,229},{6,230},{7,231},{8... | collective-permute-start | bytes 1769480 | tf_op jit(solution)/shard_map/ppermute | solution.py:54
  82.6 0.1 hop.10
  82.8 0.1 collective-permute-start.16
  82.9 4.9 %backward.1 = (f32[256,1536]{1,0:T(8,128)S(1)}, bf16[256,1536]{1,0:T(8,128)(2,1)S(1)}) custom-call(s32[5]{0:T(128)S(1)} %copy-done.3, bf16[128,3072]{1,0:T(8,128)(2,1)S(1)} %copy-done.2, bf16[128,3072]{1,0:T(8,128)(2,1)S(1)} %collective-permute-done.5.cot1, bf16[128,3072]{1,0:T(8,128)(2,1)S(1)} %collective-permute-done.6.cot2, ...), custom_call_target="tpu_custom_call" | custom-call | flops 2415919104 | bytes 10223616 | tf_op jit(solution)/shard_map/backward/pallas_call | solution.py:72
  87.8 0.1 collective-permute-start.22
  87.9 4.3 %collective-permute-done.14 = bf16[256,1536]{1,0:T(8,128)(2,1)S(1)} collective-permute-done((bf16[256,1536]{1,0:T(8,128)(2,1)S(1)}, bf16[256,1536]{1,0:T(8,128)(2,1)S(1)}, u32[]{:S(2)}, u32[]{:S(2)}) %collective-permute-start.14) | collective-permute-done | bytes 786464 | tf_op jit(solution)/shard_map/ppermute | solution.py:54
  92.3 0.2 convert_element_type.20
  92.5 2.3 %collective-permute-done.16.up = bf16[96,3072]{1,0:T(8,128)(2,1)S(1)} collective-permute-done((bf16[96,3072]{1,0:T(8,128)(2,1)S(1)}, bf16[96,3072]{1,0:T(8,128)(2,1)S(1)}, u32[]{:S(2)}, u32[]{:S(2)}) %collective-permute-start.16) | collective-permute-done | bytes 589856 | tf_op jit(solution)/shard_map/ppermute | solution.py:54
  94.8 1.2 %last_hop.1 = (f32[24,3072]{1,0:T(8,128)S(1)}, bf16[24,3072]{1,0:T(8,128)(2,1)S(1)}, bf16[24,3072]{1,0:T(8,128)(2,1)S(1)}, bf16[24,3072]{1,0:T(8,128)(2,1)S(1)}) custom-call(s32[5]{0:T(128)S(1)} %copy-done.3, bf16[96,3072]{1,0:T(8,128)(2,1)S(1)} %collective-permute-done.16.up, bf16[96,3072]{1,0:T(8,128)(2,1)S(1)} %collective-permute-done.18.down, ...), custom_call_target="tpu_custom_call" | custom-call | flops 589824 | bytes 2506752 | tf_op jit(solution)/shard_map/last_hop/pallas_call | solution.py:72
  96.0 0.1 collective-permute-start.19
  96.1 2.5 %collective-permute-start.20 = (bf16[24,3072]{1,0:T(8,128)(2,1)S(1)}, bf16[24,3072]{1,0:T(8,128)(2,1)S(1)}, u32[]{:S(2)}, u32[]{:S(2)}) collective-permute-start(bf16[24,3072]{1,0:T(8,128)(2,1)S(1)} %get-tuple-element.102), channel_id=1, source_target_pairs={{0,2},{1,3},{2,0},{3,1},{4,6},{5,7},{6,4},{7,5},{8,10},{9,11},{10,... | collective-permute-start | bytes 442376 | tf_op jit(solution)/shard_map/ppermute | solution.py:54
  98.7 1.0 collective-permute-start.21
  99.7 0.9 add_convert_fusion.2
  100.6 0.2 add_convert_fusion
  100.8 0.1 fusion
  100.9 2.4 %collective-permute-start.24 = (bf16[128,1536]{1,0:T(8,128)(2,1)S(1)}, bf16[128,1536]{1,0:T(8,128)(2,1)S(1)}, u32[]{:S(2)}, u32[]{:S(2)}) collective-permute-start(bf16[128,1536]{1,0:T(8,128)(2,1)S(1)} %get-tuple-element.120), channel_id=1, source_target_pairs={{0,20},{1,21},{2,22},{3,23},{4,16},{5,17},{6,18},{7,19},{8,28},{9,... | collective-permute-start | bytes 1179656 | tf_op jit(solution)/shard_map/ppermute | solution.py:54
  103.3 0.7 collective-permute-done.19.one
  104.0 0.9 collective-permute-done.21.three
  104.9 0.7 sum_over_x.1
  105.6 1.9 %collective-permute-start.25 = (bf16[12,3072]{1,0:T(8,128)(2,1)S(1)}, bf16[12,3072]{1,0:T(8,128)(2,1)S(1)}, u32[]{:S(2)}, u32[]{:S(2)}) collective-permute-start(bf16[12,3072]{1,0:T(8,128)(2,1)S(1)} %get-tuple-element.110), channel_id=1, source_target_pairs={{0,24},{1,25},{2,26},{3,27},{4,184},{5,185},{6,186},{7,187},{8,72}... | collective-permute-start | bytes 221192 | tf_op jit(solution)/shard_map/ppermute | solution.py:54
  107.5 6.4 %collective-permute-start.26 = (bf16[12,3072]{1,0:T(8,128)(2,1)S(1)}, bf16[12,3072]{1,0:T(8,128)(2,1)S(1)}, u32[]{:S(2)}, u32[]{:S(2)}) collective-permute-start(bf16[12,3072]{1,0:T(8,128)(2,1)S(1)} %get-tuple-element.114), channel_id=1, source_target_pairs={{0,28},{1,29},{2,30},{3,31},{4,188},{5,189},{6,190},{7,191},{8,76}... | collective-permute-start | bytes 221192 | tf_op jit(solution)/shard_map/ppermute | solution.py:54
  113.9 1.1 maximum_select_fusion
  115.0 1.1 maximum_select_fusion.1
  116.0 5.0 %collective-permute-done.26 = bf16[12,3072]{1,0:T(8,128)(2,1)S(1)} collective-permute-done((bf16[12,3072]{1,0:T(8,128)(2,1)S(1)}, bf16[12,3072]{1,0:T(8,128)(2,1)S(1)}, u32[]{:S(2)}, u32[]{:S(2)}) %collective-permute-start.26) | collective-permute-done | bytes 73760 | tf_op jit(solution)/shard_map/ppermute | solution.py:54
  121.1 0.7 convert_add_fusion
  (22 shorter events, 0.1 us)
Async XLA Ops:
  0.6 21.9 %collective-permute-start.6 = (bf16[128,3072]{1,0:T(8,128)(2,1)}, bf16[128,3072]{1,0:T(8,128)(2,1)S(1)}, u32[]{:S(2)}, u32[]{:S(2)}) collective-permute-start(bf16[128,3072]{1,0:T(8,128)(2,1)} %cot0.3), channel_id=1, source_target_pairs={{0,20},{1,21},{2,22},{3,23},{4,16},{5,17},{6,18},{7,19},{8,28},{9,... | collective-permute-start | bytes 2359304 | tf_op jit(solution)/shard_map/ppermute | solution.py:54
  3.3 6.3 %copy-start = (bf16[128,3072]{1,0:T(8,128)(2,1)S(1)}, bf16[128,3072]{1,0:T(8,128)(2,1)}, u32[]{:S(2)}) copy-start(bf16[128,3072]{1,0:T(8,128)(2,1)} %own.5) | copy-start | bytes 2359300
  3.3 8.5 %copy-start.2 = (bf16[128,3072]{1,0:T(8,128)(2,1)S(1)}, bf16[128,3072]{1,0:T(8,128)(2,1)}, u32[]{:S(2)}) copy-start(bf16[128,3072]{1,0:T(8,128)(2,1)} %cot0.3) | copy-start | bytes 2359300
  3.3 34.1 %copy-start.3 = (s32[5]{0:T(128)S(1)}, s32[5]{0:T(128)}, u32[]{:S(2)}) copy-start(s32[5]{0:T(128)} %stack.23.where) | copy-start | bytes 64
  7.6 26.4 %collective-permute-start.4 = (bf16[384,1536]{1,0:T(8,128)(2,1)}, bf16[384,1536]{1,0:T(8,128)(2,1)S(1)}, u32[]{:S(2)}, u32[]{:S(2)}) collective-permute-start(bf16[384,1536]{1,0:T(8,128)(2,1)} %dequantize.1.w0), channel_id=1, source_target_pairs={{0,3},{1,0},{2,1},{3,2},{4,7},{5,4},{6,5},{7,6},{8,11},{9,8},{10,9... | collective-permute-start | bytes 3538952 | tf_op jit(solution)/shard_map/ppermute | solution.py:54
  8.6 28.8 %collective-permute-start.3 = (bf16[384,1536]{1,0:T(8,128)(2,1)}, bf16[384,1536]{1,0:T(8,128)(2,1)}, u32[]{:S(2)}, u32[]{:S(2)}) collective-permute-start(bf16[384,1536]{1,0:T(8,128)(2,1)} %dequantize.1.w0), channel_id=1, source_target_pairs={{0,1},{1,2},{2,3},{3,0},{4,5},{5,6},{6,7},{7,4},{8,9},{9,10},{10,1... | collective-permute-start | bytes 3538952 | tf_op jit(solution)/shard_map/ppermute | solution.py:54
  9.7 20.2 %collective-permute-start.1 = (bf16[128,1536]{1,0:T(8,128)(2,1)S(1)}, bf16[128,1536]{1,0:T(8,128)(2,1)S(1)}, u32[]{:S(2)}, u32[]{:S(2)}) collective-permute-start(bf16[128,1536]{1,0:T(8,128)(2,1)S(1)} %constant_dynamic-slice_fusion), channel_id=1, source_target_pairs={{0,20},{1,21},{2,22},{3,23},{4,16},{5,17},{6,18},{7,19},{8,28},{9,... | collective-permute-start | bytes 1179656 | tf_op jit(solution)/shard_map/ppermute | solution.py:54
  11.8 18.1 %collective-permute-start.5 = (bf16[128,3072]{1,0:T(8,128)(2,1)S(1)}, bf16[128,3072]{1,0:T(8,128)(2,1)S(1)}, u32[]{:S(2)}, u32[]{:S(2)}) collective-permute-start(bf16[128,3072]{1,0:T(8,128)(2,1)S(1)} %copy-done.2), channel_id=1, source_target_pairs={{0,8},{1,9},{2,10},{3,11},{4,12},{5,13},{6,14},{7,15},{8,0},{9,1},... | collective-permute-start | bytes 2359304 | tf_op jit(solution)/shard_map/ppermute | solution.py:54
  22.6 14.8 %collective-permute-start.7 = (bf16[128,3072]{1,0:T(8,128)(2,1)S(1)}, bf16[128,3072]{1,0:T(8,128)(2,1)S(1)}, u32[]{:S(2)}, u32[]{:S(2)}) collective-permute-start(bf16[128,3072]{1,0:T(8,128)(2,1)S(1)} %collective-permute-done.6.cot2), channel_id=1, source_target_pairs={{0,8},{1,9},{2,10},{3,11},{4,12},{5,13},{6,14},{7,15},{8,0},{9,1},... | collective-permute-start | bytes 2359304 | tf_op jit(solution)/shard_map/ppermute | solution.py:54
  29.8 7.5 %collective-permute-start = (bf16[128,3072]{1,0:T(8,128)(2,1)S(1)}, bf16[128,3072]{1,0:T(8,128)(2,1)S(1)}, u32[]{:S(2)}, u32[]{:S(2)}) collective-permute-start(bf16[128,3072]{1,0:T(8,128)(2,1)S(1)} %copy-done), channel_id=1, source_target_pairs={{0,8},{1,9},{2,10},{3,11},{4,12},{5,13},{6,14},{7,15},{8,0},{9,1},... | collective-permute-start | bytes 2359304 | tf_op jit(solution)/shard_map/ppermute | solution.py:54
  29.9 7.5 %collective-permute-start.2 = (bf16[128,1536]{1,0:T(8,128)(2,1)S(1)}, bf16[128,1536]{1,0:T(8,128)(2,1)S(1)}, u32[]{:S(2)}, u32[]{:S(2)}) collective-permute-start(bf16[128,1536]{1,0:T(8,128)(2,1)S(1)} %collective-permute-done.1.pair), channel_id=1, source_target_pairs={{0,8},{1,9},{2,10},{3,11},{4,12},{5,13},{6,14},{7,15},{8,0},{9,1},... | collective-permute-start | bytes 1179656 | tf_op jit(solution)/shard_map/ppermute | solution.py:54
  40.1 10.8 %collective-permute-start.9 = (bf16[48,3072]{1,0:T(8,128)(2,1)S(1)}, bf16[48,3072]{1,0:T(8,128)(2,1)S(1)}, u32[]{:S(2)}, u32[]{:S(2)}) collective-permute-start(bf16[48,3072]{1,0:T(8,128)(2,1)S(1)} %get-tuple-element.73), channel_id=1, source_target_pairs={{0,224},{1,225},{2,226},{3,227},{4,228},{5,229},{6,230},{7,231},{8... | collective-permute-start | bytes 884744 | tf_op jit(solution)/shard_map/ppermute | solution.py:54
  46.1 8.7 %collective-permute-start.8 = (bf16[48,3072]{1,0:T(8,128)(2,1)S(1)}, bf16[48,3072]{1,0:T(8,128)(2,1)S(1)}, u32[]{:S(2)}, u32[]{:S(2)}) collective-permute-start(bf16[48,3072]{1,0:T(8,128)(2,1)S(1)} %get-tuple-element.67), channel_id=1, source_target_pairs={{0,32},{1,33},{2,34},{3,35},{4,36},{5,37},{6,38},{7,39},{8,40},{9,... | collective-permute-start | bytes 884744 | tf_op jit(solution)/shard_map/ppermute | solution.py:54
  51.0 14.0 %collective-permute-start.13 = (bf16[96,3072]{1,0:T(8,128)(2,1)S(1)}, bf16[96,3072]{1,0:T(8,128)(2,1)S(1)}, u32[]{:S(2)}, u32[]{:S(2)}) collective-permute-start(bf16[96,3072]{1,0:T(8,128)(2,1)S(1)} %hop.7), channel_id=1, source_target_pairs={{0,224},{1,225},{2,226},{3,227},{4,228},{5,229},{6,230},{7,231},{8... | collective-permute-start | bytes 1769480 | tf_op jit(solution)/shard_map/ppermute | solution.py:54
  54.9 14.3 %collective-permute-start.12 = (bf16[96,3072]{1,0:T(8,128)(2,1)S(1)}, bf16[96,3072]{1,0:T(8,128)(2,1)S(1)}, u32[]{:S(2)}, u32[]{:S(2)}) collective-permute-start(bf16[96,3072]{1,0:T(8,128)(2,1)S(1)} %hop.6), channel_id=1, source_target_pairs={{0,32},{1,33},{2,34},{3,35},{4,36},{5,37},{6,38},{7,39},{8,40},{9,... | collective-permute-start | bytes 1769480 | tf_op jit(solution)/shard_map/ppermute | solution.py:54
  56.1 13.3 %collective-permute-start.11 = (bf16[384,768]{1,0:T(8,128)(2,1)S(1)}, bf16[384,768]{1,0:T(8,128)(2,1)S(1)}, u32[]{:S(2)}, u32[]{:S(2)}) collective-permute-start(bf16[384,768]{1,0:T(8,128)(2,1)S(1)} %slice.21), channel_id=1, source_target_pairs={{0,3},{1,0},{2,1},{3,2},{4,7},{5,4},{6,5},{7,6},{8,11},{9,8},{10,9... | collective-permute-start | bytes 1769480 | tf_op jit(solution)/shard_map/ppermute | solution.py:54
  56.7 13.7 %collective-permute-start.10 = (bf16[384,768]{1,0:T(8,128)(2,1)S(1)}, bf16[384,768]{1,0:T(8,128)(2,1)S(1)}, u32[]{:S(2)}, u32[]{:S(2)}) collective-permute-start(bf16[384,768]{1,0:T(8,128)(2,1)S(1)} %slice.20), channel_id=1, source_target_pairs={{0,1},{1,2},{2,3},{3,0},{4,5},{5,6},{6,7},{7,4},{8,9},{9,10},{10,1... | collective-permute-start | bytes 1769480 | tf_op jit(solution)/shard_map/ppermute | solution.py:54
  65.1 5.3 %copy-start.1 = (bf16[384,1536]{1,0:T(8,128)(2,1)S(1)}, bf16[384,1536]{1,0:T(8,128)(2,1)}, u32[]{:S(2)}) copy-start(bf16[384,1536]{1,0:T(8,128)(2,1)} %dequantize.1.w0) | copy-start | bytes 3538948
  65.2 13.5 %collective-permute-start.17 = (bf16[96,3072]{1,0:T(8,128)(2,1)S(1)}, bf16[96,3072]{1,0:T(8,128)(2,1)S(1)}, u32[]{:S(2)}, u32[]{:S(2)}) collective-permute-start(bf16[96,3072]{1,0:T(8,128)(2,1)S(1)} %hop.9), channel_id=1, source_target_pairs={{0,224},{1,225},{2,226},{3,227},{4,228},{5,229},{6,230},{7,231},{8... | collective-permute-start | bytes 1769480 | tf_op jit(solution)/shard_map/ppermute | solution.py:54
  69.3 13.4 %collective-permute-start.15 = (bf16[96,3072]{1,0:T(8,128)(2,1)S(1)}, bf16[96,3072]{1,0:T(8,128)(2,1)S(1)}, u32[]{:S(2)}, u32[]{:S(2)}) collective-permute-start(bf16[96,3072]{1,0:T(8,128)(2,1)S(1)} %hop.8), channel_id=1, source_target_pairs={{0,32},{1,33},{2,34},{3,35},{4,36},{5,37},{6,38},{7,39},{8,40},{9,... | collective-permute-start | bytes 1769480 | tf_op jit(solution)/shard_map/ppermute | solution.py:54
  75.2 17.1 %collective-permute-start.14 = (bf16[256,1536]{1,0:T(8,128)(2,1)S(1)}, bf16[256,1536]{1,0:T(8,128)(2,1)S(1)}, u32[]{:S(2)}, u32[]{:S(2)}) collective-permute-start(bf16[256,1536]{1,0:T(8,128)(2,1)S(1)} %get-tuple-element.85), channel_id=1, source_target_pairs={{0,20},{1,21},{2,22},{3,23},{4,16},{5,17},{6,18},{7,19},{8,28},{9,... | collective-permute-start | bytes 2359304 | tf_op jit(solution)/shard_map/ppermute | solution.py:54
  78.9 13.6 %collective-permute-start.18 = (bf16[96,3072]{1,0:T(8,128)(2,1)S(1)}, bf16[96,3072]{1,0:T(8,128)(2,1)S(1)}, u32[]{:S(2)}, u32[]{:S(2)}) collective-permute-start(bf16[96,3072]{1,0:T(8,128)(2,1)S(1)} %hop.11), channel_id=1, source_target_pairs={{0,224},{1,225},{2,226},{3,227},{4,228},{5,229},{6,230},{7,231},{8... | collective-permute-start | bytes 1769480 | tf_op jit(solution)/shard_map/ppermute | solution.py:54
  82.8 12.0 %collective-permute-start.16 = (bf16[96,3072]{1,0:T(8,128)(2,1)S(1)}, bf16[96,3072]{1,0:T(8,128)(2,1)S(1)}, u32[]{:S(2)}, u32[]{:S(2)}) collective-permute-start(bf16[96,3072]{1,0:T(8,128)(2,1)S(1)} %hop.10), channel_id=1, source_target_pairs={{0,32},{1,33},{2,34},{3,35},{4,36},{5,37},{6,38},{7,39},{8,40},{9,... | collective-permute-start | bytes 1769480 | tf_op jit(solution)/shard_map/ppermute | solution.py:54
  87.8 12.8 %collective-permute-start.22 = (bf16[256,1536]{1,0:T(8,128)(2,1)S(1)}, bf16[256,1536]{1,0:T(8,128)(2,1)S(1)}, u32[]{:S(2)}, u32[]{:S(2)}) collective-permute-start(bf16[256,1536]{1,0:T(8,128)(2,1)S(1)} %get-tuple-element.104), channel_id=1, source_target_pairs={{0,8},{1,9},{2,10},{3,11},{4,12},{5,13},{6,14},{7,15},{8,0},{9,1},... | collective-permute-start | bytes 2359304 | tf_op jit(solution)/shard_map/ppermute | solution.py:54
  96.0 8.0 %collective-permute-start.19 = (bf16[24,3072]{1,0:T(8,128)(2,1)S(1)}, bf16[24,3072]{1,0:T(8,128)(2,1)S(1)}, u32[]{:S(2)}, u32[]{:S(2)}) collective-permute-start(bf16[24,3072]{1,0:T(8,128)(2,1)S(1)} %get-tuple-element.101), channel_id=1, source_target_pairs={{0,1},{1,2},{2,3},{3,0},{4,5},{5,6},{6,7},{7,4},{8,9},{9,10},{10,1... | collective-permute-start | bytes 442376 | tf_op jit(solution)/shard_map/ppermute | solution.py:54
  96.1 7.9 %collective-permute-start.20 = (bf16[24,3072]{1,0:T(8,128)(2,1)S(1)}, bf16[24,3072]{1,0:T(8,128)(2,1)S(1)}, u32[]{:S(2)}, u32[]{:S(2)}) collective-permute-start(bf16[24,3072]{1,0:T(8,128)(2,1)S(1)} %get-tuple-element.102), channel_id=1, source_target_pairs={{0,2},{1,3},{2,0},{3,1},{4,6},{5,7},{6,4},{7,5},{8,10},{9,11},{10,... | collective-permute-start | bytes 442376 | tf_op jit(solution)/shard_map/ppermute | solution.py:54
  98.7 6.2 %collective-permute-start.21 = (bf16[24,3072]{1,0:T(8,128)(2,1)S(1)}, bf16[24,3072]{1,0:T(8,128)(2,1)S(1)}, u32[]{:S(2)}, u32[]{:S(2)}) collective-permute-start(bf16[24,3072]{1,0:T(8,128)(2,1)S(1)} %get-tuple-element.103), channel_id=1, source_target_pairs={{0,3},{1,0},{2,1},{3,2},{4,7},{5,4},{6,5},{7,6},{8,11},{9,8},{10,9... | collective-permute-start | bytes 442376 | tf_op jit(solution)/shard_map/ppermute | solution.py:54
  100.6 13.3 %collective-permute-start.23 = (bf16[128,1536]{1,0:T(8,128)(2,1)}, bf16[128,1536]{1,0:T(8,128)(2,1)S(1)}, u32[]{:S(2)}, u32[]{:S(2)}) collective-permute-start(bf16[128,1536]{1,0:T(8,128)(2,1)} %get-tuple-element.118), channel_id=1, source_target_pairs={{0,8},{1,9},{2,10},{3,11},{4,12},{5,13},{6,14},{7,15},{8,0},{9,1},... | collective-permute-start | bytes 1179656 | tf_op jit(solution)/shard_map/ppermute | solution.py:54
  100.9 14.1 %collective-permute-start.24 = (bf16[128,1536]{1,0:T(8,128)(2,1)S(1)}, bf16[128,1536]{1,0:T(8,128)(2,1)S(1)}, u32[]{:S(2)}, u32[]{:S(2)}) collective-permute-start(bf16[128,1536]{1,0:T(8,128)(2,1)S(1)} %get-tuple-element.120), channel_id=1, source_target_pairs={{0,20},{1,21},{2,22},{3,23},{4,16},{5,17},{6,18},{7,19},{8,28},{9,... | collective-permute-start | bytes 1179656 | tf_op jit(solution)/shard_map/ppermute | solution.py:54
  105.6 15.5 %collective-permute-start.25 = (bf16[12,3072]{1,0:T(8,128)(2,1)S(1)}, bf16[12,3072]{1,0:T(8,128)(2,1)S(1)}, u32[]{:S(2)}, u32[]{:S(2)}) collective-permute-start(bf16[12,3072]{1,0:T(8,128)(2,1)S(1)} %get-tuple-element.110), channel_id=1, source_target_pairs={{0,24},{1,25},{2,26},{3,27},{4,184},{5,185},{6,186},{7,187},{8,72}... | collective-permute-start | bytes 221192 | tf_op jit(solution)/shard_map/ppermute | solution.py:54
  107.5 13.6 %collective-permute-start.26 = (bf16[12,3072]{1,0:T(8,128)(2,1)S(1)}, bf16[12,3072]{1,0:T(8,128)(2,1)S(1)}, u32[]{:S(2)}, u32[]{:S(2)}) collective-permute-start(bf16[12,3072]{1,0:T(8,128)(2,1)S(1)} %get-tuple-element.114), channel_id=1, source_target_pairs={{0,28},{1,29},{2,30},{3,31},{4,188},{5,189},{6,190},{7,191},{8,76}... | collective-permute-start | bytes 221192 | tf_op jit(solution)/shard_map/ppermute | solution.py:54

commit v12 on v11

--- a/solution.py
+++ b/solution.py
@@ -388,8 +388,8 @@
     token_parts = (tokens, token_sib, token_pair, send(token_pair, CORE))
     cot_parts = (cotangent, cot_sib, cot_pair, send(cot_pair, CORE))
 
-    up, down = gradient(where, token_parts, after(cot_parts, left, right), True)
-    grad = gradient(where, token_parts, after(cot_parts, up), False)
+    up, down = gradient(where, token_parts, after(cot_parts, left), True)
+    grad = gradient(where, token_parts, after(cot_parts, up, right), False)
     half = own.shape[1] // 2
     up, down = send(up, Z_UP), send(down, Z_DOWN)
     up = hop(grad[0], up, kernel=functools.partial(first_hop_kernel, upper=True))

time: 122 us -> 120 us (0.984)
  Pallas kernels: 24.2 us -> 22.5 us
    pallas_call x7, Pallas kernels: 23.5 us -> 21.8 us  [call(): pl.pallas_call(kernel, name=name, grid_spec=pltpu.PrefetchScalarGridSpec(...]
  transfers between devices with their start and end apart: 27 -> 27, of which waited for: 12 -> 13; matrix products, arithmetic and copies ran while one was open for 4% -> 4% of each run, Pallas kernels for 18% -> 19%
where the time goes in v12:
time: 120 us
  waiting for transfers between devices  46.7 us (39%)
  starting transfers between devices  44.2 us (37%)
  Pallas kernels  22.5 us (19%)
  other arithmetic  5.23 us (4%)
    ppermute x27, waiting for transfers between devices, send(): return lax.ppermute(value, AXES, pairs)  46.7 us
    ppermute x27, starting transfers between devices, send(): return lax.ppermute(value, AXES, pairs)  44.2 us
    pallas_call x7, Pallas kernels, call(): pl.pallas_call(kernel, name=name, grid_spec=pltpu.PrefetchScalarGridSpec(...  21.8 us
    select_n x2, other arithmetic, joined(): jnp.where(flag == 0, jnp.concatenate([here, there], axis=1), jnp.concaten...  3.24 us
  transfers between devices with their start and end apart: 27, of which 13 were waited for; matrix products, arithmetic and copies ran while one was open for 4% of the time, Pallas kernels for 19%

profile of v12, /device:TPU:24, one launch (start us, length us, event | category | flops | bytes accessed | tf_op | source)
XLA Modules:
  0.0 120.2 jit_solution(10376836973584219983)
XLA Ops:
  0.6 2.0 %collective-permute-start.6 = (bf16[128,3072]{1,0:T(8,128)(2,1)}, bf16[128,3072]{1,0:T(8,128)(2,1)S(1)}, u32[]{:S(2)}, u32[]{:S(2)}) collective-permute-start(bf16[128,3072]{1,0:T(8,128)(2,1)} %cot0.3), channel_id=1, source_target_pairs={{0,20},{1,21},{2,22},{3,23},{4,16},{5,17},{6,18},{7,19},{8,28},{9,... | collective-permute-start | bytes 2359304 | tf_op jit(solution)/shard_map/ppermute | solution.py:54
  2.7 0.6 stack.23.where
  3.3 4.3 %dequantize.1.w0 = bf16[384,1536]{1,0:T(8,128)(2,1)} custom-call(s32[5]{0:T(128)} %stack.23.where, bf16[384,3072]{1,0:T(8,128)(2,1)} %levels.1, f32[12,384]{1,0:T(8,128)} %bitcast.6), custom_call_target="tpu_custom_call" | custom-call | flops 589824 | bytes 3557376 | tf_op jit(solution)/shard_map/dequantize/pallas_call | solution.py:72
  7.6 2.8 %collective-permute-start.1 = (bf16[128,1536]{1,0:T(8,128)(2,1)S(1)}, bf16[128,1536]{1,0:T(8,128)(2,1)S(1)}, u32[]{:S(2)}, u32[]{:S(2)}) collective-permute-start(bf16[128,1536]{1,0:T(8,128)(2,1)S(1)} %constant_dynamic-slice_fusion), channel_id=1, source_target_pairs={{0,20},{1,21},{2,22},{3,23},{4,16},{5,17},{6,18},{7,19},{8,28},{9,... | collective-permute-start | bytes 1179656 | tf_op jit(solution)/shard_map/ppermute | solution.py:54
  10.5 0.0 collective-permute-start.5
  10.5 1.7 %collective-permute-start.4 = (bf16[384,1536]{1,0:T(8,128)(2,1)}, bf16[384,1536]{1,0:T(8,128)(2,1)S(1)}, u32[]{:S(2)}, u32[]{:S(2)}) collective-permute-start(bf16[384,1536]{1,0:T(8,128)(2,1)} %dequantize.1.w0), channel_id=1, source_target_pairs={{0,3},{1,0},{2,1},{3,2},{4,7},{5,4},{6,5},{7,6},{8,11},{9,8},{10,9... | collective-permute-start | bytes 3538952 | tf_op jit(solution)/shard_map/ppermute | solution.py:54
  12.2 10.3 %collective-permute-done.6.cot2 = bf16[128,3072]{1,0:T(8,128)(2,1)S(1)} collective-permute-done((bf16[128,3072]{1,0:T(8,128)(2,1)}, bf16[128,3072]{1,0:T(8,128)(2,1)S(1)}, u32[]{:S(2)}, u32[]{:S(2)}) %collective-permute-start.6) | collective-permute-done | bytes 786464 | tf_op jit(solution)/shard_map/ppermute | solution.py:54
  22.6 0.0 collective-permute-start.7
  22.6 7.3 %collective-permute-done.1.pair = bf16[128,1536]{1,0:T(8,128)(2,1)S(1)} collective-permute-done((bf16[128,1536]{1,0:T(8,128)(2,1)S(1)}, bf16[128,1536]{1,0:T(8,128)(2,1)S(1)}, u32[]{:S(2)}, u32[]{:S(2)}) %collective-permute-start.1) | collective-permute-done | bytes 393248 | tf_op jit(solution)/shard_map/ppermute | solution.py:54
  29.8 0.0 collective-permute-start
  29.8 0.0 collective-permute-done.5.cot1
  29.9 0.5 collective-permute-start.2
  30.4 4.4 %collective-permute-done.3.w1 = bf16[384,1536]{1,0:T(8,128)(2,1)S(1)} collective-permute-done((bf16[384,1536]{1,0:T(8,128)(2,1)}, bf16[384,1536]{1,0:T(8,128)(2,1)S(1)}, u32[]{:S(2)}, u32[]{:S(2)}) %collective-permute-start.3) | collective-permute-done | bytes 1179680 | tf_op jit(solution)/shard_map/ppermute | solution.py:54
  34.8 0.0 collective-permute-done.7.cot3
  34.8 0.0 collective-permute-done.2.psib
  34.8 0.0 collective-permute-done.sib
  34.8 2.7 %far.1 = (bf16[48,3072]{1,0:T(8,128)(2,1)S(1)}, bf16[48,3072]{1,0:T(8,128)(2,1)S(1)}) custom-call(s32[5]{0:T(128)S(1)} %copy-done.3, bf16[128,3072]{1,0:T(8,128)(2,1)S(1)} %copy-done, bf16[128,3072]{1,0:T(8,128)(2,1)S(1)} %collective-permute-done.sib, bf16[128,1536]{1,0:T(8,128)(2,1)S(1)} %collective-permute-done.1.pair, ...), custom_call_target="tpu_custom_call" | custom-call | flops 805306368 | bytes 6094848 | tf_op jit(solution)/shard_map/far/pallas_call | solution.py:72
  37.5 5.9 %collective-permute-start.9 = (bf16[48,3072]{1,0:T(8,128)(2,1)S(1)}, bf16[48,3072]{1,0:T(8,128)(2,1)S(1)}, u32[]{:S(2)}, u32[]{:S(2)}) collective-permute-start(bf16[48,3072]{1,0:T(8,128)(2,1)S(1)} %get-tuple-element.73), channel_id=1, source_target_pairs={{0,224},{1,225},{2,226},{3,227},{4,228},{5,229},{6,230},{7,231},{8... | collective-permute-start | bytes 884744 | tf_op jit(solution)/shard_map/ppermute | solution.py:54
  43.5 0.0 collective-permute-start.8
  43.5 0.0 collective-permute-done.4.w2
  43.5 4.9 %gradient.1 = (bf16[96,3072]{1,0:T(8,128)(2,1)S(1)}, bf16[96,3072]{1,0:T(8,128)(2,1)S(1)}, bf16[96,3072]{1,0:T(8,128)(2,1)S(1)}, bf16[96,3072]{1,0:T(8,128)(2,1)...) custom-call(s32[5]{0:T(128)S(1)} %copy-done.3, ...), custom_call_target="tpu_custom_call" | custom-call | flops 2415919104 | bytes 9633792 | tf_op jit(solution)/shard_map/gradient/pallas_call | solution.py:72
  48.4 0.3 collective-permute-done.9.arrived
  48.6 0.1 hop.7
  48.7 3.8 %collective-permute-start.13 = (bf16[96,3072]{1,0:T(8,128)(2,1)S(1)}, bf16[96,3072]{1,0:T(8,128)(2,1)S(1)}, u32[]{:S(2)}, u32[]{:S(2)}) collective-permute-start(bf16[96,3072]{1,0:T(8,128)(2,1)S(1)} %hop.7), channel_id=1, source_target_pairs={{0,224},{1,225},{2,226},{3,227},{4,228},{5,229},{6,230},{7,231},{8... | collective-permute-start | bytes 1769480 | tf_op jit(solution)/shard_map/ppermute | solution.py:54
  52.5 0.0 collective-permute-done.8.arrived
  52.5 0.1 hop.6
  52.6 0.1 collective-permute-start.12
  52.8 2.1 %collective-permute-start.11 = (bf16[384,768]{1,0:T(8,128)(2,1)S(1)}, bf16[384,768]{1,0:T(8,128)(2,1)S(1)}, u32[]{:S(2)}, u32[]{:S(2)}) collective-permute-start(bf16[384,768]{1,0:T(8,128)(2,1)S(1)} %slice.21), channel_id=1, source_target_pairs={{0,3},{1,0},{2,1},{3,2},{4,7},{5,4},{6,5},{7,6},{8,11},{9,8},{10,9... | collective-permute-start | bytes 1769480 | tf_op jit(solution)/shard_map/ppermute | solution.py:54
  54.9 8.2 %collective-permute-done.13.refs_0_ = bf16[96,3072]{1,0:T(8,128)(2,1)S(1)} collective-permute-done((bf16[96,3072]{1,0:T(8,128)(2,1)S(1)}, bf16[96,3072]{1,0:T(8,128)(2,1)S(1)}, u32[]{:S(2)}, u32[]{:S(2)}) %collective-permute-start.13) | collective-permute-done | bytes 589856 | tf_op jit(solution)/shard_map/ppermute | solution.py:54
  63.1 0.1 hop.9
  63.2 3.9 %collective-permute-start.17 = (bf16[96,3072]{1,0:T(8,128)(2,1)S(1)}, bf16[96,3072]{1,0:T(8,128)(2,1)S(1)}, u32[]{:S(2)}, u32[]{:S(2)}) collective-permute-start(bf16[96,3072]{1,0:T(8,128)(2,1)S(1)} %hop.9), channel_id=1, source_target_pairs={{0,224},{1,225},{2,226},{3,227},{4,228},{5,229},{6,230},{7,231},{8... | collective-permute-start | bytes 1769480 | tf_op jit(solution)/shard_map/ppermute | solution.py:54
  67.2 0.1 hop.8
  67.3 0.1 collective-permute-start.15
  67.4 1.7 %collective-permute-done.10.w3 = bf16[384,768]{1,0:T(8,128)(2,1)S(1)} collective-permute-done((bf16[384,768]{1,0:T(8,128)(2,1)S(1)}, bf16[384,768]{1,0:T(8,128)(2,1)S(1)}, u32[]{:S(2)}, u32[]{:S(2)}) %collective-permute-start.10) | collective-permute-done | bytes 589856 | tf_op jit(solution)/shard_map/ppermute | solution.py:54
  69.1 3.9 %forward.1 = (f32[128,1536]{1,0:T(8,128)S(1)}, f32[128,1536]{1,0:T(8,128)S(1)}, bf16[256,1536]{1,0:T(8,128)(2,1)S(1)}) custom-call(s32[5]{0:T(128)S(1)} %copy-done.3, bf16[128,3072]{1,0:T(8,128)(2,1)S(1)} %copy-done, bf16[128,3072]{1,0:T(8,128)(2,1)S(1)} %collective-permute-done.sib, bf16[128,1536]{1,0:T(8,128)(2,1)S(1)} %collective-permute-done.1.pair, ...), custom_call_target="tpu_custom_call" | custom-call | flops 2415919104 | bytes 9437184 | tf_op jit(solution)/shard_map/forward/pallas_call | solution.py:72
  73.0 1.8 %collective-permute-start.14 = (bf16[256,1536]{1,0:T(8,128)(2,1)S(1)}, bf16[256,1536]{1,0:T(8,128)(2,1)S(1)}, u32[]{:S(2)}, u32[]{:S(2)}) collective-permute-start(bf16[256,1536]{1,0:T(8,128)(2,1)S(1)} %get-tuple-element.85), channel_id=1, source_target_pairs={{0,20},{1,21},{2,22},{3,23},{4,16},{5,17},{6,18},{7,19},{8,28},{9,... | collective-permute-start | bytes 2359304 | tf_op jit(solution)/shard_map/ppermute | solution.py:54
  74.8 2.0 %collective-permute-done.17.refs_0_ = bf16[96,3072]{1,0:T(8,128)(2,1)S(1)} collective-permute-done((bf16[96,3072]{1,0:T(8,128)(2,1)S(1)}, bf16[96,3072]{1,0:T(8,128)(2,1)S(1)}, u32[]{:S(2)}, u32[]{:S(2)}) %collective-permute-start.17) | collective-permute-done | bytes 589856 | tf_op jit(solution)/shard_map/ppermute | solution.py:54
  76.8 0.2 hop.11
  77.0 3.8 %collective-permute-start.18 = (bf16[96,3072]{1,0:T(8,128)(2,1)S(1)}, bf16[96,3072]{1,0:T(8,128)(2,1)S(1)}, u32[]{:S(2)}, u32[]{:S(2)}) collective-permute-start(bf16[96,3072]{1,0:T(8,128)(2,1)S(1)} %hop.11), channel_id=1, source_target_pairs={{0,224},{1,225},{2,226},{3,227},{4,228},{5,229},{6,230},{7,231},{8... | collective-permute-start | bytes 1769480 | tf_op jit(solution)/shard_map/ppermute | solution.py:54
  80.7 0.1 hop.10
  80.9 0.1 collective-permute-start.16
  81.0 4.0 %backward.1 = (f32[256,1536]{1,0:T(8,128)S(1)}, bf16[256,1536]{1,0:T(8,128)(2,1)S(1)}) custom-call(s32[5]{0:T(128)S(1)} %copy-done.3, bf16[128,3072]{1,0:T(8,128)(2,1)S(1)} %copy-done.2, bf16[128,3072]{1,0:T(8,128)(2,1)S(1)} %collective-permute-done.5.cot1, bf16[128,3072]{1,0:T(8,128)(2,1)S(1)} %collective-permute-done.6.cot2, ...), custom_call_target="tpu_custom_call" | custom-call | flops 2415919104 | bytes 10223616 | tf_op jit(solution)/shard_map/backward/pallas_call | solution.py:72
  85.0 0.1 collective-permute-start.22
  85.1 5.5 %collective-permute-done.14 = bf16[256,1536]{1,0:T(8,128)(2,1)S(1)} collective-permute-done((bf16[256,1536]{1,0:T(8,128)(2,1)S(1)}, bf16[256,1536]{1,0:T(8,128)(2,1)S(1)}, u32[]{:S(2)}, u32[]{:S(2)}) %collective-permute-start.14) | collective-permute-done | bytes 786464 | tf_op jit(solution)/shard_map/ppermute | solution.py:54
  90.6 0.2 convert_element_type.20
  90.8 2.3 %collective-permute-done.16.up = bf16[96,3072]{1,0:T(8,128)(2,1)S(1)} collective-permute-done((bf16[96,3072]{1,0:T(8,128)(2,1)S(1)}, bf16[96,3072]{1,0:T(8,128)(2,1)S(1)}, u32[]{:S(2)}, u32[]{:S(2)}) %collective-permute-start.16) | collective-permute-done | bytes 589856 | tf_op jit(solution)/shard_map/ppermute | solution.py:54
  93.1 1.2 %last_hop.1 = (f32[24,3072]{1,0:T(8,128)S(1)}, bf16[24,3072]{1,0:T(8,128)(2,1)S(1)}, bf16[24,3072]{1,0:T(8,128)(2,1)S(1)}, bf16[24,3072]{1,0:T(8,128)(2,1)S(1)}) custom-call(s32[5]{0:T(128)S(1)} %copy-done.3, bf16[96,3072]{1,0:T(8,128)(2,1)S(1)} %collective-permute-done.16.up, bf16[96,3072]{1,0:T(8,128)(2,1)S(1)} %collective-permute-done.18.down, ...), custom_call_target="tpu_custom_call" | custom-call | flops 589824 | bytes 2506752 | tf_op jit(solution)/shard_map/last_hop/pallas_call | solution.py:72
  94.4 2.3 %collective-permute-start.19 = (bf16[24,3072]{1,0:T(8,128)(2,1)S(1)}, bf16[24,3072]{1,0:T(8,128)(2,1)S(1)}, u32[]{:S(2)}, u32[]{:S(2)}) collective-permute-start(bf16[24,3072]{1,0:T(8,128)(2,1)S(1)} %get-tuple-element.101), channel_id=1, source_target_pairs={{0,1},{1,2},{2,3},{3,0},{4,5},{5,6},{6,7},{7,4},{8,9},{9,10},{10,1... | collective-permute-start | bytes 442376 | tf_op jit(solution)/shard_map/ppermute | solution.py:54
  96.6 2.7 %collective-permute-start.20 = (bf16[24,3072]{1,0:T(8,128)(2,1)S(1)}, bf16[24,3072]{1,0:T(8,128)(2,1)S(1)}, u32[]{:S(2)}, u32[]{:S(2)}) collective-permute-start(bf16[24,3072]{1,0:T(8,128)(2,1)S(1)} %get-tuple-element.102), channel_id=1, source_target_pairs={{0,2},{1,3},{2,0},{3,1},{4,6},{5,7},{6,4},{7,5},{8,10},{9,11},{10,... | collective-permute-start | bytes 442376 | tf_op jit(solution)/shard_map/ppermute | solution.py:54
  99.4 1.4 %collective-permute-start.21 = (bf16[24,3072]{1,0:T(8,128)(2,1)S(1)}, bf16[24,3072]{1,0:T(8,128)(2,1)S(1)}, u32[]{:S(2)}, u32[]{:S(2)}) collective-permute-start(bf16[24,3072]{1,0:T(8,128)(2,1)S(1)} %get-tuple-element.103), channel_id=1, source_target_pairs={{0,3},{1,0},{2,1},{3,2},{4,7},{5,4},{6,5},{7,6},{8,11},{9,8},{10,9... | collective-permute-start | bytes 442376 | tf_op jit(solution)/shard_map/ppermute | solution.py:54
  100.8 0.9 add_convert_fusion.2
  101.7 0.2 add_convert_fusion
  101.9 0.1 fusion
  102.0 0.8 collective-permute-start.24
  102.7 1.3 %collective-permute-done.20.two = bf16[24,3072]{1,0:T(8,128)(2,1)S(1)} collective-permute-done((bf16[24,3072]{1,0:T(8,128)(2,1)S(1)}, bf16[24,3072]{1,0:T(8,128)(2,1)S(1)}, u32[]{:S(2)}, u32[]{:S(2)}) %collective-permute-start.20) | collective-permute-done | bytes 147488 | tf_op jit(solution)/shard_map/ppermute | solution.py:54
  104.1 0.4 collective-permute-done.21.three
  104.5 0.7 sum_over_x.1
  105.2 1.9 %collective-permute-start.25 = (bf16[12,3072]{1,0:T(8,128)(2,1)S(1)}, bf16[12,3072]{1,0:T(8,128)(2,1)S(1)}, u32[]{:S(2)}, u32[]{:S(2)}) collective-permute-start(bf16[12,3072]{1,0:T(8,128)(2,1)S(1)} %get-tuple-element.110), channel_id=1, source_target_pairs={{0,24},{1,25},{2,26},{3,27},{4,184},{5,185},{6,186},{7,187},{8,72}... | collective-permute-start | bytes 221192 | tf_op jit(solution)/shard_map/ppermute | solution.py:54
  107.1 6.2 %collective-permute-start.26 = (bf16[12,3072]{1,0:T(8,128)(2,1)S(1)}, bf16[12,3072]{1,0:T(8,128)(2,1)S(1)}, u32[]{:S(2)}, u32[]{:S(2)}) collective-permute-start(bf16[12,3072]{1,0:T(8,128)(2,1)S(1)} %get-tuple-element.114), channel_id=1, source_target_pairs={{0,28},{1,29},{2,30},{3,31},{4,188},{5,189},{6,190},{7,191},{8,76}... | collective-permute-start | bytes 221192 | tf_op jit(solution)/shard_map/ppermute | solution.py:54
  113.4 2.2 %maximum_select_fusion = bf16[128,3072]{1,0:T(8,128)(2,1)} fusion(bf16[128,1536]{1,0:T(8,128)(2,1)} %collective-permute-done.23, bf16[128,1536]{1,0:T(8,128)(2,1)S(1)} %get-tuple-element.111, pred[]{:T(512)S(6)} %eq.8), kind=kLoop, calls=%fused_computation.1 | loop fusion | flops 3538944 | bytes 1572865 | tf_op jit(solution)/shard_map/jit(_where)/select_n | solution.py:367
  115.6 1.2 collective-permute-done.24
  116.7 1.1 maximum_select_fusion.1
  117.8 1.8 %collective-permute-done.26 = bf16[12,3072]{1,0:T(8,128)(2,1)S(1)} collective-permute-done((bf16[12,3072]{1,0:T(8,128)(2,1)S(1)}, bf16[12,3072]{1,0:T(8,128)(2,1)S(1)}, u32[]{:S(2)}, u32[]{:S(2)}) %collective-permute-start.26) | collective-permute-done | bytes 73760 | tf_op jit(solution)/shard_map/ppermute | solution.py:54
  119.5 0.7 convert_add_fusion
  (22 shorter events, 0.2 us)
Async XLA Ops:
  0.6 21.9 %collective-permute-start.6 = (bf16[128,3072]{1,0:T(8,128)(2,1)}, bf16[128,3072]{1,0:T(8,128)(2,1)S(1)}, u32[]{:S(2)}, u32[]{:S(2)}) collective-permute-start(bf16[128,3072]{1,0:T(8,128)(2,1)} %cot0.3), channel_id=1, source_target_pairs={{0,20},{1,21},{2,22},{3,23},{4,16},{5,17},{6,18},{7,19},{8,28},{9,... | collective-permute-start | bytes 2359304 | tf_op jit(solution)/shard_map/ppermute | solution.py:54
  3.3 4.3 %copy-start = (bf16[128,3072]{1,0:T(8,128)(2,1)S(1)}, bf16[128,3072]{1,0:T(8,128)(2,1)}, u32[]{:S(2)}) copy-start(bf16[128,3072]{1,0:T(8,128)(2,1)} %own.5) | copy-start | bytes 2359300
  3.3 7.2 %copy-start.2 = (bf16[128,3072]{1,0:T(8,128)(2,1)S(1)}, bf16[128,3072]{1,0:T(8,128)(2,1)}, u32[]{:S(2)}) copy-start(bf16[128,3072]{1,0:T(8,128)(2,1)} %cot0.3) | copy-start | bytes 2359300
  3.3 31.5 %copy-start.3 = (s32[5]{0:T(128)S(1)}, s32[5]{0:T(128)}, u32[]{:S(2)}) copy-start(s32[5]{0:T(128)} %stack.23.where) | copy-start | bytes 64
  7.6 27.2 %collective-permute-start.3 = (bf16[384,1536]{1,0:T(8,128)(2,1)}, bf16[384,1536]{1,0:T(8,128)(2,1)S(1)}, u32[]{:S(2)}, u32[]{:S(2)}) collective-permute-start(bf16[384,1536]{1,0:T(8,128)(2,1)} %dequantize.1.w0), channel_id=1, source_target_pairs={{0,1},{1,2},{2,3},{3,0},{4,5},{5,6},{6,7},{7,4},{8,9},{9,10},{10,1... | collective-permute-start | bytes 3538952 | tf_op jit(solution)/shard_map/ppermute | solution.py:54
  7.6 22.2 %collective-permute-start.1 = (bf16[128,1536]{1,0:T(8,128)(2,1)S(1)}, bf16[128,1536]{1,0:T(8,128)(2,1)S(1)}, u32[]{:S(2)}, u32[]{:S(2)}) collective-permute-start(bf16[128,1536]{1,0:T(8,128)(2,1)S(1)} %constant_dynamic-slice_fusion), channel_id=1, source_target_pairs={{0,20},{1,21},{2,22},{3,23},{4,16},{5,17},{6,18},{7,19},{8,28},{9,... | collective-permute-start | bytes 1179656 | tf_op jit(solution)/shard_map/ppermute | solution.py:54
  10.5 19.4 %collective-permute-start.5 = (bf16[128,3072]{1,0:T(8,128)(2,1)S(1)}, bf16[128,3072]{1,0:T(8,128)(2,1)S(1)}, u32[]{:S(2)}, u32[]{:S(2)}) collective-permute-start(bf16[128,3072]{1,0:T(8,128)(2,1)S(1)} %copy-done.2), channel_id=1, source_target_pairs={{0,8},{1,9},{2,10},{3,11},{4,12},{5,13},{6,14},{7,15},{8,0},{9,1},... | collective-permute-start | bytes 2359304 | tf_op jit(solution)/shard_map/ppermute | solution.py:54
  10.5 33.0 %collective-permute-start.4 = (bf16[384,1536]{1,0:T(8,128)(2,1)}, bf16[384,1536]{1,0:T(8,128)(2,1)S(1)}, u32[]{:S(2)}, u32[]{:S(2)}) collective-permute-start(bf16[384,1536]{1,0:T(8,128)(2,1)} %dequantize.1.w0), channel_id=1, source_target_pairs={{0,3},{1,0},{2,1},{3,2},{4,7},{5,4},{6,5},{7,6},{8,11},{9,8},{10,9... | collective-permute-start | bytes 3538952 | tf_op jit(solution)/shard_map/ppermute | solution.py:54
  22.6 12.2 %collective-permute-start.7 = (bf16[128,3072]{1,0:T(8,128)(2,1)S(1)}, bf16[128,3072]{1,0:T(8,128)(2,1)S(1)}, u32[]{:S(2)}, u32[]{:S(2)}) collective-permute-start(bf16[128,3072]{1,0:T(8,128)(2,1)S(1)} %collective-permute-done.6.cot2), channel_id=1, source_target_pairs={{0,8},{1,9},{2,10},{3,11},{4,12},{5,13},{6,14},{7,15},{8,0},{9,1},... | collective-permute-start | bytes 2359304 | tf_op jit(solution)/shard_map/ppermute | solution.py:54
  29.8 5.0 %collective-permute-start = (bf16[128,3072]{1,0:T(8,128)(2,1)S(1)}, bf16[128,3072]{1,0:T(8,128)(2,1)S(1)}, u32[]{:S(2)}, u32[]{:S(2)}) collective-permute-start(bf16[128,3072]{1,0:T(8,128)(2,1)S(1)} %copy-done), channel_id=1, source_target_pairs={{0,8},{1,9},{2,10},{3,11},{4,12},{5,13},{6,14},{7,15},{8,0},{9,1},... | collective-permute-start | bytes 2359304 | tf_op jit(solution)/shard_map/ppermute | solution.py:54
  29.9 4.9 %collective-permute-start.2 = (bf16[128,1536]{1,0:T(8,128)(2,1)S(1)}, bf16[128,1536]{1,0:T(8,128)(2,1)S(1)}, u32[]{:S(2)}, u32[]{:S(2)}) collective-permute-start(bf16[128,1536]{1,0:T(8,128)(2,1)S(1)} %collective-permute-done.1.pair), channel_id=1, source_target_pairs={{0,8},{1,9},{2,10},{3,11},{4,12},{5,13},{6,14},{7,15},{8,0},{9,1},... | collective-permute-start | bytes 1179656 | tf_op jit(solution)/shard_map/ppermute | solution.py:54
  37.5 11.1 %collective-permute-start.9 = (bf16[48,3072]{1,0:T(8,128)(2,1)S(1)}, bf16[48,3072]{1,0:T(8,128)(2,1)S(1)}, u32[]{:S(2)}, u32[]{:S(2)}) collective-permute-start(bf16[48,3072]{1,0:T(8,128)(2,1)S(1)} %get-tuple-element.73), channel_id=1, source_target_pairs={{0,224},{1,225},{2,226},{3,227},{4,228},{5,229},{6,230},{7,231},{8... | collective-permute-start | bytes 884744 | tf_op jit(solution)/shard_map/ppermute | solution.py:54
  43.5 9.0 %collective-permute-start.8 = (bf16[48,3072]{1,0:T(8,128)(2,1)S(1)}, bf16[48,3072]{1,0:T(8,128)(2,1)S(1)}, u32[]{:S(2)}, u32[]{:S(2)}) collective-permute-start(bf16[48,3072]{1,0:T(8,128)(2,1)S(1)} %get-tuple-element.67), channel_id=1, source_target_pairs={{0,32},{1,33},{2,34},{3,35},{4,36},{5,37},{6,38},{7,39},{8,40},{9,... | collective-permute-start | bytes 884744 | tf_op jit(solution)/shard_map/ppermute | solution.py:54
  48.7 14.3 %collective-permute-start.13 = (bf16[96,3072]{1,0:T(8,128)(2,1)S(1)}, bf16[96,3072]{1,0:T(8,128)(2,1)S(1)}, u32[]{:S(2)}, u32[]{:S(2)}) collective-permute-start(bf16[96,3072]{1,0:T(8,128)(2,1)S(1)} %hop.7), channel_id=1, source_target_pairs={{0,224},{1,225},{2,226},{3,227},{4,228},{5,229},{6,230},{7,231},{8... | collective-permute-start | bytes 1769480 | tf_op jit(solution)/shard_map/ppermute | solution.py:54
  52.6 14.6 %collective-permute-start.12 = (bf16[96,3072]{1,0:T(8,128)(2,1)S(1)}, bf16[96,3072]{1,0:T(8,128)(2,1)S(1)}, u32[]{:S(2)}, u32[]{:S(2)}) collective-permute-start(bf16[96,3072]{1,0:T(8,128)(2,1)S(1)} %hop.6), channel_id=1, source_target_pairs={{0,32},{1,33},{2,34},{3,35},{4,36},{5,37},{6,38},{7,39},{8,40},{9,... | collective-permute-start | bytes 1769480 | tf_op jit(solution)/shard_map/ppermute | solution.py:54
  52.8 14.6 %collective-permute-start.11 = (bf16[384,768]{1,0:T(8,128)(2,1)S(1)}, bf16[384,768]{1,0:T(8,128)(2,1)S(1)}, u32[]{:S(2)}, u32[]{:S(2)}) collective-permute-start(bf16[384,768]{1,0:T(8,128)(2,1)S(1)} %slice.21), channel_id=1, source_target_pairs={{0,3},{1,0},{2,1},{3,2},{4,7},{5,4},{6,5},{7,6},{8,11},{9,8},{10,9... | collective-permute-start | bytes 1769480 | tf_op jit(solution)/shard_map/ppermute | solution.py:54
  54.9 14.2 %collective-permute-start.10 = (bf16[384,768]{1,0:T(8,128)(2,1)S(1)}, bf16[384,768]{1,0:T(8,128)(2,1)S(1)}, u32[]{:S(2)}, u32[]{:S(2)}) collective-permute-start(bf16[384,768]{1,0:T(8,128)(2,1)S(1)} %slice.20), channel_id=1, source_target_pairs={{0,1},{1,2},{2,3},{3,0},{4,5},{5,6},{6,7},{7,4},{8,9},{9,10},{10,1... | collective-permute-start | bytes 1769480 | tf_op jit(solution)/shard_map/ppermute | solution.py:54
  63.1 6.0 %copy-start.1 = (bf16[384,1536]{1,0:T(8,128)(2,1)S(1)}, bf16[384,1536]{1,0:T(8,128)(2,1)}, u32[]{:S(2)}) copy-start(bf16[384,1536]{1,0:T(8,128)(2,1)} %dequantize.1.w0) | copy-start | bytes 3538948
  63.2 13.6 %collective-permute-start.17 = (bf16[96,3072]{1,0:T(8,128)(2,1)S(1)}, bf16[96,3072]{1,0:T(8,128)(2,1)S(1)}, u32[]{:S(2)}, u32[]{:S(2)}) collective-permute-start(bf16[96,3072]{1,0:T(8,128)(2,1)S(1)} %hop.9), channel_id=1, source_target_pairs={{0,224},{1,225},{2,226},{3,227},{4,228},{5,229},{6,230},{7,231},{8... | collective-permute-start | bytes 1769480 | tf_op jit(solution)/shard_map/ppermute | solution.py:54
  67.3 13.4 %collective-permute-start.15 = (bf16[96,3072]{1,0:T(8,128)(2,1)S(1)}, bf16[96,3072]{1,0:T(8,128)(2,1)S(1)}, u32[]{:S(2)}, u32[]{:S(2)}) collective-permute-start(bf16[96,3072]{1,0:T(8,128)(2,1)S(1)} %hop.8), channel_id=1, source_target_pairs={{0,32},{1,33},{2,34},{3,35},{4,36},{5,37},{6,38},{7,39},{8,40},{9,... | collective-permute-start | bytes 1769480 | tf_op jit(solution)/shard_map/ppermute | solution.py:54
  73.0 17.6 %collective-permute-start.14 = (bf16[256,1536]{1,0:T(8,128)(2,1)S(1)}, bf16[256,1536]{1,0:T(8,128)(2,1)S(1)}, u32[]{:S(2)}, u32[]{:S(2)}) collective-permute-start(bf16[256,1536]{1,0:T(8,128)(2,1)S(1)} %get-tuple-element.85), channel_id=1, source_target_pairs={{0,20},{1,21},{2,22},{3,23},{4,16},{5,17},{6,18},{7,19},{8,28},{9,... | collective-permute-start | bytes 2359304 | tf_op jit(solution)/shard_map/ppermute | solution.py:54
  77.0 13.8 %collective-permute-start.18 = (bf16[96,3072]{1,0:T(8,128)(2,1)S(1)}, bf16[96,3072]{1,0:T(8,128)(2,1)S(1)}, u32[]{:S(2)}, u32[]{:S(2)}) collective-permute-start(bf16[96,3072]{1,0:T(8,128)(2,1)S(1)} %hop.11), channel_id=1, source_target_pairs={{0,224},{1,225},{2,226},{3,227},{4,228},{5,229},{6,230},{7,231},{8... | collective-permute-start | bytes 1769480 | tf_op jit(solution)/shard_map/ppermute | solution.py:54
  80.9 12.2 %collective-permute-start.16 = (bf16[96,3072]{1,0:T(8,128)(2,1)S(1)}, bf16[96,3072]{1,0:T(8,128)(2,1)S(1)}, u32[]{:S(2)}, u32[]{:S(2)}) collective-permute-start(bf16[96,3072]{1,0:T(8,128)(2,1)S(1)} %hop.10), channel_id=1, source_target_pairs={{0,32},{1,33},{2,34},{3,35},{4,36},{5,37},{6,38},{7,39},{8,40},{9,... | collective-permute-start | bytes 1769480 | tf_op jit(solution)/shard_map/ppermute | solution.py:54
  85.0 16.7 %collective-permute-start.22 = (bf16[256,1536]{1,0:T(8,128)(2,1)S(1)}, bf16[256,1536]{1,0:T(8,128)(2,1)S(1)}, u32[]{:S(2)}, u32[]{:S(2)}) collective-permute-start(bf16[256,1536]{1,0:T(8,128)(2,1)S(1)} %get-tuple-element.104), channel_id=1, source_target_pairs={{0,8},{1,9},{2,10},{3,11},{4,12},{5,13},{6,14},{7,15},{8,0},{9,1},... | collective-permute-start | bytes 2359304 | tf_op jit(solution)/shard_map/ppermute | solution.py:54
  94.4 8.4 %collective-permute-start.19 = (bf16[24,3072]{1,0:T(8,128)(2,1)S(1)}, bf16[24,3072]{1,0:T(8,128)(2,1)S(1)}, u32[]{:S(2)}, u32[]{:S(2)}) collective-permute-start(bf16[24,3072]{1,0:T(8,128)(2,1)S(1)} %get-tuple-element.101), channel_id=1, source_target_pairs={{0,1},{1,2},{2,3},{3,0},{4,5},{5,6},{6,7},{7,4},{8,9},{9,10},{10,1... | collective-permute-start | bytes 442376 | tf_op jit(solution)/shard_map/ppermute | solution.py:54
  96.6 7.4 %collective-permute-start.20 = (bf16[24,3072]{1,0:T(8,128)(2,1)S(1)}, bf16[24,3072]{1,0:T(8,128)(2,1)S(1)}, u32[]{:S(2)}, u32[]{:S(2)}) collective-permute-start(bf16[24,3072]{1,0:T(8,128)(2,1)S(1)} %get-tuple-element.102), channel_id=1, source_target_pairs={{0,2},{1,3},{2,0},{3,1},{4,6},{5,7},{6,4},{7,5},{8,10},{9,11},{10,... | collective-permute-start | bytes 442376 | tf_op jit(solution)/shard_map/ppermute | solution.py:54
  99.4 5.1 %collective-permute-start.21 = (bf16[24,3072]{1,0:T(8,128)(2,1)S(1)}, bf16[24,3072]{1,0:T(8,128)(2,1)S(1)}, u32[]{:S(2)}, u32[]{:S(2)}) collective-permute-start(bf16[24,3072]{1,0:T(8,128)(2,1)S(1)} %get-tuple-element.103), channel_id=1, source_target_pairs={{0,3},{1,0},{2,1},{3,2},{4,7},{5,4},{6,5},{7,6},{8,11},{9,8},{10,9... | collective-permute-start | bytes 442376 | tf_op jit(solution)/shard_map/ppermute | solution.py:54
  101.7 11.6 %collective-permute-start.23 = (bf16[128,1536]{1,0:T(8,128)(2,1)}, bf16[128,1536]{1,0:T(8,128)(2,1)}, u32[]{:S(2)}, u32[]{:S(2)}) collective-permute-start(bf16[128,1536]{1,0:T(8,128)(2,1)} %get-tuple-element.118), channel_id=1, source_target_pairs={{0,8},{1,9},{2,10},{3,11},{4,12},{5,13},{6,14},{7,15},{8,0},{9,1},... | collective-permute-start | bytes 1179656 | tf_op jit(solution)/shard_map/ppermute | solution.py:54
  102.0 14.8 %collective-permute-start.24 = (bf16[128,1536]{1,0:T(8,128)(2,1)S(1)}, bf16[128,1536]{1,0:T(8,128)(2,1)S(1)}, u32[]{:S(2)}, u32[]{:S(2)}) collective-permute-start(bf16[128,1536]{1,0:T(8,128)(2,1)S(1)} %get-tuple-element.120), channel_id=1, source_target_pairs={{0,20},{1,21},{2,22},{3,23},{4,16},{5,17},{6,18},{7,19},{8,28},{9,... | collective-permute-start | bytes 1179656 | tf_op jit(solution)/shard_map/ppermute | solution.py:54
  105.2 14.4 %collective-permute-start.25 = (bf16[12,3072]{1,0:T(8,128)(2,1)S(1)}, bf16[12,3072]{1,0:T(8,128)(2,1)S(1)}, u32[]{:S(2)}, u32[]{:S(2)}) collective-permute-start(bf16[12,3072]{1,0:T(8,128)(2,1)S(1)} %get-tuple-element.110), channel_id=1, source_target_pairs={{0,24},{1,25},{2,26},{3,27},{4,184},{5,185},{6,186},{7,187},{8,72}... | collective-permute-start | bytes 221192 | tf_op jit(solution)/shard_map/ppermute | solution.py:54
  107.1 12.4 %collective-permute-start.26 = (bf16[12,3072]{1,0:T(8,128)(2,1)S(1)}, bf16[12,3072]{1,0:T(8,128)(2,1)S(1)}, u32[]{:S(2)}, u32[]{:S(2)}) collective-permute-start(bf16[12,3072]{1,0:T(8,128)(2,1)S(1)} %get-tuple-element.114), channel_id=1, source_target_pairs={{0,28},{1,29},{2,30},{3,31},{4,188},{5,189},{6,190},{7,191},{8,76}... | collective-permute-start | bytes 221192 | tf_op jit(solution)/shard_map/ppermute | solution.py:54
